TPU v7x, 32 devices: a whole 2x2x4 slice. The times are simulated.
32 devices in a mesh: row: 2 (over x), col: 8 (over z, core), pole: 2 (over y).
Axes of the slice: x: 2, y: 2, z: 4, core: 2. Of those that a mesh axis runs over, the one named last changes fastest.
Arguments:
- inv_block: bfloat16 [2, 16384, 16384], P('pole', 'row', 'col'), may hold values from -6 to 6
- block_masks: int32 [2, 128, 128], P(None, 'row', 'col'), may hold values 0 or 1
- panel_first: bfloat16 [2, 16384, 512], P('pole', 'row'), may hold values from -0.046875 to 0.046875
- panel_second: bfloat16 [2, 16384, 512], P('pole', 'row'), may hold values from -0.046875 to 0.046875
- diag_inverse: bfloat16 [2, 2, 512, 512], P(None, 'pole'), may hold values from -6 to 6
- weights: float32 [2], P('pole'), may hold values from 0.3 to 1.2
Outputs:
- density_panels: bfloat16 [2, 16384, 512], P(None, ('row', 'col', 'pole'))
- density_diag: float32 [2, 512, 512], replicated
All inputs are finite; a program needn't handle non-finite values. No bound on the sum of `block_masks` on one device may be relied on, other than what follows from the above.
Results may differ from a plain program's by a relative error of at most 0.0043.
Values may be sent and summed in bfloat16 or wider, within the bound.
No kernel may reach another device: no remote copies, remote signals or barrier semaphores. Data moves between devices by JAX's collectives and lax.ppermute only.
A program may use at most 192 MiB of HBM per device.

v0:
```python
import jax
import jax.numpy as jnp
from jax import lax
from jax.sharding import PartitionSpec as P


def from_root(block, axis, owner):
    block = jnp.where(lax.axis_index(axis) == owner, block, jnp.zeros_like(block))
    return lax.psum(block, axis)


def apply_mask(inverse, mask_rows):
    row_count, col_count = inverse.shape
    block_size = row_count // mask_rows.shape[0]
    shaped = inverse.reshape(mask_rows.shape[0], block_size, mask_rows.shape[1], block_size)
    mask_bf = mask_rows.astype(jnp.bfloat16)[:, None, :, None]
    return (shaped * mask_bf).reshape(row_count, col_count)


def local_partial(inverse, mask_rows, factor):
    col_count = inverse.shape[1]
    n_row = lax.axis_size("row")
    n_col = lax.axis_size("col")
    col_ratio = n_col // n_row
    col_idx = lax.axis_index("col")
    offset = col_idx % col_ratio * col_count
    factor_piece = lax.dynamic_slice_in_dim(factor, offset, col_count, 0)
    factor_cols = from_root(factor_piece, "row", col_idx // col_ratio)
    masked = apply_mask(inverse, mask_rows)
    return jnp.dot(masked, factor_cols, preferred_element_type=jnp.float32)


def panel_sum(partial_value, factor, diag_inv, weight):
    n_row = lax.axis_size("row")
    n_col = lax.axis_size("col")
    diag_share = diag_inv.astype(jnp.float32) / (n_row * n_col)
    inner_term = jnp.dot(
        factor.astype(jnp.float32).T, partial_value, precision=lax.Precision.HIGHEST
    )
    result = lax.psum_scatter(
        weight * partial_value, ("col", "pole"), scatter_dimension=0, tiled=True
    )
    diag_term = weight * (diag_share - inner_term)
    return (result, diag_term)


def body(inv_block, block_masks, panel_first, panel_second, diag_inverse, weights):
    inverse = inv_block[0]
    weight = weights[0]
    partial_value = local_partial(inverse, block_masks[0], panel_first[0])
    dens_first, diag_term = panel_sum(partial_value, panel_first[0], diag_inverse[0, 0], weight)
    diag_first = lax.psum(diag_term, ("row", "col", "pole"))
    squares = lax.psum(jnp.sum(dens_first * dens_first, axis=0), ("row", "col", "pole"))
    total_rows = (
        dens_first.shape[0] * lax.axis_size("row") * lax.axis_size("col") * lax.axis_size("pole")
    )
    col_scale = jnp.sqrt(squares / total_rows + 1e-06)
    rescaled = (panel_second[0] / col_scale).astype(jnp.bfloat16)
    partial_second = local_partial(inverse, block_masks[1], rescaled)
    dens_second, diag_term_second = panel_sum(partial_second, rescaled, diag_inverse[1, 0], weight)
    diag_second = lax.psum(diag_term_second, ("row", "col", "pole"))
    density_panels = jnp.stack([dens_first, dens_second]).astype(jnp.bfloat16)
    density_diag = jnp.stack([diag_first, diag_second])
    return (density_panels, density_diag)


def solution(mesh):
    placed = (
        P("pole", "row", "col"),
        P(None, "row", "col"),
        P("pole", "row", None),
        P("pole", "row", None),
        P(None, "pole", None, None),
        P("pole"),
    )
    return jax.shard_map(
        body,
        mesh=mesh,
        in_specs=placed,
        out_specs=(P(None, ("row", "col", "pole"), None), P()),
        check_vma=False,
    )
```

profile of v0, /device:TPU:0, one launch (start us, length us, event | category | flops | bytes accessed | tf_op | source)
XLA Modules:
  0.0 807.2 jit_solution(3751553496048421852)
XLA Ops:
  7.2 0.0 all-reduce.5.cloned.1.call-start
  7.2 3.3 select_bitcast_fusion
  10.5 0.0 all-reduce.5.cloned.1.call-update
  10.5 0.0 reduce-scatter.3.cloned.1.call-start
  11.2 0.7 convert.13
  12.0 0.1 copy.8
  12.1 64.4 %all-reduce.5.cloned.1.call-done = bf16[2048,512]{1,0:T(8,128)(2,1)} async-done(((bf16[2048,512]{1,0:T(8,128)(2,1)}), bf16[2048,512]{1,0:T(8,128)(2,1)}) %all-reduce.5.cloned.1.call-update) | async-done | bytes 2097168 | tf_op jit(solution)/shard_map/psum | solution.py:9
  76.5 0.0 copy-start.1
  76.5 11.2 %mul.50 = bf16[64,128,16,128]{3,2,1,0:T(8,128)(2,1)} broadcast(bf16[64,16]{1,0:T(8,128)(2,1)S(1)} %copy.8), dimensions={0,2} | broadcast | bytes 33556480 | tf_op jit(solution)/shard_map/mul | solution.py:17
  87.7 0.0 copy-done.1
  87.7 34.9 %broadcast_multiply_fusion.1 = (f32[8192,512]{1,0:T(8,128)}, f32[8192,512]{1,0:T(8,128)}) fusion(f32[]{:T(128)} %bitcast.73, bf16[2048,512]{1,0:T(8,128)(2,1)S(1)} %copy-done.1, bf16[1024,8,16,128]{3,2,1,0:T(8,128)(2,1)} %bitcast.77, bf16[1,8192,2048]{2,1,0:T(8,128)(2,1)} %param.6), kind=kOutput, calls=%fused_computation.13 | convolution fusion | flops 17200840704 | bytes 102760448 | tf_op jit(solution)/shard_map/dot_general | solution.py:30
  122.6 0.0 copy-start
  122.6 0.0 reduce-scatter.3.cloned.1.call-update
  122.6 0.0 all-reduce.7.cloned.1.call-start
  122.7 178.7 %reduce-scatter.3.cloned.1.call-done = f32[512,512]{1,0:T(8,128)} async-done(((f32[8192,512]{1,0:T(8,128)}), f32[512,512]{1,0:T(8,128)}) %reduce-scatter.3.cloned.1.call-update) | async-done | bytes 1048592 | tf_op jit(solution)/shard_map/reduce_scatter | solution.py:40
  301.4 1.7 convert_bitcast_fusion.1
  303.1 39.1 %psum.36 = f32[512]{0:T(512)S(1)} all-reduce(f32[512]{0:T(512)S(1)} %get-tuple-element.9), channel_id=1, replica_groups=mesh['row'=2,'col'=8,'pole'=2] {'row','col','pole'}, use_global_device_ids=true, to_apply=%region_3.4 | all-reduce | flops 512 | bytes 4096 | tf_op jit(solution)/shard_map/psum | solution.py:53
  342.2 8.3 %fusion.6 = bf16[8192,512]{1,0:T(8,128)(2,1)} fusion(bf16[1,8192,512]{2,1,0:T(8,128)(2,1)} %param.9, f32[512]{0:T(512)S(1)} %add_sqrt_fusion), kind=kLoop, calls=%fused_computation.9 | loop fusion | flops 12582912 | bytes 16779264 | tf_op jit(solution)/shard_map/convert_element_type | solution.py:58
  350.6 3.3 dynamic-slice_select_fusion
  353.8 0.0 all-reduce.7.cloned.1.call-update
  353.9 0.2 all-reduce.9.cloned.1.call-start
  354.1 0.1 copy.9
  354.2 0.0 copy-done
  354.2 0.1 fusion.23
  354.3 0.2 copy.15
  354.5 0.2 copy.16
  354.7 18.8 %fusion.20 = f32[1,512,512]{1,2,0:T(8,128)} fusion(f32[8192,512]{1,0:T(8,128)} %get-tuple-element.13, bf16[1,8192,512]{2,1,0:T(8,128)(2,1)} %param.8, bf16[1,1,512,512]{2,3,1,0:T(8,128)(2,1)S(1)} %copy.15, f32[]{:T(128)} %bitcast.74), kind=kOutput, calls=%fused_computation.23 | convolution fusion | flops 25770852352 | bytes 26738692 | tf_op jit(solution)/shard_map/dot_general | solution.py:37
  373.5 43.2 %all-reduce.7.cloned.1.call-done = bf16[2048,512]{1,0:T(8,128)(2,1)} async-done(((bf16[2048,512]{1,0:T(8,128)(2,1)}), bf16[2048,512]{1,0:T(8,128)(2,1)}) %all-reduce.7.cloned.1.call-update) | async-done | bytes 2097168 | tf_op jit(solution)/shard_map/psum | solution.py:9
  416.7 11.2 %mul.55 = bf16[64,128,16,128]{3,2,1,0:T(8,128)(2,1)} broadcast(bf16[64,16]{1,0:T(8,128)(2,1)S(1)} %copy.9), dimensions={0,2} | broadcast | bytes 33556480 | tf_op jit(solution)/shard_map/mul | solution.py:17
  427.9 35.4 %broadcast_multiply_fusion = (f32[8192,512]{1,0:T(8,128)}, f32[8192,512]{1,0:T(8,128)}) fusion(f32[]{:T(128)} %bitcast.75, bf16[2048,512]{1,0:T(8,128)(2,1)} %all-reduce.7.cloned.1.call-done, bf16[1024,8,16,128]{3,2,1,0:T(8,128)(2,1)} %bitcast.78, bf16[1,8192,2048]{2,1,0:T(8,128)(2,1)} %param.6), kind=kOutput, calls=%fused_computation.12 | convolution fusion | flops 17200840704 | bytes 102760448 | tf_op jit(solution)/shard_map/dot_general | solution.py:30
  463.3 18.8 %fusion.10 = f32[1,512,512]{1,2,0:T(8,128)} fusion(bf16[8192,512]{1,0:T(8,128)(2,1)} %fusion.6, f32[8192,512]{1,0:T(8,128)} %get-tuple-element.15, bf16[1,1,512,512]{2,3,1,0:T(8,128)(2,1)S(1)} %copy.16, f32[]{:T(128)} %bitcast.76), kind=kOutput, calls=%fused_computation.19 | convolution fusion | flops 25770852352 | bytes 26738692 | tf_op jit(solution)/shard_map/dot_general | solution.py:37
  482.1 0.0 all-reduce.9.cloned.1.call-update
  482.2 0.0 reduce-scatter.5.cloned.1.call-start
  482.2 0.5 reduce-scatter.5.cloned.1.call-update
  482.8 133.6 %all-reduce.9.cloned.1.call-done = (f32[1,512,512]{1,2,0:T(8,128)}, f32[1,512,512]{1,2,0:T(8,128)}) async-done(((f32[1,512,512]{1,2,0:T(8,128)}, f32[1,512,512]{1,2,0:T(8,128)}), (f32[1,512,512]{1,2,0:T(8,128)}, f32[1,512,512]{1,2,0:T(8,128)})) %all-reduce.9.cloned.1.call-update) | async-done | bytes 2097168 | tf_op jit(solution)/shard_map/psum | solution.py:61
  616.3 1.7 pad_maximum_fusion
  618.0 1.8 copy.13
  619.9 178.5 %reduce-scatter.5.cloned.1.call-done = f32[512,512]{1,0:T(8,128)} async-done(((f32[8192,512]{1,0:T(8,128)}), f32[512,512]{1,0:T(8,128)}) %reduce-scatter.5.cloned.1.call-update) | async-done | bytes 1048592 | tf_op jit(solution)/shard_map/reduce_scatter | solution.py:40
  798.3 1.3 convert_bitcast_fusion
  799.6 1.1 pad_maximum_fusion.1
  (2 shorter events, 0.0 us)
Async XLA Ops:
  7.2 69.3 %all-reduce.5.cloned.1.call-start = ((), (), s32[]{:S(2)}) async-start(), calls=%async_computation.2 | async-start | bytes 4194304 | tf_op jit(solution)/shard_map/psum | solution.py:9
  10.5 290.8 %reduce-scatter.3.cloned.1.call-start = ((), (), s32[]{:S(2)}) async-start(), calls=%async_computation.3 | async-start | bytes 17825792 | tf_op jit(solution)/shard_map/reduce_scatter | solution.py:40
  76.5 11.2 %copy-start.1 = (bf16[2048,512]{1,0:T(8,128)(2,1)S(1)}, bf16[2048,512]{1,0:T(8,128)(2,1)}, u32[]{:S(2)}) copy-start(bf16[2048,512]{1,0:T(8,128)(2,1)} %all-reduce.5.cloned.1.call-done) | copy-start | bytes 6291460
  122.6 231.6 %copy-start = (bf16[2,1,512,512]{3,2,1,0:T(8,128)(2,1)S(1)}, bf16[2,1,512,512]{3,2,1,0:T(8,128)(2,1)}, u32[]{:S(2)}) copy-start(bf16[2,1,512,512]{3,2,1,0:T(8,128)(2,1)} %param.10) | copy-start | bytes 3145732
  122.6 294.1 %all-reduce.7.cloned.1.call-start = ((), (), s32[]{:S(2)}) async-start(), calls=%async_computation.4 | async-start | bytes 4194304 | tf_op jit(solution)/shard_map/psum | solution.py:9
  353.9 262.5 %all-reduce.9.cloned.1.call-start = ((), (), s32[]{:S(2)}) async-start(), calls=%async_computation.6 | async-start | bytes 4194304 | tf_op jit(solution)/shard_map/psum | solution.py:61
  482.2 316.2 %reduce-scatter.5.cloned.1.call-start = ((), (), s32[]{:S(2)}) async-start(), calls=%async_computation.5 | async-start | bytes 17825792 | tf_op jit(solution)/shard_map/reduce_scatter | solution.py:40
Sparse Core Ops, SparseCore 0:
  10.9 65.5 all-reduce.4
  122.7 178.5 reduce-scatter.2
  354.0 62.6 all-reduce.6
  482.3 133.9 all-reduce.8
  620.8 177.4 reduce-scatter.4
where the time goes:
time: 808 us; the launch traced here: 807 us
  waiting for transfers between devices  599 us (74%)
  matrix products  108 us (13%)
  blocking collectives  39.1 us (5%)
  local copies, waits for them, and re-layouts  24.9 us (3%)
  other arithmetic  21.4 us (3%)
  between operations  14.5 us (2%)
    reduce_scatter x2, waiting for transfers between devices, panel_sum(): lax.psum_scatter(weight * partial_value, ('col', 'pole'), scatter_dimensi...  357 us
    psum x1, waiting for transfers between devices, body(): diag_second = lax.psum(diag_term_second, ('row', 'col', 'pole'))  134 us
    psum x2, waiting for transfers between devices, from_root(): return lax.psum(block, axis)  108 us
    dot_general x2, matrix products, local_partial(): return jnp.dot(masked, factor_cols, preferred_element_type=jnp.float32)  70.4 us
    psum x1, blocking collectives, body(): lax.psum(jnp.sum(dens_first * dens_first, axis=0), ('row', 'col', 'pole'))  39.1 us
    dot_general x2, matrix products, panel_sum(): jnp.dot(factor.astype(jnp.float32).T, partial_value, precision=lax.Precis...  37.6 us
    mul x2, local copies, waits for them, and re-layouts, apply_mask(): return (shaped * mask_bf).reshape(row_count, col_count)  22.3 us
  transfers between devices with their start and end apart: 5, of which 5 were waited for; matrix products, arithmetic and copies ran while one was open for 3% of the time, Pallas kernels for 0%

commit v1 on v0

v1 whole, which is shorter than its diff:
```python
import functools

import jax
import jax.numpy as jnp
from jax import lax
from jax.experimental import pallas as pl
from jax.experimental.pallas import tpu as pltpu
from jax.sharding import PartitionSpec as P

CORES = 2
CHUNKS = 2


def shift(x, axis, step):
    size = lax.axis_size(axis)
    return lax.ppermute(x, axis, [(i, (i + step) % size) for i in range(size)])


def swap_core(x):
    size = lax.axis_size("col")
    return lax.ppermute(x, "col", [(i, i ^ 1) for i in range(size)])


def shift_z(x, step):
    size = lax.axis_size("col") // CORES
    pairs = [(i, ((i // CORES + step) % size) * CORES + i % CORES) for i in range(size * CORES)]
    return lax.ppermute(x, "col", pairs)


def after(x, *deps):
    return lax.optimization_barrier((x,) + deps)[0]


def product_kernel(zs, where_ref, weight_ref, a_ref, mask_ref, own_ref, recv_ref, away_ref, here_ref, f_ref):
    step = pl.program_id(0)

    @pl.when(jnp.logical_and(step == 0, where_ref[2] == 1))
    def _():
        f_ref[...] = own_ref[...]

    @pl.when(jnp.logical_and(step == 0, where_ref[2] == 0))
    def _():
        f_ref[...] = recv_ref[...]

    rows, cols = a_ref.shape
    groups = mask_ref.shape[1]
    shaped = a_ref[...].reshape(groups, rows // groups, cols)
    masked = (shaped * mask_ref[0][:, None, :]).reshape(rows, cols)
    part = jnp.dot(masked, f_ref[...], preferred_element_type=jnp.float32) * weight_ref[0]

    @pl.when(step < zs)
    def _():
        away_ref[...] = part.astype(away_ref.dtype)

    @pl.when(step >= zs)
    def _():
        here_ref[...] = part


def product(inverse, mask, own, recv, place, weight, n_pole):
    rows, cols = inverse.shape
    width = own.shape[1]
    blocks, groups, _ = mask.shape
    zs = blocks // (CORES * n_pole)
    block = rows // blocks

    def block_of(i, where):
        core = jnp.where(i < zs, 1 - where[0], where[0])
        return (lax.rem(i, zs) * CORES + core) * n_pole + where[1]

    return pl.pallas_call(
        functools.partial(product_kernel, zs),
        out_shape=(
            jax.ShapeDtypeStruct((zs * block, width), jnp.bfloat16),
            jax.ShapeDtypeStruct((zs * block, width), jnp.float32),
        ),
        grid_spec=pltpu.PrefetchScalarGridSpec(
            num_scalar_prefetch=1,
            grid=(CORES * zs,),
            in_specs=[
                pl.BlockSpec(memory_space=pltpu.SMEM),
                pl.BlockSpec((block, cols), lambda i, w: (block_of(i, w), 0)),
                pl.BlockSpec((1, groups, cols), lambda i, w: (block_of(i, w), 0, 0)),
                pl.BlockSpec((cols, width), lambda i, w: (0, 0)),
                pl.BlockSpec((cols, width), lambda i, w: (0, 0)),
            ],
            out_specs=(
                pl.BlockSpec((block, width), lambda i, w: (jnp.minimum(i, zs - 1), 0)),
                pl.BlockSpec((block, width), lambda i, w: (jnp.maximum(i - zs, 0), 0)),
            ),
            scratch_shapes=[pltpu.VMEM((cols, width), jnp.bfloat16)],
        ),
        compiler_params=pltpu.CompilerParams(vmem_limit_bytes=40 * 2**20),
        cost_estimate=pl.CostEstimate(
            flops=2 * CORES * zs * block * cols * width,
            bytes_accessed=2 * CORES * zs * block * cols + 6 * zs * block * width + 4 * cols * width,
            transcendentals=0,
        ),
    )(place, weight, inverse, mask, own, recv)


def sum_axes(x):
    x = x + swap_core(x)
    for axis in ("row", "pole"):
        x = x + sum(shift(x, axis, d) for d in range(1, lax.axis_size(axis)))
    return x + sum(shift_z(x, d) for d in range(1, lax.axis_size("col") // CORES))


def pick(x, index, axis):
    return lax.dynamic_index_in_dim(x, index, axis, keepdims=False)


def scatter_diag(term, diag, weight, ids):
    row, z, core, pole = ids
    n_row, n_pole = lax.axis_size("row"), lax.axis_size("pole")
    zs = lax.axis_size("col") // CORES
    size, width = term.shape
    split = (n_row, zs, CORES, n_pole, size // (n_row * zs * CORES * n_pole), width)
    term = term.reshape(split)
    send = pick(term, 1 - core, 2).astype(jnp.bfloat16)
    term = pick(term, core, 2) + swap_core(send)
    sends = [pick(term, (row + d) % n_row, 0).astype(jnp.bfloat16) for d in range(1, n_row)]
    term = pick(term, row, 0) + sum(shift(s, "row", d + 1).astype(jnp.float32) for d, s in enumerate(sends))
    sends = [pick(term, (z + d) % zs, 0).astype(jnp.bfloat16) for d in range(1, zs)]
    term = pick(term, z, 0) + sum(shift_z(s, d + 1).astype(jnp.float32) for d, s in enumerate(sends))
    base = pick(pick(pick(diag.reshape(split), row, 0), z, 0), core, 0).astype(jnp.float32) * weight
    both = jnp.stack([base, term], axis=1)
    sends = [pick(both, (pole + d) % n_pole, 0) for d in range(1, n_pole)]
    both = pick(both, pole, 0) + sum(shift(s, "pole", d + 1) for d, s in enumerate(sends))
    return both[0], both[1]


def gather_diag(piece):
    return lax.all_gather(piece.astype(jnp.bfloat16), ("row", "col", "pole"), axis=0, tiled=True).astype(jnp.float32)


def body(inv_block, block_masks, panel_first, panel_second, diag_inverse, weights):
    n_row, n_col, n_pole = (lax.axis_size(a) for a in ("row", "col", "pole"))
    row, col, pole = (lax.axis_index(a) for a in ("row", "col", "pole"))
    zs = n_col // CORES
    z, core = col // CORES, col % CORES
    inverse, weight = inv_block[0], weights[0]
    rows, cols = inverse.shape
    width = panel_first.shape[2]
    piece = width // CHUNKS
    blocks = n_col * n_pole
    block = rows // blocks
    ratio = n_col // n_row
    owner = col // ratio
    panels = (panel_first[0], panel_second[0])
    grain = rows // block_masks.shape[1]
    groups = max(1, block // grain)
    fine = block // groups
    mask = jnp.repeat(block_masks.astype(jnp.bfloat16), grain // fine, axis=1)
    mask = jnp.repeat(mask, grain, axis=2).reshape(2, blocks, groups, cols)
    mine = (row == owner).astype(jnp.int32)

    order = [(k, n) for k in range(2) for n in range(CHUNKS)]
    own, got = {}, {}
    last = None
    for k, n in order:
        start = (col % ratio) * cols
        src = lax.dynamic_slice(panels[k], (start, n * piece), (cols, piece))
        own[k, n] = src
        if last is not None:
            src = after(src, last)
        total = None
        for d in range(1, n_row):
            pairs = []
            for j in range(n_col):
                first = j // ratio
                pairs.append((first * n_col + j, ((first + d) % n_row) * n_col + j))
            arrived = lax.ppermute(src, ("row", "col"), pairs)
            total = arrived if total is None else total + arrived
        got[k, n] = src if total is None else total
        last = got[k, n]

    weight_arr = weights.reshape(1)
    local = [p.reshape(zs, CORES, n_pole, block, width) for p in panels]

    def rows_of(k, dest):
        picked = pick(pick(local[k], core, 1), dest, 1)
        return picked.reshape(zs * block, width)

    finals, terms = {}, {}
    for k, n in order:
        merged, arrived = {}, []
        for d in list(range(1, n_pole)) + [0]:
            dest = (pole + d) % n_pole
            place = jnp.stack([core, dest, mine]).astype(jnp.int32)
            away, here = product(inverse, mask[k], own[k, n], got[k, n], place, weight_arr, n_pole)
            merged[d] = here + swap_core(away).astype(jnp.float32)
            if d > 0:
                arrived.append(shift(merged[d].astype(jnp.bfloat16), "pole", d))
        term = 0.0
        for d in range(n_pole):
            term = term + lax.dot_general(
                rows_of(k, (pole + d) % n_pole), merged[d].astype(jnp.bfloat16),
                (((0,), (0,)), ((), ())), preferred_element_type=jnp.float32,
            )
        terms[k, n] = -term
        total = merged[0] + sum(a.astype(jnp.float32) for a in arrived)
        total = total.reshape(zs, block, piece)
        sends = [pick(total, (z + d) % zs, 0).astype(jnp.bfloat16) for d in range(1, zs)]
        final = pick(total, z, 0)
        for d, s in enumerate(sends):
            final = final + shift_z(s, d + 1).astype(jnp.float32)
        finals[k, n] = final

    dens = [jnp.concatenate([finals[k, n] for n in range(CHUNKS)], axis=1) for k in range(2)]
    squares = sum_axes(jnp.sum(dens[0] * dens[0], axis=0))
    scale = jnp.sqrt(squares / (rows * n_row) + 1e-06)
    out = jnp.stack([dens[0].astype(jnp.bfloat16), (dens[1] / scale).astype(jnp.bfloat16)])

    ids = (row, z, core, pole)
    pieces = []
    for k in range(2):
        term = jnp.concatenate([terms[k, n] for n in range(CHUNKS)], axis=1)
        base, inner = scatter_diag(term, diag_inverse[k, 0], weight, ids)
        if k == 1:
            index = ((row * n_col + col) * n_pole + pole) * base.shape[0]
            inner = inner / (lax.dynamic_slice(scale, (index,), (base.shape[0],))[:, None] * scale)
        pieces.append(gather_diag(base + inner))
    return out, jnp.stack(pieces)


def solution(mesh):
    placed = (
        P("pole", "row", "col"),
        P(None, "row", "col"),
        P("pole", "row", None),
        P("pole", "row", None),
        P(None, "pole", None, None),
        P("pole"),
    )
    return jax.shard_map(
        body,
        mesh=mesh,
        in_specs=placed,
        out_specs=(P(None, ("row", "col", "pole"), None), P()),
        check_vma=False,
    )
```

time: 808 us -> 437 us (0.54)
  waiting for transfers between devices: 599 us -> 85.2 us
  blocking collectives: 39.1 us -> 147 us
  matrix products: 108 us -> 9.82 us
  Pallas kernels: 0 us -> 91.8 us
  starting transfers between devices: 0.39 us -> 56.8 us
  between operations: 14.5 us -> 2.25 us
    reduce_scatter x2 -> x0, waiting for transfers between devices: 357 us -> none  [panel_sum(): lax.psum_scatter(weight * partial_value, ('col', 'pole'), scatter_dimensi...]
    psum x3 -> x0, waiting for transfers between devices: 241 us -> none  [the longest x1 134 us: body(): diag_second = lax.psum(diag_term_second, ('row', 'col', 'pole'))]
    all_gather x0 -> x2, blocking collectives: none -> 147 us  [gather_diag(): lax.all_gather(piece.astype(jnp.bfloat16), ('row', 'col', 'pole'), axis=0...]
    dot_general x4 -> x8, matrix products: 108 us -> 9.82 us  [body(): lax.dot_general(rows_of(k, (pole + d) % n_pole), merged[d].astype(jnp.bfl...]
    pallas_call x0 -> x8, Pallas kernels: none -> 91.8 us  [product(): pl.pallas_call(functools.partial(product_kernel, zs), out_shape=(jax.Shap...]
    ppermute x0 -> x46, waiting for transfers between devices: none -> 85.2 us  [the longest x21 38.4 us: shift_z(): return lax.ppermute(x, 'col', pairs)]
    ppermute x0 -> x46, starting transfers between devices: none -> 56.8 us  [the longest x21 27.8 us: shift_z(): return lax.ppermute(x, 'col', pairs)]
    psum x1 -> x0, blocking collectives: 39.1 us -> none  [body(): lax.psum(jnp.sum(dens_first * dens_first, axis=0), ('row', 'col', 'pole'))]
  transfers between devices with their start and end apart: 5 -> 46, of which waited for: 5 -> 15; matrix products, arithmetic and copies ran while one was open for 3% -> 11% of each run, Pallas kernels for 0% -> 21%
where the time goes in v1:
time: 437 us; the launch traced here: 435 us
  blocking collectives  147 us (34%)
  Pallas kernels  91.8 us (21%)
  waiting for transfers between devices  85.2 us (19%)
  starting transfers between devices  56.8 us (13%)
  local copies, waits for them, and re-layouts  25.6 us (6%)
  other arithmetic  17.2 us (4%)
  matrix products  9.82 us (2%)
    all_gather x2, blocking collectives, gather_diag(): lax.all_gather(piece.astype(jnp.bfloat16), ('row', 'col', 'pole'), axis=0...  147 us
    pallas_call x8, Pallas kernels, product(): pl.pallas_call(functools.partial(product_kernel, zs), out_shape=(jax.Shap...  91.8 us
    ppermute x21, waiting for transfers between devices, shift_z(): return lax.ppermute(x, 'col', pairs)  38.4 us
    ppermute x10, waiting for transfers between devices, shift(): return lax.ppermute(x, axis, [(i, (i + step) % size) for i in range(size)])  33 us
    ppermute x21, starting transfers between devices, shift_z(): return lax.ppermute(x, 'col', pairs)  27.8 us
    ppermute x4, starting transfers between devices, body(): arrived = lax.ppermute(src, ('row', 'col'), pairs)  15.1 us
    ppermute x4, waiting for transfers between devices, body(): arrived = lax.ppermute(src, ('row', 'col'), pairs)  13.3 us
    ppermute x10, starting transfers between devices, shift(): return lax.ppermute(x, axis, [(i, (i + step) % size) for i in range(size)])  11.8 us
  transfers between devices with their start and end apart: 46, of which 15 were waited for; matrix products, arithmetic and copies ran while one was open for 11% of the time, Pallas kernels for 21%

profile of v1, /device:TPU:0, one launch (start us, length us, event | category | flops | bytes accessed | tf_op | source)
XLA Modules:
  0.0 435.3 jit_solution(9989470614557075179)
XLA Ops:
  0.7 1.8 dynamic-slice_bitcast_fusion.3
  2.4 5.8 %collective-permute-start = (bf16[2048,256]{1,0:T(8,128)(2,1)S(1)}, bf16[2048,256]{1,0:T(8,128)(2,1)}, u32[]{:S(2)}, u32[]{:S(2)}) collective-permute-start(bf16[2048,256]{1,0:T(8,128)(2,1)S(1)} %get-tuple-element.48.own_ref), channel_id=1, source_target_pairs={{0,16},{2,18},{4,20},{6,22},{24,8},{26,10},{28,12},{30,14},{1,17},... | collective-permute-start | bytes 3145736 | tf_op jit(solution)/shard_map/ppermute | solution.py:173
  9.2 4.5 %constant_dynamic-slice_fusion.1 = (bf16[4,1,1,512,512]{4,3,2,1,0:T(8,128)(2,1)}, bf16[4,1,1,512,512]{4,3,2,1,0:T(8,128)(2,1)}) fusion(bf16[4,2,2,512,512]{4,3,2,1,0:T(8,128)(2,1)} %bitcast.201, s32[]{:T(128)S(6)} %select_n.239, s32[]{:T(128)S(6)} %select_n.241, s32[]{:T(128)S(6)} %select_n.243), kind=kLoop, calls=%fused_computation.132 | loop fusion | bytes 8388620 | tf_op jit(solution)/shard_map/jit(dynamic_index_in_dim)/dynamic_slice | solution.py:110
  13.7 2.6 dynamic-slice_bitcast_fusion.1
  16.4 13.3 %collective-permute-done.recv_ref = bf16[2048,256]{1,0:T(8,128)(2,1)} collective-permute-done((bf16[2048,256]{1,0:T(8,128)(2,1)S(1)}, bf16[2048,256]{1,0:T(8,128)(2,1)}, u32[]{:S(2)}, u32[]{:S(2)}) %collective-permute-start) | collective-permute-done | bytes 1048608 | tf_op jit(solution)/shard_map/ppermute | solution.py:173
  29.7 5.6 %collective-permute-start.7 = (bf16[2048,256]{1,0:T(8,128)(2,1)S(1)}, bf16[2048,256]{1,0:T(8,128)(2,1)}, u32[]{:S(2)}, u32[]{:S(2)}) collective-permute-start(bf16[2048,256]{1,0:T(8,128)(2,1)S(1)} %get-tuple-element.25.own_ref), channel_id=1, source_target_pairs={{0,16},{2,18},{4,20},{6,22},{24,8},{26,10},{28,12},{30,14},{1,17},... | collective-permute-start | bytes 3145736 | tf_op jit(solution)/shard_map/ppermute | solution.py:173
  38.1 1.6 broadcast_in_dim.12
  39.7 1.7 broadcast_in_dim.13.mask_ref
  41.4 2.5 constant_dynamic-slice_fusion.3
  43.9 11.5 %shard_map.78 = (bf16[2048,256]{1,0:T(8,128)(2,1)S(1)}, f32[2048,256]{1,0:T(8,128)S(1)}) custom-call(s32[3]{0:T(128)S(1)} %get-tuple-element.75.where_ref, f32[1]{0:T(128)} %copy.26.weight_ref, bf16[8192,2048]{1,0:T(8,128)(2,1)} %bitcast.181, bf16[16,4,2048]{2,1,0:T(4,128)(2,1)S(1)} %copy-done.8, bf16[2048,256]{1,0:T(8,128)(2,1)S(1)} %get-tuple-element.48.own_ref, ...), custom_call_target="tpu_custom_call" | custom-call | flops 4294967296 | bytes 22020096 | tf_op jit(solution)/shard_map/pallas_call | solution.py:71
  55.6 11.5 %shard_map.77 = (bf16[2048,256]{1,0:T(8,128)(2,1)S(1)}, f32[2048,256]{1,0:T(8,128)S(1)}) custom-call(s32[3]{0:T(128)S(1)} %get-tuple-element.74.where_ref, f32[1]{0:T(128)} %copy.26.weight_ref, bf16[8192,2048]{1,0:T(8,128)(2,1)} %bitcast.182, bf16[16,4,2048]{2,1,0:T(4,128)(2,1)S(1)} %copy-done.8, bf16[2048,256]{1,0:T(8,128)(2,1)S(1)} %get-tuple-element.48.own_ref, ...), custom_call_target="tpu_custom_call" | custom-call | flops 4294967296 | bytes 22020096 | tf_op jit(solution)/shard_map/pallas_call | solution.py:71
  67.7 1.3 collective-permute-start.14
  69.1 11.5 %shard_map.80 = (bf16[2048,256]{1,0:T(8,128)(2,1)S(1)}, f32[2048,256]{1,0:T(8,128)S(1)}) custom-call(s32[3]{0:T(128)S(1)} %get-tuple-element.75.where_ref, f32[1]{0:T(128)} %copy.26.weight_ref, bf16[8192,2048]{1,0:T(8,128)(2,1)} %bitcast.183, bf16[16,4,2048]{2,1,0:T(4,128)(2,1)S(1)} %copy-done.8, bf16[2048,256]{1,0:T(8,128)(2,1)S(1)} %get-tuple-element.25.own_ref, ...), custom_call_target="tpu_custom_call" | custom-call | flops 4294967296 | bytes 22020096 | tf_op jit(solution)/shard_map/pallas_call | solution.py:71
  80.7 11.5 %shard_map.79 = (bf16[2048,256]{1,0:T(8,128)(2,1)S(1)}, f32[2048,256]{1,0:T(8,128)S(1)}) custom-call(s32[3]{0:T(128)S(1)} %get-tuple-element.74.where_ref, f32[1]{0:T(128)} %copy.26.weight_ref, bf16[8192,2048]{1,0:T(8,128)(2,1)} %bitcast.184, bf16[16,4,2048]{2,1,0:T(4,128)(2,1)S(1)} %copy-done.8, bf16[2048,256]{1,0:T(8,128)(2,1)S(1)} %get-tuple-element.25.own_ref, ...), custom_call_target="tpu_custom_call" | custom-call | flops 4294967296 | bytes 22020096 | tf_op jit(solution)/shard_map/pallas_call | solution.py:71
  92.8 2.7 add_convert_fusion.3
  95.5 1.5 collective-permute-start.3
  97.0 2.0 fusion.65
  99.9 2.4 collective-permute-start.21
  102.2 1.3 add_convert_fusion.2
  104.0 2.0 fusion.66
  107.1 1.1 pad_maximum_fusion.1
  108.1 2.5 copy.22
  110.7 1.1 fusion.36
  111.9 9.9 %collective-permute-done.3 = bf16[2048,256]{1,0:T(8,128)(2,1)} collective-permute-done((bf16[2048,256]{1,0:T(8,128)(2,1)}, bf16[2048,256]{1,0:T(8,128)(2,1)}, u32[]{:S(2)}, u32[]{:S(2)}) %collective-permute-start.3) | collective-permute-done | bytes 1048608 | tf_op jit(solution)/shard_map/ppermute | solution.py:16
  121.8 1.8 convert_add_fusion.6
  123.6 11.3 %shard_map.82 = (bf16[2048,256]{1,0:T(8,128)(2,1)S(1)}, f32[2048,256]{1,0:T(8,128)S(1)}) custom-call(s32[3]{0:T(128)S(1)} %get-tuple-element.75.where_ref, f32[1]{0:T(128)} %copy.26.weight_ref, bf16[8192,2048]{1,0:T(8,128)(2,1)} %bitcast.185, bf16[16,4,2048]{2,1,0:T(4,128)(2,1)S(1)} %broadcast_in_dim.15.mask_ref, bf16[2048,256]{1,0:T(8,128)(2,1)S(1)} %copy-done.1, ...), custom_call_target="tpu_custom_call" | custom-call | flops 4294967296 | bytes 22020096 | tf_op jit(solution)/shard_map/pallas_call | solution.py:71
  135.1 11.3 %shard_map.81 = (bf16[2048,256]{1,0:T(8,128)(2,1)S(1)}, f32[2048,256]{1,0:T(8,128)S(1)}) custom-call(s32[3]{0:T(128)S(1)} %get-tuple-element.74.where_ref, f32[1]{0:T(128)} %copy.26.weight_ref, bf16[8192,2048]{1,0:T(8,128)(2,1)} %bitcast.186, bf16[16,4,2048]{2,1,0:T(4,128)(2,1)S(1)} %broadcast_in_dim.15.mask_ref, bf16[2048,256]{1,0:T(8,128)(2,1)S(1)} %copy-done.1, ...), custom_call_target="tpu_custom_call" | custom-call | flops 4294967296 | bytes 22020096 | tf_op jit(solution)/shard_map/pallas_call | solution.py:71
  146.5 4.2 collective-permute-start.38
  150.6 1.0 collective-permute-start.36
  152.2 4.2 collective-permute-start.6
  157.5 5.7 %collective-permute-done.6 = bf16[512,256]{1,0:T(8,128)(2,1)S(1)} collective-permute-done((bf16[512,256]{1,0:T(8,128)(2,1)S(1)}, bf16[512,256]{1,0:T(8,128)(2,1)S(1)}, u32[]{:S(2)}, u32[]{:S(2)}) %collective-permute-start.6) | collective-permute-done | bytes 262176 | tf_op jit(solution)/shard_map/ppermute | solution.py:27
  163.2 14.5 %collective-permute-done.5 = bf16[512,256]{1,0:T(8,128)(2,1)S(1)} collective-permute-done((bf16[512,256]{1,0:T(8,128)(2,1)S(1)}, bf16[512,256]{1,0:T(8,128)(2,1)S(1)}, u32[]{:S(2)}, u32[]{:S(2)}) %collective-permute-start.5) | collective-permute-done | bytes 262176 | tf_op jit(solution)/shard_map/ppermute | solution.py:27
  177.7 1.5 collective-permute-start.39
  180.1 2.2 collective-permute-done.39
  182.3 1.5 convert_add_fusion.4
  184.0 1.9 collective-permute-start.12
  185.8 1.9 collective-permute-start.11
  187.8 11.5 %shard_map.84 = (bf16[2048,256]{1,0:T(8,128)(2,1)S(1)}, f32[2048,256]{1,0:T(8,128)S(1)}) custom-call(s32[3]{0:T(128)S(1)} %get-tuple-element.75.where_ref, f32[1]{0:T(128)} %copy.26.weight_ref, bf16[8192,2048]{1,0:T(8,128)(2,1)} %bitcast.187, bf16[16,4,2048]{2,1,0:T(4,128)(2,1)S(1)} %broadcast_in_dim.15.mask_ref, ...), custom_call_target="tpu_custom_call" | custom-call | flops 4294967296 | bytes 22020096 | tf_op jit(solution)/shard_map/pallas_call | solution.py:71
  199.3 11.5 %shard_map.83 = (bf16[2048,256]{1,0:T(8,128)(2,1)S(1)}, f32[2048,256]{1,0:T(8,128)S(1)}) custom-call(s32[3]{0:T(128)S(1)} %get-tuple-element.74.where_ref, f32[1]{0:T(128)} %copy.26.weight_ref, bf16[8192,2048]{1,0:T(8,128)(2,1)} %bitcast.188, bf16[16,4,2048]{2,1,0:T(4,128)(2,1)S(1)} %broadcast_in_dim.15.mask_ref, ...), custom_call_target="tpu_custom_call" | custom-call | flops 4294967296 | bytes 22020096 | tf_op jit(solution)/shard_map/pallas_call | solution.py:71
  211.9 1.2 add_convert_fusion.1
  213.1 1.5 collective-permute-start.17
  215.4 2.0 fusion.67
  217.4 1.3 collective-permute-done.29
  218.7 1.5 collective-permute-start.30
  221.2 17.8 %collective-permute-done.30 = f32[512]{0:T(512)S(1)} collective-permute-done((f32[512]{0:T(512)S(1)}, f32[512]{0:T(512)S(1)}, u32[]{:S(2)}, u32[]{:S(2)}) %collective-permute-start.30) | collective-permute-done | bytes 2080 | tf_op jit(solution)/shard_map/ppermute | solution.py:16
  239.0 1.9 collective-permute-start.33
  241.0 1.1 collective-permute-start.32
  244.2 1.3 copy.23
  245.5 1.2 fusion.37
  246.8 69.4 %all-gather = bf16[1,512,512]{2,1,0:T(8,128)(2,1)S(1)} all-gather(bf16[1,16,512]{2,1,0:T(8,128)(2,1)S(1)} %fusion.61), channel_id=2, replica_groups=mesh['row'=2,'col'=8,'pole'=2] {'row','col','pole'}, dimensions={1}, use_global_device_ids=true | all-gather | bytes 540672 | tf_op jit(solution)/shard_map/all_gather | solution.py:134
  316.3 1.1 bitcast_add_fusion
  317.5 1.8 collective-permute-start.41
  319.3 1.5 convert_add_fusion.2
  320.8 1.7 collective-permute-done.41
  322.8 1.9 collective-permute-start.42
  324.8 2.4 collective-permute-start.20
  327.9 2.0 collective-permute-start.18
  330.1 3.1 collective-permute-start.45
  333.9 16.5 %collective-permute-done.19 = bf16[512,256]{1,0:T(8,128)(2,1)S(1)} collective-permute-done((bf16[512,256]{1,0:T(8,128)(2,1)S(1)}, bf16[512,256]{1,0:T(8,128)(2,1)S(1)}, u32[]{:S(2)}, u32[]{:S(2)}) %collective-permute-start.19) | collective-permute-done | bytes 262176 | tf_op jit(solution)/shard_map/ppermute | solution.py:27
  351.2 1.5 collective-permute-start.26
  352.7 1.9 collective-permute-start.25
  354.7 77.2 %all_gather.7 = bf16[512,512]{1,0:T(8,128)(2,1)S(1)} all-gather(bf16[16,512]{1,0:T(8,128)(2,1)S(1)} %fusion.60), channel_id=1, replica_groups=mesh['row'=2,'col'=8,'pole'=2] {'row','col','pole'}, dimensions={0}, use_global_device_ids=true | all-gather | bytes 540672 | tf_op jit(solution)/shard_map/all_gather | solution.py:134
  431.8 1.5 maximum_convert_fusion
  434.3 1.1 pad_maximum_fusion
  (159 shorter events, 18.0 us)
Async XLA Ops:
  0.6 7.6 %copy-start.21 = (bf16[2,1,512,512]{3,2,1,0:T(8,128)(2,1)S(1)}, bf16[2,1,512,512]{3,2,1,0:T(8,128)(2,1)}, u32[]{:S(2)}) copy-start(bf16[2,1,512,512]{3,2,1,0:T(8,128)(2,1)} %param.10) | copy-start | bytes 3145732
  2.4 6.6 %copy-start.24 = (s32[2,64,16]{1,2,0:T(8,128)S(1)}, s32[2,64,16]{1,2,0:T(8,128)}, u32[]{:S(2)}) copy-start(s32[2,64,16]{1,2,0:T(8,128)} %param.7) | copy-start | bytes 24580
  2.4 27.3 %collective-permute-start = (bf16[2048,256]{1,0:T(8,128)(2,1)S(1)}, bf16[2048,256]{1,0:T(8,128)(2,1)}, u32[]{:S(2)}, u32[]{:S(2)}) collective-permute-start(bf16[2048,256]{1,0:T(8,128)(2,1)S(1)} %get-tuple-element.48.own_ref), channel_id=1, source_target_pairs={{0,16},{2,18},{4,20},{6,22},{24,8},{26,10},{28,12},{30,14},{1,17},... | collective-permute-start | bytes 3145736 | tf_op jit(solution)/shard_map/ppermute | solution.py:173
  29.7 38.0 %collective-permute-start.7 = (bf16[2048,256]{1,0:T(8,128)(2,1)S(1)}, bf16[2048,256]{1,0:T(8,128)(2,1)}, u32[]{:S(2)}, u32[]{:S(2)}) collective-permute-start(bf16[2048,256]{1,0:T(8,128)(2,1)S(1)} %get-tuple-element.25.own_ref), channel_id=1, source_target_pairs={{0,16},{2,18},{4,20},{6,22},{24,8},{26,10},{28,12},{30,14},{1,17},... | collective-permute-start | bytes 3145736 | tf_op jit(solution)/shard_map/ppermute | solution.py:173
  55.5 37.3 %collective-permute-start.2 = (bf16[2048,256]{1,0:T(8,128)(2,1)S(1)}, bf16[2048,256]{1,0:T(8,128)(2,1)}, u32[]{:S(2)}, u32[]{:S(2)}) collective-permute-start(bf16[2048,256]{1,0:T(8,128)(2,1)S(1)} %get-tuple-element.24), channel_id=1, source_target_pairs={{0,2},{2,0},{4,6},{6,4},{8,10},{10,8},{12,14},{14,12},{1,3},{3,1},... | collective-permute-start | bytes 3145736 | tf_op jit(solution)/shard_map/ppermute | solution.py:21
  55.6 12.1 %copy-start = (bf16[2048,256]{1,0:T(8,128)(2,1)S(1)}, bf16[2048,256]{1,0:T(8,128)(2,1)}, u32[]{:S(2)}) copy-start(bf16[2048,256]{1,0:T(8,128)(2,1)} %get-tuple-element.30.own_ref) | copy-start | bytes 3145732
  67.1 31.9 %copy-start.6 = (f32[2048,256]{1,0:T(8,128)}, f32[2048,256]{1,0:T(8,128)S(1)}, u32[]{:S(2)}) copy-start(f32[2048,256]{1,0:T(8,128)S(1)} %get-tuple-element.21) | copy-start | bytes 6291460
  67.2 31.9 %collective-permute-start.1 = (bf16[2048,256]{1,0:T(8,128)(2,1)S(1)}, bf16[2048,256]{1,0:T(8,128)(2,1)S(1)}, u32[]{:S(2)}, u32[]{:S(2)}) collective-permute-start(bf16[2048,256]{1,0:T(8,128)(2,1)S(1)} %get-tuple-element.22), channel_id=1, source_target_pairs={{0,2},{2,0},{4,6},{6,4},{8,10},{10,8},{12,14},{14,12},{1,3},{3,1},... | collective-permute-start | bytes 3145736 | tf_op jit(solution)/shard_map/ppermute | solution.py:21
  67.7 32.1 %collective-permute-start.14 = (bf16[2048,256]{1,0:T(8,128)(2,1)S(1)}, bf16[2048,256]{1,0:T(8,128)(2,1)S(1)}, u32[]{:S(2)}, u32[]{:S(2)}) collective-permute-start(bf16[2048,256]{1,0:T(8,128)(2,1)S(1)} %copy-done), channel_id=1, source_target_pairs={{0,16},{2,18},{4,20},{6,22},{24,8},{26,10},{28,12},{30,14},{1,17},... | collective-permute-start | bytes 3145736 | tf_op jit(solution)/shard_map/ppermute | solution.py:173
  80.6 21.6 %collective-permute-start.9 = (bf16[2048,256]{1,0:T(8,128)(2,1)S(1)}, bf16[2048,256]{1,0:T(8,128)(2,1)S(1)}, u32[]{:S(2)}, u32[]{:S(2)}) collective-permute-start(bf16[2048,256]{1,0:T(8,128)(2,1)S(1)} %get-tuple-element.29), channel_id=1, source_target_pairs={{0,2},{2,0},{4,6},{6,4},{8,10},{10,8},{12,14},{14,12},{1,3},{3,1},... | collective-permute-start | bytes 3145736 | tf_op jit(solution)/shard_map/ppermute | solution.py:21
  92.3 13.8 %copy-start.4 = (f32[2048,256]{1,0:T(8,128)}, f32[2048,256]{1,0:T(8,128)S(1)}, u32[]{:S(2)}) copy-start(f32[2048,256]{1,0:T(8,128)S(1)} %get-tuple-element.26) | copy-start | bytes 6291460
  92.3 13.8 %collective-permute-start.8 = (bf16[2048,256]{1,0:T(8,128)(2,1)S(1)}, bf16[2048,256]{1,0:T(8,128)(2,1)S(1)}, u32[]{:S(2)}, u32[]{:S(2)}) collective-permute-start(bf16[2048,256]{1,0:T(8,128)(2,1)S(1)} %get-tuple-element.27), channel_id=1, source_target_pairs={{0,2},{2,0},{4,6},{6,4},{8,10},{10,8},{12,14},{14,12},{1,3},{3,1},... | collective-permute-start | bytes 3145736 | tf_op jit(solution)/shard_map/ppermute | solution.py:21
  95.5 26.3 %collective-permute-start.3 = (bf16[2048,256]{1,0:T(8,128)(2,1)}, bf16[2048,256]{1,0:T(8,128)(2,1)}, u32[]{:S(2)}, u32[]{:S(2)}) collective-permute-start(bf16[2048,256]{1,0:T(8,128)(2,1)} %add_convert_fusion.3), channel_id=1, source_target_pairs={{0,1},{1,0},{2,3},{3,2},{4,5},{5,4},{6,7},{7,6},{8,9},{9,8},{10,11... | collective-permute-start | bytes 3145736 | tf_op jit(solution)/shard_map/ppermute | solution.py:16
  99.1 7.0 %copy-start.18 = (bf16[2048,256]{1,0:T(8,128)(2,1)}, bf16[2048,256]{1,0:T(8,128)(2,1)S(1)}, u32[]{:S(2)}) copy-start(bf16[2048,256]{1,0:T(8,128)(2,1)S(1)} %collective-permute-done.1) | copy-start | bytes 3145732
  99.9 3.7 copy-start.9
  99.9 85.9 %collective-permute-start.21 = (bf16[2048,256]{1,0:T(8,128)(2,1)S(1)}, bf16[2048,256]{1,0:T(8,128)(2,1)}, u32[]{:S(2)}, u32[]{:S(2)}) collective-permute-start(bf16[2048,256]{1,0:T(8,128)(2,1)S(1)} %get-tuple-element.35.own_ref), channel_id=1, source_target_pairs={{0,16},{2,18},{4,20},{6,22},{24,8},{26,10},{28,12},{30,14},{1,17},... | collective-permute-start | bytes 3145736 | tf_op jit(solution)/shard_map/ppermute | solution.py:173
  103.5 78.7 %collective-permute-start.10 = (bf16[2048,256]{1,0:T(8,128)(2,1)}, bf16[2048,256]{1,0:T(8,128)(2,1)}, u32[]{:S(2)}, u32[]{:S(2)}) collective-permute-start(bf16[2048,256]{1,0:T(8,128)(2,1)} %add_convert_fusion.2), channel_id=1, source_target_pairs={{0,1},{1,0},{2,3},{3,2},{4,5},{5,4},{6,7},{7,6},{8,9},{9,8},{10,11... | collective-permute-start | bytes 3145736 | tf_op jit(solution)/shard_map/ppermute | solution.py:16
  107.1 14.7 %copy-start.7 = (f32[2048,256]{1,0:T(8,128)S(1)}, f32[2048,256]{1,0:T(8,128)}, u32[]{:S(2)}) copy-start(f32[2048,256]{1,0:T(8,128)} %copy-done.6) | copy-start | bytes 6291460
  111.8 11.8 %copy-start.1 = (bf16[2048,256]{1,0:T(8,128)(2,1)S(1)}, bf16[2048,256]{1,0:T(8,128)(2,1)}, u32[]{:S(2)}) copy-start(bf16[2048,256]{1,0:T(8,128)(2,1)} %get-tuple-element.30.own_ref) | copy-start | bytes 3145732
  111.8 11.8 %copy-start.10 = (bf16[2048,256]{1,0:T(8,128)(2,1)S(1)}, bf16[2048,256]{1,0:T(8,128)(2,1)}, u32[]{:S(2)}) copy-start(bf16[2048,256]{1,0:T(8,128)(2,1)} %copy-done.9) | copy-start | bytes 3145732
  111.8 23.1 %collective-permute-start.34 = (bf16[2,4,2,16,512]{4,3,2,1,0:T(8,128)(2,1)S(1)}, bf16[2,4,2,16,512]{4,3,2,1,0:T(8,128)(2,1)S(1)}, u32[]{:S(2)}, u32[]{:S(2)}) collective-permute-start(bf16[2,4,2,16,512]{4,3,2,1,0:T(8,128)(2,1)S(1)} %fusion.36), channel_id=1, source_target_pairs={{0,2},{2,0},{4,6},{6,4},{8,10},{10,8},{12,14},{14,12},{1,3},{3,1},... | collective-permute-start | bytes 786440 | tf_op jit(solution)/shard_map/ppermute | solution.py:21
  123.6 11.3 %copy-start.19 = (f32[512,512]{1,0:T(8,128)S(1)}, f32[512,512]{1,0:T(8,128)}, u32[]{:S(2)}) copy-start(f32[512,512]{1,0:T(8,128)} %copy.22) | copy-start | bytes 3145732
  135.0 11.3 %collective-permute-start.35 = (bf16[4,2,16,512]{3,2,1,0:T(8,128)(2,1)S(1)}, bf16[4,2,16,512]{3,2,1,0:T(8,128)(2,1)S(1)}, u32[]{:S(2)}, u32[]{:S(2)}) collective-permute-start(bf16[4,2,16,512]{3,2,1,0:T(8,128)(2,1)S(1)} %fusion.38), channel_id=1, source_target_pairs={{0,16},{16,0},{1,17},{17,1},{2,18},{18,2},{3,19},{19,3},{4,20},{20... | collective-permute-start | bytes 393224 | tf_op jit(solution)/shard_map/ppermute | solution.py:16
  146.5 5.8 %collective-permute-start.38 = (bf16[2,16,512]{2,1,0:T(8,128)(2,1)S(1)}, bf16[2,16,512]{2,1,0:T(8,128)(2,1)S(1)}, u32[]{:S(2)}, u32[]{:S(2)}) collective-permute-start(bf16[2,16,512]{2,1,0:T(8,128)(2,1)S(1)} %get-tuple-element.67), channel_id=1, source_target_pairs={{0,12},{2,14},{4,0},{6,2},{8,4},{10,6},{12,8},{14,10},{1,13},{3,15... | collective-permute-start | bytes 98312 | tf_op jit(solution)/shard_map/ppermute | solution.py:27
  150.6 5.8 %collective-permute-start.37 = (bf16[2,16,512]{2,1,0:T(8,128)(2,1)S(1)}, bf16[2,16,512]{2,1,0:T(8,128)(2,1)S(1)}, u32[]{:S(2)}, u32[]{:S(2)}) collective-permute-start(bf16[2,16,512]{2,1,0:T(8,128)(2,1)S(1)} %get-tuple-element.68), channel_id=1, source_target_pairs={{0,8},{2,10},{4,12},{6,14},{8,0},{10,2},{12,4},{14,6},{1,9},{3,11}... | collective-permute-start | bytes 98312 | tf_op jit(solution)/shard_map/ppermute | solution.py:27
  150.6 6.0 %collective-permute-start.36 = (bf16[2,16,512]{2,1,0:T(8,128)(2,1)S(1)}, bf16[2,16,512]{2,1,0:T(8,128)(2,1)S(1)}, u32[]{:S(2)}, u32[]{:S(2)}) collective-permute-start(bf16[2,16,512]{2,1,0:T(8,128)(2,1)S(1)} %get-tuple-element.66), channel_id=1, source_target_pairs={{0,4},{2,6},{4,8},{6,10},{8,12},{10,14},{12,0},{14,2},{1,5},{3,7},... | collective-permute-start | bytes 98312 | tf_op jit(solution)/shard_map/ppermute | solution.py:27
  151.7 30.6 %copy-start.5 = (f32[2048,256]{1,0:T(8,128)S(1)}, f32[2048,256]{1,0:T(8,128)}, u32[]{:S(2)}) copy-start(f32[2048,256]{1,0:T(8,128)} %copy-done.4) | copy-start | bytes 6291460
  151.7 30.6 %copy-start.17 = (bf16[2048,256]{1,0:T(8,128)(2,1)S(1)}, bf16[2048,256]{1,0:T(8,128)(2,1)}, u32[]{:S(2)}) copy-start(bf16[2048,256]{1,0:T(8,128)(2,1)} %copy-done.16) | copy-start | bytes 3145732
  152.2 11.0 %collective-permute-start.6 = (bf16[512,256]{1,0:T(8,128)(2,1)S(1)}, bf16[512,256]{1,0:T(8,128)(2,1)S(1)}, u32[]{:S(2)}, u32[]{:S(2)}) collective-permute-start(bf16[512,256]{1,0:T(8,128)(2,1)S(1)} %get-tuple-element.53), channel_id=1, source_target_pairs={{0,12},{2,14},{4,0},{6,2},{8,4},{10,6},{12,8},{14,10},{1,13},{3,15... | collective-permute-start | bytes 786440 | tf_op jit(solution)/shard_map/ppermute | solution.py:27
  156.5 21.3 %collective-permute-start.5 = (bf16[512,256]{1,0:T(8,128)(2,1)S(1)}, bf16[512,256]{1,0:T(8,128)(2,1)S(1)}, u32[]{:S(2)}, u32[]{:S(2)}) collective-permute-start(bf16[512,256]{1,0:T(8,128)(2,1)S(1)} %get-tuple-element.54), channel_id=1, source_target_pairs={{0,8},{2,10},{4,12},{6,14},{8,0},{10,2},{12,4},{14,6},{1,9},{3,11}... | collective-permute-start | bytes 786440 | tf_op jit(solution)/shard_map/ppermute | solution.py:27
  156.7 21.0 %collective-permute-start.4 = (bf16[512,256]{1,0:T(8,128)(2,1)S(1)}, bf16[512,256]{1,0:T(8,128)(2,1)S(1)}, u32[]{:S(2)}, u32[]{:S(2)}) collective-permute-start(bf16[512,256]{1,0:T(8,128)(2,1)S(1)} %get-tuple-element.52), channel_id=1, source_target_pairs={{0,4},{2,6},{4,8},{6,10},{8,12},{10,14},{12,0},{14,2},{1,5},{3,7},... | collective-permute-start | bytes 786440 | tf_op jit(solution)/shard_map/ppermute | solution.py:27
  163.2 48.6 %collective-permute-start.16 = (bf16[2048,256]{1,0:T(8,128)(2,1)S(1)}, bf16[2048,256]{1,0:T(8,128)(2,1)S(1)}, u32[]{:S(2)}, u32[]{:S(2)}) collective-permute-start(bf16[2048,256]{1,0:T(8,128)(2,1)S(1)} %get-tuple-element.34), channel_id=1, source_target_pairs={{0,2},{2,0},{4,6},{6,4},{8,10},{10,8},{12,14},{14,12},{1,3},{3,1},... | collective-permute-start | bytes 3145736 | tf_op jit(solution)/shard_map/ppermute | solution.py:21
  177.7 42.5 %collective-permute-start.15 = (bf16[2048,256]{1,0:T(8,128)(2,1)S(1)}, bf16[2048,256]{1,0:T(8,128)(2,1)S(1)}, u32[]{:S(2)}, u32[]{:S(2)}) collective-permute-start(bf16[2048,256]{1,0:T(8,128)(2,1)S(1)} %get-tuple-element.32), channel_id=1, source_target_pairs={{0,2},{2,0},{4,6},{6,4},{8,10},{10,8},{12,14},{14,12},{1,3},{3,1},... | collective-permute-start | bytes 3145736 | tf_op jit(solution)/shard_map/ppermute | solution.py:21
  177.7 4.5 %collective-permute-start.39 = (f32[2,16,512]{2,1,0:T(8,128)S(1)}, f32[2,16,512]{2,1,0:T(8,128)S(1)}, u32[]{:S(2)}, u32[]{:S(2)}) collective-permute-start(f32[2,16,512]{2,1,0:T(8,128)S(1)} %fusion.46), channel_id=1, source_target_pairs={{0,1},{1,0},{2,3},{3,2},{4,5},{5,4},{6,7},{7,6},{8,9},{9,8},{10,11... | collective-permute-start | bytes 196616 | tf_op jit(solution)/shard_map/ppermute | solution.py:16
  183.9 27.0 %collective-permute-start.13 = (bf16[512,256]{1,0:T(8,128)(2,1)S(1)}, bf16[512,256]{1,0:T(8,128)(2,1)S(1)}, u32[]{:S(2)}, u32[]{:S(2)}) collective-permute-start(bf16[512,256]{1,0:T(8,128)(2,1)S(1)} %get-tuple-element.56), channel_id=1, source_target_pairs={{0,12},{2,14},{4,0},{6,2},{8,4},{10,6},{12,8},{14,10},{1,13},{3,15... | collective-permute-start | bytes 786440 | tf_op jit(solution)/shard_map/ppermute | solution.py:27
  184.0 27.0 %collective-permute-start.12 = (bf16[512,256]{1,0:T(8,128)(2,1)S(1)}, bf16[512,256]{1,0:T(8,128)(2,1)S(1)}, u32[]{:S(2)}, u32[]{:S(2)}) collective-permute-start(bf16[512,256]{1,0:T(8,128)(2,1)S(1)} %get-tuple-element.57), channel_id=1, source_target_pairs={{0,8},{2,10},{4,12},{6,14},{8,0},{10,2},{12,4},{14,6},{1,9},{3,11}... | collective-permute-start | bytes 786440 | tf_op jit(solution)/shard_map/ppermute | solution.py:27
  185.8 25.6 %collective-permute-start.11 = (bf16[512,256]{1,0:T(8,128)(2,1)S(1)}, bf16[512,256]{1,0:T(8,128)(2,1)S(1)}, u32[]{:S(2)}, u32[]{:S(2)}) collective-permute-start(bf16[512,256]{1,0:T(8,128)(2,1)S(1)} %get-tuple-element.55), channel_id=1, source_target_pairs={{0,4},{2,6},{4,8},{6,10},{8,12},{10,14},{12,0},{14,2},{1,5},{3,7},... | collective-permute-start | bytes 786440 | tf_op jit(solution)/shard_map/ppermute | solution.py:27
  210.8 32.3 %copy-start.2 = (f32[2048,256]{1,0:T(8,128)}, f32[2048,256]{1,0:T(8,128)S(1)}, u32[]{:S(2)}) copy-start(f32[2048,256]{1,0:T(8,128)S(1)} %get-tuple-element.36) | copy-start | bytes 6291460
  210.9 30.1 %collective-permute-start.23 = (bf16[2048,256]{1,0:T(8,128)(2,1)S(1)}, bf16[2048,256]{1,0:T(8,128)(2,1)S(1)}, u32[]{:S(2)}, u32[]{:S(2)}) collective-permute-start(bf16[2048,256]{1,0:T(8,128)(2,1)S(1)} %get-tuple-element.39), channel_id=1, source_target_pairs={{0,2},{2,0},{4,6},{6,4},{8,10},{10,8},{12,14},{14,12},{1,3},{3,1},... | collective-permute-start | bytes 3145736 | tf_op jit(solution)/shard_map/ppermute | solution.py:21
  211.0 32.2 %collective-permute-start.22 = (bf16[2048,256]{1,0:T(8,128)(2,1)S(1)}, bf16[2048,256]{1,0:T(8,128)(2,1)S(1)}, u32[]{:S(2)}, u32[]{:S(2)}) collective-permute-start(bf16[2048,256]{1,0:T(8,128)(2,1)S(1)} %get-tuple-element.37), channel_id=1, source_target_pairs={{0,2},{2,0},{4,6},{6,4},{8,10},{10,8},{12,14},{14,12},{1,3},{3,1},... | collective-permute-start | bytes 3145736 | tf_op jit(solution)/shard_map/ppermute | solution.py:21
  211.7 3.4 collective-permute-start.28
  213.1 7.1 %copy-start.11 = (bf16[4,1,1,512,512]{4,3,2,1,0:T(8,128)(2,1)S(1)}, bf16[4,1,1,512,512]{4,3,2,1,0:T(8,128)(2,1)}, u32[]{:S(2)}) copy-start(bf16[4,1,1,512,512]{4,3,2,1,0:T(8,128)(2,1)} %get-tuple-element.46) | copy-start | bytes 6291460
  213.1 106.2 %collective-permute-start.17 = (bf16[2048,256]{1,0:T(8,128)(2,1)}, bf16[2048,256]{1,0:T(8,128)(2,1)}, u32[]{:S(2)}, u32[]{:S(2)}) collective-permute-start(bf16[2048,256]{1,0:T(8,128)(2,1)} %add_convert_fusion.1), channel_id=1, source_target_pairs={{0,1},{1,0},{2,3},{3,2},{4,5},{5,4},{6,7},{7,6},{8,9},{9,8},{10,11... | collective-permute-start | bytes 3145736 | tf_op jit(solution)/shard_map/ppermute | solution.py:16
  215.1 3.6 collective-permute-start.29
  218.7 20.3 %collective-permute-start.30 = (f32[512]{0:T(512)S(1)}, f32[512]{0:T(512)S(1)}, u32[]{:S(2)}, u32[]{:S(2)}) collective-permute-start(f32[512]{0:T(512)S(1)} %add.444), channel_id=1, source_target_pairs={{0,1},{1,0},{2,3},{3,2},{4,5},{5,4},{6,7},{7,6},{8,9},{9,8},{10,11... | collective-permute-start | bytes 6152 | tf_op jit(solution)/shard_map/ppermute | solution.py:16
  239.0 77.2 %collective-permute-start.33 = (f32[512]{0:T(512)S(1)}, f32[512]{0:T(512)S(1)}, u32[]{:S(2)}, u32[]{:S(2)}) collective-permute-start(f32[512]{0:T(512)S(1)} %add.445), channel_id=1, source_target_pairs={{0,12},{2,14},{4,0},{6,2},{8,4},{10,6},{12,8},{14,10},{1,13},{3,15... | collective-permute-start | bytes 6152 | tf_op jit(solution)/shard_map/ppermute | solution.py:27
  240.8 75.4 %collective-permute-start.31 = (f32[512]{0:T(512)S(1)}, f32[512]{0:T(512)S(1)}, u32[]{:S(2)}, u32[]{:S(2)}) collective-permute-start(f32[512]{0:T(512)S(1)} %add.445), channel_id=1, source_target_pairs={{0,4},{2,6},{4,8},{6,10},{8,12},{10,14},{12,0},{14,2},{1,5},{3,7},... | collective-permute-start | bytes 6152 | tf_op jit(solution)/shard_map/ppermute | solution.py:27
  241.0 75.2 %collective-permute-start.32 = (f32[512]{0:T(512)S(1)}, f32[512]{0:T(512)S(1)}, u32[]{:S(2)}, u32[]{:S(2)}) collective-permute-start(f32[512]{0:T(512)S(1)} %add.445), channel_id=1, source_target_pairs={{0,8},{2,10},{4,12},{6,14},{8,0},{10,2},{12,4},{14,6},{1,9},{3,11}... | collective-permute-start | bytes 6152 | tf_op jit(solution)/shard_map/ppermute | solution.py:27
  245.5 73.8 %copy-start.15 = (bf16[2048,256]{1,0:T(8,128)(2,1)S(1)}, bf16[2048,256]{1,0:T(8,128)(2,1)}, u32[]{:S(2)}) copy-start(bf16[2048,256]{1,0:T(8,128)(2,1)} %copy-done.14) | copy-start | bytes 3145732
  246.7 69.6 %collective-permute-start.40 = (bf16[2,4,2,16,512]{4,3,2,1,0:T(8,128)(2,1)S(1)}, bf16[2,4,2,16,512]{4,3,2,1,0:T(8,128)(2,1)S(1)}, u32[]{:S(2)}, u32[]{:S(2)}) collective-permute-start(bf16[2,4,2,16,512]{4,3,2,1,0:T(8,128)(2,1)S(1)} %fusion.37), channel_id=1, source_target_pairs={{0,2},{2,0},{4,6},{6,4},{8,10},{10,8},{12,14},{14,12},{1,3},{3,1},... | collective-permute-start | bytes 786440 | tf_op jit(solution)/shard_map/ppermute | solution.py:21
  316.3 34.4 %collective-permute-start.24 = (bf16[2048,256]{1,0:T(8,128)(2,1)}, bf16[2048,256]{1,0:T(8,128)(2,1)S(1)}, u32[]{:S(2)}, u32[]{:S(2)}) collective-permute-start(bf16[2048,256]{1,0:T(8,128)(2,1)} %copy-done.22), channel_id=1, source_target_pairs={{0,1},{1,0},{2,3},{3,2},{4,5},{5,4},{6,7},{7,6},{8,9},{9,8},{10,11... | collective-permute-start | bytes 3145736 | tf_op jit(solution)/shard_map/ppermute | solution.py:16
  317.5 5.0 %collective-permute-start.41 = (bf16[4,2,16,512]{3,2,1,0:T(8,128)(2,1)S(1)}, bf16[4,2,16,512]{3,2,1,0:T(8,128)(2,1)S(1)}, u32[]{:S(2)}, u32[]{:S(2)}) collective-permute-start(bf16[4,2,16,512]{3,2,1,0:T(8,128)(2,1)S(1)} %fusion.39), channel_id=1, source_target_pairs={{0,16},{16,0},{1,17},{17,1},{2,18},{18,2},{3,19},{19,3},{4,20},{20... | collective-permute-start | bytes 393224 | tf_op jit(solution)/shard_map/ppermute | solution.py:16
  322.6 4.6 %collective-permute-start.44 = (bf16[2,16,512]{2,1,0:T(8,128)(2,1)S(1)}, bf16[2,16,512]{2,1,0:T(8,128)(2,1)S(1)}, u32[]{:S(2)}, u32[]{:S(2)}) collective-permute-start(bf16[2,16,512]{2,1,0:T(8,128)(2,1)S(1)} %get-tuple-element.70), channel_id=1, source_target_pairs={{0,12},{2,14},{4,0},{6,2},{8,4},{10,6},{12,8},{14,10},{1,13},{3,15... | collective-permute-start | bytes 98312 | tf_op jit(solution)/shard_map/ppermute | solution.py:27
  322.7 28.1 %copy-start.3 = (f32[2048,256]{1,0:T(8,128)S(1)}, f32[2048,256]{1,0:T(8,128)}, u32[]{:S(2)}) copy-start(f32[2048,256]{1,0:T(8,128)} %copy-done.2) | copy-start | bytes 6291460
  322.7 28.1 %copy-start.13 = (bf16[2048,256]{1,0:T(8,128)(2,1)S(1)}, bf16[2048,256]{1,0:T(8,128)(2,1)}, u32[]{:S(2)}) copy-start(bf16[2048,256]{1,0:T(8,128)(2,1)} %copy-done.12) | copy-start | bytes 3145732
  322.7 5.2 %collective-permute-start.43 = (bf16[2,16,512]{2,1,0:T(8,128)(2,1)S(1)}, bf16[2,16,512]{2,1,0:T(8,128)(2,1)S(1)}, u32[]{:S(2)}, u32[]{:S(2)}) collective-permute-start(bf16[2,16,512]{2,1,0:T(8,128)(2,1)S(1)} %get-tuple-element.71), channel_id=1, source_target_pairs={{0,8},{2,10},{4,12},{6,14},{8,0},{10,2},{12,4},{14,6},{1,9},{3,11}... | collective-permute-start | bytes 98312 | tf_op jit(solution)/shard_map/ppermute | solution.py:27
  322.8 7.3 %collective-permute-start.42 = (bf16[2,16,512]{2,1,0:T(8,128)(2,1)S(1)}, bf16[2,16,512]{2,1,0:T(8,128)(2,1)S(1)}, u32[]{:S(2)}, u32[]{:S(2)}) collective-permute-start(bf16[2,16,512]{2,1,0:T(8,128)(2,1)S(1)} %get-tuple-element.69), channel_id=1, source_target_pairs={{0,4},{2,6},{4,8},{6,10},{8,12},{10,14},{12,0},{14,2},{1,5},{3,7},... | collective-permute-start | bytes 98312 | tf_op jit(solution)/shard_map/ppermute | solution.py:27
  324.8 9.2 %collective-permute-start.20 = (bf16[512,256]{1,0:T(8,128)(2,1)S(1)}, bf16[512,256]{1,0:T(8,128)(2,1)S(1)}, u32[]{:S(2)}, u32[]{:S(2)}) collective-permute-start(bf16[512,256]{1,0:T(8,128)(2,1)S(1)} %get-tuple-element.59), channel_id=1, source_target_pairs={{0,12},{2,14},{4,0},{6,2},{8,4},{10,6},{12,8},{14,10},{1,13},{3,15... | collective-permute-start | bytes 786440 | tf_op jit(solution)/shard_map/ppermute | solution.py:27
  327.2 23.3 %collective-permute-start.19 = (bf16[512,256]{1,0:T(8,128)(2,1)S(1)}, bf16[512,256]{1,0:T(8,128)(2,1)S(1)}, u32[]{:S(2)}, u32[]{:S(2)}) collective-permute-start(bf16[512,256]{1,0:T(8,128)(2,1)S(1)} %get-tuple-element.60), channel_id=1, source_target_pairs={{0,8},{2,10},{4,12},{6,14},{8,0},{10,2},{12,4},{14,6},{1,9},{3,11}... | collective-permute-start | bytes 786440 | tf_op jit(solution)/shard_map/ppermute | solution.py:27
  327.9 22.6 %collective-permute-start.18 = (bf16[512,256]{1,0:T(8,128)(2,1)S(1)}, bf16[512,256]{1,0:T(8,128)(2,1)S(1)}, u32[]{:S(2)}, u32[]{:S(2)}) collective-permute-start(bf16[512,256]{1,0:T(8,128)(2,1)S(1)} %get-tuple-element.58), channel_id=1, source_target_pairs={{0,4},{2,6},{4,8},{6,10},{8,12},{10,14},{12,0},{14,2},{1,5},{3,7},... | collective-permute-start | bytes 786440 | tf_op jit(solution)/shard_map/ppermute | solution.py:27
  330.1 20.5 %collective-permute-start.45 = (f32[2,16,512]{2,1,0:T(8,128)S(1)}, f32[2,16,512]{2,1,0:T(8,128)S(1)}, u32[]{:S(2)}, u32[]{:S(2)}) collective-permute-start(f32[2,16,512]{2,1,0:T(8,128)S(1)} %fusion.41), channel_id=1, source_target_pairs={{0,1},{1,0},{2,3},{3,2},{4,5},{5,4},{6,7},{7,6},{8,9},{9,8},{10,11... | collective-permute-start | bytes 196616 | tf_op jit(solution)/shard_map/ppermute | solution.py:16
  351.1 82.2 %collective-permute-start.27 = (bf16[512,256]{1,0:T(8,128)(2,1)S(1)}, bf16[512,256]{1,0:T(8,128)(2,1)S(1)}, u32[]{:S(2)}, u32[]{:S(2)}) collective-permute-start(bf16[512,256]{1,0:T(8,128)(2,1)S(1)} %get-tuple-element.62), channel_id=1, source_target_pairs={{0,12},{2,14},{4,0},{6,2},{8,4},{10,6},{12,8},{14,10},{1,13},{3,15... | collective-permute-start | bytes 786440 | tf_op jit(solution)/shard_map/ppermute | solution.py:27
  351.2 82.1 %collective-permute-start.26 = (bf16[512,256]{1,0:T(8,128)(2,1)S(1)}, bf16[512,256]{1,0:T(8,128)(2,1)S(1)}, u32[]{:S(2)}, u32[]{:S(2)}) collective-permute-start(bf16[512,256]{1,0:T(8,128)(2,1)S(1)} %get-tuple-element.63), channel_id=1, source_target_pairs={{0,8},{2,10},{4,12},{6,14},{8,0},{10,2},{12,4},{14,6},{1,9},{3,11}... | collective-permute-start | bytes 786440 | tf_op jit(solution)/shard_map/ppermute | solution.py:27
  352.7 80.6 %collective-permute-start.25 = (bf16[512,256]{1,0:T(8,128)(2,1)S(1)}, bf16[512,256]{1,0:T(8,128)(2,1)S(1)}, u32[]{:S(2)}, u32[]{:S(2)}) collective-permute-start(bf16[512,256]{1,0:T(8,128)(2,1)S(1)} %get-tuple-element.61), channel_id=1, source_target_pairs={{0,4},{2,6},{4,8},{6,10},{8,12},{10,14},{12,0},{14,2},{1,5},{3,7},... | collective-permute-start | bytes 786440 | tf_op jit(solution)/shard_map/ppermute | solution.py:27
  (7 other events, 11.5 us)

commit v2 on v0

v2 whole, which is shorter than its diff:
```python
import functools

import jax
import jax.numpy as jnp
from jax import lax
from jax.experimental import pallas as pl
from jax.experimental.pallas import tpu as pltpu
from jax.sharding import PartitionSpec as P

CORES = 2
PACK = 16
PARTS = ((0, 0, 2), (0, 2, 2), (1, 0, 2), (1, 2, 2))


def swap(x, axis, mask):
    size = lax.axis_size(axis)
    return lax.ppermute(x, axis, [(i, i ^ mask) for i in range(size)])


def swap_core(x, mask=1):
    return swap(x, "col", mask)


def swap_z(x, mask):
    return swap(x, "col", mask * CORES)


def swap_row(x, mask):
    return swap(x, "row", mask)


def swap_pole(x, mask):
    return swap(x, "pole", mask)


def after(x, *deps):
    if not deps:
        return x
    return lax.optimization_barrier((x,) + deps)[0]


def pick(x, index, axis):
    return lax.dynamic_index_in_dim(x, index, axis, keepdims=False)


def halve_step(sources, axis, index, bit, kind):
    size = sources[0].shape[axis]
    low = (index >> bit) & 1
    send, keep = 0.0, 0.0
    for x in sources:
        pairs = x.reshape(x.shape[:axis] + (size // 2, 2) + x.shape[axis + 1:])
        send = send + pick(pairs, 1 - low, axis + 1).astype(jnp.float32)
        keep = keep + pick(pairs, low, axis + 1).astype(jnp.float32)
    return send.astype(kind), keep


def halve(x, axis, index, exchange, kind):
    sources, bit = [x], 0
    while sources[0].shape[axis] > 1:
        send, keep = halve_step(sources, axis, index, bit, kind)
        sources = [keep, exchange(send, 1 << bit)]
        bit += 1
    x = sum(y.astype(jnp.float32) for y in sources)
    return x.reshape(x.shape[:axis] + x.shape[axis + 1:])


class ZSum:
    def __init__(self, sources, z):
        self.sources, self.z, self.bit = sources, z, 0

    def step(self):
        send, keep = halve_step(self.sources, 0, self.z, self.bit, jnp.bfloat16)
        self.sources = [keep, swap_z(send, 1 << self.bit)]
        self.bit += 1
        return send, keep

    def done(self):
        return self.sources[0].shape[0] == 1

    def result(self):
        x = sum(y.astype(jnp.float32) for y in self.sources)
        return x.reshape(x.shape[1:])


def double(x, axis, index, size, exchange):
    x = jnp.expand_dims(x, axis)
    bits = size.bit_length() - 1
    for bit in reversed(range(bits)):
        other = exchange(x, 1 << bit)
        low = (index >> bit) & 1
        both = jnp.where(low == 0, jnp.stack([x, other], axis + 1), jnp.stack([other, x], axis + 1))
        x = both.reshape(x.shape[:axis] + (2 * x.shape[axis],) + x.shape[axis + 1:])
    return x


def masked_product(a_ref, mask_ref, f_ref, weight_ref):
    rows, cols = a_ref.shape
    groups = mask_ref.shape[1]
    shaped = a_ref[...].reshape(groups, rows // (groups * PACK), PACK, cols)
    masked = (shaped * mask_ref[0][:, None]).reshape(rows, cols)
    return jnp.dot(masked, f_ref[...], preferred_element_type=jnp.float32) * weight_ref[0]


def away_kernel(where_ref, weight_ref, a_ref, mask_ref, f_ref, out_ref):
    out_ref[...] = masked_product(a_ref, mask_ref, f_ref, weight_ref).astype(out_ref.dtype)


def here_kernel(pieces, where_ref, weight_ref, a_ref, mask_ref, f_ref, recv_ref, panel_ref, start_ref, *outs):
    total = masked_product(a_ref, mask_ref, f_ref, weight_ref) + recv_ref[...].astype(jnp.float32)
    width = total.shape[1] // pieces
    for n in range(pieces):
        outs[n][...] = total[:, n * width:(n + 1) * width].astype(outs[n].dtype)
    term = lax.dot_general(
        panel_ref[...], total.astype(jnp.bfloat16), (((0,), (0,)), ((), ())), preferred_element_type=jnp.float32
    )
    term_ref = outs[pieces]

    @pl.when(pl.program_id(0) == 0)
    def _():
        term_ref[...] = start_ref[...] - term

    @pl.when(pl.program_id(0) > 0)
    def _():
        term_ref[...] = term_ref[...] - term


def product(inverse, mask, factor, place, weight, n_pole, merge=None):
    cols = inverse.shape[1]
    width = factor.shape[1]
    blocks, groups = mask.shape[:2]
    zs = blocks // (CORES * n_pole)
    block = inverse.shape[0] // blocks

    def block_of(i, where):
        return (i * CORES + where[0]) * n_pole + where[1]

    in_specs = [
        pl.BlockSpec(memory_space=pltpu.SMEM),
        pl.BlockSpec((block, cols), lambda i, w: (block_of(i, w), 0)),
        pl.BlockSpec((1, groups, PACK, cols), lambda i, w: (block_of(i, w), 0, 0, 0)),
        pl.BlockSpec((cols, width), lambda i, w: (0, 0)),
    ]
    flops = 2 * zs * block * cols
    nbytes = zs * block * width
    if merge is None:
        kernel, extra = away_kernel, ()
        out_shape = jax.ShapeDtypeStruct((zs * block, width), jnp.bfloat16)
        out_specs = pl.BlockSpec((block, width), lambda i, w: (i, 0))
    else:
        recv, panel, start, pieces, kind = merge
        extra = (recv, panel, start)
        kernel = functools.partial(here_kernel, pieces)
        full = panel.shape[1]
        in_specs += [
            pl.BlockSpec((block, width), lambda i, w: (i, 0)),
            pl.BlockSpec((block, full), lambda i, w: (block_of(i, w), 0)),
            pl.BlockSpec((full, width), lambda i, w: (0, 0)),
        ]
        piece = width // pieces
        out_shape = [jax.ShapeDtypeStruct((zs * block, piece), kind)] * pieces
        out_shape.append(jax.ShapeDtypeStruct((full, width), jnp.float32))
        out_specs = [pl.BlockSpec((block, piece), lambda i, w: (i, 0))] * pieces
        out_specs.append(pl.BlockSpec((full, width), lambda i, w: (0, 0)))
    return pl.pallas_call(
        kernel,
        out_shape=out_shape,
        grid_spec=pltpu.PrefetchScalarGridSpec(
            num_scalar_prefetch=1, grid=(zs,), in_specs=in_specs, out_specs=out_specs
        ),
        compiler_params=pltpu.CompilerParams(vmem_limit_bytes=40 * 2**20),
        cost_estimate=pl.CostEstimate(flops=flops, bytes_accessed=nbytes, transcendentals=0),
    )(place, weight, inverse, mask, factor, *extra)


def fetch_factor(panel, first, width, ids, last):
    row, col, cols = ids
    n_row, n_col = lax.axis_size("row"), lax.axis_size("col")
    zs = n_col // CORES
    ratio = n_col // n_row

    def mirror(j):
        return (zs - 1 - j // CORES) * CORES + j % CORES

    far = cols * 5 // 16 if n_row == 2 and zs > 1 else 0
    near = cols - far
    start = (col % ratio) * cols
    own = lax.dynamic_slice(panel, (start, first), (cols, width))
    parts = [(own[:near], lambda j: j)]
    if far > 0:
        other = (mirror(col) % ratio) * cols + near
        parts.append((lax.dynamic_slice(panel, (other, first), (far, width)), mirror))
    got = []
    for src, source in parts:
        if last is not None:
            src = after(src, *last)
        total = None
        for d in range(1, n_row):
            pairs = []
            for j in range(n_col):
                owner = j // ratio
                pairs.append((owner * n_col + source(j), ((owner + d) % n_row) * n_col + j))
            arrived = lax.ppermute(src, ("row", "col"), pairs)
            total = arrived if total is None else total + arrived
        got.append(src if total is None else total)
    return own, got


def body(inv_block, block_masks, panel_first, panel_second, diag_inverse, weights):
    n_row, n_col, n_pole = (lax.axis_size(a) for a in ("row", "col", "pole"))
    row, col, pole = (lax.axis_index(a) for a in ("row", "col", "pole"))
    zs = n_col // CORES
    z, core = col // CORES, col % CORES
    inverse, weight = inv_block[0], weights[0]
    rows, cols = inverse.shape
    width = panel_first.shape[2]
    quarter = width // 4
    blocks = n_col * n_pole
    block = rows // blocks
    panels = (panel_first[0], panel_second[0])
    grain = rows // block_masks.shape[1]
    groups = max(1, block // grain)
    fine = block // groups

    fetched, last = [], None
    for k, first, size in PARTS:
        own, last = fetch_factor(panels[k], first * quarter, size * quarter, (row, col, cols), last)
        fetched.append((own, last))
    mine = row == col // (n_col // n_row)

    masks = []
    for k in range(2):
        mask = jnp.repeat(block_masks[k].astype(jnp.bfloat16), grain // fine, axis=0)
        mask = jnp.repeat(mask, grain, axis=1).reshape(blocks, groups, 1, cols)
        masks.append(jnp.broadcast_to(mask, (blocks, groups, PACK, cols)))
    got, *masks = lax.optimization_barrier((fetched[0][1], *masks))
    fetched[0] = (fetched[0][0], got)

    def take(part, *deps):
        own, got = fetched[part]
        return jnp.where(mine, own, after(jnp.concatenate(got, axis=0), *deps))

    def place(c, d, *deps):
        return after(jnp.stack([c, (pole + d) % n_pole]).astype(jnp.int32), *deps)

    dests = list(range(1, n_pole)) + [0]
    factor = take(0)
    token = ()
    units = []
    terms = [[], []]
    for part, (k, first, size) in enumerate(PARTS):
        wide = size * quarter
        pieces = max(1, size // 2)
        received = {}
        for d in dests:
            away = product(inverse, masks[k], factor, place(1 - core, d, *token), weights, n_pole)
            token = (away,)
            received[d] = swap_core(away)
        term = jnp.zeros((width, wide), jnp.float32)
        arrived = [[] for _ in range(pieces)]
        upcoming = None
        final = part + 1 == len(PARTS)
        for d in sorted(dests) if final else dests:
            if d == 0:
                if not final:
                    upcoming = take(part + 1, *token)
                    token += (upcoming,)
                for unit in units:
                    if not unit.done():
                        token += unit.step()
            kind = jnp.bfloat16 if d > 0 else jnp.float32
            *out, term = product(
                inverse, masks[k], factor, place(core, d, *token), weights, n_pole,
                (received[d], panels[k], term, pieces, kind),
            )
            token = (out[0],)
            if d == 0:
                sums = out
            else:
                pairs = [(i, (i + d) % n_pole) for i in range(n_pole)]
                before = ()
                for n in range(pieces):
                    came = lax.ppermute(after(out[n], *before), "pole", pairs)
                    before = (came,)
                    arrived[n].append(came)
        terms[k].append(term)
        factor = upcoming
        for n in range(pieces):
            sources = [x.reshape(zs, block, x.shape[1]) for x in [sums[n]] + arrived[n]]
            units.append(ZSum(sources, z))
            units[-1].k = k
    finals, gate = [[], []], ()
    for unit in units:
        while not unit.done():
            sent = unit.step()
            if unit is units[-2] or unit.bit == 1:
                gate = gate[:2] + sent
        finals[unit.k].append(unit.result())

    dens = [jnp.concatenate(f, axis=1) for f in finals]
    squares = jnp.sum(dens[0] * dens[0], axis=0)
    for exchange, size in ((swap_core, CORES), (swap_row, n_row), (swap_z, zs), (swap_pole, n_pole)):
        for bit in range(size.bit_length() - 1):
            squares = squares + exchange(squares, 1 << bit)
    scale = jnp.sqrt(squares / (rows * n_row) + 1e-06)
    out = jnp.stack([dens[0].astype(jnp.bfloat16), (dens[1] / scale).astype(jnp.bfloat16)])

    each = width // (n_row * blocks)
    split = (2, n_row, zs, CORES, n_pole, each, width)
    term = jnp.stack([jnp.concatenate(t, axis=1) for t in terms]).reshape(split)
    term = halve(term, 3, core, swap_core, jnp.bfloat16)
    term = halve(term, 1, row, swap_row, jnp.bfloat16)
    term = halve(term, 1, z, swap_z, jnp.bfloat16)
    base = pick(pick(pick(diag_inverse.reshape(split), core, 3), row, 1), z, 1).astype(jnp.float32) * weight
    both = halve(jnp.stack([base, term]), 2, pole, swap_pole, jnp.float32)
    base, term = both[0], both[1]
    index = ((row * n_col + col) * n_pole + pole) * each
    inner = term[1] / (lax.dynamic_slice(scale, (index,), (each,))[:, None] * scale)
    piece = (base + jnp.stack([term[0], inner])).astype(jnp.bfloat16)
    piece = double(after(piece, *gate), 1, pole, n_pole, swap_pole)
    piece = double(piece, 1, z, zs, swap_z)
    piece = double(piece, 1, row, n_row, swap_row)
    piece = double(piece, 3, core, CORES, swap_core)
    return out, piece.reshape(2, width, width).astype(jnp.float32)


def solution(mesh):
    placed = (
        P("pole", "row", "col"),
        P(None, "row", "col"),
        P("pole", "row", None),
        P("pole", "row", None),
        P(None, "pole", None, None),
        P("pole"),
    )
    return jax.shard_map(
        body,
        mesh=mesh,
        in_specs=placed,
        out_specs=(P(None, ("row", "col", "pole"), None), P()),
        check_vma=False,
    )
```

time: 808 us -> 358 us (0.44)
  waiting for transfers between devices: 599 us -> 120 us
  Pallas kernels: 0 us -> 118 us
  matrix products: 108 us -> 0 us
  starting transfers between devices: 0.39 us -> 47.9 us
  blocking collectives: 39.1 us -> 0 us
  other arithmetic: 21.4 us -> 41.4 us
  between operations: 14.5 us -> 2.34 us
    reduce_scatter x2 -> x0, waiting for transfers between devices: 357 us -> none  [panel_sum(): lax.psum_scatter(weight * partial_value, ('col', 'pole'), scatter_dimensi...]
    psum x3 -> x0, waiting for transfers between devices: 241 us -> none  [the longest x1 134 us: body(): diag_second = lax.psum(diag_term_second, ('row', 'col', 'pole'))]
    ppermute x0 -> x43, waiting for transfers between devices: none -> 120 us  [the longest x31 76 us: swap(): return lax.ppermute(x, axis, [(i, i ^ mask) for i in range(size)])]
    pallas_call x0 -> x16, Pallas kernels: none -> 118 us  [product(): pl.pallas_call(kernel, out_shape=out_shape, grid_spec=pltpu.PrefetchScala...]
    dot_general x4 -> x0, matrix products: 108 us -> none  [the longest x2 70.4 us: local_partial(): return jnp.dot(masked, factor_cols, preferred_element_type=jnp.float32)]
    ppermute x0 -> x43, starting transfers between devices: none -> 47.9 us  [the longest x8 24.8 us: fetch_factor(): arrived = lax.ppermute(src, ('row', 'col'), pairs)]
    psum x1 -> x0, blocking collectives: 39.1 us -> none  [body(): lax.psum(jnp.sum(dens_first * dens_first, axis=0), ('row', 'col', 'pole'))]
    mul x2 -> x0, local copies, waits for them, and re-layouts: 22.3 us -> none  [apply_mask(): return (shaped * mask_bf).reshape(row_count, col_count)]
  transfers between devices with their start and end apart: 5 -> 43, of which waited for: 5 -> 18; matrix products, arithmetic and copies ran while one was open for 3% -> 12% of each run, Pallas kernels for 0% -> 29%
where the time goes in v2:
time: 358 us; the launch traced here: 356 us
  waiting for transfers between devices  120 us (34%)
  Pallas kernels  118 us (33%)
  starting transfers between devices  47.9 us (13%)
  other arithmetic  41.4 us (12%)
  local copies, waits for them, and re-layouts  26.8 us (7%)
    pallas_call x16, Pallas kernels, product(): pl.pallas_call(kernel, out_shape=out_shape, grid_spec=pltpu.PrefetchScala...  118 us
    ppermute x31, waiting for transfers between devices, swap(): return lax.ppermute(x, axis, [(i, i ^ mask) for i in range(size)])  76 us
    ppermute x8, waiting for transfers between devices, fetch_factor(): arrived = lax.ppermute(src, ('row', 'col'), pairs)  44 us
    ppermute x8, starting transfers between devices, fetch_factor(): arrived = lax.ppermute(src, ('row', 'col'), pairs)  24.8 us
    ppermute x31, starting transfers between devices, swap(): return lax.ppermute(x, axis, [(i, i ^ mask) for i in range(size)])  18.2 us
    unnamed x76, local copies, waits for them, and re-layouts  14.3 us
    convert_element_type x10, other arithmetic, halve_step(): return (send.astype(kind), keep)  10.2 us
  transfers between devices with their start and end apart: 43, of which 18 were waited for; matrix products, arithmetic and copies ran while one was open for 12% of the time, Pallas kernels for 29%

profile of v2, /device:TPU:0, one launch (start us, length us, event | category | flops | bytes accessed | tf_op | source)
XLA Modules:
  0.0 356.2 jit_solution(16982084938885393924)
XLA Ops:
  0.7 2.3 dynamic-slice_bitcast_fusion.2
  2.9 4.9 %collective-permute-start = (bf16[1408,256]{1,0:T(8,128)(2,1)S(1)}, bf16[1408,256]{1,0:T(8,128)(2,1)S(1)}, u32[]{:S(2)}, u32[]{:S(2)}) collective-permute-start(bf16[1408,256]{1,0:T(8,128)(2,1)S(1)} %get-tuple-element.103), channel_id=1, source_target_pairs={{0,16},{2,18},{4,20},{6,22},{24,8},{26,10},{28,12},{30,14},{1,17},... | collective-permute-start | bytes 2162696 | tf_op jit(solution)/shard_map/ppermute | solution.py:202
  11.2 18.9 %collective-permute-done = bf16[1408,256]{1,0:T(8,128)(2,1)S(1)} collective-permute-done((bf16[1408,256]{1,0:T(8,128)(2,1)S(1)}, bf16[1408,256]{1,0:T(8,128)(2,1)S(1)}, u32[]{:S(2)}, u32[]{:S(2)}) %collective-permute-start) | collective-permute-done | bytes 720928 | tf_op jit(solution)/shard_map/ppermute | solution.py:202
  30.2 2.6 broadcast_in_dim.31.mask_ref
  33.3 2.6 maximum_select_fusion.f_ref
  35.9 6.1 %shard_map.77 = bf16[2048,256]{1,0:T(8,128)(2,1)S(1)} custom-call(s32[2]{0:T(128)S(1)} %get-tuple-element.80.where_ref, f32[1]{0:T(128)} %copy.39.weight_ref, bf16[8192,2048]{1,0:T(8,128)(2,1)} %bitcast.184, bf16[16,4,16,2048]{3,2,1,0:T(8,128)(2,1)S(1)} %broadcast_in_dim.28.mask_ref, bf16[2048,256]{1,0:T(8,128)(2,1)S(1)} %maximum_select_fusion.f_ref), custom_call_target="tpu_custom_call" | custom-call | flops 8388608 | bytes 524288 | tf_op jit(solution)/shard_map/pallas_call | solution.py:164
  42.1 5.3 %collective-permute-start.3 = (bf16[1408,256]{1,0:T(8,128)(2,1)}, bf16[1408,256]{1,0:T(8,128)(2,1)}, u32[]{:S(2)}, u32[]{:S(2)}) collective-permute-start(bf16[1408,256]{1,0:T(8,128)(2,1)} %get-tuple-element.53), channel_id=1, source_target_pairs={{0,16},{2,18},{4,20},{6,22},{24,8},{26,10},{28,12},{30,14},{1,17},... | collective-permute-start | bytes 2162696 | tf_op jit(solution)/shard_map/ppermute | solution.py:202
  48.1 2.2 copy-done.5
  50.3 6.4 %shard_map.78 = bf16[2048,256]{1,0:T(8,128)(2,1)S(1)} custom-call(s32[2]{0:T(128)S(1)} %pad_add_fusion.where_ref, f32[1]{0:T(128)} %copy.39.weight_ref, bf16[8192,2048]{1,0:T(8,128)(2,1)} %bitcast.185, bf16[16,4,16,2048]{3,2,1,0:T(8,128)(2,1)S(1)} %copy-done.5, bf16[2048,256]{1,0:T(8,128)(2,1)S(1)} %maximum_select_fusion.f_ref), custom_call_target="tpu_custom_call" | custom-call | flops 8388608 | bytes 524288 | tf_op jit(solution)/shard_map/pallas_call | solution.py:164
  57.0 12.8 %collective-permute-done.3 = bf16[1408,256]{1,0:T(8,128)(2,1)} collective-permute-done((bf16[1408,256]{1,0:T(8,128)(2,1)}, bf16[1408,256]{1,0:T(8,128)(2,1)}, u32[]{:S(2)}, u32[]{:S(2)}) %collective-permute-start.3) | collective-permute-done | bytes 720928 | tf_op jit(solution)/shard_map/ppermute | solution.py:202
  71.1 8.8 %shard_map.79 = (bf16[2048,256]{1,0:T(8,128)(2,1)}, f32[512,256]{1,0:T(8,128)S(1)}) custom-call(s32[2]{0:T(128)S(1)} %get-tuple-element.84.where_ref, f32[1]{0:T(128)} %copy.39.weight_ref, bf16[8192,2048]{1,0:T(8,128)(2,1)} %bitcast.186, bf16[16,4,16,2048]{3,2,1,0:T(8,128)(2,1)S(1)} %copy-done.6, bf16[2048,256]{1,0:T(8,128)(2,1)S(1)} %maximum_select_fusion.f_ref, ...), custom_call_target="tpu_custom_call" | custom-call | flops 8388608 | bytes 524288 | tf_op jit(solution)/shard_map/pallas_call | solution.py:164
  79.8 1.5 collective-permute-start.6
  81.4 1.5 bitcast_select_fusion.2.f_ref
  82.8 7.7 %shard_map.80 = (f32[2048,256]{1,0:T(8,128)S(1)}, f32[512,256]{1,0:T(8,128)S(1)}) custom-call(s32[2]{0:T(128)S(1)} %pad_add_fusion.1.where_ref, f32[1]{0:T(128)} %copy.39.weight_ref, bf16[8192,2048]{1,0:T(8,128)(2,1)} %bitcast.187, bf16[16,4,16,2048]{3,2,1,0:T(8,128)(2,1)S(1)} %copy-done.6, bf16[2048,256]{1,0:T(8,128)(2,1)S(1)} %maximum_select_fusion.f_ref, ...), custom_call_target="tpu_custom_call" | custom-call | flops 8388608 | bytes 524288 | tf_op jit(solution)/shard_map/pallas_call | solution.py:164
  91.9 6.9 %shard_map.81 = bf16[2048,256]{1,0:T(8,128)(2,1)} custom-call(s32[2]{0:T(128)S(1)} %get-tuple-element.80.where_ref, f32[1]{0:T(128)} %copy.39.weight_ref, bf16[8192,2048]{1,0:T(8,128)(2,1)} %bitcast.188, bf16[16,4,16,2048]{3,2,1,0:T(8,128)(2,1)S(1)} %copy-done.6, bf16[2048,256]{1,0:T(8,128)(2,1)S(1)} %bitcast_select_fusion.2.f_ref), custom_call_target="tpu_custom_call" | custom-call | flops 8388608 | bytes 524288 | tf_op jit(solution)/shard_map/pallas_call | solution.py:164
  98.8 2.6 dynamic-slice_bitcast_fusion
  101.4 5.3 %collective-permute-start.10 = (bf16[1408,256]{1,0:T(8,128)(2,1)}, bf16[1408,256]{1,0:T(8,128)(2,1)}, u32[]{:S(2)}, u32[]{:S(2)}) collective-permute-start(bf16[1408,256]{1,0:T(8,128)(2,1)} %get-tuple-element.63), channel_id=1, source_target_pairs={{0,16},{2,18},{4,20},{6,22},{24,8},{26,10},{28,12},{30,14},{1,17},... | collective-permute-start | bytes 2162696 | tf_op jit(solution)/shard_map/ppermute | solution.py:202
  106.6 1.8 dynamic-slice_bitcast_fusion.4
  109.8 6.9 %shard_map.82 = bf16[2048,256]{1,0:T(8,128)(2,1)} custom-call(s32[2]{0:T(128)S(1)} %pad_add_fusion.where_ref, f32[1]{0:T(128)} %copy.39.weight_ref, bf16[8192,2048]{1,0:T(8,128)(2,1)} %bitcast.189, bf16[16,4,16,2048]{3,2,1,0:T(8,128)(2,1)S(1)} %copy-done.6, bf16[2048,256]{1,0:T(8,128)(2,1)S(1)} %bitcast_select_fusion.2.f_ref), custom_call_target="tpu_custom_call" | custom-call | flops 8388608 | bytes 524288 | tf_op jit(solution)/shard_map/pallas_call | solution.py:164
  117.0 12.2 %collective-permute-done.10 = bf16[1408,256]{1,0:T(8,128)(2,1)} collective-permute-done((bf16[1408,256]{1,0:T(8,128)(2,1)}, bf16[1408,256]{1,0:T(8,128)(2,1)}, u32[]{:S(2)}, u32[]{:S(2)}) %collective-permute-start.10) | collective-permute-done | bytes 720928 | tf_op jit(solution)/shard_map/ppermute | solution.py:202
  129.1 5.3 %collective-permute-start.17 = (bf16[1408,256]{1,0:T(8,128)(2,1)}, bf16[1408,256]{1,0:T(8,128)(2,1)}, u32[]{:S(2)}, u32[]{:S(2)}) collective-permute-start(bf16[1408,256]{1,0:T(8,128)(2,1)} %get-tuple-element.74), channel_id=1, source_target_pairs={{0,16},{2,18},{4,20},{6,22},{24,8},{26,10},{28,12},{30,14},{1,17},... | collective-permute-start | bytes 2162696 | tf_op jit(solution)/shard_map/ppermute | solution.py:202
  135.7 2.2 copy-done.7
  137.9 8.8 %shard_map.83 = (bf16[2048,256]{1,0:T(8,128)(2,1)}, f32[512,256]{1,0:T(8,128)S(1)}) custom-call(s32[2]{0:T(128)S(1)} %get-tuple-element.84.where_ref, f32[1]{0:T(128)} %copy.39.weight_ref, bf16[8192,2048]{1,0:T(8,128)(2,1)} %bitcast.190, bf16[16,4,16,2048]{3,2,1,0:T(8,128)(2,1)S(1)} %copy-done.7, bf16[2048,256]{1,0:T(8,128)(2,1)S(1)} %bitcast_select_fusion.2.f_ref, ...), custom_call_target="tpu_custom_call" | custom-call | flops 8388608 | bytes 524288 | tf_op jit(solution)/shard_map/pallas_call | solution.py:164
  147.2 2.1 fusion.11
  149.3 1.6 collective-permute-start.7
  150.9 1.5 bitcast_select_fusion.1.f_ref
  152.4 8.2 %shard_map.84 = (f32[2048,256]{1,0:T(8,128)S(1)}, f32[512,256]{1,0:T(8,128)S(1)}) custom-call(s32[2]{0:T(128)S(1)} %pad_add_fusion.1.where_ref, f32[1]{0:T(128)} %copy.39.weight_ref, bf16[8192,2048]{1,0:T(8,128)(2,1)} %bitcast.191, bf16[16,4,16,2048]{3,2,1,0:T(8,128)(2,1)S(1)} %copy-done.8, bf16[2048,256]{1,0:T(8,128)(2,1)S(1)} %bitcast_select_fusion.2.f_ref, ...), custom_call_target="tpu_custom_call" | custom-call | flops 8388608 | bytes 524288 | tf_op jit(solution)/shard_map/pallas_call | solution.py:164
  160.7 6.4 %shard_map.85 = bf16[2048,256]{1,0:T(8,128)(2,1)S(1)} custom-call(s32[2]{0:T(128)S(1)} %get-tuple-element.80.where_ref, f32[1]{0:T(128)} %copy.39.weight_ref, bf16[8192,2048]{1,0:T(8,128)(2,1)} %bitcast.192, bf16[16,4,16,2048]{3,2,1,0:T(8,128)(2,1)S(1)} %copy-done, bf16[2048,256]{1,0:T(8,128)(2,1)S(1)} %bitcast_select_fusion.1.f_ref), custom_call_target="tpu_custom_call" | custom-call | flops 8388608 | bytes 524288 | tf_op jit(solution)/shard_map/pallas_call | solution.py:164
  168.6 1.5 convert_add_fusion.3
  171.0 1.7 fusion.20
  173.3 2.2 copy-done.1
  175.5 6.2 %shard_map.86 = bf16[2048,256]{1,0:T(8,128)(2,1)S(1)} custom-call(s32[2]{0:T(128)S(1)} %pad_add_fusion.where_ref, f32[1]{0:T(128)} %copy.39.weight_ref, bf16[8192,2048]{1,0:T(8,128)(2,1)} %bitcast.193, bf16[16,4,16,2048]{3,2,1,0:T(8,128)(2,1)S(1)} %copy-done.1, bf16[2048,256]{1,0:T(8,128)(2,1)S(1)} %bitcast_select_fusion.1.f_ref), custom_call_target="tpu_custom_call" | custom-call | flops 8388608 | bytes 524288 | tf_op jit(solution)/shard_map/pallas_call | solution.py:164
  183.2 12.3 %collective-permute-done.8 = bf16[1,512,256]{2,1,0:T(8,128)(2,1)S(1)} collective-permute-done((bf16[1,512,256]{2,1,0:T(8,128)(2,1)}, bf16[1,512,256]{2,1,0:T(8,128)(2,1)S(1)}, u32[]{:S(2)}, u32[]{:S(2)}) %collective-permute-start.8) | collective-permute-done | bytes 262176 | tf_op jit(solution)/shard_map/ppermute | solution.py:17
  195.5 1.9 fusion.22
  198.7 8.7 %shard_map.87 = (bf16[2048,256]{1,0:T(8,128)(2,1)}, f32[512,256]{1,0:T(8,128)S(1)}) custom-call(s32[2]{0:T(128)S(1)} %get-tuple-element.84.where_ref, f32[1]{0:T(128)} %copy.39.weight_ref, bf16[8192,2048]{1,0:T(8,128)(2,1)} %bitcast.194, bf16[16,4,16,2048]{3,2,1,0:T(8,128)(2,1)S(1)} %copy-done.2, bf16[2048,256]{1,0:T(8,128)(2,1)S(1)} %bitcast_select_fusion.1.f_ref, ...), custom_call_target="tpu_custom_call" | custom-call | flops 8388608 | bytes 524288 | tf_op jit(solution)/shard_map/pallas_call | solution.py:164
  207.5 1.6 collective-permute-start.20
  209.0 1.5 bitcast_select_fusion.f_ref
  210.5 7.7 %shard_map.88 = (f32[2048,256]{1,0:T(8,128)S(1)}, f32[512,256]{1,0:T(8,128)S(1)}) custom-call(s32[2]{0:T(128)S(1)} %pad_add_fusion.1.where_ref, f32[1]{0:T(128)} %copy.39.weight_ref, bf16[8192,2048]{1,0:T(8,128)(2,1)} %bitcast.195, bf16[16,4,16,2048]{3,2,1,0:T(8,128)(2,1)S(1)} %copy-done.2, bf16[2048,256]{1,0:T(8,128)(2,1)S(1)} %bitcast_select_fusion.1.f_ref, ...), custom_call_target="tpu_custom_call" | custom-call | flops 8388608 | bytes 524288 | tf_op jit(solution)/shard_map/pallas_call | solution.py:164
  219.0 7.0 %shard_map.89 = bf16[2048,256]{1,0:T(8,128)(2,1)} custom-call(s32[2]{0:T(128)S(1)} %get-tuple-element.80.where_ref, f32[1]{0:T(128)} %copy.39.weight_ref, bf16[8192,2048]{1,0:T(8,128)(2,1)} %bitcast.196, bf16[16,4,16,2048]{3,2,1,0:T(8,128)(2,1)S(1)} %copy-done.2, bf16[2048,256]{1,0:T(8,128)(2,1)S(1)} %bitcast_select_fusion.f_ref), custom_call_target="tpu_custom_call" | custom-call | flops 8388608 | bytes 524288 | tf_op jit(solution)/shard_map/pallas_call | solution.py:164
  226.1 6.1 %shard_map.90 = bf16[2048,256]{1,0:T(8,128)(2,1)S(1)} custom-call(s32[2]{0:T(128)S(1)} %pad_add_fusion.where_ref, f32[1]{0:T(128)} %copy.39.weight_ref, bf16[8192,2048]{1,0:T(8,128)(2,1)} %bitcast.197, bf16[16,4,16,2048]{3,2,1,0:T(8,128)(2,1)S(1)} %copy-done.2, bf16[2048,256]{1,0:T(8,128)(2,1)S(1)} %bitcast_select_fusion.f_ref), custom_call_target="tpu_custom_call" | custom-call | flops 8388608 | bytes 524288 | tf_op jit(solution)/shard_map/pallas_call | solution.py:164
  237.1 13.8 %collective-permute-done.15 = bf16[1,512,256]{2,1,0:T(8,128)(2,1)} collective-permute-done((bf16[1,512,256]{2,1,0:T(8,128)(2,1)}, bf16[1,512,256]{2,1,0:T(8,128)(2,1)}, u32[]{:S(2)}, u32[]{:S(2)}) %collective-permute-start.15) | collective-permute-done | bytes 262176 | tf_op jit(solution)/shard_map/ppermute | solution.py:17
  250.9 1.7 fusion.24
  252.6 2.3 fusion.13
  254.9 7.9 %shard_map.91 = (f32[2048,256]{1,0:T(8,128)S(1)}, f32[512,256]{1,0:T(8,128)S(1)}) custom-call(s32[2]{0:T(128)S(1)} %pad_add_fusion.1.where_ref, f32[1]{0:T(128)} %copy.39.weight_ref, bf16[8192,2048]{1,0:T(8,128)(2,1)} %bitcast.198, bf16[16,4,16,2048]{3,2,1,0:T(8,128)(2,1)S(1)} %copy-done.3, bf16[2048,256]{1,0:T(8,128)(2,1)S(1)} %bitcast_select_fusion.f_ref, ...), custom_call_target="tpu_custom_call" | custom-call | flops 8388608 | bytes 524288 | tf_op jit(solution)/shard_map/pallas_call | solution.py:164
  264.2 7.9 %shard_map.92 = (bf16[2048,256]{1,0:T(8,128)(2,1)S(1)}, f32[512,256]{1,0:T(8,128)S(1)}) custom-call(s32[2]{0:T(128)S(1)} %get-tuple-element.84.where_ref, f32[1]{0:T(128)} %copy.39.weight_ref, bf16[8192,2048]{1,0:T(8,128)(2,1)} %bitcast.199, bf16[16,4,16,2048]{3,2,1,0:T(8,128)(2,1)S(1)} %copy-done.3, bf16[2048,256]{1,0:T(8,128)(2,1)S(1)} %bitcast_select_fusion.f_ref, ...), custom_call_target="tpu_custom_call" | custom-call | flops 8388608 | bytes 524288 | tf_op jit(solution)/shard_map/pallas_call | solution.py:164
  277.4 2.1 collective-permute-done.29
  279.6 3.6 %collective-permute-done.30 = f32[512]{0:T(512)S(1)} collective-permute-done((f32[512]{0:T(512)S(1)}, f32[512]{0:T(512)S(1)}, u32[]{:S(2)}, u32[]{:S(2)}) %collective-permute-start.30) | collective-permute-done | bytes 2080 | tf_op jit(solution)/shard_map/ppermute | solution.py:17
  283.8 3.9 %collective-permute-done.31 = f32[512]{0:T(512)S(1)} collective-permute-done((f32[512]{0:T(512)S(1)}, f32[512]{0:T(512)S(1)}, u32[]{:S(2)}, u32[]{:S(2)}) %collective-permute-start.31) | collective-permute-done | bytes 2080 | tf_op jit(solution)/shard_map/ppermute | solution.py:17
  288.2 1.8 fusion.4
  291.8 1.5 collective-permute-start.34
  295.8 2.6 collective-permute-done.34
  300.8 8.2 %collective-permute-done.35 = bf16[2,2,2,16,512]{4,3,2,0,1:T(8,128)(2,1)S(1)} collective-permute-done((bf16[2,2,2,16,512]{4,3,2,0,1:T(8,128)(2,1)S(1)}, bf16[2,2,2,16,512]{4,3,2,0,1:T(8,128)(2,1)S(1)}, u32[]{:S(2)}, u32[]{:S(2)}) %collective-permute-start.35) | collective-permute-done | bytes 131104 | tf_op jit(solution)/shard_map/ppermute | solution.py:17
  309.8 2.4 collective-permute-start.22
  312.1 2.4 collective-permute-done.36
  314.6 1.6 collective-permute-start.37
  316.2 4.0 %collective-permute-done.22 = bf16[1,512,256]{2,1,0:T(8,128)(2,1)S(1)} collective-permute-done((bf16[1,512,256]{2,1,0:T(8,128)(2,1)S(1)}, bf16[1,512,256]{2,1,0:T(8,128)(2,1)S(1)}, u32[]{:S(2)}, u32[]{:S(2)}) %collective-permute-start.22) | collective-permute-done | bytes 262176 | tf_op jit(solution)/shard_map/ppermute | solution.py:17
  322.1 1.6 collective-permute-start.38
  323.7 2.4 collective-permute-done.38
  326.2 2.9 collective-permute-start.26
  329.1 2.8 collective-permute-done.39
  332.2 7.5 %collective-permute-done.40 = bf16[2,2,2,16,512]{4,3,0,2,1:T(8,128)(2,1)S(1)} collective-permute-done((bf16[2,2,2,16,512]{4,3,0,2,1:T(8,128)(2,1)S(1)}, bf16[2,2,2,16,512]{4,3,0,2,1:T(8,128)(2,1)S(1)}, u32[]{:S(2)}, u32[]{:S(2)}) %collective-permute-start.40) | collective-permute-done | bytes 131104 | tf_op jit(solution)/shard_map/ppermute | solution.py:17
  342.6 3.7 %collective-permute-done.41 = bf16[2,1,4,2,16,512]{5,4,3,2,0,1:T(8,128)(2,1)S(1)} collective-permute-done((bf16[2,1,4,2,16,512]{5,4,3,2,0,1:T(8,128)(2,1)S(1)}, bf16[2,1,4,2,16,512]{5,4,3,2,0,1:T(8,128)(2,1)S(1)}, u32[]{:S(2)}, u32[]{:S(2)}) %collective-permute-start.41) | collective-permute-done | bytes 262176 | tf_op jit(solution)/shard_map/ppermute | solution.py:17
  346.6 5.7 %collective-permute-done.27 = bf16[1,512,256]{2,1,0:T(8,128)(2,1)S(1)} collective-permute-done((bf16[1,512,256]{2,1,0:T(8,128)(2,1)S(1)}, bf16[1,512,256]{2,1,0:T(8,128)(2,1)S(1)}, u32[]{:S(2)}, u32[]{:S(2)}) %collective-permute-start.27) | collective-permute-done | bytes 262176 | tf_op jit(solution)/shard_map/ppermute | solution.py:17
  354.6 1.6 convert.14
  (192 shorter events, 44.6 us)
Async XLA Ops:
  0.6 9.7 %copy-start.37 = (s32[2,64,16]{1,2,0:T(8,128)S(1)}, s32[2,64,16]{1,2,0:T(8,128)}, u32[]{:S(2)}) copy-start(s32[2,64,16]{1,2,0:T(8,128)} %param.7) | copy-start | bytes 24580
  2.9 27.2 %collective-permute-start = (bf16[1408,256]{1,0:T(8,128)(2,1)S(1)}, bf16[1408,256]{1,0:T(8,128)(2,1)S(1)}, u32[]{:S(2)}, u32[]{:S(2)}) collective-permute-start(bf16[1408,256]{1,0:T(8,128)(2,1)S(1)} %get-tuple-element.103), channel_id=1, source_target_pairs={{0,16},{2,18},{4,20},{6,22},{24,8},{26,10},{28,12},{30,14},{1,17},... | collective-permute-start | bytes 2162696 | tf_op jit(solution)/shard_map/ppermute | solution.py:202
  9.0 2.3 collective-permute-start.1
  11.2 21.5 %copy-start.36 = (bf16[640,256]{1,0:T(8,128)(2,1)}, bf16[640,256]{1,0:T(8,128)(2,1)S(1)}, u32[]{:S(2)}) copy-start(bf16[640,256]{1,0:T(8,128)(2,1)S(1)} %collective-permute-done.1) | copy-start | bytes 983044
  33.3 8.7 %copy-start.4 = (bf16[16,4,16,2048]{3,2,1,0:T(8,128)(2,1)}, bf16[16,4,16,2048]{3,2,1,0:T(8,128)(2,1)S(1)}, u32[]{:S(2)}) copy-start(bf16[16,4,16,2048]{3,2,1,0:T(8,128)(2,1)S(1)} %broadcast_in_dim.28.mask_ref) | copy-start | bytes 12582916
  42.0 29.0 %collective-permute-start.2 = (bf16[2048,256]{1,0:T(8,128)(2,1)S(1)}, bf16[2048,256]{1,0:T(8,128)(2,1)}, u32[]{:S(2)}, u32[]{:S(2)}) collective-permute-start(bf16[2048,256]{1,0:T(8,128)(2,1)S(1)} %shard_map.77), channel_id=1, source_target_pairs={{0,2},{2,0},{4,6},{6,4},{8,10},{10,8},{12,14},{14,12},{1,3},{3,1},... | collective-permute-start | bytes 3145736 | tf_op jit(solution)/shard_map/ppermute | solution.py:17
  42.1 27.8 %collective-permute-start.3 = (bf16[1408,256]{1,0:T(8,128)(2,1)}, bf16[1408,256]{1,0:T(8,128)(2,1)}, u32[]{:S(2)}, u32[]{:S(2)}) collective-permute-start(bf16[1408,256]{1,0:T(8,128)(2,1)} %get-tuple-element.53), channel_id=1, source_target_pairs={{0,16},{2,18},{4,20},{6,22},{24,8},{26,10},{28,12},{30,14},{1,17},... | collective-permute-start | bytes 2162696 | tf_op jit(solution)/shard_map/ppermute | solution.py:202
  47.4 9.7 %collective-permute-start.4 = (bf16[640,256]{1,0:T(8,128)(2,1)S(1)}, bf16[640,256]{1,0:T(8,128)(2,1)S(1)}, u32[]{:S(2)}, u32[]{:S(2)}) collective-permute-start(bf16[640,256]{1,0:T(8,128)(2,1)S(1)} %get-tuple-element.54), channel_id=1, source_target_pairs={{12,16},{14,18},{8,20},{10,22},{20,8},{22,10},{16,12},{18,14},{13,... | collective-permute-start | bytes 983048 | tf_op jit(solution)/shard_map/ppermute | solution.py:202
  50.3 20.8 %copy-start.6 = (bf16[16,4,16,2048]{3,2,1,0:T(8,128)(2,1)S(1)}, bf16[16,4,16,2048]{3,2,1,0:T(8,128)(2,1)}, u32[]{:S(2)}) copy-start(bf16[16,4,16,2048]{3,2,1,0:T(8,128)(2,1)} %copy-done.4) | copy-start | bytes 12582916
  56.7 26.2 %collective-permute-start.5 = (bf16[2048,256]{1,0:T(8,128)(2,1)S(1)}, bf16[2048,256]{1,0:T(8,128)(2,1)S(1)}, u32[]{:S(2)}, u32[]{:S(2)}) collective-permute-start(bf16[2048,256]{1,0:T(8,128)(2,1)S(1)} %shard_map.78), channel_id=1, source_target_pairs={{0,2},{2,0},{4,6},{6,4},{8,10},{10,8},{12,14},{14,12},{1,3},{3,1},... | collective-permute-start | bytes 3145736 | tf_op jit(solution)/shard_map/ppermute | solution.py:17
  79.8 67.4 %collective-permute-start.6 = (bf16[2048,256]{1,0:T(8,128)(2,1)}, bf16[2048,256]{1,0:T(8,128)(2,1)}, u32[]{:S(2)}, u32[]{:S(2)}) collective-permute-start(bf16[2048,256]{1,0:T(8,128)(2,1)} %get-tuple-element.52), channel_id=1, source_target_pairs={{0,1},{1,0},{2,3},{3,2},{4,5},{5,4},{6,7},{7,6},{8,9},{9,8},{10,11... | collective-permute-start | bytes 3145736 | tf_op jit(solution)/shard_map/ppermute | solution.py:282
  98.8 36.9 %collective-permute-start.9 = (bf16[2048,256]{1,0:T(8,128)(2,1)}, bf16[2048,256]{1,0:T(8,128)(2,1)}, u32[]{:S(2)}, u32[]{:S(2)}) collective-permute-start(bf16[2048,256]{1,0:T(8,128)(2,1)} %shard_map.81), channel_id=1, source_target_pairs={{0,2},{2,0},{4,6},{6,4},{8,10},{10,8},{12,14},{14,12},{1,3},{3,1},... | collective-permute-start | bytes 3145736 | tf_op jit(solution)/shard_map/ppermute | solution.py:17
  101.4 27.8 %collective-permute-start.10 = (bf16[1408,256]{1,0:T(8,128)(2,1)}, bf16[1408,256]{1,0:T(8,128)(2,1)}, u32[]{:S(2)}, u32[]{:S(2)}) collective-permute-start(bf16[1408,256]{1,0:T(8,128)(2,1)} %get-tuple-element.63), channel_id=1, source_target_pairs={{0,16},{2,18},{4,20},{6,22},{24,8},{26,10},{28,12},{30,14},{1,17},... | collective-permute-start | bytes 2162696 | tf_op jit(solution)/shard_map/ppermute | solution.py:202
  108.5 8.5 %collective-permute-start.11 = (bf16[640,256]{1,0:T(8,128)(2,1)S(1)}, bf16[640,256]{1,0:T(8,128)(2,1)}, u32[]{:S(2)}, u32[]{:S(2)}) collective-permute-start(bf16[640,256]{1,0:T(8,128)(2,1)S(1)} %get-tuple-element.64), channel_id=1, source_target_pairs={{12,16},{14,18},{8,20},{10,22},{20,8},{22,10},{16,12},{18,14},{13,... | collective-permute-start | bytes 983048 | tf_op jit(solution)/shard_map/ppermute | solution.py:202
  116.7 35.7 %collective-permute-start.12 = (bf16[2048,256]{1,0:T(8,128)(2,1)}, bf16[2048,256]{1,0:T(8,128)(2,1)}, u32[]{:S(2)}, u32[]{:S(2)}) collective-permute-start(bf16[2048,256]{1,0:T(8,128)(2,1)} %shard_map.82), channel_id=1, source_target_pairs={{0,2},{2,0},{4,6},{6,4},{8,10},{10,8},{12,14},{14,12},{1,3},{3,1},... | collective-permute-start | bytes 3145736 | tf_op jit(solution)/shard_map/ppermute | solution.py:17
  129.1 52.6 %collective-permute-start.17 = (bf16[1408,256]{1,0:T(8,128)(2,1)}, bf16[1408,256]{1,0:T(8,128)(2,1)}, u32[]{:S(2)}, u32[]{:S(2)}) collective-permute-start(bf16[1408,256]{1,0:T(8,128)(2,1)} %get-tuple-element.74), channel_id=1, source_target_pairs={{0,16},{2,18},{4,20},{6,22},{24,8},{26,10},{28,12},{30,14},{1,17},... | collective-permute-start | bytes 2162696 | tf_op jit(solution)/shard_map/ppermute | solution.py:202
  137.9 9.3 %copy-start.16 = (f32[2048,256]{1,0:T(8,128)S(1)}, f32[2048,256]{1,0:T(8,128)}, u32[]{:S(2)}) copy-start(f32[2048,256]{1,0:T(8,128)} %copy-done.15) | copy-start | bytes 6291460
  146.7 50.8 %collective-permute-start.13 = (bf16[2048,256]{1,0:T(8,128)(2,1)}, bf16[2048,256]{1,0:T(8,128)(2,1)}, u32[]{:S(2)}, u32[]{:S(2)}) collective-permute-start(bf16[2048,256]{1,0:T(8,128)(2,1)} %get-tuple-element.62), channel_id=1, source_target_pairs={{0,1},{1,0},{2,3},{3,2},{4,5},{5,4},{6,7},{7,6},{8,9},{9,8},{10,11... | collective-permute-start | bytes 3145736 | tf_op jit(solution)/shard_map/ppermute | solution.py:282
  149.3 20.7 %collective-permute-start.7 = (bf16[2,512,256]{2,1,0:T(8,128)(2,1)}, bf16[2,512,256]{2,1,0:T(8,128)(2,1)}, u32[]{:S(2)}, u32[]{:S(2)}) collective-permute-start(bf16[2,512,256]{2,1,0:T(8,128)(2,1)} %fusion.11), channel_id=1, source_target_pairs={{0,4},{2,6},{4,0},{6,2},{8,12},{10,14},{12,8},{14,10},{1,5},{3,7},... | collective-permute-start | bytes 1572872 | tf_op jit(solution)/shard_map/ppermute | solution.py:17
  152.4 8.3 %copy-start = (bf16[16,4,16,2048]{3,2,1,0:T(8,128)(2,1)S(1)}, bf16[16,4,16,2048]{3,2,1,0:T(8,128)(2,1)}, u32[]{:S(2)}) copy-start(bf16[16,4,16,2048]{3,2,1,0:T(8,128)(2,1)} %broadcast_in_dim.31.mask_ref) | copy-start | bytes 12582916
  167.1 31.6 %collective-permute-start.16 = (bf16[2048,256]{1,0:T(8,128)(2,1)S(1)}, bf16[2048,256]{1,0:T(8,128)(2,1)}, u32[]{:S(2)}, u32[]{:S(2)}) collective-permute-start(bf16[2048,256]{1,0:T(8,128)(2,1)S(1)} %shard_map.85), channel_id=1, source_target_pairs={{0,2},{2,0},{4,6},{6,4},{8,10},{10,8},{12,14},{14,12},{1,3},{3,1},... | collective-permute-start | bytes 3145736 | tf_op jit(solution)/shard_map/ppermute | solution.py:17
  167.2 14.5 %collective-permute-start.18 = (bf16[640,256]{1,0:T(8,128)(2,1)}, bf16[640,256]{1,0:T(8,128)(2,1)}, u32[]{:S(2)}, u32[]{:S(2)}) collective-permute-start(bf16[640,256]{1,0:T(8,128)(2,1)} %get-tuple-element.75), channel_id=1, source_target_pairs={{12,16},{14,18},{8,20},{10,22},{20,8},{22,10},{16,12},{18,14},{13,... | collective-permute-start | bytes 983048 | tf_op jit(solution)/shard_map/ppermute | solution.py:202
  172.7 22.8 %collective-permute-start.8 = (bf16[1,512,256]{2,1,0:T(8,128)(2,1)}, bf16[1,512,256]{2,1,0:T(8,128)(2,1)S(1)}, u32[]{:S(2)}, u32[]{:S(2)}) collective-permute-start(bf16[1,512,256]{2,1,0:T(8,128)(2,1)} %fusion.20), channel_id=1, source_target_pairs={{0,8},{2,10},{4,12},{6,14},{8,0},{10,2},{12,4},{14,6},{1,9},{3,11}... | collective-permute-start | bytes 786440 | tf_op jit(solution)/shard_map/ppermute | solution.py:17
  175.5 21.9 %copy-start.14 = (f32[2048,256]{1,0:T(8,128)S(1)}, f32[2048,256]{1,0:T(8,128)}, u32[]{:S(2)}) copy-start(f32[2048,256]{1,0:T(8,128)} %copy-done.13) | copy-start | bytes 6291460
  181.7 13.8 %copy-start.25 = (f32[2,1,512,256]{3,2,1,0:T(8,128)S(1)}, f32[2,1,512,256]{3,2,1,0:T(8,128)}, u32[]{:S(2)}) copy-start(f32[2,1,512,256]{3,2,1,0:T(8,128)} %copy-done.24) | copy-start | bytes 3145732
  181.7 28.8 %collective-permute-start.19 = (bf16[2048,256]{1,0:T(8,128)(2,1)S(1)}, bf16[2048,256]{1,0:T(8,128)(2,1)S(1)}, u32[]{:S(2)}, u32[]{:S(2)}) collective-permute-start(bf16[2048,256]{1,0:T(8,128)(2,1)S(1)} %shard_map.86), channel_id=1, source_target_pairs={{0,2},{2,0},{4,6},{6,4},{8,10},{10,8},{12,14},{14,12},{1,3},{3,1},... | collective-permute-start | bytes 3145736 | tf_op jit(solution)/shard_map/ppermute | solution.py:17
  181.8 16.9 %copy-start.2 = (bf16[16,4,16,2048]{3,2,1,0:T(8,128)(2,1)S(1)}, bf16[16,4,16,2048]{3,2,1,0:T(8,128)(2,1)}, u32[]{:S(2)}) copy-start(bf16[16,4,16,2048]{3,2,1,0:T(8,128)(2,1)} %broadcast_in_dim.31.mask_ref) | copy-start | bytes 12582916
  198.6 35.3 %collective-permute-start.14 = (bf16[2,512,256]{2,1,0:T(8,128)(2,1)S(1)}, bf16[2,512,256]{2,1,0:T(8,128)(2,1)S(1)}, u32[]{:S(2)}, u32[]{:S(2)}) collective-permute-start(bf16[2,512,256]{2,1,0:T(8,128)(2,1)S(1)} %fusion.12), channel_id=1, source_target_pairs={{0,4},{2,6},{4,0},{6,2},{8,12},{10,14},{12,8},{14,10},{1,5},{3,7},... | collective-permute-start | bytes 1572872 | tf_op jit(solution)/shard_map/ppermute | solution.py:17
  207.5 45.2 %collective-permute-start.20 = (bf16[2048,256]{1,0:T(8,128)(2,1)}, bf16[2048,256]{1,0:T(8,128)(2,1)}, u32[]{:S(2)}, u32[]{:S(2)}) collective-permute-start(bf16[2048,256]{1,0:T(8,128)(2,1)} %get-tuple-element.73), channel_id=1, source_target_pairs={{0,1},{1,0},{2,3},{3,2},{4,5},{5,4},{6,7},{7,6},{8,9},{9,8},{10,11... | collective-permute-start | bytes 3145736 | tf_op jit(solution)/shard_map/ppermute | solution.py:282
  219.0 7.0 %copy-start.11 = (f32[2048,256]{1,0:T(8,128)}, f32[2048,256]{1,0:T(8,128)S(1)}, u32[]{:S(2)}) copy-start(f32[2048,256]{1,0:T(8,128)S(1)} %get-tuple-element.79) | copy-start | bytes 6291460
  232.2 22.7 %collective-permute-start.23 = (bf16[2048,256]{1,0:T(8,128)(2,1)S(1)}, bf16[2048,256]{1,0:T(8,128)(2,1)}, u32[]{:S(2)}, u32[]{:S(2)}) collective-permute-start(bf16[2048,256]{1,0:T(8,128)(2,1)S(1)} %shard_map.90), channel_id=1, source_target_pairs={{0,2},{2,0},{4,6},{6,4},{8,10},{10,8},{12,14},{14,12},{1,3},{3,1},... | collective-permute-start | bytes 3145736 | tf_op jit(solution)/shard_map/ppermute | solution.py:17
  232.2 31.9 %collective-permute-start.24 = (bf16[2048,256]{1,0:T(8,128)(2,1)}, bf16[2048,256]{1,0:T(8,128)(2,1)}, u32[]{:S(2)}, u32[]{:S(2)}) collective-permute-start(bf16[2048,256]{1,0:T(8,128)(2,1)} %shard_map.89), channel_id=1, source_target_pairs={{0,2},{2,0},{4,6},{6,4},{8,10},{10,8},{12,14},{14,12},{1,3},{3,1},... | collective-permute-start | bytes 3145736 | tf_op jit(solution)/shard_map/ppermute | solution.py:17
  235.8 15.1 %collective-permute-start.15 = (bf16[1,512,256]{2,1,0:T(8,128)(2,1)}, bf16[1,512,256]{2,1,0:T(8,128)(2,1)}, u32[]{:S(2)}, u32[]{:S(2)}) collective-permute-start(bf16[1,512,256]{2,1,0:T(8,128)(2,1)} %fusion.19), channel_id=1, source_target_pairs={{0,8},{2,10},{4,12},{6,14},{8,0},{10,2},{12,4},{14,6},{1,9},{3,11}... | collective-permute-start | bytes 786440 | tf_op jit(solution)/shard_map/ppermute | solution.py:17
  235.8 15.1 %copy-start.27 = (f32[2,1,512,256]{3,2,1,0:T(8,128)S(1)}, f32[2,1,512,256]{3,2,1,0:T(8,128)}, u32[]{:S(2)}) copy-start(f32[2,1,512,256]{3,2,1,0:T(8,128)} %copy-done.26) | copy-start | bytes 3145732
  235.8 15.1 %copy-start.35 = (bf16[2,512,256]{2,1,0:T(8,128)(2,1)S(1)}, bf16[2,512,256]{2,1,0:T(8,128)(2,1)}, u32[]{:S(2)}) copy-start(bf16[2,512,256]{2,1,0:T(8,128)(2,1)} %copy-done.34) | copy-start | bytes 1572868
  235.8 19.1 %copy-start.3 = (bf16[16,4,16,2048]{3,2,1,0:T(8,128)(2,1)S(1)}, bf16[16,4,16,2048]{3,2,1,0:T(8,128)(2,1)}, u32[]{:S(2)}) copy-start(bf16[16,4,16,2048]{3,2,1,0:T(8,128)(2,1)} %broadcast_in_dim.31.mask_ref) | copy-start | bytes 12582916
  237.1 35.2 %copy-start.22 = (f32[512,512]{1,0:T(8,128)}, f32[512,512]{1,0:T(8,128)S(1)}, u32[]{:S(2)}) copy-start(f32[512,512]{1,0:T(8,128)S(1)} %pad_maximum_fusion.4) | copy-start | bytes 3145732
  264.2 8.0 %copy-start.19 = (f32[512,256]{1,0:T(8,128)S(1)}, f32[512,256]{1,0:T(8,128)}, u32[]{:S(2)}) copy-start(f32[512,256]{1,0:T(8,128)} %copy-done.18) | copy-start | bytes 1572868
  273.3 15.0 %collective-permute-start.33 = (bf16[2,2,4,1,2,16,512]{6,5,4,2,1,0,3:T(8,128)(2,1)}, bf16[2,2,4,1,2,16,512]{6,5,4,2,1,0,3:T(8,128)(2,1)}, u32[]{:S(2)}, u32[]{:S(2)}) collective-permute-start(bf16[2,2,4,1,2,16,512]{6,5,4,2,1,0,3:T(8,128)(2,1)} %fusion.15), channel_id=1, source_target_pairs={{0,2},{2,0},{4,6},{6,4},{8,10},{10,8},{12,14},{14,12},{1,3},{3,1},... | collective-permute-start | bytes 1572872 | tf_op jit(solution)/shard_map/ppermute | solution.py:17
  274.8 1.2 collective-permute-start.28
  276.0 3.6 %collective-permute-start.29 = (f32[512]{0:T(512)S(1)}, f32[512]{0:T(512)S(1)}, u32[]{:S(2)}, u32[]{:S(2)}) collective-permute-start(f32[512]{0:T(512)S(1)} %add.368), channel_id=1, source_target_pairs={{0,16},{16,0},{1,17},{17,1},{2,18},{18,2},{3,19},{19,3},{4,20},{20... | collective-permute-start | bytes 6152 | tf_op jit(solution)/shard_map/ppermute | solution.py:17
  279.6 3.6 %collective-permute-start.30 = (f32[512]{0:T(512)S(1)}, f32[512]{0:T(512)S(1)}, u32[]{:S(2)}, u32[]{:S(2)}) collective-permute-start(f32[512]{0:T(512)S(1)} %add.369), channel_id=1, source_target_pairs={{0,4},{2,6},{4,0},{6,2},{8,12},{10,14},{12,8},{14,10},{1,5},{3,7},... | collective-permute-start | bytes 6152 | tf_op jit(solution)/shard_map/ppermute | solution.py:17
  283.2 4.5 %collective-permute-start.31 = (f32[512]{0:T(512)S(1)}, f32[512]{0:T(512)S(1)}, u32[]{:S(2)}, u32[]{:S(2)}) collective-permute-start(f32[512]{0:T(512)S(1)} %add.370), channel_id=1, source_target_pairs={{0,8},{2,10},{4,12},{6,14},{8,0},{10,2},{12,4},{14,6},{1,9},{3,11}... | collective-permute-start | bytes 6152 | tf_op jit(solution)/shard_map/ppermute | solution.py:17
  287.7 6.8 %copy-start.21 = (bf16[2048,256]{1,0:T(8,128)(2,1)S(1)}, bf16[2048,256]{1,0:T(8,128)(2,1)}, u32[]{:S(2)}) copy-start(bf16[2048,256]{1,0:T(8,128)(2,1)} %copy-done.20) | copy-start | bytes 3145732
  287.7 11.9 %copy-start.12 = (f32[2048,256]{1,0:T(8,128)S(1)}, f32[2048,256]{1,0:T(8,128)}, u32[]{:S(2)}) copy-start(f32[2048,256]{1,0:T(8,128)} %copy-done.11) | copy-start | bytes 6291460
  287.7 6.4 %collective-permute-start.32 = (f32[512]{0:T(512)S(1)}, f32[512]{0:T(512)S(1)}, u32[]{:S(2)}, u32[]{:S(2)}) collective-permute-start(f32[512]{0:T(512)S(1)} %add.371), channel_id=1, source_target_pairs={{0,1},{1,0},{2,3},{3,2},{4,5},{5,4},{6,7},{7,6},{8,9},{9,8},{10,11... | collective-permute-start | bytes 6152 | tf_op jit(solution)/shard_map/ppermute | solution.py:17
  291.8 6.6 %collective-permute-start.34 = (bf16[2,1,4,2,16,512]{5,4,3,2,0,1:T(8,128)(2,1)}, bf16[2,1,4,2,16,512]{5,4,3,2,0,1:T(8,128)(2,1)S(1)}, u32[]{:S(2)}, u32[]{:S(2)}) collective-permute-start(bf16[2,1,4,2,16,512]{5,4,3,2,0,1:T(8,128)(2,1)} %fusion.25), channel_id=1, source_target_pairs={{0,16},{16,0},{1,17},{17,1},{2,18},{18,2},{3,19},{19,3},{4,20},{20... | collective-permute-start | bytes 786440 | tf_op jit(solution)/shard_map/ppermute | solution.py:17
  294.2 15.5 %collective-permute-start.21 = (bf16[2,512,256]{2,1,0:T(8,128)(2,1)}, bf16[2,512,256]{2,1,0:T(8,128)(2,1)S(1)}, u32[]{:S(2)}, u32[]{:S(2)}) collective-permute-start(bf16[2,512,256]{2,1,0:T(8,128)(2,1)} %fusion.13), channel_id=1, source_target_pairs={{0,4},{2,6},{4,0},{6,2},{8,12},{10,14},{12,8},{14,10},{1,5},{3,7},... | collective-permute-start | bytes 1572872 | tf_op jit(solution)/shard_map/ppermute | solution.py:17
  294.5 26.6 %collective-permute-start.25 = (bf16[2048,256]{1,0:T(8,128)(2,1)S(1)}, bf16[2048,256]{1,0:T(8,128)(2,1)S(1)}, u32[]{:S(2)}, u32[]{:S(2)}) collective-permute-start(bf16[2048,256]{1,0:T(8,128)(2,1)S(1)} %copy-done.21), channel_id=1, source_target_pairs={{0,1},{1,0},{2,3},{3,2},{4,5},{5,4},{6,7},{7,6},{8,9},{9,8},{10,11... | collective-permute-start | bytes 3145736 | tf_op jit(solution)/shard_map/ppermute | solution.py:282
  299.5 9.5 %collective-permute-start.35 = (bf16[2,2,2,16,512]{4,3,2,0,1:T(8,128)(2,1)S(1)}, bf16[2,2,2,16,512]{4,3,2,0,1:T(8,128)(2,1)S(1)}, u32[]{:S(2)}, u32[]{:S(2)}) collective-permute-start(bf16[2,2,2,16,512]{4,3,2,0,1:T(8,128)(2,1)S(1)} %fusion.26), channel_id=1, source_target_pairs={{0,4},{2,6},{4,0},{6,2},{8,12},{10,14},{12,8},{14,10},{1,5},{3,7},... | collective-permute-start | bytes 393224 | tf_op jit(solution)/shard_map/ppermute | solution.py:17
  300.8 20.3 %copy-start.10 = (f32[2048,256]{1,0:T(8,128)S(1)}, f32[2048,256]{1,0:T(8,128)}, u32[]{:S(2)}) copy-start(f32[2048,256]{1,0:T(8,128)} %copy-done.9) | copy-start | bytes 6291460
  309.0 5.5 %collective-permute-start.36 = (bf16[2,1,2,16,512]{4,3,2,0,1:T(8,128)(2,1)S(1)}, bf16[2,1,2,16,512]{4,3,2,0,1:T(8,128)(2,1)S(1)}, u32[]{:S(2)}, u32[]{:S(2)}) collective-permute-start(bf16[2,1,2,16,512]{4,3,2,0,1:T(8,128)(2,1)S(1)} %fusion.30), channel_id=1, source_target_pairs={{0,8},{2,10},{4,12},{6,14},{8,0},{10,2},{12,4},{14,6},{1,9},{3,11}... | collective-permute-start | bytes 196616 | tf_op jit(solution)/shard_map/ppermute | solution.py:17
  309.8 10.4 %collective-permute-start.22 = (bf16[1,512,256]{2,1,0:T(8,128)(2,1)S(1)}, bf16[1,512,256]{2,1,0:T(8,128)(2,1)S(1)}, u32[]{:S(2)}, u32[]{:S(2)}) collective-permute-start(bf16[1,512,256]{2,1,0:T(8,128)(2,1)S(1)} %fusion.18), channel_id=1, source_target_pairs={{0,8},{2,10},{4,12},{6,14},{8,0},{10,2},{12,4},{14,6},{1,9},{3,11}... | collective-permute-start | bytes 786440 | tf_op jit(solution)/shard_map/ppermute | solution.py:17
  314.6 6.6 %collective-permute-start.37 = (f32[2,2,1,16,512]{4,3,2,1,0:T(8,128)S(1)}, f32[2,2,1,16,512]{4,3,2,1,0:T(8,128)S(1)}, u32[]{:S(2)}, u32[]{:S(2)}) collective-permute-start(f32[2,2,1,16,512]{4,3,2,1,0:T(8,128)S(1)} %fusion.27), channel_id=1, source_target_pairs={{0,1},{1,0},{2,3},{3,2},{4,5},{5,4},{6,7},{7,6},{8,9},{9,8},{10,11... | collective-permute-start | bytes 393224 | tf_op jit(solution)/shard_map/ppermute | solution.py:17
  322.1 4.0 %collective-permute-start.38 = (bf16[2,1,16,512]{3,2,0,1:T(8,128)(2,1)S(1)}, bf16[2,1,16,512]{3,2,0,1:T(8,128)(2,1)S(1)}, u32[]{:S(2)}, u32[]{:S(2)}) collective-permute-start(bf16[2,1,16,512]{3,2,0,1:T(8,128)(2,1)S(1)} %bitcast.225), channel_id=1, source_target_pairs={{0,1},{1,0},{2,3},{3,2},{4,5},{5,4},{6,7},{7,6},{8,9},{9,8},{10,11... | collective-permute-start | bytes 98312 | tf_op jit(solution)/shard_map/ppermute | solution.py:17
  326.1 5.8 %collective-permute-start.39 = (bf16[2,1,2,16,512]{4,3,0,2,1:T(8,128)(2,1)S(1)}, bf16[2,1,2,16,512]{4,3,0,2,1:T(8,128)(2,1)S(1)}, u32[]{:S(2)}, u32[]{:S(2)}) collective-permute-start(bf16[2,1,2,16,512]{4,3,0,2,1:T(8,128)(2,1)S(1)} %maximum_select_fusion.6), channel_id=1, source_target_pairs={{0,8},{2,10},{4,12},{6,14},{8,0},{10,2},{12,4},{14,6},{1,9},{3,11}... | collective-permute-start | bytes 196616 | tf_op jit(solution)/shard_map/ppermute | solution.py:17
  326.2 14.9 %collective-permute-start.26 = (bf16[2,512,256]{2,1,0:T(8,128)(2,1)S(1)}, bf16[2,512,256]{2,1,0:T(8,128)(2,1)}, u32[]{:S(2)}, u32[]{:S(2)}) collective-permute-start(bf16[2,512,256]{2,1,0:T(8,128)(2,1)S(1)} %fusion.14), channel_id=1, source_target_pairs={{0,4},{2,6},{4,0},{6,2},{8,12},{10,14},{12,8},{14,10},{1,5},{3,7},... | collective-permute-start | bytes 1572872 | tf_op jit(solution)/shard_map/ppermute | solution.py:17
  331.9 7.9 %collective-permute-start.40 = (bf16[2,2,2,16,512]{4,3,0,2,1:T(8,128)(2,1)S(1)}, bf16[2,2,2,16,512]{4,3,0,2,1:T(8,128)(2,1)S(1)}, u32[]{:S(2)}, u32[]{:S(2)}) collective-permute-start(bf16[2,2,2,16,512]{4,3,0,2,1:T(8,128)(2,1)S(1)} %maximum_select_fusion.5), channel_id=1, source_target_pairs={{0,4},{2,6},{4,0},{6,2},{8,12},{10,14},{12,8},{14,10},{1,5},{3,7},... | collective-permute-start | bytes 393224 | tf_op jit(solution)/shard_map/ppermute | solution.py:17
  339.8 6.4 %collective-permute-start.41 = (bf16[2,1,4,2,16,512]{5,4,3,2,0,1:T(8,128)(2,1)S(1)}, bf16[2,1,4,2,16,512]{5,4,3,2,0,1:T(8,128)(2,1)S(1)}, u32[]{:S(2)}, u32[]{:S(2)}) collective-permute-start(bf16[2,1,4,2,16,512]{5,4,3,2,0,1:T(8,128)(2,1)S(1)} %bitcast.213), channel_id=1, source_target_pairs={{0,16},{16,0},{1,17},{17,1},{2,18},{18,2},{3,19},{19,3},{4,20},{20... | collective-permute-start | bytes 786440 | tf_op jit(solution)/shard_map/ppermute | solution.py:17
  342.1 10.1 %collective-permute-start.27 = (bf16[1,512,256]{2,1,0:T(8,128)(2,1)S(1)}, bf16[1,512,256]{2,1,0:T(8,128)(2,1)S(1)}, u32[]{:S(2)}, u32[]{:S(2)}) collective-permute-start(bf16[1,512,256]{2,1,0:T(8,128)(2,1)S(1)} %fusion.16), channel_id=1, source_target_pairs={{0,8},{2,10},{4,12},{6,14},{8,0},{10,2},{12,4},{14,6},{1,9},{3,11}... | collective-permute-start | bytes 786440 | tf_op jit(solution)/shard_map/ppermute | solution.py:17
  346.3 8.1 %collective-permute-start.42 = (bf16[2,2,4,1,2,16,512]{6,5,4,2,1,0,3:T(8,128)(2,1)S(1)}, bf16[2,2,4,1,2,16,512]{6,5,4,2,1,0,3:T(8,128)(2,1)S(1)}, u32[]{:S(2)}, u32[]{:S(2)}) collective-permute-start(bf16[2,2,4,1,2,16,512]{6,5,4,2,1,0,3:T(8,128)(2,1)S(1)} %maximum_select_fusion.2), channel_id=1, source_target_pairs={{0,2},{2,0},{4,6},{6,4},{8,10},{10,8},{12,14},{14,12},{1,3},{3,1},... | collective-permute-start | bytes 1572872 | tf_op jit(solution)/shard_map/ppermute | solution.py:17
  346.4 6.9 %copy-start.29 = (f32[1,512,256]{2,1,0:T(8,128)S(1)}, f32[1,512,256]{2,1,0:T(8,128)}, u32[]{:S(2)}) copy-start(f32[1,512,256]{2,1,0:T(8,128)} %convert_add_fusion.4) | copy-start | bytes 1572868
  346.5 6.9 %copy-start.32 = (bf16[1,512,256]{2,1,0:T(8,128)(2,1)S(1)}, bf16[1,512,256]{2,1,0:T(8,128)(2,1)}, u32[]{:S(2)}) copy-start(bf16[1,512,256]{2,1,0:T(8,128)(2,1)} %get-tuple-element.92) | copy-start | bytes 786436
  346.5 6.9 %copy-start.33 = (bf16[1,512,256]{2,1,0:T(8,128)(2,1)S(1)}, bf16[1,512,256]{2,1,0:T(8,128)(2,1)}, u32[]{:S(2)}) copy-start(bf16[1,512,256]{2,1,0:T(8,128)(2,1)} %get-tuple-element.94) | copy-start | bytes 786436
  (17 other events, 37.9 us)

commit v3 on v2

--- a/solution.py
+++ b/solution.py
@@ -9,7 +9,8 @@
 
 CORES = 2
 PACK = 16
-PARTS = ((0, 0, 2), (0, 2, 2), (1, 0, 2), (1, 2, 2))
+AWAY = 2
+PARTS = ((0, 0, 4, 1), (1, 0, 4, 2))
 
 
 def swap(x, axis, mask):
@@ -54,9 +55,11 @@
     return send.astype(kind), keep
 
 
-def halve(x, axis, index, exchange, kind):
+def halve(x, axis, index, exchange, kind, before_last=()):
     sources, bit = [x], 0
     while sources[0].shape[axis] > 1:
+        if sources[0].shape[axis] == 2:
+            sources[0] = after(sources[0], *before_last)
         send, keep = halve_step(sources, axis, index, bit, kind)
         sources = [keep, exchange(send, 1 << bit)]
         bit += 1
@@ -101,12 +104,17 @@
     return jnp.dot(masked, f_ref[...], preferred_element_type=jnp.float32) * weight_ref[0]
 
 
-def away_kernel(where_ref, weight_ref, a_ref, mask_ref, f_ref, out_ref):
-    out_ref[...] = masked_product(a_ref, mask_ref, f_ref, weight_ref).astype(out_ref.dtype)
-
-
-def here_kernel(pieces, where_ref, weight_ref, a_ref, mask_ref, f_ref, recv_ref, panel_ref, start_ref, *outs):
-    total = masked_product(a_ref, mask_ref, f_ref, weight_ref) + recv_ref[...].astype(jnp.float32)
+def away_kernel(where_ref, weight_ref, a_ref, mask_ref, f_ref, *outs):
+    total = masked_product(a_ref, mask_ref, f_ref, weight_ref)
+    width = total.shape[1] // len(outs)
+    for n, out_ref in enumerate(outs):
+        out_ref[...] = total[:, n * width:(n + 1) * width].astype(out_ref.dtype)
+
+
+def here_kernel(pieces, where_ref, weight_ref, a_ref, mask_ref, f_ref, panel_ref, start_ref, *refs):
+    recvs, outs = refs[:AWAY], refs[AWAY:]
+    total = masked_product(a_ref, mask_ref, f_ref, weight_ref)
+    total = total + jnp.concatenate([r[...].astype(jnp.float32) for r in recvs], axis=1)
     width = total.shape[1] // pieces
     for n in range(pieces):
         outs[n][...] = total[:, n * width:(n + 1) * width].astype(outs[n].dtype)
@@ -144,18 +152,18 @@
     nbytes = zs * block * width
     if merge is None:
         kernel, extra = away_kernel, ()
-        out_shape = jax.ShapeDtypeStruct((zs * block, width), jnp.bfloat16)
-        out_specs = pl.BlockSpec((block, width), lambda i, w: (i, 0))
+        part = width // AWAY
+        out_shape = [jax.ShapeDtypeStruct((zs * block, part), jnp.bfloat16)] * AWAY
+        out_specs = [pl.BlockSpec((block, part), lambda i, w: (i, 0))] * AWAY
     else:
         recv, panel, start, pieces, kind = merge
-        extra = (recv, panel, start)
+        extra = (panel, start, *recv)
         kernel = functools.partial(here_kernel, pieces)
         full = panel.shape[1]
         in_specs += [
-            pl.BlockSpec((block, width), lambda i, w: (i, 0)),
             pl.BlockSpec((block, full), lambda i, w: (block_of(i, w), 0)),
             pl.BlockSpec((full, width), lambda i, w: (0, 0)),
-        ]
+        ] + [pl.BlockSpec((block, width // AWAY), lambda i, w: (i, 0))] * AWAY
         piece = width // pieces
         out_shape = [jax.ShapeDtypeStruct((zs * block, piece), kind)] * pieces
         out_shape.append(jax.ShapeDtypeStruct((full, width), jnp.float32))
@@ -175,34 +183,16 @@
 def fetch_factor(panel, first, width, ids, last):
     row, col, cols = ids
     n_row, n_col = lax.axis_size("row"), lax.axis_size("col")
-    zs = n_col // CORES
     ratio = n_col // n_row
-
-    def mirror(j):
-        return (zs - 1 - j // CORES) * CORES + j % CORES
-
-    far = cols * 5 // 16 if n_row == 2 and zs > 1 else 0
-    near = cols - far
     start = (col % ratio) * cols
     own = lax.dynamic_slice(panel, (start, first), (cols, width))
-    parts = [(own[:near], lambda j: j)]
-    if far > 0:
-        other = (mirror(col) % ratio) * cols + near
-        parts.append((lax.dynamic_slice(panel, (other, first), (far, width)), mirror))
-    got = []
-    for src, source in parts:
-        if last is not None:
-            src = after(src, *last)
-        total = None
-        for d in range(1, n_row):
-            pairs = []
-            for j in range(n_col):
-                owner = j // ratio
-                pairs.append((owner * n_col + source(j), ((owner + d) % n_row) * n_col + j))
-            arrived = lax.ppermute(src, ("row", "col"), pairs)
-            total = arrived if total is None else total + arrived
-        got.append(src if total is None else total)
-    return own, got
+    src = after(own, *last)
+    got = None
+    for d in range(1, n_row):
+        pairs = [((j // ratio) * n_col + j, ((j // ratio + d) % n_row) * n_col + j) for j in range(n_col)]
+        arrived = lax.ppermute(src, ("row", "col"), pairs)
+        got = arrived if got is None else got + arrived
+    return own, own if got is None else got
 
 
 def body(inv_block, block_masks, panel_first, panel_second, diag_inverse, weights):
@@ -221,10 +211,11 @@
     groups = max(1, block // grain)
     fine = block // groups
 
-    fetched, last = [], None
-    for k, first, size in PARTS:
+    fetched, last = [], ()
+    for k, first, size, _ in PARTS:
         own, last = fetch_factor(panels[k], first * quarter, size * quarter, (row, col, cols), last)
         fetched.append((own, last))
+        last = (last,)
     mine = row == col // (n_col // n_row)
 
     masks = []
@@ -237,7 +228,7 @@
 
     def take(part, *deps):
         own, got = fetched[part]
-        return jnp.where(mine, own, after(jnp.concatenate(got, axis=0), *deps))
+        return jnp.where(mine, own, after(got, *deps))
 
     def place(c, d, *deps):
         return after(jnp.stack([c, (pole + d) % n_pole]).astype(jnp.int32), *deps)
@@ -247,23 +238,18 @@
     token = ()
     units = []
     terms = [[], []]
-    for part, (k, first, size) in enumerate(PARTS):
+    for part, (k, first, size, pieces) in enumerate(PARTS):
         wide = size * quarter
-        pieces = max(1, size // 2)
         received = {}
         for d in dests:
             away = product(inverse, masks[k], factor, place(1 - core, d, *token), weights, n_pole)
-            token = (away,)
-            received[d] = swap_core(away)
+            token = (away[0],)
+            received[d] = [swap_core(x) for x in away]
         term = jnp.zeros((width, wide), jnp.float32)
         arrived = [[] for _ in range(pieces)]
-        upcoming = None
         final = part + 1 == len(PARTS)
-        for d in sorted(dests) if final else dests:
+        for d in dests:
             if d == 0:
-                if not final:
-                    upcoming = take(part + 1, *token)
-                    token += (upcoming,)
                 for unit in units:
                     if not unit.done():
                         token += unit.step()
@@ -283,18 +269,26 @@
                     before = (came,)
                     arrived[n].append(came)
         terms[k].append(term)
-        factor = upcoming
+        if not final:
+            factor = take(part + 1, *token)
         for n in range(pieces):
             sources = [x.reshape(zs, block, x.shape[1]) for x in [sums[n]] + arrived[n]]
             units.append(ZSum(sources, z))
             units[-1].k = k
-    finals, gate = [[], []], ()
+    first, second, third = (), (), ()
+    for unit in units[:-1]:
+        if not unit.done():
+            first += unit.step()
+    second = units[-1].step()
+    for unit in units[:-1]:
+        while not unit.done():
+            second += unit.step()
+    while not units[-1].done():
+        third = units[-1].step()
+    finals = [[], []]
     for unit in units:
-        while not unit.done():
-            sent = unit.step()
-            if unit is units[-2] or unit.bit == 1:
-                gate = gate[:2] + sent
         finals[unit.k].append(unit.result())
+    second += tuple(finals[0])
 
     dens = [jnp.concatenate(f, axis=1) for f in finals]
     squares = jnp.sum(dens[0] * dens[0], axis=0)
@@ -308,19 +302,18 @@
     split = (2, n_row, zs, CORES, n_pole, each, width)
     term = jnp.stack([jnp.concatenate(t, axis=1) for t in terms]).reshape(split)
     term = halve(term, 3, core, swap_core, jnp.bfloat16)
-    term = halve(term, 1, row, swap_row, jnp.bfloat16)
-    term = halve(term, 1, z, swap_z, jnp.bfloat16)
+    term = halve(after(term, *first), 1, row, swap_row, jnp.bfloat16)
+    term = halve(term, 1, z, swap_z, jnp.bfloat16, second)
     base = pick(pick(pick(diag_inverse.reshape(split), core, 3), row, 1), z, 1).astype(jnp.float32) * weight
     both = halve(jnp.stack([base, term]), 2, pole, swap_pole, jnp.float32)
-    base, term = both[0], both[1]
-    index = ((row * n_col + col) * n_pole + pole) * each
-    inner = term[1] / (lax.dynamic_slice(scale, (index,), (each,))[:, None] * scale)
-    piece = (base + jnp.stack([term[0], inner])).astype(jnp.bfloat16)
-    piece = double(after(piece, *gate), 1, pole, n_pole, swap_pole)
-    piece = double(piece, 1, z, zs, swap_z)
-    piece = double(piece, 1, row, n_row, swap_row)
+    piece = jnp.concatenate([both[0] + both[1] * jnp.array([1, 0], jnp.float32)[:, None, None], both[1, 1:]])
+    piece = double(piece.astype(jnp.bfloat16), 1, pole, n_pole, swap_pole)
+    piece = double(after(piece, *third), 1, z, zs, swap_z)
+    piece = double(after(piece, scale), 1, row, n_row, swap_row)
     piece = double(piece, 3, core, CORES, swap_core)
-    return out, piece.reshape(2, width, width).astype(jnp.float32)
+    piece = piece.reshape(3, width, width).astype(jnp.float32)
+    scaled = piece[1] + piece[2] / (scale[:, None] * scale)
+    return out, jnp.stack([piece[0], scaled])
 
 
 def solution(mesh):

time: 358 us -> 287 us (0.80)
  Pallas kernels: 118 us -> 73.4 us
  other arithmetic: 41.4 us -> 30.4 us
  starting transfers between devices: 47.9 us -> 37.9 us
    pallas_call x16 -> x8, Pallas kernels: 118 us -> 73.4 us  [product(): pl.pallas_call(kernel, out_shape=out_shape, grid_spec=pltpu.PrefetchScala...]
    ppermute x8 -> x2, starting transfers between devices: 24.8 us -> 10.5 us  [fetch_factor(): arrived = lax.ppermute(src, ('row', 'col'), pairs)]
    ppermute x31 -> x29, starting transfers between devices: 18.2 us -> 24.5 us  [swap(): return lax.ppermute(x, axis, [(i, i ^ mask) for i in range(size)])]
    concatenate x5 -> x2, other arithmetic: 5.32 us -> 0.08 us  [body(): jnp.concatenate([both[0] + both[1] * jnp.array([1, 0], jnp.float32)[:, No...]
    slice x3 -> x2, local copies, waits for them, and re-layouts: 4.84 us -> 0.57 us  [the longest x1 0.56 us: body(): return (out, jnp.stack([piece[0], scaled]))]
    ppermute x4 -> x3, waiting for transfers between devices: 0.01 us -> 4.08 us  [body(): came = lax.ppermute(after(out[n], *before), 'pole', pairs)]
    ppermute x8 -> x2, waiting for transfers between devices: 44 us -> 40.3 us  [fetch_factor(): arrived = lax.ppermute(src, ('row', 'col'), pairs)]
    ppermute x31 -> x29, waiting for transfers between devices: 76 us -> 73.3 us  [swap(): return lax.ppermute(x, axis, [(i, i ^ mask) for i in range(size)])]
  transfers between devices with their start and end apart: 43 -> 34, of which waited for: 18 -> 20; matrix products, arithmetic and copies ran while one was open for 12% -> 10% of each run, Pallas kernels for 29% -> 26%
where the time goes in v3:
time: 287 us; the launch traced here: 286 us
  waiting for transfers between devices  118 us (41%)
  Pallas kernels  73.4 us (26%)
  starting transfers between devices  37.9 us (13%)
  other arithmetic  30.4 us (11%)
  local copies, waits for them, and re-layouts  24.8 us (9%)
    pallas_call x8, Pallas kernels, product(): pl.pallas_call(kernel, out_shape=out_shape, grid_spec=pltpu.PrefetchScala...  73.4 us
    ppermute x29, waiting for transfers between devices, swap(): return lax.ppermute(x, axis, [(i, i ^ mask) for i in range(size)])  73.3 us
    ppermute x2, waiting for transfers between devices, fetch_factor(): arrived = lax.ppermute(src, ('row', 'col'), pairs)  40.3 us
    ppermute x29, starting transfers between devices, swap(): return lax.ppermute(x, axis, [(i, i ^ mask) for i in range(size)])  24.5 us
    unnamed x54, local copies, waits for them, and re-layouts  13.5 us
    ppermute x2, starting transfers between devices, fetch_factor(): arrived = lax.ppermute(src, ('row', 'col'), pairs)  10.5 us
    convert_element_type x8, other arithmetic, halve_step(): return (send.astype(kind), keep)  8.79 us
    dynamic_slice x2, local copies, waits for them, and re-layouts, fetch_factor(): own = lax.dynamic_slice(panel, (start, first), (cols, width))  6.2 us
  transfers between devices with their start and end apart: 34, of which 20 were waited for; matrix products, arithmetic and copies ran while one was open for 10% of the time, Pallas kernels for 26%

profile of v3, /device:TPU:0, one launch (start us, length us, event | category | flops | bytes accessed | tf_op | source)
XLA Modules:
  0.0 286.0 jit_solution(4876859986378573018)
XLA Ops:
  0.7 3.0 %dynamic-slice_bitcast_fusion.1 = bf16[2048,512]{1,0:T(8,128)(2,1)} fusion(bf16[1,8192,512]{2,1,0:T(8,128)(2,1)} %param.9, s32[]{:T(128)S(6)} %select_n.234), kind=kLoop, calls=%fused_computation.9 | loop fusion | bytes 4194308 | tf_op jit(solution)/shard_map/dynamic_slice | solution.py:188
  3.7 5.0 %collective-permute-start = (bf16[2048,512]{1,0:T(8,128)(2,1)}, bf16[2048,512]{1,0:T(8,128)(2,1)S(1)}, u32[]{:S(2)}, u32[]{:S(2)}) collective-permute-start(bf16[2048,512]{1,0:T(8,128)(2,1)} %dynamic-slice_bitcast_fusion.1), channel_id=1, source_target_pairs={{0,16},{2,18},{4,20},{6,22},{24,8},{26,10},{28,12},{30,14},{1,17},... | collective-permute-start | bytes 6291464 | tf_op jit(solution)/shard_map/ppermute | solution.py:193
  10.3 3.2 %dynamic-slice_bitcast_fusion = bf16[2048,512]{1,0:T(8,128)(2,1)} fusion(bf16[1,8192,512]{2,1,0:T(8,128)(2,1)} %param.10, s32[]{:T(128)S(6)} %select_n.234), kind=kLoop, calls=%fused_computation.7 | loop fusion | bytes 4194308 | tf_op jit(solution)/shard_map/dynamic_slice | solution.py:188
  13.4 40.3 %collective-permute-done = bf16[2048,512]{1,0:T(8,128)(2,1)S(1)} collective-permute-done((bf16[2048,512]{1,0:T(8,128)(2,1)}, bf16[2048,512]{1,0:T(8,128)(2,1)S(1)}, u32[]{:S(2)}, u32[]{:S(2)}) %collective-permute-start) | collective-permute-done | bytes 2097184 | tf_op jit(solution)/shard_map/ppermute | solution.py:193
  54.3 3.0 %broadcast_in_dim.36.mask_ref = bf16[16,4,16,2048]{3,2,1,0:T(8,128)(2,1)} broadcast(bf16[16,4,2048]{2,1,0:T(4,128)(2,1)S(1)} %broadcast_in_dim.35), dimensions={0,1,3} | broadcast | bytes 4456448 | tf_op jit(solution)/shard_map/broadcast_in_dim | solution.py:225
  57.3 5.6 %collective-permute-start.8 = (bf16[2048,512]{1,0:T(8,128)(2,1)}, bf16[2048,512]{1,0:T(8,128)(2,1)}, u32[]{:S(2)}, u32[]{:S(2)}) collective-permute-start(bf16[2048,512]{1,0:T(8,128)(2,1)} %dynamic-slice_bitcast_fusion), channel_id=1, source_target_pairs={{0,16},{2,18},{4,20},{6,22},{24,8},{26,10},{28,12},{30,14},{1,17},... | collective-permute-start | bytes 6291464 | tf_op jit(solution)/shard_map/ppermute | solution.py:193
  62.8 2.2 broadcast_select_fusion.1.f_ref
  65.0 8.6 %shard_map.86 = (bf16[2048,256]{1,0:T(8,128)(2,1)}, bf16[2048,256]{1,0:T(8,128)(2,1)}) custom-call(s32[2]{0:T(128)S(1)} %pad_add_fusion.3.where_ref, f32[1]{0:T(128)} %copy.37.weight_ref, bf16[8192,2048]{1,0:T(8,128)(2,1)} %bitcast.154, bf16[16,4,16,2048]{3,2,1,0:T(8,128)(2,1)S(1)} %broadcast_in_dim.33.mask_ref, ...), custom_call_target="tpu_custom_call" | custom-call | flops 8388608 | bytes 1048576 | tf_op jit(solution)/shard_map/pallas_call | solution.py:172
  74.2 2.2 copy-done.3
  76.4 7.6 %shard_map.87 = (bf16[2048,256]{1,0:T(8,128)(2,1)S(1)}, bf16[2048,256]{1,0:T(8,128)(2,1)S(1)}) custom-call(s32[2]{0:T(128)S(1)} %get-tuple-element.54.where_ref, f32[1]{0:T(128)} %copy.37.weight_ref, bf16[8192,2048]{1,0:T(8,128)(2,1)} %bitcast.155, bf16[16,4,16,2048]{3,2,1,0:T(8,128)(2,1)S(1)} %copy-done.3, bf16[2048,512]{1,0:T(8,128)(2,1)S(1)} %broadcast_select_fusion.1.f_ref), custom_call_target="tpu_custom_call" | custom-call | flops 8388608 | bytes 1048576 | tf_op jit(solution)/shard_map/pallas_call | solution.py:172
  85.7 1.2 copy-done.16
  86.9 10.3 %shard_map.88 = (bf16[2048,512]{1,0:T(8,128)(2,1)}, f32[512,512]{1,0:T(8,128)S(1)}) custom-call(s32[2]{0:T(128)S(1)} %get-tuple-element.56.where_ref, f32[1]{0:T(128)} %copy.37.weight_ref, bf16[8192,2048]{1,0:T(8,128)(2,1)} %bitcast.156, bf16[16,4,16,2048]{3,2,1,0:T(8,128)(2,1)S(1)} %copy-done.3, bf16[2048,512]{1,0:T(8,128)(2,1)S(1)} %broadcast_select_fusion.1.f_ref, ...), custom_call_target="tpu_custom_call" | custom-call | flops 8388608 | bytes 1048576 | tf_op jit(solution)/shard_map/pallas_call | solution.py:172
  97.3 1.5 collective-permute-start.5
  98.9 9.3 %shard_map.89 = (f32[2048,512]{1,0:T(8,128)S(1)}, f32[512,512]{1,0:T(8,128)S(1)}) custom-call(s32[2]{0:T(128)S(1)} %pad_add_fusion.1.where_ref, f32[1]{0:T(128)} %copy.37.weight_ref, bf16[8192,2048]{1,0:T(8,128)(2,1)} %bitcast.157, bf16[16,4,16,2048]{3,2,1,0:T(8,128)(2,1)} %copy-done.2, bf16[2048,512]{1,0:T(8,128)(2,1)S(1)} %broadcast_select_fusion.1.f_ref, ...), custom_call_target="tpu_custom_call" | custom-call | flops 8388608 | bytes 1048576 | tf_op jit(solution)/shard_map/pallas_call | solution.py:172
  108.1 2.0 copy-done.4
  110.2 2.6 broadcast_select_fusion.f_ref
  113.4 8.6 %shard_map.90 = (bf16[2048,256]{1,0:T(8,128)(2,1)}, bf16[2048,256]{1,0:T(8,128)(2,1)}) custom-call(s32[2]{0:T(128)S(1)} %pad_add_fusion.3.where_ref, f32[1]{0:T(128)} %copy.37.weight_ref, bf16[8192,2048]{1,0:T(8,128)(2,1)} %bitcast.158, bf16[16,4,16,2048]{3,2,1,0:T(8,128)(2,1)S(1)} %copy-done, bf16[2048,512]{1,0:T(8,128)(2,1)S(1)} %broadcast_select_fusion.f_ref), custom_call_target="tpu_custom_call" | custom-call | flops 8388608 | bytes 1048576 | tf_op jit(solution)/shard_map/pallas_call | solution.py:172
  122.5 8.6 %shard_map.91 = (bf16[2048,256]{1,0:T(8,128)(2,1)}, bf16[2048,256]{1,0:T(8,128)(2,1)}) custom-call(s32[2]{0:T(128)S(1)} %get-tuple-element.54.where_ref, f32[1]{0:T(128)} %copy.37.weight_ref, bf16[8192,2048]{1,0:T(8,128)(2,1)} %bitcast.159, bf16[16,4,16,2048]{3,2,1,0:T(8,128)(2,1)S(1)} %copy-done, bf16[2048,512]{1,0:T(8,128)(2,1)S(1)} %broadcast_select_fusion.f_ref), custom_call_target="tpu_custom_call" | custom-call | flops 8388608 | bytes 1048576 | tf_op jit(solution)/shard_map/pallas_call | solution.py:172
  131.7 2.2 copy-done.1
  133.8 10.5 %shard_map.92 = (bf16[2048,256]{1,0:T(8,128)(2,1)}, bf16[2048,256]{1,0:T(8,128)(2,1)S(1)}, f32[512,512]{1,0:T(8,128)S(1)}) custom-call(s32[2]{0:T(128)S(1)} %get-tuple-element.56.where_ref, f32[1]{0:T(128)} %copy.37.weight_ref, bf16[8192,2048]{1,0:T(8,128)(2,1)} %bitcast.160, bf16[16,4,16,2048]{3,2,1,0:T(8,128)(2,1)S(1)} %copy-done.1, ...), custom_call_target="tpu_custom_call" | custom-call | flops 8388608 | bytes 1048576 | tf_op jit(solution)/shard_map/pallas_call | solution.py:172
  145.2 2.6 fusion.2
  147.8 1.6 collective-permute-start.6
  149.4 1.2 copy-done.18
  150.6 9.8 %shard_map.93 = (f32[2048,256]{1,0:T(8,128)S(1)}, f32[2048,256]{1,0:T(8,128)S(1)}, f32[512,512]{1,0:T(8,128)S(1)}) custom-call(s32[2]{0:T(128)S(1)} %pad_add_fusion.1.where_ref, f32[1]{0:T(128)} %copy.37.weight_ref, bf16[8192,2048]{1,0:T(8,128)(2,1)} %bitcast.161, bf16[16,4,16,2048]{3,2,1,0:T(8,128)(2,1)} %broadcast_in_dim.36.mask_ref, ...), custom_call_target="tpu_custom_call" | custom-call | flops 8388608 | bytes 1048576 | tf_op jit(solution)/shard_map/pallas_call | solution.py:172
  160.5 1.3 copy-done.12
  163.6 2.3 convert_add_fusion
  166.0 3.8 %collective-permute-done.13 = bf16[2048,256]{1,0:T(8,128)(2,1)} collective-permute-done((bf16[2048,256]{1,0:T(8,128)(2,1)}, bf16[2048,256]{1,0:T(8,128)(2,1)}, u32[]{:S(2)}, u32[]{:S(2)}) %collective-permute-start.13) | collective-permute-done | bytes 1048608 | tf_op jit(solution)/shard_map/ppermute | solution.py:268
  169.8 2.1 fusion.16
  171.9 1.6 collective-permute-start.14
  173.5 2.0 fusion.13
  175.9 1.4 fusion.8
  178.2 1.1 convert_add_fusion.2
  179.3 12.8 %collective-permute-done.14 = bf16[2,512,256]{2,1,0:T(8,128)(2,1)} collective-permute-done((bf16[2,512,256]{2,1,0:T(8,128)(2,1)}, bf16[2,512,256]{2,1,0:T(8,128)(2,1)}, u32[]{:S(2)}, u32[]{:S(2)}) %collective-permute-start.14) | collective-permute-done | bytes 524320 | tf_op jit(solution)/shard_map/ppermute | solution.py:18
  193.1 1.7 collective-permute-start.15
  194.8 13.6 %collective-permute-done.7 = bf16[1,512,512]{2,1,0:T(8,128)(2,1)} collective-permute-done((bf16[1,512,512]{2,1,0:T(8,128)(2,1)}, bf16[1,512,512]{2,1,0:T(8,128)(2,1)}, u32[]{:S(2)}, u32[]{:S(2)}) %collective-permute-start.7) | collective-permute-done | bytes 524320 | tf_op jit(solution)/shard_map/ppermute | solution.py:18
  208.4 1.4 fusion.15
  210.2 1.2 multiply_reduce_fusion
  211.4 5.0 %collective-permute-done.25 = bf16[2,1,4,2,16,512]{5,4,3,2,1,0:T(8,128)(2,1)S(1)} collective-permute-done((bf16[2,1,4,2,16,512]{5,4,3,2,1,0:T(8,128)(2,1)S(1)}, bf16[2,1,4,2,16,512]{5,4,3,2,1,0:T(8,128)(2,1)S(1)}, u32[]{:S(2)}, u32[]{:S(2)}) %collective-permute-start.25) | collective-permute-done | bytes 262176 | tf_op jit(solution)/shard_map/ppermute | solution.py:18
  216.5 1.0 convert_add_fusion.6
  217.8 5.1 %collective-permute-done.26 = bf16[2,2,2,16,512]{4,3,2,0,1:T(8,128)(2,1)S(1)} collective-permute-done((bf16[2,2,2,16,512]{4,3,2,0,1:T(8,128)(2,1)S(1)}, bf16[2,2,2,16,512]{4,3,2,0,1:T(8,128)(2,1)S(1)}, u32[]{:S(2)}, u32[]{:S(2)}) %collective-permute-start.26) | collective-permute-done | bytes 131104 | tf_op jit(solution)/shard_map/ppermute | solution.py:18
  223.9 2.5 collective-permute-start.17
  226.5 1.9 collective-permute-done.27
  229.4 4.0 %collective-permute-done.28 = f32[2,2,1,16,512]{4,3,2,1,0:T(8,128)S(1)} collective-permute-done((f32[2,2,1,16,512]{4,3,2,1,0:T(8,128)S(1)}, f32[2,2,1,16,512]{4,3,2,1,0:T(8,128)S(1)}, u32[]{:S(2)}, u32[]{:S(2)}) %collective-permute-start.28) | collective-permute-done | bytes 131104 | tf_op jit(solution)/shard_map/ppermute | solution.py:18
  233.6 3.2 %collective-permute-done.17 = bf16[2,512,256]{2,1,0:T(8,128)(2,1)S(1)} collective-permute-done((bf16[2,512,256]{2,1,0:T(8,128)(2,1)S(1)}, bf16[2,512,256]{2,1,0:T(8,128)(2,1)S(1)}, u32[]{:S(2)}, u32[]{:S(2)}) %collective-permute-start.17) | collective-permute-done | bytes 524320 | tf_op jit(solution)/shard_map/ppermute | solution.py:18
  237.6 2.1 collective-permute-start.18
  240.5 3.4 %collective-permute-done.29 = bf16[3,1,16,512]{3,2,0,1:T(8,128)(2,1)S(1)} collective-permute-done((bf16[3,1,16,512]{3,2,0,1:T(8,128)(2,1)S(1)}, bf16[3,1,16,512]{3,2,0,1:T(8,128)(2,1)S(1)}, u32[]{:S(2)}, u32[]{:S(2)}) %collective-permute-start.29) | collective-permute-done | bytes 49184 | tf_op jit(solution)/shard_map/ppermute | solution.py:18
  243.9 4.8 %collective-permute-done.18 = bf16[1,512,256]{2,1,0:T(8,128)(2,1)S(1)} collective-permute-done((bf16[1,512,256]{2,1,0:T(8,128)(2,1)S(1)}, bf16[1,512,256]{2,1,0:T(8,128)(2,1)S(1)}, u32[]{:S(2)}, u32[]{:S(2)}) %collective-permute-start.18) | collective-permute-done | bytes 262176 | tf_op jit(solution)/shard_map/ppermute | solution.py:18
  248.6 1.0 convert_add_fusion.5
  249.8 1.1 collective-permute-done.19
  251.0 1.6 collective-permute-start.20
  252.6 2.0 collective-permute-done.20
  254.5 2.9 %collective-permute-start.21 = (f32[512]{0:T(512)S(1)}, f32[512]{0:T(512)S(1)}, u32[]{:S(2)}, u32[]{:S(2)}) collective-permute-start(f32[512]{0:T(512)S(1)} %add.278), channel_id=1, source_target_pairs={{0,4},{2,6},{4,0},{6,2},{8,12},{10,14},{12,8},{14,10},{1,5},{3,7},... | collective-permute-start | bytes 6152 | tf_op jit(solution)/shard_map/ppermute | solution.py:18
  257.5 1.6 collective-permute-done.21
  259.0 1.9 collective-permute-start.22
  261.0 2.6 collective-permute-done.22
  263.7 2.0 collective-permute-start.31
  265.7 1.5 collective-permute-done.23
  267.3 2.2 collective-permute-done.31
  269.5 1.7 collective-permute-start.32
  271.2 6.2 %collective-permute-done.32 = bf16[3,1,4,2,16,512]{5,4,3,2,0,1:T(8,128)(2,1)S(1)} collective-permute-done((bf16[3,1,4,2,16,512]{5,4,3,2,0,1:T(8,128)(2,1)S(1)}, bf16[3,1,4,2,16,512]{5,4,3,2,0,1:T(8,128)(2,1)S(1)}, u32[]{:S(2)}, u32[]{:S(2)}) %collective-permute-start.32) | collective-permute-done | bytes 393248 | tf_op jit(solution)/shard_map/ppermute | solution.py:18
  278.5 2.4 collective-permute-done.33
  280.9 1.7 fusion.1
  283.5 1.5 pad_maximum_fusion
  285.0 1.1 pad_maximum_fusion.1
  (129 shorter events, 17.0 us)
Async XLA Ops:
  0.6 8.1 %copy-start.25 = (s32[2,64,16]{1,2,0:T(8,128)S(1)}, s32[2,64,16]{1,2,0:T(8,128)}, u32[]{:S(2)}) copy-start(s32[2,64,16]{1,2,0:T(8,128)} %param.8) | copy-start | bytes 24580
  3.7 50.0 %collective-permute-start = (bf16[2048,512]{1,0:T(8,128)(2,1)}, bf16[2048,512]{1,0:T(8,128)(2,1)S(1)}, u32[]{:S(2)}, u32[]{:S(2)}) collective-permute-start(bf16[2048,512]{1,0:T(8,128)(2,1)} %dynamic-slice_bitcast_fusion.1), channel_id=1, source_target_pairs={{0,16},{2,18},{4,20},{6,22},{24,8},{26,10},{28,12},{30,14},{1,17},... | collective-permute-start | bytes 6291464 | tf_op jit(solution)/shard_map/ppermute | solution.py:193
  53.7 3.5 %copy-start.23 = (bf16[2048,512]{1,0:T(8,128)(2,1)}, bf16[2048,512]{1,0:T(8,128)(2,1)S(1)}, u32[]{:S(2)}) copy-start(bf16[2048,512]{1,0:T(8,128)(2,1)S(1)} %collective-permute-done) | copy-start | bytes 6291460
  54.3 10.7 %copy-start.2 = (bf16[16,4,16,2048]{3,2,1,0:T(8,128)(2,1)}, bf16[16,4,16,2048]{3,2,1,0:T(8,128)(2,1)S(1)}, u32[]{:S(2)}) copy-start(bf16[16,4,16,2048]{3,2,1,0:T(8,128)(2,1)S(1)} %broadcast_in_dim.33.mask_ref) | copy-start | bytes 12582916
  57.3 52.9 %collective-permute-start.8 = (bf16[2048,512]{1,0:T(8,128)(2,1)}, bf16[2048,512]{1,0:T(8,128)(2,1)}, u32[]{:S(2)}, u32[]{:S(2)}) collective-permute-start(bf16[2048,512]{1,0:T(8,128)(2,1)} %dynamic-slice_bitcast_fusion), channel_id=1, source_target_pairs={{0,16},{2,18},{4,20},{6,22},{24,8},{26,10},{28,12},{30,14},{1,17},... | collective-permute-start | bytes 6291464 | tf_op jit(solution)/shard_map/ppermute | solution.py:193
  73.7 11.0 %collective-permute-start.1 = (bf16[2048,256]{1,0:T(8,128)(2,1)}, bf16[2048,256]{1,0:T(8,128)(2,1)S(1)}, u32[]{:S(2)}, u32[]{:S(2)}) collective-permute-start(bf16[2048,256]{1,0:T(8,128)(2,1)} %get-tuple-element.39), channel_id=1, source_target_pairs={{0,2},{2,0},{4,6},{6,4},{8,10},{10,8},{12,14},{14,12},{1,3},{3,1},... | collective-permute-start | bytes 3145736 | tf_op jit(solution)/shard_map/ppermute | solution.py:18
  73.7 11.9 %collective-permute-start.2 = (bf16[2048,256]{1,0:T(8,128)(2,1)}, bf16[2048,256]{1,0:T(8,128)(2,1)}, u32[]{:S(2)}, u32[]{:S(2)}) collective-permute-start(bf16[2048,256]{1,0:T(8,128)(2,1)} %get-tuple-element.43), channel_id=1, source_target_pairs={{0,2},{2,0},{4,6},{6,4},{8,10},{10,8},{12,14},{14,12},{1,3},{3,1},... | collective-permute-start | bytes 3145736 | tf_op jit(solution)/shard_map/ppermute | solution.py:18
  74.2 2.2 copy-start.3
  84.0 14.8 %collective-permute-start.3 = (bf16[2048,256]{1,0:T(8,128)(2,1)S(1)}, bf16[2048,256]{1,0:T(8,128)(2,1)S(1)}, u32[]{:S(2)}, u32[]{:S(2)}) collective-permute-start(bf16[2048,256]{1,0:T(8,128)(2,1)S(1)} %get-tuple-element.41), channel_id=1, source_target_pairs={{0,2},{2,0},{4,6},{6,4},{8,10},{10,8},{12,14},{14,12},{1,3},{3,1},... | collective-permute-start | bytes 3145736 | tf_op jit(solution)/shard_map/ppermute | solution.py:18
  84.1 14.8 %collective-permute-start.4 = (bf16[2048,256]{1,0:T(8,128)(2,1)S(1)}, bf16[2048,256]{1,0:T(8,128)(2,1)S(1)}, u32[]{:S(2)}, u32[]{:S(2)}) collective-permute-start(bf16[2048,256]{1,0:T(8,128)(2,1)S(1)} %get-tuple-element.47), channel_id=1, source_target_pairs={{0,2},{2,0},{4,6},{6,4},{8,10},{10,8},{12,14},{14,12},{1,3},{3,1},... | collective-permute-start | bytes 3145736 | tf_op jit(solution)/shard_map/ppermute | solution.py:18
  84.6 1.0 copy-start.15
  85.7 1.2 copy-start.16
  97.3 47.9 %collective-permute-start.5 = (bf16[2048,512]{1,0:T(8,128)(2,1)}, bf16[2048,512]{1,0:T(8,128)(2,1)}, u32[]{:S(2)}, u32[]{:S(2)}) collective-permute-start(bf16[2048,512]{1,0:T(8,128)(2,1)} %get-tuple-element.44), channel_id=1, source_target_pairs={{0,1},{1,0},{2,3},{3,2},{4,5},{5,4},{6,7},{7,6},{8,9},{9,8},{10,11... | collective-permute-start | bytes 6291464 | tf_op jit(solution)/shard_map/ppermute | solution.py:268
  108.1 2.0 copy-start.4
  110.2 2.6 copy-start.6
  110.2 3.2 %copy-start = (bf16[16,4,16,2048]{3,2,1,0:T(8,128)(2,1)S(1)}, bf16[16,4,16,2048]{3,2,1,0:T(8,128)(2,1)}, u32[]{:S(2)}) copy-start(bf16[16,4,16,2048]{3,2,1,0:T(8,128)(2,1)} %broadcast_in_dim.36.mask_ref) | copy-start | bytes 12582916
  122.0 9.7 %collective-permute-start.10 = (bf16[2048,256]{1,0:T(8,128)(2,1)}, bf16[2048,256]{1,0:T(8,128)(2,1)}, u32[]{:S(2)}, u32[]{:S(2)}) collective-permute-start(bf16[2048,256]{1,0:T(8,128)(2,1)} %get-tuple-element.57), channel_id=1, source_target_pairs={{0,2},{2,0},{4,6},{6,4},{8,10},{10,8},{12,14},{14,12},{1,3},{3,1},... | collective-permute-start | bytes 3145736 | tf_op jit(solution)/shard_map/ppermute | solution.py:18
  122.0 9.7 %collective-permute-start.9 = (bf16[2048,256]{1,0:T(8,128)(2,1)}, bf16[2048,256]{1,0:T(8,128)(2,1)}, u32[]{:S(2)}, u32[]{:S(2)}) collective-permute-start(bf16[2048,256]{1,0:T(8,128)(2,1)} %get-tuple-element.53), channel_id=1, source_target_pairs={{0,2},{2,0},{4,6},{6,4},{8,10},{10,8},{12,14},{14,12},{1,3},{3,1},... | collective-permute-start | bytes 3145736 | tf_op jit(solution)/shard_map/ppermute | solution.py:18
  131.1 18.3 %collective-permute-start.11 = (bf16[2048,256]{1,0:T(8,128)(2,1)}, bf16[2048,256]{1,0:T(8,128)(2,1)}, u32[]{:S(2)}, u32[]{:S(2)}) collective-permute-start(bf16[2048,256]{1,0:T(8,128)(2,1)} %get-tuple-element.55), channel_id=1, source_target_pairs={{0,2},{2,0},{4,6},{6,4},{8,10},{10,8},{12,14},{14,12},{1,3},{3,1},... | collective-permute-start | bytes 3145736 | tf_op jit(solution)/shard_map/ppermute | solution.py:18
  131.1 18.3 %collective-permute-start.12 = (bf16[2048,256]{1,0:T(8,128)(2,1)}, bf16[2048,256]{1,0:T(8,128)(2,1)}, u32[]{:S(2)}, u32[]{:S(2)}) collective-permute-start(bf16[2048,256]{1,0:T(8,128)(2,1)} %get-tuple-element.61), channel_id=1, source_target_pairs={{0,2},{2,0},{4,6},{6,4},{8,10},{10,8},{12,14},{14,12},{1,3},{3,1},... | collective-permute-start | bytes 3145736 | tf_op jit(solution)/shard_map/ppermute | solution.py:18
  131.6 2.2 copy-start.1
  133.8 11.4 %copy-start.5 = (f32[2048,512]{1,0:T(8,128)S(1)}, f32[2048,512]{1,0:T(8,128)}, u32[]{:S(2)}) copy-start(f32[2048,512]{1,0:T(8,128)} %copy-done.4) | copy-start | bytes 12582916
  144.3 3.5 %copy-start.17 = (f32[512,512]{1,0:T(8,128)}, f32[512,512]{1,0:T(8,128)S(1)}, u32[]{:S(2)}) copy-start(f32[512,512]{1,0:T(8,128)S(1)} %get-tuple-element.60.start_ref) | copy-start | bytes 3145732
  144.3 3.5 %copy-start.19 = (bf16[2048,256]{1,0:T(8,128)(2,1)}, bf16[2048,256]{1,0:T(8,128)(2,1)S(1)}, u32[]{:S(2)}) copy-start(bf16[2048,256]{1,0:T(8,128)(2,1)S(1)} %get-tuple-element.65) | copy-start | bytes 3145732
  144.3 25.4 %collective-permute-start.13 = (bf16[2048,256]{1,0:T(8,128)(2,1)}, bf16[2048,256]{1,0:T(8,128)(2,1)}, u32[]{:S(2)}, u32[]{:S(2)}) collective-permute-start(bf16[2048,256]{1,0:T(8,128)(2,1)} %get-tuple-element.58), channel_id=1, source_target_pairs={{0,1},{1,0},{2,3},{3,2},{4,5},{5,4},{6,7},{7,6},{8,9},{9,8},{10,11... | collective-permute-start | bytes 3145736 | tf_op jit(solution)/shard_map/ppermute | solution.py:268
  147.8 25.6 %collective-permute-start.6 = (bf16[2,512,512]{2,1,0:T(8,128)(2,1)}, bf16[2,512,512]{2,1,0:T(8,128)(2,1)}, u32[]{:S(2)}, u32[]{:S(2)}) collective-permute-start(bf16[2,512,512]{2,1,0:T(8,128)(2,1)} %fusion.2), channel_id=1, source_target_pairs={{0,4},{2,6},{4,0},{6,2},{8,12},{10,14},{12,8},{14,10},{1,5},{3,7},... | collective-permute-start | bytes 3145736 | tf_op jit(solution)/shard_map/ppermute | solution.py:18
  149.4 1.2 copy-start.18
  150.6 12.1 %copy-start.7 = (f32[512,512]{1,0:T(8,128)S(1)}, f32[512,512]{1,0:T(8,128)}, u32[]{:S(2)}) copy-start(f32[512,512]{1,0:T(8,128)} %copy-done.6) | copy-start | bytes 3145732
  160.5 1.3 copy-start.12
  161.8 1.0 copy-start.8
  161.8 1.8 copy-start.10
  163.6 12.3 %collective-permute-start.24 = (bf16[2,2,4,1,2,16,512]{6,5,4,2,1,0,3:T(8,128)(2,1)}, bf16[2,2,4,1,2,16,512]{6,5,4,2,1,0,3:T(8,128)(2,1)}, u32[]{:S(2)}, u32[]{:S(2)}) collective-permute-start(bf16[2,2,4,1,2,16,512]{6,5,4,2,1,0,3:T(8,128)(2,1)} %fusion.18), channel_id=1, source_target_pairs={{0,2},{2,0},{4,6},{6,4},{8,10},{10,8},{12,14},{14,12},{1,3},{3,1},... | collective-permute-start | bytes 1572872 | tf_op jit(solution)/shard_map/ppermute | solution.py:18
  163.6 6.2 %copy-start.13 = (f32[2048,256]{1,0:T(8,128)S(1)}, f32[2048,256]{1,0:T(8,128)}, u32[]{:S(2)}) copy-start(f32[2048,256]{1,0:T(8,128)} %copy-done.12) | copy-start | bytes 6291460
  166.0 9.5 %copy-start.21 = (f32[2,1,512,512]{3,2,1,0:T(8,128)}, f32[2,1,512,512]{3,2,1,0:T(8,128)S(1)}, u32[]{:S(2)}) copy-start(f32[2,1,512,512]{3,2,1,0:T(8,128)S(1)} %convert_add_fusion) | copy-start | bytes 6291460
  169.8 6.2 %copy-start.9 = (f32[512,512]{1,0:T(8,128)S(1)}, f32[512,512]{1,0:T(8,128)}, u32[]{:S(2)}) copy-start(f32[512,512]{1,0:T(8,128)} %copy-done.8) | copy-start | bytes 3145732
  171.9 20.3 %collective-permute-start.14 = (bf16[2,512,256]{2,1,0:T(8,128)(2,1)}, bf16[2,512,256]{2,1,0:T(8,128)(2,1)}, u32[]{:S(2)}, u32[]{:S(2)}) collective-permute-start(bf16[2,512,256]{2,1,0:T(8,128)(2,1)} %fusion.16), channel_id=1, source_target_pairs={{0,4},{2,6},{4,0},{6,2},{8,12},{10,14},{12,8},{14,10},{1,5},{3,7},... | collective-permute-start | bytes 1572872 | tf_op jit(solution)/shard_map/ppermute | solution.py:18
  175.5 1.9 copy-start.20
  175.5 32.9 %collective-permute-start.7 = (bf16[1,512,512]{2,1,0:T(8,128)(2,1)}, bf16[1,512,512]{2,1,0:T(8,128)(2,1)}, u32[]{:S(2)}, u32[]{:S(2)}) collective-permute-start(bf16[1,512,512]{2,1,0:T(8,128)(2,1)} %fusion.13), channel_id=1, source_target_pairs={{0,8},{2,10},{4,12},{6,14},{8,0},{10,2},{12,4},{14,6},{1,9},{3,11}... | collective-permute-start | bytes 1572872 | tf_op jit(solution)/shard_map/ppermute | solution.py:18
  175.9 2.2 copy-start.14
  177.4 31.0 %copy-start.22 = (f32[2,1,512,512]{3,2,1,0:T(8,128)S(1)}, f32[2,1,512,512]{3,2,1,0:T(8,128)}, u32[]{:S(2)}) copy-start(f32[2,1,512,512]{3,2,1,0:T(8,128)} %copy-done.21) | copy-start | bytes 6291460
  177.4 40.2 %collective-permute-start.16 = (bf16[2048,256]{1,0:T(8,128)(2,1)S(1)}, bf16[2048,256]{1,0:T(8,128)(2,1)S(1)}, u32[]{:S(2)}, u32[]{:S(2)}) collective-permute-start(bf16[2048,256]{1,0:T(8,128)(2,1)S(1)} %copy-done.20), channel_id=1, source_target_pairs={{0,1},{1,0},{2,3},{3,2},{4,5},{5,4},{6,7},{7,6},{8,9},{9,8},{10,11... | collective-permute-start | bytes 3145736 | tf_op jit(solution)/shard_map/ppermute | solution.py:268
  193.1 23.4 %collective-permute-start.15 = (bf16[1,512,256]{2,1,0:T(8,128)(2,1)S(1)}, bf16[1,512,256]{2,1,0:T(8,128)(2,1)S(1)}, u32[]{:S(2)}, u32[]{:S(2)}) collective-permute-start(bf16[1,512,256]{2,1,0:T(8,128)(2,1)S(1)} %fusion.20), channel_id=1, source_target_pairs={{0,8},{2,10},{4,12},{6,14},{8,0},{10,2},{12,4},{14,6},{1,9},{3,11}... | collective-permute-start | bytes 786440 | tf_op jit(solution)/shard_map/ppermute | solution.py:18
  209.9 6.4 %collective-permute-start.25 = (bf16[2,1,4,2,16,512]{5,4,3,2,1,0:T(8,128)(2,1)S(1)}, bf16[2,1,4,2,16,512]{5,4,3,2,1,0:T(8,128)(2,1)S(1)}, u32[]{:S(2)}, u32[]{:S(2)}) collective-permute-start(bf16[2,1,4,2,16,512]{5,4,3,2,1,0:T(8,128)(2,1)S(1)} %dynamic-slice_convert_fusion), channel_id=1, source_target_pairs={{0,16},{16,0},{1,17},{17,1},{2,18},{18,2},{3,19},{19,3},{4,20},{20... | collective-permute-start | bytes 786440 | tf_op jit(solution)/shard_map/ppermute | solution.py:18
  211.4 6.2 %copy-start.11 = (f32[2048,256]{1,0:T(8,128)S(1)}, f32[2048,256]{1,0:T(8,128)}, u32[]{:S(2)}) copy-start(f32[2048,256]{1,0:T(8,128)} %copy-done.10) | copy-start | bytes 6291460
  216.4 6.4 %collective-permute-start.26 = (bf16[2,2,2,16,512]{4,3,2,0,1:T(8,128)(2,1)S(1)}, bf16[2,2,2,16,512]{4,3,2,0,1:T(8,128)(2,1)S(1)}, u32[]{:S(2)}, u32[]{:S(2)}) collective-permute-start(bf16[2,2,2,16,512]{4,3,2,0,1:T(8,128)(2,1)S(1)} %fusion.21), channel_id=1, source_target_pairs={{0,4},{2,6},{4,0},{6,2},{8,12},{10,14},{12,8},{14,10},{1,5},{3,7},... | collective-permute-start | bytes 393224 | tf_op jit(solution)/shard_map/ppermute | solution.py:18
  222.9 5.5 %collective-permute-start.27 = (bf16[2,1,2,16,512]{4,3,2,0,1:T(8,128)(2,1)S(1)}, bf16[2,1,2,16,512]{4,3,2,0,1:T(8,128)(2,1)S(1)}, u32[]{:S(2)}, u32[]{:S(2)}) collective-permute-start(bf16[2,1,2,16,512]{4,3,2,0,1:T(8,128)(2,1)S(1)} %add_convert_fusion), channel_id=1, source_target_pairs={{0,8},{2,10},{4,12},{6,14},{8,0},{10,2},{12,4},{14,6},{1,9},{3,11}... | collective-permute-start | bytes 196616 | tf_op jit(solution)/shard_map/ppermute | solution.py:18
  223.1 10.4 %copy-start.26 = (f32[2]{0:T(128)S(1)}, f32[2]{0:T(128)}, u32[]{:S(2)}) copy-start(f32[2]{0:T(128)} %constant.285.clone) | copy-start | bytes 28
  223.9 12.8 %collective-permute-start.17 = (bf16[2,512,256]{2,1,0:T(8,128)(2,1)S(1)}, bf16[2,512,256]{2,1,0:T(8,128)(2,1)S(1)}, u32[]{:S(2)}, u32[]{:S(2)}) collective-permute-start(bf16[2,512,256]{2,1,0:T(8,128)(2,1)S(1)} %fusion.17), channel_id=1, source_target_pairs={{0,4},{2,6},{4,0},{6,2},{8,12},{10,14},{12,8},{14,10},{1,5},{3,7},... | collective-permute-start | bytes 1572872 | tf_op jit(solution)/shard_map/ppermute | solution.py:18
  228.4 5.0 %collective-permute-start.28 = (f32[2,2,1,16,512]{4,3,2,1,0:T(8,128)S(1)}, f32[2,2,1,16,512]{4,3,2,1,0:T(8,128)S(1)}, u32[]{:S(2)}, u32[]{:S(2)}) collective-permute-start(f32[2,2,1,16,512]{4,3,2,1,0:T(8,128)S(1)} %fusion.22), channel_id=1, source_target_pairs={{0,1},{1,0},{2,3},{3,2},{4,5},{5,4},{6,7},{7,6},{8,9},{9,8},{10,11... | collective-permute-start | bytes 393224 | tf_op jit(solution)/shard_map/ppermute | solution.py:18
  236.8 0.8 copy-start.24
  237.6 11.0 %collective-permute-start.18 = (bf16[1,512,256]{2,1,0:T(8,128)(2,1)S(1)}, bf16[1,512,256]{2,1,0:T(8,128)(2,1)S(1)}, u32[]{:S(2)}, u32[]{:S(2)}) collective-permute-start(bf16[1,512,256]{2,1,0:T(8,128)(2,1)S(1)} %fusion.19), channel_id=1, source_target_pairs={{0,8},{2,10},{4,12},{6,14},{8,0},{10,2},{12,4},{14,6},{1,9},{3,11}... | collective-permute-start | bytes 786440 | tf_op jit(solution)/shard_map/ppermute | solution.py:18
  239.7 4.1 %collective-permute-start.29 = (bf16[3,1,16,512]{3,2,0,1:T(8,128)(2,1)S(1)}, bf16[3,1,16,512]{3,2,0,1:T(8,128)(2,1)S(1)}, u32[]{:S(2)}, u32[]{:S(2)}) collective-permute-start(bf16[3,1,16,512]{3,2,0,1:T(8,128)(2,1)S(1)} %pad_maximum_fusion.4), channel_id=1, source_target_pairs={{0,1},{1,0},{2,3},{3,2},{4,5},{5,4},{6,7},{7,6},{8,9},{9,8},{10,11... | collective-permute-start | bytes 147464 | tf_op jit(solution)/shard_map/ppermute | solution.py:18
  249.7 14.0 %collective-permute-start.30 = (bf16[3,1,2,16,512]{4,3,0,2,1:T(8,128)(2,1)S(1)}, bf16[3,1,2,16,512]{4,3,0,2,1:T(8,128)(2,1)S(1)}, u32[]{:S(2)}, u32[]{:S(2)}) collective-permute-start(bf16[3,1,2,16,512]{4,3,0,2,1:T(8,128)(2,1)S(1)} %bitcast.176), channel_id=1, source_target_pairs={{0,8},{2,10},{4,12},{6,14},{8,0},{10,2},{12,4},{14,6},{1,9},{3,11}... | collective-permute-start | bytes 294920 | tf_op jit(solution)/shard_map/ppermute | solution.py:18
  249.7 1.2 collective-permute-start.19
  251.0 3.6 %collective-permute-start.20 = (f32[512]{0:T(512)S(1)}, f32[512]{0:T(512)S(1)}, u32[]{:S(2)}, u32[]{:S(2)}) collective-permute-start(f32[512]{0:T(512)S(1)} %add.277), channel_id=1, source_target_pairs={{0,16},{16,0},{1,17},{17,1},{2,18},{18,2},{3,19},{19,3},{4,20},{20... | collective-permute-start | bytes 6152 | tf_op jit(solution)/shard_map/ppermute | solution.py:18
  254.5 4.5 %collective-permute-start.21 = (f32[512]{0:T(512)S(1)}, f32[512]{0:T(512)S(1)}, u32[]{:S(2)}, u32[]{:S(2)}) collective-permute-start(f32[512]{0:T(512)S(1)} %add.278), channel_id=1, source_target_pairs={{0,4},{2,6},{4,0},{6,2},{8,12},{10,14},{12,8},{14,10},{1,5},{3,7},... | collective-permute-start | bytes 6152 | tf_op jit(solution)/shard_map/ppermute | solution.py:18
  259.0 4.6 %collective-permute-start.22 = (f32[512]{0:T(512)S(1)}, f32[512]{0:T(512)S(1)}, u32[]{:S(2)}, u32[]{:S(2)}) collective-permute-start(f32[512]{0:T(512)S(1)} %add.279), channel_id=1, source_target_pairs={{0,8},{2,10},{4,12},{6,14},{8,0},{10,2},{12,4},{14,6},{1,9},{3,11}... | collective-permute-start | bytes 6152 | tf_op jit(solution)/shard_map/ppermute | solution.py:18
  263.6 3.6 %collective-permute-start.23 = (f32[512]{0:T(512)S(1)}, f32[512]{0:T(512)S(1)}, u32[]{:S(2)}, u32[]{:S(2)}) collective-permute-start(f32[512]{0:T(512)S(1)} %add.280), channel_id=1, source_target_pairs={{0,1},{1,0},{2,3},{3,2},{4,5},{5,4},{6,7},{7,6},{8,9},{9,8},{10,11... | collective-permute-start | bytes 6152 | tf_op jit(solution)/shard_map/ppermute | solution.py:18
  263.7 5.7 %collective-permute-start.31 = (bf16[3,2,2,16,512]{4,3,0,2,1:T(8,128)(2,1)S(1)}, bf16[3,2,2,16,512]{4,3,0,2,1:T(8,128)(2,1)S(1)}, u32[]{:S(2)}, u32[]{:S(2)}) collective-permute-start(bf16[3,2,2,16,512]{4,3,0,2,1:T(8,128)(2,1)S(1)} %maximum_select_fusion.4), channel_id=1, source_target_pairs={{0,4},{2,6},{4,0},{6,2},{8,12},{10,14},{12,8},{14,10},{1,5},{3,7},... | collective-permute-start | bytes 589832 | tf_op jit(solution)/shard_map/ppermute | solution.py:18
  269.5 7.8 %collective-permute-start.32 = (bf16[3,1,4,2,16,512]{5,4,3,2,0,1:T(8,128)(2,1)S(1)}, bf16[3,1,4,2,16,512]{5,4,3,2,0,1:T(8,128)(2,1)S(1)}, u32[]{:S(2)}, u32[]{:S(2)}) collective-permute-start(bf16[3,1,4,2,16,512]{5,4,3,2,0,1:T(8,128)(2,1)S(1)} %bitcast.167), channel_id=1, source_target_pairs={{0,16},{16,0},{1,17},{17,1},{2,18},{18,2},{3,19},{19,3},{4,20},{20... | collective-permute-start | bytes 1179656 | tf_op jit(solution)/shard_map/ppermute | solution.py:18
  278.3 2.6 collective-permute-start.33

commit v4 on v0

v4 whole, which is shorter than its diff:
```python
import jax
import jax.numpy as jnp
from jax import lax
from jax.experimental import pallas as pl
from jax.experimental.pallas import tpu as pltpu
from jax.sharding import PartitionSpec as P

CORES = 2
AWAY = 2
CHUNKS = 2


def swap(x, axis, mask):
    size = lax.axis_size(axis)
    return lax.ppermute(x, axis, [(i, i ^ mask) for i in range(size)])


def swap_core(x, mask=1):
    return swap(x, "col", mask)


def swap_z(x, mask):
    return swap(x, "col", mask * CORES)


def swap_row(x, mask):
    return swap(x, "row", mask)


def swap_pole(x, mask):
    return swap(x, "pole", mask)


def after(x, *deps):
    if not deps:
        return x
    return lax.optimization_barrier((x,) + deps)[0]


def pick(x, index, axis):
    return lax.dynamic_index_in_dim(x, index, axis, keepdims=False)


def halve(x, axis, index, exchange, kind):
    bit = 0
    while x.shape[axis] > 1:
        size = x.shape[axis]
        pairs = x.reshape(x.shape[:axis] + (size // 2, 2) + x.shape[axis + 1:])
        low = (index >> bit) & 1
        send = pick(pairs, 1 - low, axis + 1).astype(kind)
        x = pick(pairs, low, axis + 1).astype(jnp.float32) + exchange(send, 1 << bit).astype(jnp.float32)
        bit += 1
    return x.reshape(x.shape[:axis] + x.shape[axis + 1:])


def split_three(x):
    terms = []
    for _ in range(3):
        high = lax.reduce_precision(x, 8, 7)
        terms.append(high.astype(jnp.bfloat16))
        x = x - high
    return jnp.stack(terms)


def double(x, squares, axis, index, bit, exchange):
    count = x.size // x.shape[-1]
    message = jnp.concatenate([x.reshape(count, x.shape[-1]), split_three(squares)])
    other = exchange(message, 1 << bit)
    squares = squares + jnp.sum(other[count:].astype(jnp.float32), axis=0)
    other = other[:count].reshape(x.shape)
    low = (index >> bit) & 1
    both = jnp.where(low == 0, jnp.stack([x, other], axis + 1), jnp.stack([other, x], axis + 1))
    return both.reshape(x.shape[:axis] + (2 * x.shape[axis],) + x.shape[axis + 1:]), squares


class ZSum:
    def __init__(self, sources, z):
        self.sources, self.z, self.bit = [(x, 0) for x in sources], z, 0
        self.bits = sources[0].shape[0].bit_length() - 1

    def part(self, flip, *deps):
        total = 0.0
        for x, depth in self.sources:
            spread = 1 << (self.bit - depth + flip)
            index = (self.z >> depth) & (spread - 1)
            if flip:
                index = index ^ (spread >> 1)
            x = x.reshape((x.shape[0] // spread, spread) + x.shape[1:])
            total = total + pick(after(x, *deps), index, 1).astype(jnp.float32)
        return total

    def step(self, *deps):
        send = self.part(1, *deps).astype(jnp.bfloat16)
        came = swap_z(send, 1 << self.bit)
        self.bit += 1
        self.sources.append((came, self.bit))
        return send

    def done(self):
        return self.bit == self.bits

    def result(self, *deps):
        x = self.part(0, *deps)
        return x.reshape(x.shape[1:])


def mask_kernel(a_ref, mask_ref, *outs):
    rows, cols = a_ref.shape
    groups = mask_ref.shape[2]
    shaped = a_ref[...].reshape(groups, rows // groups, cols)
    for k, out_ref in enumerate(outs):
        out_ref[...] = (shaped * mask_ref[k, 0][:, None, :]).reshape(rows, cols)


def apply_masks(inverse, mask):
    rows, cols = inverse.shape
    count, blocks, groups, _ = mask.shape
    block = rows // blocks
    spec = pl.BlockSpec((block, cols), lambda i: (i, 0))
    return pl.pallas_call(
        mask_kernel,
        out_shape=[jax.ShapeDtypeStruct((rows, cols), inverse.dtype)] * count,
        grid=(blocks,),
        in_specs=[spec, pl.BlockSpec((count, 1, groups, cols), lambda i: (0, i, 0, 0))],
        out_specs=[spec] * count,
        compiler_params=pltpu.CompilerParams(vmem_limit_bytes=40 * 2**20),
        cost_estimate=pl.CostEstimate(flops=2 * rows * cols, bytes_accessed=6 * rows * cols, transcendentals=0),
    )(inverse, mask)


def weighted_product(a_ref, f_ref, weight_ref):
    return jnp.dot(a_ref[...], f_ref[...], preferred_element_type=jnp.float32) * weight_ref[0]


def away_kernel(where_ref, weight_ref, a_ref, f_ref, *outs):
    total = weighted_product(a_ref, f_ref, weight_ref)
    width = total.shape[1] // len(outs)
    for n, out_ref in enumerate(outs):
        out_ref[...] = total[:, n * width:(n + 1) * width].astype(out_ref.dtype)


def here_kernel(where_ref, weight_ref, a_ref, f_ref, panel_ref, start_ref, *refs):
    recvs, (out_ref, term_ref) = refs[:AWAY], refs[AWAY:]
    total = weighted_product(a_ref, f_ref, weight_ref)
    total = total + jnp.concatenate([r[...].astype(jnp.float32) for r in recvs], axis=1)
    out_ref[...] = total.astype(out_ref.dtype)
    term = lax.dot_general(
        panel_ref[...], total.astype(jnp.bfloat16), (((0,), (0,)), ((), ())), preferred_element_type=jnp.float32
    )

    @pl.when(pl.program_id(0) == 0)
    def _():
        term_ref[...] = start_ref[...] - term

    @pl.when(pl.program_id(0) > 0)
    def _():
        term_ref[...] = term_ref[...] - term


def product(masked, factor, place, weight, sizes, merge=None):
    zs, block, n_pole = sizes
    cols = masked.shape[1]
    width = factor.shape[1]

    def block_of(i, where):
        return (i * CORES + where[0]) * n_pole + where[1]

    in_specs = [
        pl.BlockSpec(memory_space=pltpu.SMEM),
        pl.BlockSpec((block, cols), lambda i, w: (block_of(i, w), 0)),
        pl.BlockSpec((cols, width), lambda i, w: (0, 0)),
    ]
    part = [pl.BlockSpec((block, width // AWAY), lambda i, w: (i, 0))] * AWAY
    if merge is None:
        kernel, extra = away_kernel, ()
        out_shape = [jax.ShapeDtypeStruct((zs * block, width // AWAY), jnp.bfloat16)] * AWAY
        out_specs = part
    else:
        recv, panel, start, kind = merge
        kernel, extra = here_kernel, (panel, start, *recv)
        full = panel.shape[1]
        term = pl.BlockSpec((full, width), lambda i, w: (0, 0))
        in_specs += [pl.BlockSpec((block, full), lambda i, w: (block_of(i, w), 0)), term] + part
        out_shape = [jax.ShapeDtypeStruct((zs * block, width), kind), jax.ShapeDtypeStruct((full, width), jnp.float32)]
        out_specs = [pl.BlockSpec((block, width), lambda i, w: (i, 0)), term]
    return pl.pallas_call(
        kernel,
        out_shape=out_shape,
        grid_spec=pltpu.PrefetchScalarGridSpec(
            num_scalar_prefetch=1, grid=(zs,), in_specs=in_specs, out_specs=out_specs
        ),
        compiler_params=pltpu.CompilerParams(vmem_limit_bytes=40 * 2**20),
        cost_estimate=pl.CostEstimate(
            flops=2 * zs * block * cols, bytes_accessed=zs * block * width, transcendentals=0
        ),
    )(place, weight, masked, factor, *extra)


def fetch_factor(own):
    n_row, n_col = lax.axis_size("row"), lax.axis_size("col")
    if n_row == 2:
        return swap_row(own, 1)
    ratio = n_col // n_row
    got = own
    for d in range(1, n_row):
        pairs = [((j // ratio) * n_col + j, ((j // ratio + d) % n_row) * n_col + j) for j in range(n_col)]
        arrived = lax.ppermute(own, ("row", "col"), pairs)
        got = arrived if d == 1 else got + arrived
    return got


def body(inv_block, block_masks, panel_first, panel_second, diag_inverse, weights):
    n_row, n_col, n_pole = (lax.axis_size(a) for a in ("row", "col", "pole"))
    row, col, pole = (lax.axis_index(a) for a in ("row", "col", "pole"))
    zs = n_col // CORES
    z, core = col // CORES, col % CORES
    inverse, weight = inv_block[0], weights[0]
    rows, cols = inverse.shape
    width = panel_first.shape[2]
    wide = width // CHUNKS
    blocks = n_col * n_pole
    block = rows // blocks
    sizes = (zs, block, n_pole)
    panels = (panel_first[0], panel_second[0])
    grain = rows // block_masks.shape[1]
    groups = max(1, block // grain)
    parts = [(k, n) for k in range(2) for n in range(CHUNKS)]

    ratio = n_col // n_row
    mine = row == col // ratio
    own, got = [], []
    for k, n in parts:
        piece = lax.dynamic_slice(panels[k], (col % ratio * cols, n * wide), (cols, wide))
        own.append(piece)
        got.append(fetch_factor(after(piece, *got[-1:])))

    mask = jnp.repeat(block_masks.astype(jnp.bfloat16), grain * groups // block, axis=1)
    mask = jnp.repeat(mask, grain, axis=2).reshape(2, blocks, groups, cols)
    masked = apply_masks(inverse, mask)

    def place(c, d, *deps):
        return after(jnp.stack([c, (pole + d) % n_pole]).astype(jnp.int32), *deps)

    dests = list(range(1, n_pole)) + [0]
    token = (masked[0],)
    units, terms = [], []
    for part, (k, n) in enumerate(parts):
        factor = jnp.where(mine, own[part], after(got[part], *token))
        received, arrived = {}, []
        for d in dests:
            away = product(masked[k], factor, place(1 - core, d, *token), weights, sizes)
            token = (away[0],)
            received[d] = [swap_core(x) for x in away]
        term = jnp.zeros((width, wide), jnp.float32)
        for d in dests if part + 1 < len(parts) else dests[::-1]:
            if d == 0:
                for unit in units:
                    if not unit.done():
                        token += (unit.step(),)
            kind = jnp.bfloat16 if d > 0 else jnp.float32
            out, term = product(
                masked[k], factor, place(core, d, *token), weights, sizes, (received[d], panels[k], term, kind)
            )
            token = (out,)
            if d == 0:
                kept = out
            else:
                arrived.append(lax.ppermute(out, "pole", [(i, (i + d) % n_pole) for i in range(n_pole)]))
        terms.append(term)
        units.append(ZSum([x.reshape(zs, block, wide) for x in [kept] + arrived], z))

    each = width // (n_row * blocks)
    split = (2, n_row, zs, CORES, n_pole, each, width)
    term = jnp.stack([jnp.concatenate(terms[k * CHUNKS:(k + 1) * CHUNKS], axis=1) for k in range(2)]).reshape(split)
    term = halve(term, 3, core, swap_core, jnp.bfloat16)
    term = halve(term, 1, row, swap_row, jnp.bfloat16)
    token = (term,)
    for unit in units[:-1]:
        while not unit.done():
            token += (unit.step(term),)
    first = jnp.concatenate([u.result(*token[1:]) for u in units[:CHUNKS]], axis=1)
    squares = jnp.sum(first * first, axis=0)
    term = halve(after(term, *token[1:]), 1, z, swap_z, jnp.bfloat16)
    base = pick(pick(pick(diag_inverse.reshape(split), core, 3), row, 1), z, 1).astype(jnp.float32) * weight
    both = halve(jnp.stack([base, term]), 2, pole, swap_pole, jnp.float32)
    base, term = both[0], both[1]
    piece = jnp.stack([base[0] + term[0], base[1], term[1]]).astype(jnp.bfloat16)
    piece = piece[:, None, None, None, None]
    for bit in reversed(range(n_pole.bit_length() - 1)):
        piece, squares = double(piece, squares, 4, pole, bit, swap_pole)
    piece = after(piece, units[-1].step(piece))
    for bit in reversed(range(zs.bit_length() - 1)):
        piece, squares = double(piece, squares, 2, z, bit, swap_z)
    while not units[-1].done():
        piece = after(piece, units[-1].step(piece))
    for bit in reversed(range(n_row.bit_length() - 1)):
        piece, squares = double(piece, squares, 1, row, bit, swap_row)
    piece, squares = double(piece, squares, 3, core, 0, swap_core)
    scale = jnp.sqrt(squares / (rows * n_row) + 1e-06)
    piece = piece.reshape(3, width, width).astype(jnp.float32)
    scaled = piece[1] + piece[2] / (scale[:, None] * scale)
    second = jnp.concatenate([u.result() for u in units[CHUNKS:]], axis=1) / scale
    return jnp.stack([first.astype(jnp.bfloat16), second.astype(jnp.bfloat16)]), jnp.stack([piece[0], scaled])


def solution(mesh):
    placed = (
        P("pole", "row", "col"),
        P(None, "row", "col"),
        P("pole", "row", None),
        P("pole", "row", None),
        P(None, "pole", None, None),
        P("pole"),
    )
    return jax.shard_map(
        body,
        mesh=mesh,
        in_specs=placed,
        out_specs=(P(None, ("row", "col", "pole"), None), P()),
        check_vma=False,
    )
```

time: 808 us -> 315 us (0.39)
  waiting for transfers between devices: 599 us -> 67.9 us
  Pallas kernels: 0 us -> 152 us
  matrix products: 108 us -> 0 us
  blocking collectives: 39.1 us -> 0 us
  starting transfers between devices: 0.39 us -> 31.2 us
  other arithmetic: 21.4 us -> 36 us
  between operations: 14.5 us -> 2.07 us
    reduce_scatter x2 -> x0, waiting for transfers between devices: 357 us -> none  [panel_sum(): lax.psum_scatter(weight * partial_value, ('col', 'pole'), scatter_dimensi...]
    psum x3 -> x0, waiting for transfers between devices: 241 us -> none  [the longest x1 134 us: body(): diag_second = lax.psum(diag_term_second, ('row', 'col', 'pole'))]
    pallas_call x0 -> x17, Pallas kernels: none -> 152 us  [the longest x16 117 us: product(): pl.pallas_call(kernel, out_shape=out_shape, grid_spec=pltpu.PrefetchScala...]
    dot_general x4 -> x0, matrix products: 108 us -> none  [the longest x2 70.4 us: local_partial(): return jnp.dot(masked, factor_cols, preferred_element_type=jnp.float32)]
    ppermute x0 -> x42, waiting for transfers between devices: none -> 67.9 us  [the longest x38 67.9 us: swap(): return lax.ppermute(x, axis, [(i, i ^ mask) for i in range(size)])]
    psum x1 -> x0, blocking collectives: 39.1 us -> none  [body(): lax.psum(jnp.sum(dens_first * dens_first, axis=0), ('row', 'col', 'pole'))]
    ppermute x0 -> x42, starting transfers between devices: none -> 31.2 us  [the longest x38 26.7 us: swap(): return lax.ppermute(x, axis, [(i, i ^ mask) for i in range(size)])]
    mul x2 -> x0, local copies, waits for them, and re-layouts: 22.3 us -> none  [apply_mask(): return (shaped * mask_bf).reshape(row_count, col_count)]
  transfers between devices with their start and end apart: 5 -> 42, of which waited for: 5 -> 12; matrix products, arithmetic and copies ran while one was open for 3% -> 11% of each run, Pallas kernels for 0% -> 46%
where the time goes in v4:
time: 315 us; the launch traced here: 313 us
  Pallas kernels  152 us (48%)
  waiting for transfers between devices  67.9 us (22%)
  other arithmetic  36 us (11%)
  starting transfers between devices  31.2 us (10%)
  local copies, waits for them, and re-layouts  23.9 us (8%)
    pallas_call x16, Pallas kernels, product(): pl.pallas_call(kernel, out_shape=out_shape, grid_spec=pltpu.PrefetchScala...  117 us
    ppermute x38, waiting for transfers between devices, swap(): return lax.ppermute(x, axis, [(i, i ^ mask) for i in range(size)])  67.9 us
    pallas_call x1, Pallas kernels, apply_masks(): pl.pallas_call(mask_kernel, out_shape=[jax.ShapeDtypeStruct((rows, cols),...  35.3 us
    ppermute x38, starting transfers between devices, swap(): return lax.ppermute(x, axis, [(i, i ^ mask) for i in range(size)])  26.7 us
    unnamed x62, local copies, waits for them, and re-layouts  14.7 us
    convert_element_type x8, other arithmetic, step(): send = self.part(1, *deps).astype(jnp.bfloat16)  12.8 us
  transfers between devices with their start and end apart: 42, of which 12 were waited for; matrix products, arithmetic and copies ran while one was open for 11% of the time, Pallas kernels for 46%

profile of v4, /device:TPU:0, one launch (start us, length us, event | category | flops | bytes accessed | tf_op | source)
XLA Modules:
  0.0 313.5 jit_solution(5268939788315868137)
XLA Ops:
  0.7 1.7 dynamic-slice_bitcast_fusion.2
  2.3 3.0 collective-permute-start
  5.9 35.3 %shard_map.77 = (bf16[8192,2048]{1,0:T(8,128)(2,1)}, bf16[8192,2048]{1,0:T(8,128)(2,1)}) custom-call(bf16[8192,2048]{1,0:T(8,128)(2,1)} %bitcast.195, bf16[2,16,4,2048]{3,2,1,0:T(4,128)(2,1)S(1)} %reshape_reshape.64.mask_ref), custom_call_target="tpu_custom_call" | custom-call | flops 33554432 | bytes 100663296 | tf_op jit(solution)/shard_map/pallas_call | solution.py:120
  42.3 6.1 %shard_map.78 = (bf16[2048,128]{1,0:T(8,128)(2,1)S(1)}, bf16[2048,128]{1,0:T(8,128)(2,1)S(1)}) custom-call(s32[2]{0:T(128)S(1)} %pad_add_fusion.3.where_ref, f32[1]{0:T(128)} %copy.135.weight_ref, bf16[8192,2048]{1,0:T(8,128)(2,1)} %get-tuple-element.78.a_ref, bf16[2048,256]{1,0:T(8,128)(2,1)S(1)} %broadcast_select_fusion.3.f_ref), custom_call_target="tpu_custom_call" | custom-call | flops 8388608 | bytes 524288 | tf_op jit(solution)/shard_map/pallas_call | solution.py:186
  49.0 6.8 %shard_map.79 = (bf16[2048,128]{1,0:T(8,128)(2,1)S(1)}, bf16[2048,128]{1,0:T(8,128)(2,1)S(1)}) custom-call(s32[2]{0:T(128)S(1)} %get-tuple-element.125.where_ref, f32[1]{0:T(128)} %copy.135.weight_ref, bf16[8192,2048]{1,0:T(8,128)(2,1)} %get-tuple-element.78.a_ref, bf16[2048,256]{1,0:T(8,128)(2,1)S(1)} %broadcast_select_fusion.3.f_ref), custom_call_target="tpu_custom_call" | custom-call | flops 8388608 | bytes 524288 | tf_op jit(solution)/shard_map/pallas_call | solution.py:186
  56.5 8.4 %shard_map.80 = (bf16[2048,256]{1,0:T(8,128)(2,1)}, f32[512,256]{1,0:T(8,128)S(1)}) custom-call(s32[2]{0:T(128)S(1)} %get-tuple-element.130.where_ref, f32[1]{0:T(128)} %copy.135.weight_ref, bf16[8192,2048]{1,0:T(8,128)(2,1)} %get-tuple-element.78.a_ref, bf16[2048,256]{1,0:T(8,128)(2,1)S(1)} %broadcast_select_fusion.3.f_ref, ...), custom_call_target="tpu_custom_call" | custom-call | flops 8388608 | bytes 524288 | tf_op jit(solution)/shard_map/pallas_call | solution.py:186
  64.9 2.0 collective-permute-start.8
  66.9 7.5 %shard_map.81 = (f32[2048,256]{1,0:T(8,128)S(1)}, f32[512,256]{1,0:T(8,128)S(1)}) custom-call(s32[2]{0:T(128)S(1)} %pad_add_fusion.1.where_ref, f32[1]{0:T(128)} %copy.135.weight_ref, bf16[8192,2048]{1,0:T(8,128)(2,1)} %get-tuple-element.78.a_ref, bf16[2048,256]{1,0:T(8,128)(2,1)S(1)} %broadcast_select_fusion.3.f_ref, bf16[8192,512]{1,0:T(8,128)(2,1)S(1)} %bitcast.176, ...), custom_call_target="tpu_custom_call" | custom-call | flops 8388608 | bytes 524288 | tf_op jit(solution)/shard_map/pallas_call | solution.py:186
  74.6 6.9 %shard_map.82 = (bf16[2048,128]{1,0:T(8,128)(2,1)S(1)}, bf16[2048,128]{1,0:T(8,128)(2,1)}) custom-call(s32[2]{0:T(128)S(1)} %pad_add_fusion.3.where_ref, f32[1]{0:T(128)} %copy.135.weight_ref, bf16[8192,2048]{1,0:T(8,128)(2,1)} %get-tuple-element.78.a_ref, bf16[2048,256]{1,0:T(8,128)(2,1)S(1)} %broadcast_select_fusion.2.f_ref), custom_call_target="tpu_custom_call" | custom-call | flops 8388608 | bytes 524288 | tf_op jit(solution)/shard_map/pallas_call | solution.py:186
  81.5 3.0 dynamic-slice_bitcast_fusion
  84.5 2.7 collective-permute-start.11
  87.5 6.9 %shard_map.83 = (bf16[2048,128]{1,0:T(8,128)(2,1)}, bf16[2048,128]{1,0:T(8,128)(2,1)}) custom-call(s32[2]{0:T(128)S(1)} %get-tuple-element.125.where_ref, f32[1]{0:T(128)} %copy.135.weight_ref, bf16[8192,2048]{1,0:T(8,128)(2,1)} %get-tuple-element.78.a_ref, bf16[2048,256]{1,0:T(8,128)(2,1)S(1)} %broadcast_select_fusion.2.f_ref), custom_call_target="tpu_custom_call" | custom-call | flops 8388608 | bytes 524288 | tf_op jit(solution)/shard_map/pallas_call | solution.py:186
  94.9 3.4 %copy-done = bf16[1,8192,512]{2,1,0:T(8,128)(2,1)S(1)} copy-done((bf16[1,8192,512]{2,1,0:T(8,128)(2,1)S(1)}, bf16[1,8192,512]{2,1,0:T(8,128)(2,1)}, u32[]{:S(2)}) %copy-start) | copy-done | bytes 8388632
  98.3 8.4 %shard_map.84 = (bf16[2048,256]{1,0:T(8,128)(2,1)}, f32[512,256]{1,0:T(8,128)S(1)}) custom-call(s32[2]{0:T(128)S(1)} %get-tuple-element.130.where_ref, f32[1]{0:T(128)} %copy.135.weight_ref, bf16[8192,2048]{1,0:T(8,128)(2,1)} %get-tuple-element.78.a_ref, bf16[2048,256]{1,0:T(8,128)(2,1)S(1)} %broadcast_select_fusion.2.f_ref, ...), custom_call_target="tpu_custom_call" | custom-call | flops 8388608 | bytes 524288 | tf_op jit(solution)/shard_map/pallas_call | solution.py:186
  107.2 1.2 fusion.12
  108.3 1.6 collective-permute-start.14
  110.0 7.5 %shard_map.85 = (f32[2048,256]{1,0:T(8,128)S(1)}, f32[512,256]{1,0:T(8,128)S(1)}) custom-call(s32[2]{0:T(128)S(1)} %pad_add_fusion.1.where_ref, f32[1]{0:T(128)} %copy.135.weight_ref, bf16[8192,2048]{1,0:T(8,128)(2,1)} %get-tuple-element.78.a_ref, bf16[2048,256]{1,0:T(8,128)(2,1)S(1)} %broadcast_select_fusion.2.f_ref, bf16[8192,512]{1,0:T(8,128)(2,1)S(1)} %bitcast.178, ...), custom_call_target="tpu_custom_call" | custom-call | flops 8388608 | bytes 524288 | tf_op jit(solution)/shard_map/pallas_call | solution.py:186
  117.5 2.1 broadcast_select_fusion.1.f_ref
  119.7 6.8 %shard_map.86 = (bf16[2048,128]{1,0:T(8,128)(2,1)S(1)}, bf16[2048,128]{1,0:T(8,128)(2,1)}) custom-call(s32[2]{0:T(128)S(1)} %pad_add_fusion.3.where_ref, f32[1]{0:T(128)} %copy.135.weight_ref, bf16[8192,2048]{1,0:T(8,128)(2,1)} %get-tuple-element.105.a_ref, bf16[2048,256]{1,0:T(8,128)(2,1)S(1)} %broadcast_select_fusion.1.f_ref), custom_call_target="tpu_custom_call" | custom-call | flops 8388608 | bytes 524288 | tf_op jit(solution)/shard_map/pallas_call | solution.py:186
  127.0 6.9 %shard_map.87 = (bf16[2048,128]{1,0:T(8,128)(2,1)}, bf16[2048,128]{1,0:T(8,128)(2,1)}) custom-call(s32[2]{0:T(128)S(1)} %get-tuple-element.125.where_ref, f32[1]{0:T(128)} %copy.135.weight_ref, bf16[8192,2048]{1,0:T(8,128)(2,1)} %get-tuple-element.105.a_ref, bf16[2048,256]{1,0:T(8,128)(2,1)S(1)} %broadcast_select_fusion.1.f_ref), custom_call_target="tpu_custom_call" | custom-call | flops 8388608 | bytes 524288 | tf_op jit(solution)/shard_map/pallas_call | solution.py:186
  135.0 2.0 fusion.19
  137.0 3.4 %copy-done.1 = bf16[1,8192,512]{2,1,0:T(8,128)(2,1)S(1)} copy-done((bf16[1,8192,512]{2,1,0:T(8,128)(2,1)S(1)}, bf16[1,8192,512]{2,1,0:T(8,128)(2,1)}, u32[]{:S(2)}) %copy-start.1) | copy-done | bytes 8388632
  140.4 8.4 %shard_map.88 = (bf16[2048,256]{1,0:T(8,128)(2,1)}, f32[512,256]{1,0:T(8,128)S(1)}) custom-call(s32[2]{0:T(128)S(1)} %get-tuple-element.130.where_ref, f32[1]{0:T(128)} %copy.135.weight_ref, bf16[8192,2048]{1,0:T(8,128)(2,1)} %get-tuple-element.105.a_ref, bf16[2048,256]{1,0:T(8,128)(2,1)S(1)} %broadcast_select_fusion.1.f_ref, ...), custom_call_target="tpu_custom_call" | custom-call | flops 8388608 | bytes 524288 | tf_op jit(solution)/shard_map/pallas_call | solution.py:186
  148.8 1.5 collective-permute-start.20
  150.4 1.2 fusion.13
  152.1 7.7 %shard_map.89 = (f32[2048,256]{1,0:T(8,128)S(1)}, f32[512,256]{1,0:T(8,128)S(1)}) custom-call(s32[2]{0:T(128)S(1)} %pad_add_fusion.1.where_ref, f32[1]{0:T(128)} %copy.135.weight_ref, bf16[8192,2048]{1,0:T(8,128)(2,1)} %get-tuple-element.105.a_ref, bf16[2048,256]{1,0:T(8,128)(2,1)S(1)} %broadcast_select_fusion.1.f_ref, bf16[8192,512]{1,0:T(8,128)(2,1)S(1)} %bitcast.180, ...), custom_call_target="tpu_custom_call" | custom-call | flops 8388608 | bytes 524288 | tf_op jit(solution)/shard_map/pallas_call | solution.py:186
  159.8 2.1 broadcast_select_fusion.f_ref
  161.9 6.9 %shard_map.90 = (bf16[2048,128]{1,0:T(8,128)(2,1)}, bf16[2048,128]{1,0:T(8,128)(2,1)}) custom-call(s32[2]{0:T(128)S(1)} %pad_add_fusion.3.where_ref, f32[1]{0:T(128)} %copy.135.weight_ref, bf16[8192,2048]{1,0:T(8,128)(2,1)} %get-tuple-element.105.a_ref, bf16[2048,256]{1,0:T(8,128)(2,1)S(1)} %broadcast_select_fusion.f_ref), custom_call_target="tpu_custom_call" | custom-call | flops 8388608 | bytes 524288 | tf_op jit(solution)/shard_map/pallas_call | solution.py:186
  168.8 6.9 %shard_map.91 = (bf16[2048,128]{1,0:T(8,128)(2,1)}, bf16[2048,128]{1,0:T(8,128)(2,1)}) custom-call(s32[2]{0:T(128)S(1)} %get-tuple-element.125.where_ref, f32[1]{0:T(128)} %copy.135.weight_ref, bf16[8192,2048]{1,0:T(8,128)(2,1)} %get-tuple-element.105.a_ref, bf16[2048,256]{1,0:T(8,128)(2,1)S(1)} %broadcast_select_fusion.f_ref), custom_call_target="tpu_custom_call" | custom-call | flops 8388608 | bytes 524288 | tf_op jit(solution)/shard_map/pallas_call | solution.py:186
  177.6 1.5 pad_maximum_fusion.1
  179.1 2.4 fusion.18
  181.4 2.0 fusion.14
  183.4 3.4 %copy-done.2 = bf16[1,8192,512]{2,1,0:T(8,128)(2,1)S(1)} copy-done((bf16[1,8192,512]{2,1,0:T(8,128)(2,1)S(1)}, bf16[1,8192,512]{2,1,0:T(8,128)(2,1)}, u32[]{:S(2)}) %copy-start.2) | copy-done | bytes 8388632
  186.8 7.5 %shard_map.92 = (f32[2048,256]{1,0:T(8,128)S(1)}, f32[512,256]{1,0:T(8,128)S(1)}) custom-call(s32[2]{0:T(128)S(1)} %pad_add_fusion.1.where_ref, f32[1]{0:T(128)} %copy.135.weight_ref, bf16[8192,2048]{1,0:T(8,128)(2,1)} %get-tuple-element.105.a_ref, bf16[2048,256]{1,0:T(8,128)(2,1)S(1)} %broadcast_select_fusion.f_ref, bf16[8192,512]{1,0:T(8,128)(2,1)S(1)} %bitcast.181, ...), custom_call_target="tpu_custom_call" | custom-call | flops 8388608 | bytes 524288 | tf_op jit(solution)/shard_map/pallas_call | solution.py:186
  194.4 1.3 copy-done.6
  195.7 7.5 %shard_map.93 = (bf16[2048,256]{1,0:T(8,128)(2,1)S(1)}, f32[512,256]{1,0:T(8,128)S(1)}) custom-call(s32[2]{0:T(128)S(1)} %get-tuple-element.130.where_ref, f32[1]{0:T(128)} %copy.135.weight_ref, bf16[8192,2048]{1,0:T(8,128)(2,1)} %get-tuple-element.105.a_ref, bf16[2048,256]{1,0:T(8,128)(2,1)S(1)} %broadcast_select_fusion.f_ref, ...), custom_call_target="tpu_custom_call" | custom-call | flops 8388608 | bytes 524288 | tf_op jit(solution)/shard_map/pallas_call | solution.py:186
  203.4 1.1 fusion.11
  204.7 1.6 collective-permute-start.27
  207.0 1.5 fusion.8
  210.2 1.8 collective-permute-start.26
  212.9 1.4 collective-permute-start.28
  214.3 1.6 collective-permute-start.29
  216.4 2.4 collective-permute-done.26
  218.8 1.1 fusion.17
  219.9 4.5 %collective-permute-done.27 = bf16[2,512,256]{2,1,0:T(8,128)(2,1)} collective-permute-done((bf16[2,512,256]{2,1,0:T(8,128)(2,1)}, bf16[2,512,256]{2,1,0:T(8,128)(2,1)}, u32[]{:S(2)}, u32[]{:S(2)}) %collective-permute-start.27) | collective-permute-done | bytes 524320 | tf_op jit(solution)/shard_map/ppermute | solution.py:15
  224.5 1.9 fusion.21
  226.3 12.7 %collective-permute-done.29 = bf16[1,512,256]{2,1,0:T(8,128)(2,1)S(1)} collective-permute-done((bf16[1,512,256]{2,1,0:T(8,128)(2,1)}, bf16[1,512,256]{2,1,0:T(8,128)(2,1)S(1)}, u32[]{:S(2)}, u32[]{:S(2)}) %collective-permute-start.29) | collective-permute-done | bytes 262176 | tf_op jit(solution)/shard_map/ppermute | solution.py:15
  239.1 1.2 convert_bitcast_fusion
  240.4 3.7 %collective-permute-done.32 = bf16[2,2,2,16,512]{4,3,2,0,1:T(8,128)(2,1)S(1)} collective-permute-done((bf16[2,2,2,16,512]{4,3,2,0,1:T(8,128)(2,1)S(1)}, bf16[2,2,2,16,512]{4,3,2,0,1:T(8,128)(2,1)S(1)}, u32[]{:S(2)}, u32[]{:S(2)}) %collective-permute-start.32) | collective-permute-done | bytes 131104 | tf_op jit(solution)/shard_map/ppermute | solution.py:15
  245.2 1.9 convert_bitcast_fusion.1
  247.2 2.3 collective-permute-done.33
  250.2 5.1 %collective-permute-done.34 = f32[2,2,1,16,512]{4,3,2,1,0:T(8,128)S(1)} collective-permute-done((f32[2,2,1,16,512]{4,3,2,1,0:T(8,128)S(1)}, f32[2,2,1,16,512]{4,3,2,1,0:T(8,128)S(1)}, u32[]{:S(2)}, u32[]{:S(2)}) %collective-permute-start.34) | collective-permute-done | bytes 131104 | tf_op jit(solution)/shard_map/ppermute | solution.py:15
  255.9 3.7 %collective-permute-done.35 = bf16[51,512]{1,0:T(8,128)(2,1)S(1)} collective-permute-done((bf16[51,512]{1,0:T(8,128)(2,1)S(1)}, bf16[51,512]{1,0:T(8,128)(2,1)S(1)}, u32[]{:S(2)}, u32[]{:S(2)}) %collective-permute-start.35) | collective-permute-done | bytes 52256 | tf_op jit(solution)/shard_map/ppermute | solution.py:15
  261.5 2.2 collective-permute-start.36
  263.7 3.7 %collective-permute-done.37 = bf16[99,512]{1,0:T(8,128)(2,1)S(1)} collective-permute-done((bf16[99,512]{1,0:T(8,128)(2,1)S(1)}, bf16[99,512]{1,0:T(8,128)(2,1)S(1)}, u32[]{:S(2)}, u32[]{:S(2)}) %collective-permute-start.37) | collective-permute-done | bytes 101408 | tf_op jit(solution)/shard_map/ppermute | solution.py:15
  267.8 9.3 %collective-permute-done.38 = bf16[195,512]{1,0:T(8,128)(2,1)S(1)} collective-permute-done((bf16[195,512]{1,0:T(8,128)(2,1)S(1)}, bf16[195,512]{1,0:T(8,128)(2,1)S(1)}, u32[]{:S(2)}, u32[]{:S(2)}) %collective-permute-start.38) | collective-permute-done | bytes 199712 | tf_op jit(solution)/shard_map/ppermute | solution.py:15
  277.3 2.1 fusion.22
  280.2 1.4 collective-permute-start.30
  281.6 5.9 %collective-permute-done.40 = bf16[387,512]{1,0:T(8,128)(2,1)} collective-permute-done((bf16[387,512]{1,0:T(8,128)(2,1)S(1)}, bf16[387,512]{1,0:T(8,128)(2,1)}, u32[]{:S(2)}, u32[]{:S(2)}) %collective-permute-start.40) | collective-permute-done | bytes 396320 | tf_op jit(solution)/shard_map/ppermute | solution.py:15
  290.9 1.2 fusion.16
  292.1 13.8 %collective-permute-done.39 = bf16[1,512,256]{2,1,0:T(8,128)(2,1)} collective-permute-done((bf16[1,512,256]{2,1,0:T(8,128)(2,1)}, bf16[1,512,256]{2,1,0:T(8,128)(2,1)}, u32[]{:S(2)}, u32[]{:S(2)}) %collective-permute-start.39) | collective-permute-done | bytes 262176 | tf_op jit(solution)/shard_map/ppermute | solution.py:15
  305.9 1.4 fusion.15
  307.4 1.2 slice.111
  310.9 1.5 pad_maximum_fusion
  (186 shorter events, 24.4 us)
Async XLA Ops:
  0.6 4.7 %copy-start.28 = (s32[2,64,16]{1,2,0:T(8,128)S(1)}, s32[2,64,16]{1,2,0:T(8,128)}, u32[]{:S(2)}) copy-start(s32[2,64,16]{1,2,0:T(8,128)} %param.7) | copy-start | bytes 24580
  2.3 39.7 %collective-permute-start = (bf16[2048,256]{1,0:T(8,128)(2,1)S(1)}, bf16[2048,256]{1,0:T(8,128)(2,1)}, u32[]{:S(2)}, u32[]{:S(2)}) collective-permute-start(bf16[2048,256]{1,0:T(8,128)(2,1)S(1)} %get-tuple-element.163), channel_id=1, source_target_pairs={{0,16},{16,0},{1,17},{17,1},{2,18},{18,2},{3,19},{19,3},{4,20},{20... | collective-permute-start | bytes 3145736 | tf_op jit(solution)/shard_map/ppermute | solution.py:15
  42.0 32.4 %collective-permute-start.5 = (bf16[2048,256]{1,0:T(8,128)(2,1)S(1)}, bf16[2048,256]{1,0:T(8,128)(2,1)S(1)}, u32[]{:S(2)}, u32[]{:S(2)}) collective-permute-start(bf16[2048,256]{1,0:T(8,128)(2,1)S(1)} %get-tuple-element.92), channel_id=1, source_target_pairs={{0,16},{16,0},{1,17},{17,1},{2,18},{18,2},{3,19},{19,3},{4,20},{20... | collective-permute-start | bytes 3145736 | tf_op jit(solution)/shard_map/ppermute | solution.py:15
  48.3 8.1 %collective-permute-start.1 = (bf16[2048,128]{1,0:T(8,128)(2,1)S(1)}, bf16[2048,128]{1,0:T(8,128)(2,1)S(1)}, u32[]{:S(2)}, u32[]{:S(2)}) collective-permute-start(bf16[2048,128]{1,0:T(8,128)(2,1)S(1)} %get-tuple-element.81), channel_id=1, source_target_pairs={{0,2},{2,0},{4,6},{6,4},{8,10},{10,8},{12,14},{14,12},{1,3},{3,1},... | collective-permute-start | bytes 1572872 | tf_op jit(solution)/shard_map/ppermute | solution.py:15
  48.4 8.0 %collective-permute-start.2 = (bf16[2048,128]{1,0:T(8,128)(2,1)S(1)}, bf16[2048,128]{1,0:T(8,128)(2,1)S(1)}, u32[]{:S(2)}, u32[]{:S(2)}) collective-permute-start(bf16[2048,128]{1,0:T(8,128)(2,1)S(1)} %get-tuple-element.85), channel_id=1, source_target_pairs={{0,2},{2,0},{4,6},{6,4},{8,10},{10,8},{12,14},{14,12},{1,3},{3,1},... | collective-permute-start | bytes 1572872 | tf_op jit(solution)/shard_map/ppermute | solution.py:15
  49.0 7.5 %slice-start = ((s8[8388608]{0:T(1024)(128)(4,1)}), s8[4194304]{0:T(1024)(128)(4,1)S(1)}, s32[]{:S(2)}) async-start(s8[8388608]{0:T(1024)(128)(4,1)} %bitcast.173), calls=%async_computation | async-start | bytes 8388608
  49.0 7.5 %slice-start.1 = ((s8[8388608]{0:T(1024)(128)(4,1)}), s8[4194304]{0:T(1024)(128)(4,1)S(1)}, s32[]{:S(2)}) async-start(s8[8388608]{0:T(1024)(128)(4,1)} %bitcast.173), calls=%async_computation.1 | async-start | bytes 8388608
  55.8 11.1 %collective-permute-start.3 = (bf16[2048,128]{1,0:T(8,128)(2,1)S(1)}, bf16[2048,128]{1,0:T(8,128)(2,1)S(1)}, u32[]{:S(2)}, u32[]{:S(2)}) collective-permute-start(bf16[2048,128]{1,0:T(8,128)(2,1)S(1)} %get-tuple-element.83), channel_id=1, source_target_pairs={{0,2},{2,0},{4,6},{6,4},{8,10},{10,8},{12,14},{14,12},{1,3},{3,1},... | collective-permute-start | bytes 1572872 | tf_op jit(solution)/shard_map/ppermute | solution.py:15
  55.9 10.9 %collective-permute-start.4 = (bf16[2048,128]{1,0:T(8,128)(2,1)S(1)}, bf16[2048,128]{1,0:T(8,128)(2,1)S(1)}, u32[]{:S(2)}, u32[]{:S(2)}) collective-permute-start(bf16[2048,128]{1,0:T(8,128)(2,1)S(1)} %get-tuple-element.89), channel_id=1, source_target_pairs={{0,2},{2,0},{4,6},{6,4},{8,10},{10,8},{12,14},{14,12},{1,3},{3,1},... | collective-permute-start | bytes 1572872 | tf_op jit(solution)/shard_map/ppermute | solution.py:15
  64.9 42.3 %collective-permute-start.8 = (bf16[2048,256]{1,0:T(8,128)(2,1)}, bf16[2048,256]{1,0:T(8,128)(2,1)}, u32[]{:S(2)}, u32[]{:S(2)}) collective-permute-start(bf16[2048,256]{1,0:T(8,128)(2,1)} %get-tuple-element.86), channel_id=1, source_target_pairs={{0,1},{1,0},{2,3},{3,2},{4,5},{5,4},{6,7},{7,6},{8,9},{9,8},{10,11... | collective-permute-start | bytes 3145736 | tf_op jit(solution)/shard_map/ppermute | solution.py:268
  74.4 7.1 %copy-start.8 = (f32[2048,256]{1,0:T(8,128)}, f32[2048,256]{1,0:T(8,128)S(1)}, u32[]{:S(2)}) copy-start(f32[2048,256]{1,0:T(8,128)S(1)} %get-tuple-element.90) | copy-start | bytes 6291460
  74.4 7.1 %copy-start.12 = (f32[512,256]{1,0:T(8,128)}, f32[512,256]{1,0:T(8,128)S(1)}, u32[]{:S(2)}) copy-start(f32[512,256]{1,0:T(8,128)S(1)} %get-tuple-element.118) | copy-start | bytes 1572868
  81.5 13.1 %collective-permute-start.6 = (bf16[2048,128]{1,0:T(8,128)(2,1)S(1)}, bf16[2048,128]{1,0:T(8,128)(2,1)S(1)}, u32[]{:S(2)}, u32[]{:S(2)}) collective-permute-start(bf16[2048,128]{1,0:T(8,128)(2,1)S(1)} %get-tuple-element.94), channel_id=1, source_target_pairs={{0,2},{2,0},{4,6},{6,4},{8,10},{10,8},{12,14},{14,12},{1,3},{3,1},... | collective-permute-start | bytes 1572872 | tf_op jit(solution)/shard_map/ppermute | solution.py:15
  84.5 33.0 %collective-permute-start.11 = (bf16[2048,256]{1,0:T(8,128)(2,1)}, bf16[2048,256]{1,0:T(8,128)(2,1)}, u32[]{:S(2)}, u32[]{:S(2)}) collective-permute-start(bf16[2048,256]{1,0:T(8,128)(2,1)} %get-tuple-element.106), channel_id=1, source_target_pairs={{0,16},{16,0},{1,17},{17,1},{2,18},{18,2},{3,19},{19,3},{4,20},{20... | collective-permute-start | bytes 3145736 | tf_op jit(solution)/shard_map/ppermute | solution.py:15
  87.2 7.6 %collective-permute-start.7 = (bf16[2048,128]{1,0:T(8,128)(2,1)}, bf16[2048,128]{1,0:T(8,128)(2,1)}, u32[]{:S(2)}, u32[]{:S(2)}) collective-permute-start(bf16[2048,128]{1,0:T(8,128)(2,1)} %get-tuple-element.98), channel_id=1, source_target_pairs={{0,2},{2,0},{4,6},{6,4},{8,10},{10,8},{12,14},{14,12},{1,3},{3,1},... | collective-permute-start | bytes 1572872 | tf_op jit(solution)/shard_map/ppermute | solution.py:15
  94.3 15.6 %collective-permute-start.9 = (bf16[2048,128]{1,0:T(8,128)(2,1)}, bf16[2048,128]{1,0:T(8,128)(2,1)S(1)}, u32[]{:S(2)}, u32[]{:S(2)}) collective-permute-start(bf16[2048,128]{1,0:T(8,128)(2,1)} %get-tuple-element.96), channel_id=1, source_target_pairs={{0,2},{2,0},{4,6},{6,4},{8,10},{10,8},{12,14},{14,12},{1,3},{3,1},... | collective-permute-start | bytes 1572872 | tf_op jit(solution)/shard_map/ppermute | solution.py:15
  94.6 15.3 %collective-permute-start.10 = (bf16[2048,128]{1,0:T(8,128)(2,1)}, bf16[2048,128]{1,0:T(8,128)(2,1)S(1)}, u32[]{:S(2)}, u32[]{:S(2)}) collective-permute-start(bf16[2048,128]{1,0:T(8,128)(2,1)} %get-tuple-element.102), channel_id=1, source_target_pairs={{0,2},{2,0},{4,6},{6,4},{8,10},{10,8},{12,14},{14,12},{1,3},{3,1},... | collective-permute-start | bytes 1572872 | tf_op jit(solution)/shard_map/ppermute | solution.py:15
  94.9 3.4 %copy-start = (bf16[1,8192,512]{2,1,0:T(8,128)(2,1)S(1)}, bf16[1,8192,512]{2,1,0:T(8,128)(2,1)}, u32[]{:S(2)}) copy-start(bf16[1,8192,512]{2,1,0:T(8,128)(2,1)} %param.8) | copy-start | bytes 25165828
  98.2 8.9 %copy-start.9 = (f32[2048,256]{1,0:T(8,128)S(1)}, f32[2048,256]{1,0:T(8,128)}, u32[]{:S(2)}) copy-start(f32[2048,256]{1,0:T(8,128)} %copy-done.8) | copy-start | bytes 6291460
  106.7 43.7 %collective-permute-start.15 = (bf16[2048,256]{1,0:T(8,128)(2,1)}, bf16[2048,256]{1,0:T(8,128)(2,1)}, u32[]{:S(2)}, u32[]{:S(2)}) collective-permute-start(bf16[2048,256]{1,0:T(8,128)(2,1)} %get-tuple-element.99), channel_id=1, source_target_pairs={{0,1},{1,0},{2,3},{3,2},{4,5},{5,4},{6,7},{7,6},{8,9},{9,8},{10,11... | collective-permute-start | bytes 3145736 | tf_op jit(solution)/shard_map/ppermute | solution.py:268
  108.3 25.5 %collective-permute-start.14 = (bf16[2,512,256]{2,1,0:T(8,128)(2,1)S(1)}, bf16[2,512,256]{2,1,0:T(8,128)(2,1)S(1)}, u32[]{:S(2)}, u32[]{:S(2)}) collective-permute-start(bf16[2,512,256]{2,1,0:T(8,128)(2,1)S(1)} %fusion.12), channel_id=1, source_target_pairs={{0,4},{2,6},{4,0},{6,2},{8,12},{10,14},{12,8},{14,10},{1,5},{3,7},... | collective-permute-start | bytes 1572872 | tf_op jit(solution)/shard_map/ppermute | solution.py:15
  117.5 9.0 %copy-start.10 = (f32[2048,256]{1,0:T(8,128)}, f32[2048,256]{1,0:T(8,128)S(1)}, u32[]{:S(2)}) copy-start(f32[2048,256]{1,0:T(8,128)S(1)} %get-tuple-element.103) | copy-start | bytes 6291460
  117.5 8.9 %copy-start.13 = (f32[512,256]{1,0:T(8,128)}, f32[512,256]{1,0:T(8,128)S(1)}, u32[]{:S(2)}) copy-start(f32[512,256]{1,0:T(8,128)S(1)} %get-tuple-element.119) | copy-start | bytes 1572868
  126.5 7.8 %collective-permute-start.12 = (bf16[2048,128]{1,0:T(8,128)(2,1)S(1)}, bf16[2048,128]{1,0:T(8,128)(2,1)S(1)}, u32[]{:S(2)}, u32[]{:S(2)}) collective-permute-start(bf16[2048,128]{1,0:T(8,128)(2,1)S(1)} %get-tuple-element.108), channel_id=1, source_target_pairs={{0,2},{2,0},{4,6},{6,4},{8,10},{10,8},{12,14},{14,12},{1,3},{3,1},... | collective-permute-start | bytes 1572872 | tf_op jit(solution)/shard_map/ppermute | solution.py:15
  126.5 33.3 %collective-permute-start.18 = (bf16[2048,256]{1,0:T(8,128)(2,1)}, bf16[2048,256]{1,0:T(8,128)(2,1)}, u32[]{:S(2)}, u32[]{:S(2)}) collective-permute-start(bf16[2048,256]{1,0:T(8,128)(2,1)} %get-tuple-element.122), channel_id=1, source_target_pairs={{0,16},{16,0},{1,17},{17,1},{2,18},{18,2},{3,19},{19,3},{4,20},{20... | collective-permute-start | bytes 3145736 | tf_op jit(solution)/shard_map/ppermute | solution.py:15
  126.9 10.2 %collective-permute-start.13 = (bf16[2048,128]{1,0:T(8,128)(2,1)}, bf16[2048,128]{1,0:T(8,128)(2,1)}, u32[]{:S(2)}, u32[]{:S(2)}) collective-permute-start(bf16[2048,128]{1,0:T(8,128)(2,1)} %get-tuple-element.112), channel_id=1, source_target_pairs={{0,2},{2,0},{4,6},{6,4},{8,10},{10,8},{12,14},{14,12},{1,3},{3,1},... | collective-permute-start | bytes 1572872 | tf_op jit(solution)/shard_map/ppermute | solution.py:15
  133.9 18.2 %collective-permute-start.16 = (bf16[2048,128]{1,0:T(8,128)(2,1)}, bf16[2048,128]{1,0:T(8,128)(2,1)S(1)}, u32[]{:S(2)}, u32[]{:S(2)}) collective-permute-start(bf16[2048,128]{1,0:T(8,128)(2,1)} %get-tuple-element.110), channel_id=1, source_target_pairs={{0,2},{2,0},{4,6},{6,4},{8,10},{10,8},{12,14},{14,12},{1,3},{3,1},... | collective-permute-start | bytes 1572872 | tf_op jit(solution)/shard_map/ppermute | solution.py:15
  134.7 17.4 %collective-permute-start.17 = (bf16[2048,128]{1,0:T(8,128)(2,1)}, bf16[2048,128]{1,0:T(8,128)(2,1)S(1)}, u32[]{:S(2)}, u32[]{:S(2)}) collective-permute-start(bf16[2048,128]{1,0:T(8,128)(2,1)} %get-tuple-element.116), channel_id=1, source_target_pairs={{0,2},{2,0},{4,6},{6,4},{8,10},{10,8},{12,14},{14,12},{1,3},{3,1},... | collective-permute-start | bytes 1572872 | tf_op jit(solution)/shard_map/ppermute | solution.py:15
  137.0 3.4 %copy-start.1 = (bf16[1,8192,512]{2,1,0:T(8,128)(2,1)S(1)}, bf16[1,8192,512]{2,1,0:T(8,128)(2,1)}, u32[]{:S(2)}) copy-start(bf16[1,8192,512]{2,1,0:T(8,128)(2,1)} %param.9) | copy-start | bytes 25165828
  140.4 10.0 %copy-start.11 = (f32[2048,256]{1,0:T(8,128)S(1)}, f32[2048,256]{1,0:T(8,128)}, u32[]{:S(2)}) copy-start(f32[2048,256]{1,0:T(8,128)} %copy-done.10) | copy-start | bytes 6291460
  148.8 32.6 %collective-permute-start.20 = (bf16[2048,256]{1,0:T(8,128)(2,1)}, bf16[2048,256]{1,0:T(8,128)(2,1)}, u32[]{:S(2)}, u32[]{:S(2)}) collective-permute-start(bf16[2048,256]{1,0:T(8,128)(2,1)} %get-tuple-element.113), channel_id=1, source_target_pairs={{0,1},{1,0},{2,3},{3,2},{4,5},{5,4},{6,7},{7,6},{8,9},{9,8},{10,11... | collective-permute-start | bytes 3145736 | tf_op jit(solution)/shard_map/ppermute | solution.py:268
  151.6 24.7 %collective-permute-start.19 = (bf16[2,512,256]{2,1,0:T(8,128)(2,1)S(1)}, bf16[2,512,256]{2,1,0:T(8,128)(2,1)S(1)}, u32[]{:S(2)}, u32[]{:S(2)}) collective-permute-start(bf16[2,512,256]{2,1,0:T(8,128)(2,1)S(1)} %fusion.13), channel_id=1, source_target_pairs={{0,4},{2,6},{4,0},{6,2},{8,12},{10,14},{12,8},{14,10},{1,5},{3,7},... | collective-permute-start | bytes 1572872 | tf_op jit(solution)/shard_map/ppermute | solution.py:15
  159.8 9.1 %copy-start.3 = (f32[2048,256]{1,0:T(8,128)}, f32[2048,256]{1,0:T(8,128)S(1)}, u32[]{:S(2)}) copy-start(f32[2048,256]{1,0:T(8,128)S(1)} %get-tuple-element.117) | copy-start | bytes 6291460
  159.8 9.0 %copy-start.14 = (f32[512,256]{1,0:T(8,128)}, f32[512,256]{1,0:T(8,128)S(1)}, u32[]{:S(2)}) copy-start(f32[512,256]{1,0:T(8,128)S(1)} %get-tuple-element.120) | copy-start | bytes 1572868
  175.7 7.7 %collective-permute-start.21 = (bf16[2048,128]{1,0:T(8,128)(2,1)}, bf16[2048,128]{1,0:T(8,128)(2,1)S(1)}, u32[]{:S(2)}, u32[]{:S(2)}) collective-permute-start(bf16[2048,128]{1,0:T(8,128)(2,1)} %get-tuple-element.126), channel_id=1, source_target_pairs={{0,2},{2,0},{4,6},{6,4},{8,10},{10,8},{12,14},{14,12},{1,3},{3,1},... | collective-permute-start | bytes 1572872 | tf_op jit(solution)/shard_map/ppermute | solution.py:15
  175.7 7.7 %collective-permute-start.22 = (bf16[2048,128]{1,0:T(8,128)(2,1)}, bf16[2048,128]{1,0:T(8,128)(2,1)}, u32[]{:S(2)}, u32[]{:S(2)}) collective-permute-start(bf16[2048,128]{1,0:T(8,128)(2,1)} %get-tuple-element.128), channel_id=1, source_target_pairs={{0,2},{2,0},{4,6},{6,4},{8,10},{10,8},{12,14},{14,12},{1,3},{3,1},... | collective-permute-start | bytes 1572872 | tf_op jit(solution)/shard_map/ppermute | solution.py:15
  176.2 19.4 %collective-permute-start.23 = (bf16[2048,128]{1,0:T(8,128)(2,1)}, bf16[2048,128]{1,0:T(8,128)(2,1)S(1)}, u32[]{:S(2)}, u32[]{:S(2)}) collective-permute-start(bf16[2048,128]{1,0:T(8,128)(2,1)} %get-tuple-element.124), channel_id=1, source_target_pairs={{0,2},{2,0},{4,6},{6,4},{8,10},{10,8},{12,14},{14,12},{1,3},{3,1},... | collective-permute-start | bytes 1572872 | tf_op jit(solution)/shard_map/ppermute | solution.py:15
  177.1 18.6 %collective-permute-start.24 = (bf16[2048,128]{1,0:T(8,128)(2,1)}, bf16[2048,128]{1,0:T(8,128)(2,1)S(1)}, u32[]{:S(2)}, u32[]{:S(2)}) collective-permute-start(bf16[2048,128]{1,0:T(8,128)(2,1)} %get-tuple-element.132), channel_id=1, source_target_pairs={{0,2},{2,0},{4,6},{6,4},{8,10},{10,8},{12,14},{14,12},{1,3},{3,1},... | collective-permute-start | bytes 1572872 | tf_op jit(solution)/shard_map/ppermute | solution.py:15
  177.6 3.9 %copy-start.4 = (f32[2048,256]{1,0:T(8,128)S(1)}, f32[2048,256]{1,0:T(8,128)}, u32[]{:S(2)}) copy-start(f32[2048,256]{1,0:T(8,128)} %copy-done.3) | copy-start | bytes 6291460
  179.0 24.3 %copy-start.18 = (f32[512,512]{1,0:T(8,128)}, f32[512,512]{1,0:T(8,128)S(1)}, u32[]{:S(2)}) copy-start(f32[512,512]{1,0:T(8,128)S(1)} %pad_maximum_fusion.1) | copy-start | bytes 3145732
  183.4 3.4 %copy-start.2 = (bf16[1,8192,512]{2,1,0:T(8,128)(2,1)S(1)}, bf16[1,8192,512]{2,1,0:T(8,128)(2,1)}, u32[]{:S(2)}) copy-start(bf16[1,8192,512]{2,1,0:T(8,128)(2,1)} %param.9) | copy-start | bytes 25165828
  195.7 7.5 %copy-start.15 = (f32[512,256]{1,0:T(8,128)S(1)}, f32[512,256]{1,0:T(8,128)}, u32[]{:S(2)}) copy-start(f32[512,256]{1,0:T(8,128)} %copy-done.14) | copy-start | bytes 1572868
  204.7 2.3 collective-permute-start.25
  204.7 11.2 %copy-start.17 = (bf16[2048,256]{1,0:T(8,128)(2,1)S(1)}, bf16[2048,256]{1,0:T(8,128)(2,1)}, u32[]{:S(2)}) copy-start(bf16[2048,256]{1,0:T(8,128)(2,1)} %copy-done.16) | copy-start | bytes 3145732
  204.7 19.7 %copy-start.5 = (f32[2048,256]{1,0:T(8,128)S(1)}, f32[2048,256]{1,0:T(8,128)}, u32[]{:S(2)}) copy-start(f32[2048,256]{1,0:T(8,128)} %copy-done.3) | copy-start | bytes 6291460
  204.7 19.7 %collective-permute-start.27 = (bf16[2,512,256]{2,1,0:T(8,128)(2,1)}, bf16[2,512,256]{2,1,0:T(8,128)(2,1)}, u32[]{:S(2)}, u32[]{:S(2)}) collective-permute-start(bf16[2,512,256]{2,1,0:T(8,128)(2,1)} %fusion.14), channel_id=1, source_target_pairs={{0,4},{2,6},{4,0},{6,2},{8,12},{10,14},{12,8},{14,10},{1,5},{3,7},... | collective-permute-start | bytes 1572872 | tf_op jit(solution)/shard_map/ppermute | solution.py:15
  210.2 8.6 %collective-permute-start.26 = (bf16[2,1,4,2,16,512]{5,4,3,2,0,1:T(8,128)(2,1)}, bf16[2,1,4,2,16,512]{5,4,3,2,0,1:T(8,128)(2,1)S(1)}, u32[]{:S(2)}, u32[]{:S(2)}) collective-permute-start(bf16[2,1,4,2,16,512]{5,4,3,2,0,1:T(8,128)(2,1)} %fusion.20), channel_id=1, source_target_pairs={{0,16},{16,0},{1,17},{17,1},{2,18},{18,2},{3,19},{19,3},{4,20},{20... | collective-permute-start | bytes 786440 | tf_op jit(solution)/shard_map/ppermute | solution.py:15
  212.0 27.2 %copy-start.27 = (bf16[2,512,256]{2,1,0:T(8,128)(2,1)S(1)}, bf16[2,512,256]{2,1,0:T(8,128)(2,1)}, u32[]{:S(2)}) copy-start(bf16[2,512,256]{2,1,0:T(8,128)(2,1)} %copy-done.26) | copy-start | bytes 1572868
  212.9 26.1 %collective-permute-start.28 = (bf16[1,512,256]{2,1,0:T(8,128)(2,1)}, bf16[1,512,256]{2,1,0:T(8,128)(2,1)S(1)}, u32[]{:S(2)}, u32[]{:S(2)}) collective-permute-start(bf16[1,512,256]{2,1,0:T(8,128)(2,1)} %fusion.19), channel_id=1, source_target_pairs={{0,8},{2,10},{4,12},{6,14},{8,0},{10,2},{12,4},{14,6},{1,9},{3,11}... | collective-permute-start | bytes 786440 | tf_op jit(solution)/shard_map/ppermute | solution.py:15
  214.3 24.7 %collective-permute-start.29 = (bf16[1,512,256]{2,1,0:T(8,128)(2,1)}, bf16[1,512,256]{2,1,0:T(8,128)(2,1)S(1)}, u32[]{:S(2)}, u32[]{:S(2)}) collective-permute-start(bf16[1,512,256]{2,1,0:T(8,128)(2,1)} %fusion.18), channel_id=1, source_target_pairs={{0,8},{2,10},{4,12},{6,14},{8,0},{10,2},{12,4},{14,6},{1,9},{3,11}... | collective-permute-start | bytes 786440 | tf_op jit(solution)/shard_map/ppermute | solution.py:15
  215.9 43.8 %collective-permute-start.31 = (bf16[2048,256]{1,0:T(8,128)(2,1)S(1)}, bf16[2048,256]{1,0:T(8,128)(2,1)S(1)}, u32[]{:S(2)}, u32[]{:S(2)}) collective-permute-start(bf16[2048,256]{1,0:T(8,128)(2,1)S(1)} %copy-done.17), channel_id=1, source_target_pairs={{0,1},{1,0},{2,3},{3,2},{4,5},{5,4},{6,7},{7,6},{8,9},{9,8},{10,11... | collective-permute-start | bytes 3145736 | tf_op jit(solution)/shard_map/ppermute | solution.py:268
  224.5 20.7 %copy-start.25 = (bf16[2,512,256]{2,1,0:T(8,128)(2,1)S(1)}, bf16[2,512,256]{2,1,0:T(8,128)(2,1)}, u32[]{:S(2)}) copy-start(bf16[2,512,256]{2,1,0:T(8,128)(2,1)} %copy-done.24) | copy-start | bytes 1572868
  239.1 5.0 %collective-permute-start.32 = (bf16[2,2,2,16,512]{4,3,2,0,1:T(8,128)(2,1)S(1)}, bf16[2,2,2,16,512]{4,3,2,0,1:T(8,128)(2,1)S(1)}, u32[]{:S(2)}, u32[]{:S(2)}) collective-permute-start(bf16[2,2,2,16,512]{4,3,2,0,1:T(8,128)(2,1)S(1)} %fusion.23), channel_id=1, source_target_pairs={{0,4},{2,6},{4,0},{6,2},{8,12},{10,14},{12,8},{14,10},{1,5},{3,7},... | collective-permute-start | bytes 393224 | tf_op jit(solution)/shard_map/ppermute | solution.py:15
  244.1 5.4 %collective-permute-start.33 = (bf16[2,1,2,16,512]{4,3,2,0,1:T(8,128)(2,1)S(1)}, bf16[2,1,2,16,512]{4,3,2,0,1:T(8,128)(2,1)S(1)}, u32[]{:S(2)}, u32[]{:S(2)}) collective-permute-start(bf16[2,1,2,16,512]{4,3,2,0,1:T(8,128)(2,1)S(1)} %dynamic-slice_convert_fusion.1), channel_id=1, source_target_pairs={{0,8},{2,10},{4,12},{6,14},{8,0},{10,2},{12,4},{14,6},{1,9},{3,11}... | collective-permute-start | bytes 196616 | tf_op jit(solution)/shard_map/ppermute | solution.py:15
  247.1 12.6 %copy-start.7 = (f32[2048,256]{1,0:T(8,128)S(1)}, f32[2048,256]{1,0:T(8,128)}, u32[]{:S(2)}) copy-start(f32[2048,256]{1,0:T(8,128)} %copy-done.6) | copy-start | bytes 6291460
  249.6 5.6 %collective-permute-start.34 = (f32[2,2,1,16,512]{4,3,2,1,0:T(8,128)S(1)}, f32[2,2,1,16,512]{4,3,2,1,0:T(8,128)S(1)}, u32[]{:S(2)}, u32[]{:S(2)}) collective-permute-start(f32[2,2,1,16,512]{4,3,2,1,0:T(8,128)S(1)} %fusion.24), channel_id=1, source_target_pairs={{0,1},{1,0},{2,3},{3,2},{4,5},{5,4},{6,7},{7,6},{8,9},{9,8},{10,11... | collective-permute-start | bytes 393224 | tf_op jit(solution)/shard_map/ppermute | solution.py:15
  255.3 4.2 %collective-permute-start.35 = (bf16[51,512]{1,0:T(8,128)(2,1)S(1)}, bf16[51,512]{1,0:T(8,128)(2,1)S(1)}, u32[]{:S(2)}, u32[]{:S(2)}) collective-permute-start(bf16[51,512]{1,0:T(8,128)(2,1)S(1)} %pad_maximum_fusion.8), channel_id=1, source_target_pairs={{0,1},{1,0},{2,3},{3,2},{4,5},{5,4},{6,7},{7,6},{8,9},{9,8},{10,11... | collective-permute-start | bytes 156680 | tf_op jit(solution)/shard_map/ppermute | solution.py:15
  260.7 6.7 %collective-permute-start.37 = (bf16[99,512]{1,0:T(8,128)(2,1)S(1)}, bf16[99,512]{1,0:T(8,128)(2,1)S(1)}, u32[]{:S(2)}, u32[]{:S(2)}) collective-permute-start(bf16[99,512]{1,0:T(8,128)(2,1)S(1)} %pad_maximum_fusion.7), channel_id=1, source_target_pairs={{0,8},{2,10},{4,12},{6,14},{8,0},{10,2},{12,4},{14,6},{1,9},{3,11}... | collective-permute-start | bytes 304136 | tf_op jit(solution)/shard_map/ppermute | solution.py:15
  261.5 15.8 %collective-permute-start.36 = (bf16[2,512,256]{2,1,0:T(8,128)(2,1)S(1)}, bf16[2,512,256]{2,1,0:T(8,128)(2,1)S(1)}, u32[]{:S(2)}, u32[]{:S(2)}) collective-permute-start(bf16[2,512,256]{2,1,0:T(8,128)(2,1)S(1)} %fusion.10), channel_id=1, source_target_pairs={{0,4},{2,6},{4,0},{6,2},{8,12},{10,14},{12,8},{14,10},{1,5},{3,7},... | collective-permute-start | bytes 1572872 | tf_op jit(solution)/shard_map/ppermute | solution.py:15
  267.5 9.7 %collective-permute-start.38 = (bf16[195,512]{1,0:T(8,128)(2,1)S(1)}, bf16[195,512]{1,0:T(8,128)(2,1)S(1)}, u32[]{:S(2)}, u32[]{:S(2)}) collective-permute-start(bf16[195,512]{1,0:T(8,128)(2,1)S(1)} %pad_maximum_fusion.6), channel_id=1, source_target_pairs={{0,4},{2,6},{4,0},{6,2},{8,12},{10,14},{12,8},{14,10},{1,5},{3,7},... | collective-permute-start | bytes 599048 | tf_op jit(solution)/shard_map/ppermute | solution.py:15
  279.5 8.0 %collective-permute-start.40 = (bf16[387,512]{1,0:T(8,128)(2,1)S(1)}, bf16[387,512]{1,0:T(8,128)(2,1)}, u32[]{:S(2)}, u32[]{:S(2)}) collective-permute-start(bf16[387,512]{1,0:T(8,128)(2,1)S(1)} %pad_maximum_fusion.5), channel_id=1, source_target_pairs={{0,16},{16,0},{1,17},{17,1},{2,18},{18,2},{3,19},{19,3},{4,20},{20... | collective-permute-start | bytes 1188872 | tf_op jit(solution)/shard_map/ppermute | solution.py:15
  280.2 10.8 %collective-permute-start.30 = (bf16[1,512,256]{2,1,0:T(8,128)(2,1)}, bf16[1,512,256]{2,1,0:T(8,128)(2,1)S(1)}, u32[]{:S(2)}, u32[]{:S(2)}) collective-permute-start(bf16[1,512,256]{2,1,0:T(8,128)(2,1)} %fusion.21), channel_id=1, source_target_pairs={{0,8},{2,10},{4,12},{6,14},{8,0},{10,2},{12,4},{14,6},{1,9},{3,11}... | collective-permute-start | bytes 786440 | tf_op jit(solution)/shard_map/ppermute | solution.py:15
  290.3 17.1 %collective-permute-start.41 = (bf16[771,512]{1,0:T(8,128)(2,1)}, bf16[771,512]{1,0:T(8,128)(2,1)}, u32[]{:S(2)}, u32[]{:S(2)}) collective-permute-start(bf16[771,512]{1,0:T(8,128)(2,1)} %pad_maximum_fusion.4), channel_id=1, source_target_pairs={{0,2},{2,0},{4,6},{6,4},{8,10},{10,8},{12,14},{14,12},{1,3},{3,1},... | collective-permute-start | bytes 2368520 | tf_op jit(solution)/shard_map/ppermute | solution.py:15
  290.3 15.6 %collective-permute-start.39 = (bf16[1,512,256]{2,1,0:T(8,128)(2,1)}, bf16[1,512,256]{2,1,0:T(8,128)(2,1)}, u32[]{:S(2)}, u32[]{:S(2)}) collective-permute-start(bf16[1,512,256]{2,1,0:T(8,128)(2,1)} %fusion.22), channel_id=1, source_target_pairs={{0,8},{2,10},{4,12},{6,14},{8,0},{10,2},{12,4},{14,6},{1,9},{3,11}... | collective-permute-start | bytes 786440 | tf_op jit(solution)/shard_map/ppermute | solution.py:15
  (9 other events, 11.2 us)

commit v5 on v4

--- a/solution.py
+++ b/solution.py
@@ -7,7 +7,7 @@
 
 CORES = 2
 AWAY = 2
-CHUNKS = 2
+PIECES = (1, 2)
 
 
 def swap(x, axis, mask):
@@ -104,46 +104,28 @@
         return x.reshape(x.shape[1:])
 
 
-def mask_kernel(a_ref, mask_ref, *outs):
+def weighted_product(a_ref, mask_ref, f_ref, weight_ref):
     rows, cols = a_ref.shape
-    groups = mask_ref.shape[2]
+    groups = mask_ref.shape[1]
     shaped = a_ref[...].reshape(groups, rows // groups, cols)
-    for k, out_ref in enumerate(outs):
-        out_ref[...] = (shaped * mask_ref[k, 0][:, None, :]).reshape(rows, cols)
-
-
-def apply_masks(inverse, mask):
-    rows, cols = inverse.shape
-    count, blocks, groups, _ = mask.shape
-    block = rows // blocks
-    spec = pl.BlockSpec((block, cols), lambda i: (i, 0))
-    return pl.pallas_call(
-        mask_kernel,
-        out_shape=[jax.ShapeDtypeStruct((rows, cols), inverse.dtype)] * count,
-        grid=(blocks,),
-        in_specs=[spec, pl.BlockSpec((count, 1, groups, cols), lambda i: (0, i, 0, 0))],
-        out_specs=[spec] * count,
-        compiler_params=pltpu.CompilerParams(vmem_limit_bytes=40 * 2**20),
-        cost_estimate=pl.CostEstimate(flops=2 * rows * cols, bytes_accessed=6 * rows * cols, transcendentals=0),
-    )(inverse, mask)
-
-
-def weighted_product(a_ref, f_ref, weight_ref):
-    return jnp.dot(a_ref[...], f_ref[...], preferred_element_type=jnp.float32) * weight_ref[0]
-
-
-def away_kernel(where_ref, weight_ref, a_ref, f_ref, *outs):
-    total = weighted_product(a_ref, f_ref, weight_ref)
+    masked = (shaped * mask_ref[0][:, None, :]).reshape(rows, cols)
+    return jnp.dot(masked, f_ref[...], preferred_element_type=jnp.float32) * weight_ref[0]
+
+
+def away_kernel(where_ref, weight_ref, a_ref, mask_ref, f_ref, *outs):
+    total = weighted_product(a_ref, mask_ref, f_ref, weight_ref)
     width = total.shape[1] // len(outs)
     for n, out_ref in enumerate(outs):
         out_ref[...] = total[:, n * width:(n + 1) * width].astype(out_ref.dtype)
 
 
-def here_kernel(where_ref, weight_ref, a_ref, f_ref, panel_ref, start_ref, *refs):
-    recvs, (out_ref, term_ref) = refs[:AWAY], refs[AWAY:]
-    total = weighted_product(a_ref, f_ref, weight_ref)
+def here_kernel(where_ref, weight_ref, a_ref, mask_ref, f_ref, panel_ref, start_ref, *refs):
+    recvs, outs, term_ref = refs[:AWAY], refs[AWAY:-1], refs[-1]
+    total = weighted_product(a_ref, mask_ref, f_ref, weight_ref)
     total = total + jnp.concatenate([r[...].astype(jnp.float32) for r in recvs], axis=1)
-    out_ref[...] = total.astype(out_ref.dtype)
+    width = total.shape[1] // len(outs)
+    for n, out_ref in enumerate(outs):
+        out_ref[...] = total[:, n * width:(n + 1) * width].astype(out_ref.dtype)
     term = lax.dot_general(
         panel_ref[...], total.astype(jnp.bfloat16), (((0,), (0,)), ((), ())), preferred_element_type=jnp.float32
     )
@@ -157,9 +139,9 @@
         term_ref[...] = term_ref[...] - term
 
 
-def product(masked, factor, place, weight, sizes, merge=None):
+def product(inverse, mask, factor, place, weight, sizes, merge=None):
     zs, block, n_pole = sizes
-    cols = masked.shape[1]
+    cols = inverse.shape[1]
     width = factor.shape[1]
 
     def block_of(i, where):
@@ -168,6 +150,7 @@
     in_specs = [
         pl.BlockSpec(memory_space=pltpu.SMEM),
         pl.BlockSpec((block, cols), lambda i, w: (block_of(i, w), 0)),
+        pl.BlockSpec((1, mask.shape[1], cols), lambda i, w: (block_of(i, w), 0, 0)),
         pl.BlockSpec((cols, width), lambda i, w: (0, 0)),
     ]
     part = [pl.BlockSpec((block, width // AWAY), lambda i, w: (i, 0))] * AWAY
@@ -176,13 +159,15 @@
         out_shape = [jax.ShapeDtypeStruct((zs * block, width // AWAY), jnp.bfloat16)] * AWAY
         out_specs = part
     else:
-        recv, panel, start, kind = merge
+        recv, panel, start, kind, pieces = merge
         kernel, extra = here_kernel, (panel, start, *recv)
         full = panel.shape[1]
         term = pl.BlockSpec((full, width), lambda i, w: (0, 0))
         in_specs += [pl.BlockSpec((block, full), lambda i, w: (block_of(i, w), 0)), term] + part
-        out_shape = [jax.ShapeDtypeStruct((zs * block, width), kind), jax.ShapeDtypeStruct((full, width), jnp.float32)]
-        out_specs = [pl.BlockSpec((block, width), lambda i, w: (i, 0)), term]
+        piece = width // pieces
+        out_shape = [jax.ShapeDtypeStruct((zs * block, piece), kind)] * pieces
+        out_shape.append(jax.ShapeDtypeStruct((full, width), jnp.float32))
+        out_specs = [pl.BlockSpec((block, piece), lambda i, w: (i, 0))] * pieces + [term]
     return pl.pallas_call(
         kernel,
         out_shape=out_shape,
@@ -193,7 +178,7 @@
         cost_estimate=pl.CostEstimate(
             flops=2 * zs * block * cols, bytes_accessed=zs * block * width, transcendentals=0
         ),
-    )(place, weight, masked, factor, *extra)
+    )(place, weight, inverse, mask, factor, *extra)
 
 
 def fetch_factor(own):
@@ -217,70 +202,71 @@
     inverse, weight = inv_block[0], weights[0]
     rows, cols = inverse.shape
     width = panel_first.shape[2]
-    wide = width // CHUNKS
     blocks = n_col * n_pole
     block = rows // blocks
     sizes = (zs, block, n_pole)
     panels = (panel_first[0], panel_second[0])
     grain = rows // block_masks.shape[1]
     groups = max(1, block // grain)
-    parts = [(k, n) for k in range(2) for n in range(CHUNKS)]
 
     ratio = n_col // n_row
     mine = row == col // ratio
     own, got = [], []
-    for k, n in parts:
-        piece = lax.dynamic_slice(panels[k], (col % ratio * cols, n * wide), (cols, wide))
+    for panel in panels:
+        piece = lax.dynamic_slice(panel, (col % ratio * cols, 0), (cols, width))
         own.append(piece)
-        got.append(fetch_factor(after(piece, *got[-1:])))
-
-    mask = jnp.repeat(block_masks.astype(jnp.bfloat16), grain * groups // block, axis=1)
-    mask = jnp.repeat(mask, grain, axis=2).reshape(2, blocks, groups, cols)
-    masked = apply_masks(inverse, mask)
+        got.append(fetch_factor(after(piece, *got)))
+
+    masks = []
+    for k in range(2):
+        mask = jnp.repeat(block_masks[k].astype(jnp.bfloat16), grain * groups // block, axis=0)
+        masks.append(jnp.repeat(mask, grain, axis=1).reshape(blocks, groups, cols))
 
     def place(c, d, *deps):
         return after(jnp.stack([c, (pole + d) % n_pole]).astype(jnp.int32), *deps)
 
     dests = list(range(1, n_pole)) + [0]
-    token = (masked[0],)
+    token = tuple(masks)
     units, terms = [], []
-    for part, (k, n) in enumerate(parts):
-        factor = jnp.where(mine, own[part], after(got[part], *token))
-        received, arrived = {}, []
+    for k in range(2):
+        factor = jnp.where(mine, own[k], after(got[k], *token))
+        received, arrived = {}, [[] for _ in range(PIECES[k])]
         for d in dests:
-            away = product(masked[k], factor, place(1 - core, d, *token), weights, sizes)
+            away = product(inverse, masks[k], factor, place(1 - core, d, *token), weights, sizes)
             token = (away[0],)
             received[d] = [swap_core(x) for x in away]
-        term = jnp.zeros((width, wide), jnp.float32)
-        for d in dests if part + 1 < len(parts) else dests[::-1]:
+        term = jnp.zeros((width, width), jnp.float32)
+        for d in dests:
             if d == 0:
-                for unit in units:
-                    if not unit.done():
-                        token += (unit.step(),)
+                token += tuple(unit.step() for unit in units)
             kind = jnp.bfloat16 if d > 0 else jnp.float32
-            out, term = product(
-                masked[k], factor, place(core, d, *token), weights, sizes, (received[d], panels[k], term, kind)
-            )
-            token = (out,)
-            if d == 0:
-                kept = out
-            else:
-                arrived.append(lax.ppermute(out, "pole", [(i, (i + d) % n_pole) for i in range(n_pole)]))
+            merge = (received[d], panels[k], term, kind, PIECES[k])
+            *out, term = product(inverse, masks[k], factor, place(core, d, *token), weights, sizes, merge)
+            token = (out[0],)
+            if d > 0:
+                before = ()
+                for n, x in enumerate(out):
+                    came = lax.ppermute(after(x, *before), "pole", [(i, (i + d) % n_pole) for i in range(n_pole)])
+                    before = (came,)
+                    arrived[n].append(came)
         terms.append(term)
-        units.append(ZSum([x.reshape(zs, block, wide) for x in [kept] + arrived], z))
-
+        for n, kept in enumerate(out):
+            units.append(ZSum([x.reshape(zs, block, x.shape[1]) for x in [kept] + arrived[n]], z))
+
+    zero, early, last = units
     each = width // (n_row * blocks)
     split = (2, n_row, zs, CORES, n_pole, each, width)
-    term = jnp.stack([jnp.concatenate(terms[k * CHUNKS:(k + 1) * CHUNKS], axis=1) for k in range(2)]).reshape(split)
-    term = halve(term, 3, core, swap_core, jnp.bfloat16)
+    term = halve(jnp.stack(terms).reshape(split), 3, core, swap_core, jnp.bfloat16)
+    term = after(term, early.step(*token))
     term = halve(term, 1, row, swap_row, jnp.bfloat16)
-    token = (term,)
-    for unit in units[:-1]:
-        while not unit.done():
-            token += (unit.step(term),)
-    first = jnp.concatenate([u.result(*token[1:]) for u in units[:CHUNKS]], axis=1)
+    while not zero.done():
+        term = after(term, zero.step())
+    term = halve(term, 1, z, swap_z, jnp.bfloat16)
+    while not early.done():
+        term = after(term, early.step(term))
+    first = zero.result(term)
     squares = jnp.sum(first * first, axis=0)
-    term = halve(after(term, *token[1:]), 1, z, swap_z, jnp.bfloat16)
+    term = after(term, squares, last.step(term))
     base = pick(pick(pick(diag_inverse.reshape(split), core, 3), row, 1), z, 1).astype(jnp.float32) * weight
     both = halve(jnp.stack([base, term]), 2, pole, swap_pole, jnp.float32)
     base, term = both[0], both[1]
@@ -288,18 +274,19 @@
     piece = piece[:, None, None, None, None]
     for bit in reversed(range(n_pole.bit_length() - 1)):
         piece, squares = double(piece, squares, 4, pole, bit, swap_pole)
-    piece = after(piece, units[-1].step(piece))
+    while not last.done():
+        piece = after(piece, last.step(piece))
     for bit in reversed(range(zs.bit_length() - 1)):
         piece, squares = double(piece, squares, 2, z, bit, swap_z)
-    while not units[-1].done():
-        piece = after(piece, units[-1].step(piece))
     for bit in reversed(range(n_row.bit_length() - 1)):
         piece, squares = double(piece, squares, 1, row, bit, swap_row)
+    second = jnp.concatenate([early.result(), last.result()], axis=1)
+    piece = after(piece, second)
     piece, squares = double(piece, squares, 3, core, 0, swap_core)
     scale = jnp.sqrt(squares / (rows * n_row) + 1e-06)
     piece = piece.reshape(3, width, width).astype(jnp.float32)
     scaled = piece[1] + piece[2] / (scale[:, None] * scale)
-    second = jnp.concatenate([u.result() for u in units[CHUNKS:]], axis=1) / scale
+    second = second / scale
     return jnp.stack([first.astype(jnp.bfloat16), second.astype(jnp.bfloat16)]), jnp.stack([piece[0], scaled])
 
 

time: 315 us -> 289 us (0.917)
  Pallas kernels: 152 us -> 73.6 us
  waiting for transfers between devices: 67.9 us -> 133 us
  local copies, waits for them, and re-layouts: 23.9 us -> 17.1 us
  other arithmetic: 36 us -> 30.4 us
    ppermute x38 -> x26, waiting for transfers between devices: 67.9 us -> 129 us  [swap(): return lax.ppermute(x, axis, [(i, i ^ mask) for i in range(size)])]
    pallas_call x16 -> x8, Pallas kernels: 117 us -> 73.6 us  [product(): pl.pallas_call(kernel, out_shape=out_shape, grid_spec=pltpu.PrefetchScala...]
    pallas_call x1 -> x0, Pallas kernels: 35.3 us -> none  [apply_masks(): pl.pallas_call(mask_kernel, out_shape=[jax.ShapeDtypeStruct((rows, cols),...]
    unnamed x62 -> x50, local copies, waits for them, and re-layouts: 14.7 us -> 7.95 us
    concatenate x4 -> x0, other arithmetic: 4.79 us -> none  [the longest x2 3.2 us: body(): jnp.concatenate([u.result(*token[1:]) for u in units[:CHUNKS]], axis=1)]
    ppermute x4 -> x3, waiting for transfers between devices: 0.01 us -> 4.28 us  [body(): lax.ppermute(after(x, *before), 'pole', [(i, (i + d) % n_pole) for i in r...]
    convert_element_type x8 -> x6, other arithmetic: 12.8 us -> 10.3 us  [step(): send = self.part(1, *deps).astype(jnp.bfloat16)]
    ppermute x38 -> x26, starting transfers between devices: 26.7 us -> 26.7 us  [swap(): return lax.ppermute(x, axis, [(i, i ^ mask) for i in range(size)])]
  transfers between devices with their start and end apart: 42 -> 29, of which waited for: 12 -> 16; matrix products, arithmetic and copies ran while one was open for 11% -> 9% of each run, Pallas kernels for 46% -> 26%
where the time goes in v5:
time: 289 us; the launch traced here: 288 us
  waiting for transfers between devices  133 us (46%)
  Pallas kernels  73.6 us (25%)
  starting transfers between devices  31.2 us (11%)
  other arithmetic  30.4 us (11%)
  local copies, waits for them, and re-layouts  17.1 us (6%)
    ppermute x26, waiting for transfers between devices, swap(): return lax.ppermute(x, axis, [(i, i ^ mask) for i in range(size)])  129 us
    pallas_call x8, Pallas kernels, product(): pl.pallas_call(kernel, out_shape=out_shape, grid_spec=pltpu.PrefetchScala...  73.6 us
    ppermute x26, starting transfers between devices, swap(): return lax.ppermute(x, axis, [(i, i ^ mask) for i in range(size)])  26.7 us
    convert_element_type x6, other arithmetic, step(): send = self.part(1, *deps).astype(jnp.bfloat16)  10.3 us
    unnamed x50, local copies, waits for them, and re-layouts  7.95 us
    dynamic_slice x2, local copies, waits for them, and re-layouts, body(): piece = lax.dynamic_slice(panel, (col % ratio * cols, 0), (cols, width))  6.15 us
  transfers between devices with their start and end apart: 29, of which 16 were waited for; matrix products, arithmetic and copies ran while one was open for 9% of the time, Pallas kernels for 26%

profile of v5, /device:TPU:0, one launch (start us, length us, event | category | flops | bytes accessed | tf_op | source)
XLA Modules:
  0.0 287.5 jit_solution(11302007752972622835)
XLA Ops:
  0.7 3.0 %dynamic-slice_bitcast_fusion.1 = bf16[2048,512]{1,0:T(8,128)(2,1)} fusion(bf16[1,8192,512]{2,1,0:T(8,128)(2,1)} %param.8, s32[]{:T(128)S(6)} %select_n.269), kind=kLoop, calls=%fused_computation.8 | loop fusion | bytes 4194308 | tf_op jit(solution)/shard_map/dynamic_slice | solution.py:216
  3.7 2.9 %collective-permute-start = (bf16[2048,512]{1,0:T(8,128)(2,1)}, bf16[2048,512]{1,0:T(8,128)(2,1)S(1)}, u32[]{:S(2)}, u32[]{:S(2)}) collective-permute-start(bf16[2048,512]{1,0:T(8,128)(2,1)} %dynamic-slice_bitcast_fusion.1), channel_id=1, source_target_pairs={{0,16},{16,0},{1,17},{17,1},{2,18},{18,2},{3,19},{19,3},{4,20},{20... | collective-permute-start | bytes 6291464 | tf_op jit(solution)/shard_map/ppermute | solution.py:15
  8.2 3.1 %dynamic-slice_bitcast_fusion = bf16[2048,512]{1,0:T(8,128)(2,1)} fusion(bf16[1,8192,512]{2,1,0:T(8,128)(2,1)} %param.9, s32[]{:T(128)S(6)} %select_n.269), kind=kLoop, calls=%fused_computation.7 | loop fusion | bytes 4194308 | tf_op jit(solution)/shard_map/dynamic_slice | solution.py:216
  11.3 41.2 %collective-permute-done = bf16[2048,512]{1,0:T(8,128)(2,1)S(1)} collective-permute-done((bf16[2048,512]{1,0:T(8,128)(2,1)}, bf16[2048,512]{1,0:T(8,128)(2,1)S(1)}, u32[]{:S(2)}, u32[]{:S(2)}) %collective-permute-start) | collective-permute-done | bytes 2097184 | tf_op jit(solution)/shard_map/ppermute | solution.py:15
  52.5 1.3 copy-done.17
  53.8 1.7 collective-permute-start.5
  55.5 2.2 broadcast_select_fusion.1.f_ref
  57.7 8.7 %shard_map.77 = (bf16[2048,256]{1,0:T(8,128)(2,1)}, bf16[2048,256]{1,0:T(8,128)(2,1)}) custom-call(s32[2]{0:T(128)S(1)} %pad_add_fusion.3.where_ref, f32[1]{0:T(128)} %copy.119.weight_ref, bf16[8192,2048]{1,0:T(8,128)(2,1)} %bitcast.150, bf16[16,4,2048]{2,1,0:T(4,128)(2,1)S(1)} %reshape_reshape.52.mask_ref, bf16[2048,512]{1,0:T(8,128)(2,1)S(1)} %broadcast_select_fusion.1.f_ref), custom_call_target="tpu_custom_call" | custom-call | flops 8388608 | bytes 1048576 | tf_op jit(solution)/shard_map/pallas_call | solution.py:171
  67.0 7.7 %shard_map.78 = (bf16[2048,256]{1,0:T(8,128)(2,1)S(1)}, bf16[2048,256]{1,0:T(8,128)(2,1)S(1)}) custom-call(s32[2]{0:T(128)S(1)} %get-tuple-element.68.where_ref, f32[1]{0:T(128)} %copy.119.weight_ref, bf16[8192,2048]{1,0:T(8,128)(2,1)} %bitcast.151, bf16[16,4,2048]{2,1,0:T(4,128)(2,1)S(1)} %reshape_reshape.52.mask_ref, ...), custom_call_target="tpu_custom_call" | custom-call | flops 8388608 | bytes 1048576 | tf_op jit(solution)/shard_map/pallas_call | solution.py:171
  75.4 0.9 copy-done.1
  76.3 10.5 %shard_map.79 = (bf16[2048,512]{1,0:T(8,128)(2,1)}, f32[512,512]{1,0:T(8,128)S(1)}) custom-call(s32[2]{0:T(128)S(1)} %get-tuple-element.70.where_ref, f32[1]{0:T(128)} %copy.119.weight_ref, bf16[8192,2048]{1,0:T(8,128)(2,1)} %bitcast.152, bf16[16,4,2048]{2,1,0:T(4,128)(2,1)S(1)} %copy-done.1, bf16[2048,512]{1,0:T(8,128)(2,1)S(1)} %broadcast_select_fusion.1.f_ref, ...), custom_call_target="tpu_custom_call" | custom-call | flops 8388608 | bytes 1048576 | tf_op jit(solution)/shard_map/pallas_call | solution.py:171
  86.8 1.5 collective-permute-start.8
  88.4 9.2 %shard_map.80 = (f32[2048,512]{1,0:T(8,128)S(1)}, f32[512,512]{1,0:T(8,128)S(1)}) custom-call(s32[2]{0:T(128)S(1)} %pad_add_fusion.1.where_ref, f32[1]{0:T(128)} %copy.119.weight_ref, bf16[8192,2048]{1,0:T(8,128)(2,1)} %bitcast.153, bf16[16,4,2048]{2,1,0:T(4,128)(2,1)S(1)} %copy-done.2, bf16[2048,512]{1,0:T(8,128)(2,1)S(1)} %broadcast_select_fusion.1.f_ref, ...), custom_call_target="tpu_custom_call" | custom-call | flops 8388608 | bytes 1048576 | tf_op jit(solution)/shard_map/pallas_call | solution.py:171
  97.6 2.0 copy-done.3
  99.6 1.3 collective-permute-done.5
  100.9 2.2 broadcast_select_fusion.f_ref
  103.1 8.7 %shard_map.81 = (bf16[2048,256]{1,0:T(8,128)(2,1)}, bf16[2048,256]{1,0:T(8,128)(2,1)}) custom-call(s32[2]{0:T(128)S(1)} %pad_add_fusion.3.where_ref, f32[1]{0:T(128)} %copy.119.weight_ref, bf16[8192,2048]{1,0:T(8,128)(2,1)} %bitcast.154, bf16[16,4,2048]{2,1,0:T(4,128)(2,1)S(1)} %reshape_reshape.53.mask_ref, bf16[2048,512]{1,0:T(8,128)(2,1)S(1)} %broadcast_select_fusion.f_ref), custom_call_target="tpu_custom_call" | custom-call | flops 8388608 | bytes 1048576 | tf_op jit(solution)/shard_map/pallas_call | solution.py:171
  112.4 8.7 %shard_map.82 = (bf16[2048,256]{1,0:T(8,128)(2,1)}, bf16[2048,256]{1,0:T(8,128)(2,1)}) custom-call(s32[2]{0:T(128)S(1)} %get-tuple-element.68.where_ref, f32[1]{0:T(128)} %copy.119.weight_ref, bf16[8192,2048]{1,0:T(8,128)(2,1)} %bitcast.155, bf16[16,4,2048]{2,1,0:T(4,128)(2,1)S(1)} %reshape_reshape.53.mask_ref, bf16[2048,512]{1,0:T(8,128)(2,1)S(1)} %broadcast_select_fusion.f_ref), custom_call_target="tpu_custom_call" | custom-call | flops 8388608 | bytes 1048576 | tf_op jit(solution)/shard_map/pallas_call | solution.py:171
  121.6 10.6 %shard_map.83 = (bf16[2048,256]{1,0:T(8,128)(2,1)}, bf16[2048,256]{1,0:T(8,128)(2,1)S(1)}, f32[512,512]{1,0:T(8,128)S(1)}) custom-call(s32[2]{0:T(128)S(1)} %get-tuple-element.70.where_ref, f32[1]{0:T(128)} %copy.119.weight_ref, bf16[8192,2048]{1,0:T(8,128)(2,1)} %bitcast.156, bf16[16,4,2048]{2,1,0:T(4,128)(2,1)S(1)} %reshape_reshape.53.mask_ref, ...), custom_call_target="tpu_custom_call" | custom-call | flops 8388608 | bytes 1048576 | tf_op jit(solution)/shard_map/pallas_call | solution.py:171
  132.1 1.5 collective-permute-start.12
  133.6 1.2 collective-permute-done.8
  134.7 2.5 fusion.2
  137.3 9.6 %shard_map.84 = (f32[2048,256]{1,0:T(8,128)S(1)}, f32[2048,256]{1,0:T(8,128)S(1)}, f32[512,512]{1,0:T(8,128)S(1)}) custom-call(s32[2]{0:T(128)S(1)} %pad_add_fusion.1.where_ref, f32[1]{0:T(128)} %copy.119.weight_ref, bf16[8192,2048]{1,0:T(8,128)(2,1)} %bitcast.157, bf16[16,4,2048]{2,1,0:T(4,128)(2,1)S(1)} %reshape_reshape.53.mask_ref, ...), custom_call_target="tpu_custom_call" | custom-call | flops 8388608 | bytes 1048576 | tf_op jit(solution)/shard_map/pallas_call | solution.py:171
  146.9 1.3 copy-done.9
  148.2 1.4 copy-done.11
  149.6 0.9 fusion.12
  150.7 1.6 collective-permute-start.14
  153.0 1.4 fusion.7
  154.4 3.1 %collective-permute-done.12 = bf16[2048,256]{1,0:T(8,128)(2,1)} collective-permute-done((bf16[2048,256]{1,0:T(8,128)(2,1)}, bf16[2048,256]{1,0:T(8,128)(2,1)}, u32[]{:S(2)}, u32[]{:S(2)}) %collective-permute-start.12) | collective-permute-done | bytes 1048608 | tf_op jit(solution)/shard_map/ppermute | solution.py:249
  157.5 2.0 fusion.10
  159.5 2.1 collective-permute-start.13
  161.7 15.0 %collective-permute-done.14 = bf16[2,512,512]{2,1,0:T(8,128)(2,1)} collective-permute-done((bf16[2,512,512]{2,1,0:T(8,128)(2,1)}, bf16[2,512,512]{2,1,0:T(8,128)(2,1)}, u32[]{:S(2)}, u32[]{:S(2)}) %collective-permute-start.14) | collective-permute-done | bytes 1048608 | tf_op jit(solution)/shard_map/ppermute | solution.py:15
  176.6 2.6 fusion.9
  179.4 1.7 collective-permute-start.15
  181.5 3.2 %collective-permute-start.18 = (bf16[1,512,512]{2,1,0:T(8,128)(2,1)}, bf16[1,512,512]{2,1,0:T(8,128)(2,1)S(1)}, u32[]{:S(2)}, u32[]{:S(2)}) collective-permute-start(bf16[1,512,512]{2,1,0:T(8,128)(2,1)} %fusion.9), channel_id=1, source_target_pairs={{0,8},{2,10},{4,12},{6,14},{8,0},{10,2},{12,4},{14,6},{1,9},{3,11}... | collective-permute-start | bytes 1572872 | tf_op jit(solution)/shard_map/ppermute | solution.py:15
  184.7 1.5 collective-permute-start.20
  186.2 11.6 %collective-permute-done.15 = bf16[2,2,2,16,512]{4,3,2,1,0:T(8,128)(2,1)S(1)} collective-permute-done((bf16[2,2,2,16,512]{4,3,2,1,0:T(8,128)(2,1)S(1)}, bf16[2,2,2,16,512]{4,3,2,1,0:T(8,128)(2,1)S(1)}, u32[]{:S(2)}, u32[]{:S(2)}) %collective-permute-start.15) | collective-permute-done | bytes 131104 | tf_op jit(solution)/shard_map/ppermute | solution.py:15
  198.5 0.9 multiply_bitcast_fusion
  199.4 12.4 %collective-permute-done.16 = bf16[2,1,2,16,512]{4,3,2,1,0:T(8,128)(2,1)S(1)} collective-permute-done((bf16[2,1,2,16,512]{4,3,2,1,0:T(8,128)(2,1)S(1)}, bf16[2,1,2,16,512]{4,3,2,1,0:T(8,128)(2,1)S(1)}, u32[]{:S(2)}, u32[]{:S(2)}) %collective-permute-start.16) | collective-permute-done | bytes 65568 | tf_op jit(solution)/shard_map/ppermute | solution.py:15
  211.8 2.1 fusion.15
  214.0 2.7 convert_bitcast_fusion
  216.9 1.6 collective-permute-start.22
  218.6 3.4 %collective-permute-done.22 = f32[2,2,1,16,512]{4,3,2,1,0:T(8,128)S(1)} collective-permute-done((f32[2,2,1,16,512]{4,3,2,1,0:T(8,128)S(1)}, f32[2,2,1,16,512]{4,3,2,1,0:T(8,128)S(1)}, u32[]{:S(2)}, u32[]{:S(2)}) %collective-permute-start.22) | collective-permute-done | bytes 131104 | tf_op jit(solution)/shard_map/ppermute | solution.py:15
  222.0 1.6 collective-permute-start.23
  223.6 2.6 collective-permute-done.23
  226.4 2.8 collective-permute-done.21
  229.1 0.9 fusion.16
  230.0 2.3 collective-permute-start.25
  232.3 3.5 %collective-permute-done.25 = bf16[99,512]{1,0:T(8,128)(2,1)S(1)} collective-permute-done((bf16[99,512]{1,0:T(8,128)(2,1)S(1)}, bf16[99,512]{1,0:T(8,128)(2,1)S(1)}, u32[]{:S(2)}, u32[]{:S(2)}) %collective-permute-start.25) | collective-permute-done | bytes 101408 | tf_op jit(solution)/shard_map/ppermute | solution.py:15
  235.9 1.7 collective-permute-start.26
  237.7 4.1 %collective-permute-done.26 = bf16[195,512]{1,0:T(8,128)(2,1)S(1)} collective-permute-done((bf16[195,512]{1,0:T(8,128)(2,1)S(1)}, bf16[195,512]{1,0:T(8,128)(2,1)S(1)}, u32[]{:S(2)}, u32[]{:S(2)}) %collective-permute-start.26) | collective-permute-done | bytes 199712 | tf_op jit(solution)/shard_map/ppermute | solution.py:15
  242.0 0.8 pad_maximum_fusion.3
  242.7 8.1 %collective-permute-done.27 = bf16[387,512]{1,0:T(8,128)(2,1)S(1)} collective-permute-done((bf16[387,512]{1,0:T(8,128)(2,1)}, bf16[387,512]{1,0:T(8,128)(2,1)S(1)}, u32[]{:S(2)}, u32[]{:S(2)}) %collective-permute-start.27) | collective-permute-done | bytes 396320 | tf_op jit(solution)/shard_map/ppermute | solution.py:15
  250.8 0.7 copy-done.23
  251.8 0.8 convert_reduce_fusion.1
  252.6 0.9 pad_maximum_fusion.2
  253.5 2.8 collective-permute-start.19
  256.5 18.7 %collective-permute-done.19 = bf16[1,512,256]{2,1,0:T(8,128)(2,1)} collective-permute-done((bf16[1,512,256]{2,1,0:T(8,128)(2,1)}, bf16[1,512,256]{2,1,0:T(8,128)(2,1)}, u32[]{:S(2)}, u32[]{:S(2)}) %collective-permute-start.19) | collective-permute-done | bytes 262176 | tf_op jit(solution)/shard_map/ppermute | solution.py:15
  275.1 1.4 fusion.14
  276.5 3.9 %collective-permute-done.24 = bf16[1,512,256]{2,1,0:T(8,128)(2,1)} collective-permute-done((bf16[1,512,256]{2,1,0:T(8,128)(2,1)}, bf16[1,512,256]{2,1,0:T(8,128)(2,1)}, u32[]{:S(2)}, u32[]{:S(2)}) %collective-permute-start.24) | collective-permute-done | bytes 262176 | tf_op jit(solution)/shard_map/ppermute | solution.py:15
  280.5 1.1 fusion.13
  282.3 1.2 slice.123
  285.0 1.5 pad_maximum_fusion
  286.5 1.1 pad_maximum_fusion.1
  (133 shorter events, 8.8 us)
Async XLA Ops:
  0.6 6.0 %copy-start.24 = (s32[2,64,16]{1,2,0:T(8,128)S(1)}, s32[2,64,16]{1,2,0:T(8,128)}, u32[]{:S(2)}) copy-start(s32[2,64,16]{1,2,0:T(8,128)} %param.7) | copy-start | bytes 24580
  3.7 48.8 %collective-permute-start = (bf16[2048,512]{1,0:T(8,128)(2,1)}, bf16[2048,512]{1,0:T(8,128)(2,1)S(1)}, u32[]{:S(2)}, u32[]{:S(2)}) collective-permute-start(bf16[2048,512]{1,0:T(8,128)(2,1)} %dynamic-slice_bitcast_fusion.1), channel_id=1, source_target_pairs={{0,16},{16,0},{1,17},{17,1},{2,18},{18,2},{3,19},{19,3},{4,20},{20... | collective-permute-start | bytes 6291464 | tf_op jit(solution)/shard_map/ppermute | solution.py:15
  7.0 60.0 %copy-start = (bf16[16,4,2048]{2,1,0:T(4,128)(2,1)}, bf16[16,4,2048]{2,1,0:T(4,128)(2,1)S(1)}, u32[]{:S(2)}) copy-start(bf16[16,4,2048]{2,1,0:T(4,128)(2,1)S(1)} %reshape_reshape.52.mask_ref) | copy-start | bytes 786436
  52.5 1.3 copy-start.17
  53.8 47.1 %collective-permute-start.5 = (bf16[2048,512]{1,0:T(8,128)(2,1)}, bf16[2048,512]{1,0:T(8,128)(2,1)}, u32[]{:S(2)}, u32[]{:S(2)}) collective-permute-start(bf16[2048,512]{1,0:T(8,128)(2,1)} %dynamic-slice_bitcast_fusion), channel_id=1, source_target_pairs={{0,16},{16,0},{1,17},{17,1},{2,18},{18,2},{3,19},{19,3},{4,20},{20... | collective-permute-start | bytes 6291464 | tf_op jit(solution)/shard_map/ppermute | solution.py:15
  66.4 8.8 %collective-permute-start.1 = (bf16[2048,256]{1,0:T(8,128)(2,1)}, bf16[2048,256]{1,0:T(8,128)(2,1)}, u32[]{:S(2)}, u32[]{:S(2)}) collective-permute-start(bf16[2048,256]{1,0:T(8,128)(2,1)} %get-tuple-element.53), channel_id=1, source_target_pairs={{0,2},{2,0},{4,6},{6,4},{8,10},{10,8},{12,14},{14,12},{1,3},{3,1},... | collective-permute-start | bytes 3145736 | tf_op jit(solution)/shard_map/ppermute | solution.py:15
  66.4 8.8 %collective-permute-start.2 = (bf16[2048,256]{1,0:T(8,128)(2,1)}, bf16[2048,256]{1,0:T(8,128)(2,1)}, u32[]{:S(2)}, u32[]{:S(2)}) collective-permute-start(bf16[2048,256]{1,0:T(8,128)(2,1)} %get-tuple-element.57), channel_id=1, source_target_pairs={{0,2},{2,0},{4,6},{6,4},{8,10},{10,8},{12,14},{14,12},{1,3},{3,1},... | collective-permute-start | bytes 3145736 | tf_op jit(solution)/shard_map/ppermute | solution.py:15
  74.7 13.7 %collective-permute-start.3 = (bf16[2048,256]{1,0:T(8,128)(2,1)S(1)}, bf16[2048,256]{1,0:T(8,128)(2,1)S(1)}, u32[]{:S(2)}, u32[]{:S(2)}) collective-permute-start(bf16[2048,256]{1,0:T(8,128)(2,1)S(1)} %get-tuple-element.55), channel_id=1, source_target_pairs={{0,2},{2,0},{4,6},{6,4},{8,10},{10,8},{12,14},{14,12},{1,3},{3,1},... | collective-permute-start | bytes 3145736 | tf_op jit(solution)/shard_map/ppermute | solution.py:15
  74.8 13.7 %collective-permute-start.4 = (bf16[2048,256]{1,0:T(8,128)(2,1)S(1)}, bf16[2048,256]{1,0:T(8,128)(2,1)S(1)}, u32[]{:S(2)}, u32[]{:S(2)}) collective-permute-start(bf16[2048,256]{1,0:T(8,128)(2,1)S(1)} %get-tuple-element.61), channel_id=1, source_target_pairs={{0,2},{2,0},{4,6},{6,4},{8,10},{10,8},{12,14},{14,12},{1,3},{3,1},... | collective-permute-start | bytes 3145736 | tf_op jit(solution)/shard_map/ppermute | solution.py:15
  75.4 1.0 copy-start.1
  76.3 12.1 %copy-start.2 = (bf16[16,4,2048]{2,1,0:T(4,128)(2,1)S(1)}, bf16[16,4,2048]{2,1,0:T(4,128)(2,1)}, u32[]{:S(2)}) copy-start(bf16[16,4,2048]{2,1,0:T(4,128)(2,1)} %copy-done) | copy-start | bytes 786436
  86.8 47.9 %collective-permute-start.8 = (bf16[2048,512]{1,0:T(8,128)(2,1)}, bf16[2048,512]{1,0:T(8,128)(2,1)}, u32[]{:S(2)}, u32[]{:S(2)}) collective-permute-start(bf16[2048,512]{1,0:T(8,128)(2,1)} %get-tuple-element.58), channel_id=1, source_target_pairs={{0,1},{1,0},{2,3},{3,2},{4,5},{5,4},{6,7},{7,6},{8,9},{9,8},{10,11... | collective-permute-start | bytes 6291464 | tf_op jit(solution)/shard_map/ppermute | solution.py:249
  97.6 2.0 copy-start.3
  99.6 3.5 %copy-start.5 = (f32[512,512]{1,0:T(8,128)}, f32[512,512]{1,0:T(8,128)S(1)}, u32[]{:S(2)}) copy-start(f32[512,512]{1,0:T(8,128)S(1)} %get-tuple-element.63) | copy-start | bytes 3145732
  111.8 9.7 %collective-permute-start.6 = (bf16[2048,256]{1,0:T(8,128)(2,1)}, bf16[2048,256]{1,0:T(8,128)(2,1)}, u32[]{:S(2)}, u32[]{:S(2)}) collective-permute-start(bf16[2048,256]{1,0:T(8,128)(2,1)} %get-tuple-element.67), channel_id=1, source_target_pairs={{0,2},{2,0},{4,6},{6,4},{8,10},{10,8},{12,14},{14,12},{1,3},{3,1},... | collective-permute-start | bytes 3145736 | tf_op jit(solution)/shard_map/ppermute | solution.py:15
  111.8 9.7 %collective-permute-start.7 = (bf16[2048,256]{1,0:T(8,128)(2,1)}, bf16[2048,256]{1,0:T(8,128)(2,1)}, u32[]{:S(2)}, u32[]{:S(2)}) collective-permute-start(bf16[2048,256]{1,0:T(8,128)(2,1)} %get-tuple-element.71), channel_id=1, source_target_pairs={{0,2},{2,0},{4,6},{6,4},{8,10},{10,8},{12,14},{14,12},{1,3},{3,1},... | collective-permute-start | bytes 3145736 | tf_op jit(solution)/shard_map/ppermute | solution.py:15
  121.1 16.2 %collective-permute-start.10 = (bf16[2048,256]{1,0:T(8,128)(2,1)}, bf16[2048,256]{1,0:T(8,128)(2,1)}, u32[]{:S(2)}, u32[]{:S(2)}) collective-permute-start(bf16[2048,256]{1,0:T(8,128)(2,1)} %get-tuple-element.75), channel_id=1, source_target_pairs={{0,2},{2,0},{4,6},{6,4},{8,10},{10,8},{12,14},{14,12},{1,3},{3,1},... | collective-permute-start | bytes 3145736 | tf_op jit(solution)/shard_map/ppermute | solution.py:15
  121.1 16.2 %collective-permute-start.9 = (bf16[2048,256]{1,0:T(8,128)(2,1)}, bf16[2048,256]{1,0:T(8,128)(2,1)}, u32[]{:S(2)}, u32[]{:S(2)}) collective-permute-start(bf16[2048,256]{1,0:T(8,128)(2,1)} %get-tuple-element.69), channel_id=1, source_target_pairs={{0,2},{2,0},{4,6},{6,4},{8,10},{10,8},{12,14},{14,12},{1,3},{3,1},... | collective-permute-start | bytes 3145736 | tf_op jit(solution)/shard_map/ppermute | solution.py:15
  121.6 13.2 %copy-start.4 = (f32[2048,512]{1,0:T(8,128)S(1)}, f32[2048,512]{1,0:T(8,128)}, u32[]{:S(2)}) copy-start(f32[2048,512]{1,0:T(8,128)} %copy-done.3) | copy-start | bytes 12582916
  132.1 5.2 %copy-start.13 = (bf16[2048,256]{1,0:T(8,128)(2,1)}, bf16[2048,256]{1,0:T(8,128)(2,1)S(1)}, u32[]{:S(2)}) copy-start(bf16[2048,256]{1,0:T(8,128)(2,1)S(1)} %get-tuple-element.92) | copy-start | bytes 3145732
  132.1 25.4 %collective-permute-start.12 = (bf16[2048,256]{1,0:T(8,128)(2,1)}, bf16[2048,256]{1,0:T(8,128)(2,1)}, u32[]{:S(2)}, u32[]{:S(2)}) collective-permute-start(bf16[2048,256]{1,0:T(8,128)(2,1)} %get-tuple-element.72), channel_id=1, source_target_pairs={{0,1},{1,0},{2,3},{3,2},{4,5},{5,4},{6,7},{7,6},{8,9},{9,8},{10,11... | collective-permute-start | bytes 3145736 | tf_op jit(solution)/shard_map/ppermute | solution.py:249
  137.3 12.3 %copy-start.6 = (f32[512,512]{1,0:T(8,128)S(1)}, f32[512,512]{1,0:T(8,128)}, u32[]{:S(2)}) copy-start(f32[512,512]{1,0:T(8,128)} %copy-done.5) | copy-start | bytes 3145732
  146.9 1.3 copy-start.9
  148.2 1.4 copy-start.11
  149.6 1.1 copy-start.8
  149.6 3.4 %copy-start.7 = (f32[512,512]{1,0:T(8,128)S(1)}, f32[512,512]{1,0:T(8,128)}, u32[]{:S(2)}) copy-start(f32[512,512]{1,0:T(8,128)} %copy-done.5) | copy-start | bytes 3145732
  150.7 6.8 %copy-start.12 = (f32[2048,256]{1,0:T(8,128)S(1)}, f32[2048,256]{1,0:T(8,128)}, u32[]{:S(2)}) copy-start(f32[2048,256]{1,0:T(8,128)} %copy-done.11) | copy-start | bytes 6291460
  150.7 2.3 collective-permute-start.11
  150.7 25.9 %collective-permute-start.14 = (bf16[2,512,512]{2,1,0:T(8,128)(2,1)}, bf16[2,512,512]{2,1,0:T(8,128)(2,1)}, u32[]{:S(2)}, u32[]{:S(2)}) collective-permute-start(bf16[2,512,512]{2,1,0:T(8,128)(2,1)} %fusion.2), channel_id=1, source_target_pairs={{0,4},{2,6},{4,0},{6,2},{8,12},{10,14},{12,8},{14,10},{1,5},{3,7},... | collective-permute-start | bytes 3145736 | tf_op jit(solution)/shard_map/ppermute | solution.py:15
  154.4 5.1 %copy-start.15 = (f32[2,2,4,2,16,512]{5,4,3,2,0,1:T(8,128)}, f32[2,2,4,2,16,512]{5,4,3,2,0,1:T(8,128)S(1)}, u32[]{:S(2)}) copy-start(f32[2,2,4,2,16,512]{5,4,3,2,0,1:T(8,128)S(1)} %fusion.7) | copy-start | bytes 3145732
  159.5 19.7 %copy-start.16 = (f32[2,2,4,2,16,512]{5,4,3,2,0,1:T(8,128)S(1)}, f32[2,2,4,2,16,512]{5,4,3,2,0,1:T(8,128)}, u32[]{:S(2)}) copy-start(f32[2,2,4,2,16,512]{5,4,3,2,0,1:T(8,128)} %copy-done.15) | copy-start | bytes 3145732
  159.5 19.7 %collective-permute-start.13 = (bf16[2,1,4,2,16,512]{5,4,3,2,0,1:T(8,128)(2,1)S(1)}, bf16[2,1,4,2,16,512]{5,4,3,2,0,1:T(8,128)(2,1)S(1)}, u32[]{:S(2)}, u32[]{:S(2)}) collective-permute-start(bf16[2,1,4,2,16,512]{5,4,3,2,0,1:T(8,128)(2,1)S(1)} %dynamic-slice_convert_fusion), channel_id=1, source_target_pairs={{0,16},{16,0},{1,17},{17,1},{2,18},{18,2},{3,19},{19,3},{4,20},{20... | collective-permute-start | bytes 786440 | tf_op jit(solution)/shard_map/ppermute | solution.py:15
  176.6 8.1 %copy-start.14 = (bf16[2048,256]{1,0:T(8,128)(2,1)S(1)}, bf16[2048,256]{1,0:T(8,128)(2,1)}, u32[]{:S(2)}) copy-start(bf16[2048,256]{1,0:T(8,128)(2,1)} %copy-done.13) | copy-start | bytes 3145732
  179.4 18.4 %collective-permute-start.15 = (bf16[2,2,2,16,512]{4,3,2,1,0:T(8,128)(2,1)S(1)}, bf16[2,2,2,16,512]{4,3,2,1,0:T(8,128)(2,1)S(1)}, u32[]{:S(2)}, u32[]{:S(2)}) collective-permute-start(bf16[2,2,2,16,512]{4,3,2,1,0:T(8,128)(2,1)S(1)} %fusion.17), channel_id=1, source_target_pairs={{0,4},{2,6},{4,0},{6,2},{8,12},{10,14},{12,8},{14,10},{1,5},{3,7},... | collective-permute-start | bytes 393224 | tf_op jit(solution)/shard_map/ppermute | solution.py:15
  181.0 30.8 %collective-permute-start.17 = (bf16[2,512,256]{2,1,0:T(8,128)(2,1)}, bf16[2,512,256]{2,1,0:T(8,128)(2,1)S(1)}, u32[]{:S(2)}, u32[]{:S(2)}) collective-permute-start(bf16[2,512,256]{2,1,0:T(8,128)(2,1)} %fusion.10), channel_id=1, source_target_pairs={{0,4},{2,6},{4,0},{6,2},{8,12},{10,14},{12,8},{14,10},{1,5},{3,7},... | collective-permute-start | bytes 1572872 | tf_op jit(solution)/shard_map/ppermute | solution.py:15
  181.5 32.5 %collective-permute-start.18 = (bf16[1,512,512]{2,1,0:T(8,128)(2,1)}, bf16[1,512,512]{2,1,0:T(8,128)(2,1)S(1)}, u32[]{:S(2)}, u32[]{:S(2)}) collective-permute-start(bf16[1,512,512]{2,1,0:T(8,128)(2,1)} %fusion.9), channel_id=1, source_target_pairs={{0,8},{2,10},{4,12},{6,14},{8,0},{10,2},{12,4},{14,6},{1,9},{3,11}... | collective-permute-start | bytes 1572872 | tf_op jit(solution)/shard_map/ppermute | solution.py:15
  184.7 32.0 %collective-permute-start.20 = (bf16[2048,256]{1,0:T(8,128)(2,1)S(1)}, bf16[2048,256]{1,0:T(8,128)(2,1)S(1)}, u32[]{:S(2)}, u32[]{:S(2)}) collective-permute-start(bf16[2048,256]{1,0:T(8,128)(2,1)S(1)} %copy-done.14), channel_id=1, source_target_pairs={{0,1},{1,0},{2,3},{3,2},{4,5},{5,4},{6,7},{7,6},{8,9},{9,8},{10,11... | collective-permute-start | bytes 3145736 | tf_op jit(solution)/shard_map/ppermute | solution.py:249
  197.8 14.0 %collective-permute-start.16 = (bf16[2,1,2,16,512]{4,3,2,1,0:T(8,128)(2,1)S(1)}, bf16[2,1,2,16,512]{4,3,2,1,0:T(8,128)(2,1)S(1)}, u32[]{:S(2)}, u32[]{:S(2)}) collective-permute-start(bf16[2,1,2,16,512]{4,3,2,1,0:T(8,128)(2,1)S(1)} %dynamic-slice_convert_fusion.2), channel_id=1, source_target_pairs={{0,8},{2,10},{4,12},{6,14},{8,0},{10,2},{12,4},{14,6},{1,9},{3,11}... | collective-permute-start | bytes 196616 | tf_op jit(solution)/shard_map/ppermute | solution.py:15
  211.8 2.1 copy-start.20
  211.8 4.9 %copy-start.10 = (f32[2048,256]{1,0:T(8,128)S(1)}, f32[2048,256]{1,0:T(8,128)}, u32[]{:S(2)}) copy-start(f32[2048,256]{1,0:T(8,128)} %copy-done.9) | copy-start | bytes 6291460
  216.7 13.3 %copy-start.19 = (bf16[2048,256]{1,0:T(8,128)(2,1)}, bf16[2048,256]{1,0:T(8,128)(2,1)S(1)}, u32[]{:S(2)}) copy-start(bf16[2048,256]{1,0:T(8,128)(2,1)S(1)} %collective-permute-done.20) | copy-start | bytes 3145732
  216.9 5.0 %collective-permute-start.22 = (f32[2,2,1,16,512]{4,3,2,1,0:T(8,128)S(1)}, f32[2,2,1,16,512]{4,3,2,1,0:T(8,128)S(1)}, u32[]{:S(2)}, u32[]{:S(2)}) collective-permute-start(f32[2,2,1,16,512]{4,3,2,1,0:T(8,128)S(1)} %fusion.18), channel_id=1, source_target_pairs={{0,1},{1,0},{2,3},{3,2},{4,5},{5,4},{6,7},{7,6},{8,9},{9,8},{10,11... | collective-permute-start | bytes 393224 | tf_op jit(solution)/shard_map/ppermute | solution.py:15
  218.5 10.6 %collective-permute-start.21 = (bf16[2,512,256]{2,1,0:T(8,128)(2,1)S(1)}, bf16[2,512,256]{2,1,0:T(8,128)(2,1)S(1)}, u32[]{:S(2)}, u32[]{:S(2)}) collective-permute-start(bf16[2,512,256]{2,1,0:T(8,128)(2,1)S(1)} %fusion.11), channel_id=1, source_target_pairs={{0,4},{2,6},{4,0},{6,2},{8,12},{10,14},{12,8},{14,10},{1,5},{3,7},... | collective-permute-start | bytes 1572872 | tf_op jit(solution)/shard_map/ppermute | solution.py:15
  222.0 4.2 %collective-permute-start.23 = (bf16[51,512]{1,0:T(8,128)(2,1)S(1)}, bf16[51,512]{1,0:T(8,128)(2,1)S(1)}, u32[]{:S(2)}, u32[]{:S(2)}) collective-permute-start(bf16[51,512]{1,0:T(8,128)(2,1)S(1)} %pad_maximum_fusion.6), channel_id=1, source_target_pairs={{0,1},{1,0},{2,3},{3,2},{4,5},{5,4},{6,7},{7,6},{8,9},{9,8},{10,11... | collective-permute-start | bytes 156680 | tf_op jit(solution)/shard_map/ppermute | solution.py:15
  229.1 0.9 copy-start.21
  230.0 5.8 %collective-permute-start.25 = (bf16[99,512]{1,0:T(8,128)(2,1)S(1)}, bf16[99,512]{1,0:T(8,128)(2,1)S(1)}, u32[]{:S(2)}, u32[]{:S(2)}) collective-permute-start(bf16[99,512]{1,0:T(8,128)(2,1)S(1)} %pad_maximum_fusion.5), channel_id=1, source_target_pairs={{0,8},{2,10},{4,12},{6,14},{8,0},{10,2},{12,4},{14,6},{1,9},{3,11}... | collective-permute-start | bytes 304136 | tf_op jit(solution)/shard_map/ppermute | solution.py:15
  235.9 5.8 %collective-permute-start.26 = (bf16[195,512]{1,0:T(8,128)(2,1)S(1)}, bf16[195,512]{1,0:T(8,128)(2,1)S(1)}, u32[]{:S(2)}, u32[]{:S(2)}) collective-permute-start(bf16[195,512]{1,0:T(8,128)(2,1)S(1)} %pad_maximum_fusion.4), channel_id=1, source_target_pairs={{0,4},{2,6},{4,0},{6,2},{8,12},{10,14},{12,8},{14,10},{1,5},{3,7},... | collective-permute-start | bytes 599048 | tf_op jit(solution)/shard_map/ppermute | solution.py:15
  242.7 8.1 %collective-permute-start.27 = (bf16[387,512]{1,0:T(8,128)(2,1)}, bf16[387,512]{1,0:T(8,128)(2,1)S(1)}, u32[]{:S(2)}, u32[]{:S(2)}) collective-permute-start(bf16[387,512]{1,0:T(8,128)(2,1)} %pad_maximum_fusion.3), channel_id=1, source_target_pairs={{0,16},{16,0},{1,17},{17,1},{2,18},{18,2},{3,19},{19,3},{4,20},{20... | collective-permute-start | bytes 1188872 | tf_op jit(solution)/shard_map/ppermute | solution.py:15
  250.8 0.7 copy-start.23
  251.8 28.7 %copy-start.22 = (bf16[2,512,256]{2,1,0:T(8,128)(2,1)S(1)}, bf16[2,512,256]{2,1,0:T(8,128)(2,1)}, u32[]{:S(2)}) copy-start(bf16[2,512,256]{2,1,0:T(8,128)(2,1)} %copy-done.21) | copy-start | bytes 1572868
  253.5 28.1 %collective-permute-start.28 = (bf16[771,512]{1,0:T(8,128)(2,1)}, bf16[771,512]{1,0:T(8,128)(2,1)}, u32[]{:S(2)}, u32[]{:S(2)}) collective-permute-start(bf16[771,512]{1,0:T(8,128)(2,1)} %pad_maximum_fusion.2), channel_id=1, source_target_pairs={{0,2},{2,0},{4,6},{6,4},{8,10},{10,8},{12,14},{14,12},{1,3},{3,1},... | collective-permute-start | bytes 2368520 | tf_op jit(solution)/shard_map/ppermute | solution.py:15
  253.5 21.6 %collective-permute-start.19 = (bf16[1,512,256]{2,1,0:T(8,128)(2,1)}, bf16[1,512,256]{2,1,0:T(8,128)(2,1)}, u32[]{:S(2)}, u32[]{:S(2)}) collective-permute-start(bf16[1,512,256]{2,1,0:T(8,128)(2,1)} %fusion.15), channel_id=1, source_target_pairs={{0,8},{2,10},{4,12},{6,14},{8,0},{10,2},{12,4},{14,6},{1,9},{3,11}... | collective-permute-start | bytes 786440 | tf_op jit(solution)/shard_map/ppermute | solution.py:15
  256.3 24.1 %collective-permute-start.24 = (bf16[1,512,256]{2,1,0:T(8,128)(2,1)}, bf16[1,512,256]{2,1,0:T(8,128)(2,1)}, u32[]{:S(2)}, u32[]{:S(2)}) collective-permute-start(bf16[1,512,256]{2,1,0:T(8,128)(2,1)} %fusion.16), channel_id=1, source_target_pairs={{0,8},{2,10},{4,12},{6,14},{8,0},{10,2},{12,4},{14,6},{1,9},{3,11}... | collective-permute-start | bytes 786440 | tf_op jit(solution)/shard_map/ppermute | solution.py:15
  285.0 1.5 copy-start.18

commit v6 on v5

--- a/solution.py
+++ b/solution.py
@@ -181,17 +181,32 @@
     )(place, weight, inverse, mask, factor, *extra)
 
 
-def fetch_factor(own):
+def fetch_factor(panel, cols, row, col, *deps):
     n_row, n_col = lax.axis_size("row"), lax.axis_size("col")
-    if n_row == 2:
-        return swap_row(own, 1)
-    ratio = n_col // n_row
-    got = own
-    for d in range(1, n_row):
-        pairs = [((j // ratio) * n_col + j, ((j // ratio + d) % n_row) * n_col + j) for j in range(n_col)]
-        arrived = lax.ppermute(own, ("row", "col"), pairs)
-        got = arrived if d == 1 else got + arrived
-    return got
+    zs, ratio, width = n_col // CORES, n_col // n_row, panel.shape[1]
+
+    def mirror(j):
+        return (zs - 1 - j // CORES) * CORES + j % CORES
+
+    def cross(x, place):
+        got = None
+        for d in range(1, n_row):
+            pairs = []
+            for j in range(n_col):
+                owner = j // ratio
+                pairs.append((owner * n_col + place(j), (owner + d) % n_row * n_col + place(j)))
+            arrived = lax.ppermute(x, ("row", "col"), pairs)
+            got = arrived if got is None else got + arrived
+        return x if got is None else got
+
+    far = cols // 4 if n_row == 2 and zs > 1 else 0
+    own = lax.dynamic_slice(panel, (col % ratio * cols, 0), (cols, width))
+    got = [cross(after(own[:cols - far], *deps), lambda j: j)]
+    if far > 0:
+        other = lax.dynamic_slice(panel, (mirror(col) % ratio * cols + cols - far, 0), (far, width))
+        crossed = cross(after(other, *deps), mirror)
+        got.append(lax.ppermute(crossed, "col", [(j, mirror(j)) for j in range(n_col)]))
+    return own, got
 
 
 def body(inv_block, block_masks, panel_first, panel_second, diag_inverse, weights):
@@ -213,9 +228,9 @@
     mine = row == col // ratio
     own, got = [], []
     for panel in panels:
-        piece = lax.dynamic_slice(panel, (col % ratio * cols, 0), (cols, width))
-        own.append(piece)
-        got.append(fetch_factor(after(piece, *got)))
+        mine_rows, others = fetch_factor(panel, cols, row, col, *(got[-1] if got else ()))
+        own.append(mine_rows)
+        got.append(others)
 
     masks = []
     for k in range(2):
@@ -229,7 +244,7 @@
     token = tuple(masks)
     units, terms = [], []
     for k in range(2):
-        factor = jnp.where(mine, own[k], after(got[k], *token))
+        factor = jnp.where(mine, own[k], after(jnp.concatenate(got[k]), *token))
         received, arrived = {}, [[] for _ in range(PIECES[k])]
         for d in dests:
             away = product(inverse, masks[k], factor, place(1 - core, d, *token), weights, sizes)
@@ -258,17 +273,19 @@
     split = (2, n_row, zs, CORES, n_pole, each, width)
     term = halve(jnp.stack(terms).reshape(split), 3, core, swap_core, jnp.bfloat16)
     term = after(term, early.step(*token))
+    if not zero.done():
+        term = after(term, zero.step())
     term = halve(term, 1, row, swap_row, jnp.bfloat16)
+    term = after(term, last.step(term))
+    term = halve(term, 1, z, swap_z, jnp.bfloat16)
     while not zero.done():
-        term = after(term, zero.step())
-    term = halve(term, 1, z, swap_z, jnp.bfloat16)
+        term = after(term, zero.step(term))
     while not early.done():
         term = after(term, early.step(term))
     first = zero.result(term)
     squares = jnp.sum(first * first, axis=0)
-    term = after(term, squares, last.step(term))
     base = pick(pick(pick(diag_inverse.reshape(split), core, 3), row, 1), z, 1).astype(jnp.float32) * weight
-    both = halve(jnp.stack([base, term]), 2, pole, swap_pole, jnp.float32)
+    both = halve(jnp.stack([base, after(term, squares)]), 2, pole, swap_pole, jnp.float32)
     base, term = both[0], both[1]
     piece = jnp.stack([base[0] + term[0], base[1], term[1]]).astype(jnp.bfloat16)
     piece = piece[:, None, None, None, None]
@@ -276,17 +293,17 @@
         piece, squares = double(piece, squares, 4, pole, bit, swap_pole)
     while not last.done():
         piece = after(piece, last.step(piece))
+    piece, second = lax.optimization_barrier((piece, early.result(piece)))
     for bit in reversed(range(zs.bit_length() - 1)):
         piece, squares = double(piece, squares, 2, z, bit, swap_z)
+    piece, *second = lax.optimization_barrier((piece, second, last.result(piece)))
     for bit in reversed(range(n_row.bit_length() - 1)):
         piece, squares = double(piece, squares, 1, row, bit, swap_row)
-    second = jnp.concatenate([early.result(), last.result()], axis=1)
-    piece = after(piece, second)
     piece, squares = double(piece, squares, 3, core, 0, swap_core)
     scale = jnp.sqrt(squares / (rows * n_row) + 1e-06)
     piece = piece.reshape(3, width, width).astype(jnp.float32)
     scaled = piece[1] + piece[2] / (scale[:, None] * scale)
-    second = second / scale
+    second = jnp.concatenate(second, axis=1) / scale
     return jnp.stack([first.astype(jnp.bfloat16), second.astype(jnp.bfloat16)]), jnp.stack([piece[0], scaled])
 
 

time: 289 us -> 290 us (level)
  waiting for transfers between devices: 133 us -> 111 us
  starting transfers between devices: 31.2 us -> 49.1 us
  other arithmetic: 30.4 us -> 34.7 us
  local copies, waits for them, and re-layouts: 17.1 us -> 20.8 us
    ppermute x26 -> x24, waiting for transfers between devices: 129 us -> 84.7 us  [swap(): return lax.ppermute(x, axis, [(i, i ^ mask) for i in range(size)])]
    ppermute x0 -> x6, waiting for transfers between devices: none -> 26.5 us  [the longest x4 18.7 us: cross(): arrived = lax.ppermute(x, ('row', 'col'), pairs)]
    ppermute x0 -> x6, starting transfers between devices: none -> 16.5 us  [the longest x4 14.1 us: cross(): arrived = lax.ppermute(x, ('row', 'col'), pairs)]
    slice x0 -> x2, local copies, waits for them, and re-layouts: none -> 5.39 us  [fetch_factor(): got = [cross(after(own[:cols - far], *deps), lambda j: j)]]
    ppermute x3, waiting for transfers between devices: 4.28 us -> 0.01 us  [body(): lax.ppermute(after(x, *before), 'pole', [(i, (i + d) % n_pole) for i in r...]
    dynamic_slice x2, local copies, waits for them, and re-layouts: 6.15 us -> 2.16 us  [fetch_factor(): lax.dynamic_slice(panel, (mirror(col) % ratio * cols + cols - far, 0), (f...]
    ppermute x26 -> x24, starting transfers between devices: 26.7 us -> 28.9 us  [swap(): return lax.ppermute(x, axis, [(i, i ^ mask) for i in range(size)])]
    unnamed x50 -> x38, local copies, waits for them, and re-layouts: 7.95 us -> 9.3 us
  transfers between devices with their start and end apart: 29 -> 33, of which waited for: 16 -> 15; matrix products, arithmetic and copies ran while one was open for 9% -> 11% of each run, Pallas kernels for 26% -> 25%
where the time goes in v6:
time: 290 us; the launch traced here: 289 us
  waiting for transfers between devices  111 us (38%)
  Pallas kernels  71.1 us (25%)
  starting transfers between devices  49.1 us (17%)
  other arithmetic  34.7 us (12%)
  local copies, waits for them, and re-layouts  20.8 us (7%)
    ppermute x24, waiting for transfers between devices, swap(): return lax.ppermute(x, axis, [(i, i ^ mask) for i in range(size)])  84.7 us
    pallas_call x8, Pallas kernels, product(): pl.pallas_call(kernel, out_shape=out_shape, grid_spec=pltpu.PrefetchScala...  71.1 us
    ppermute x24, starting transfers between devices, swap(): return lax.ppermute(x, axis, [(i, i ^ mask) for i in range(size)])  28.9 us
    ppermute x4, waiting for transfers between devices, cross(): arrived = lax.ppermute(x, ('row', 'col'), pairs)  18.7 us
    ppermute x4, starting transfers between devices, cross(): arrived = lax.ppermute(x, ('row', 'col'), pairs)  14.1 us
    convert_element_type x6, other arithmetic, step(): send = self.part(1, *deps).astype(jnp.bfloat16)  11.9 us
    unnamed x38, local copies, waits for them, and re-layouts  9.3 us
    ppermute x2, waiting for transfers between devices, fetch_factor(): lax.ppermute(crossed, 'col', [(j, mirror(j)) for j in range(n_col)])  7.81 us
  transfers between devices with their start and end apart: 33, of which 15 were waited for; matrix products, arithmetic and copies ran while one was open for 11% of the time, Pallas kernels for 25%

profile of v6, /device:TPU:0, one launch (start us, length us, event | category | flops | bytes accessed | tf_op | source)
XLA Modules:
  0.0 288.8 jit_solution(5332380929194286999)
XLA Ops:
  0.7 2.7 dynamic-slice_bitcast_fusion.1
  3.3 4.9 %collective-permute-start = (bf16[1536,512]{1,0:T(8,128)(2,1)}, bf16[1536,512]{1,0:T(8,128)(2,1)S(1)}, u32[]{:S(2)}, u32[]{:S(2)}) collective-permute-start(bf16[1536,512]{1,0:T(8,128)(2,1)} %dynamic-slice_bitcast_fusion.1), channel_id=1, source_target_pairs={{0,16},{2,18},{4,20},{6,22},{24,8},{26,10},{28,12},{30,14},{1,17},... | collective-permute-start | bytes 4718600 | tf_op jit(solution)/shard_map/ppermute | solution.py:198
  8.3 1.1 dynamic-slice_bitcast_fusion.3
  9.4 1.3 collective-permute-start.1
  10.7 14.1 %collective-permute-done.1 = bf16[512,512]{1,0:T(8,128)(2,1)} collective-permute-done((bf16[512,512]{1,0:T(8,128)(2,1)S(1)}, bf16[512,512]{1,0:T(8,128)(2,1)}, u32[]{:S(2)}, u32[]{:S(2)}) %collective-permute-start.1) | collective-permute-done | bytes 524320 | tf_op jit(solution)/shard_map/ppermute | solution.py:198
  24.8 1.6 collective-permute-start.2
  27.8 1.1 dynamic-slice_bitcast_fusion.2
  28.9 2.7 dynamic-slice_bitcast_fusion
  31.7 7.8 %collective-permute-done.2 = bf16[512,512]{1,0:T(8,128)(2,1)} collective-permute-done((bf16[512,512]{1,0:T(8,128)(2,1)}, bf16[512,512]{1,0:T(8,128)(2,1)}, u32[]{:S(2)}, u32[]{:S(2)}) %collective-permute-start.2) | collective-permute-done | bytes 524320 | tf_op jit(solution)/shard_map/ppermute | solution.py:208
  39.5 2.6 collective-permute-done
  42.1 1.2 pad_maximum_fusion
  43.3 1.3 collective-permute-start.8
  44.6 2.2 bitcast_select_fusion.1.f_ref
  46.8 8.4 %shard_map.77 = (bf16[2048,256]{1,0:T(8,128)(2,1)}, bf16[2048,256]{1,0:T(8,128)(2,1)S(1)}) custom-call(s32[2]{0:T(128)S(1)} %pad_add_fusion.3.where_ref, f32[1]{0:T(128)} %copy.127.weight_ref, bf16[8192,2048]{1,0:T(8,128)(2,1)} %bitcast.159, bf16[16,4,2048]{2,1,0:T(4,128)(2,1)S(1)} %reshape_reshape.52.mask_ref, bf16[2048,512]{1,0:T(8,128)(2,1)S(1)} %bitcast_select_fusion.1.f_ref), custom_call_target="tpu_custom_call" | custom-call | flops 8388608 | bytes 1048576 | tf_op jit(solution)/shard_map/pallas_call | solution.py:171
  55.2 1.0 copy-done.13
  56.2 6.6 %collective-permute-start.7 = (bf16[1536,512]{1,0:T(8,128)(2,1)}, bf16[1536,512]{1,0:T(8,128)(2,1)}, u32[]{:S(2)}, u32[]{:S(2)}) collective-permute-start(bf16[1536,512]{1,0:T(8,128)(2,1)} %dynamic-slice_bitcast_fusion), channel_id=1, source_target_pairs={{0,16},{2,18},{4,20},{6,22},{24,8},{26,10},{28,12},{30,14},{1,17},... | collective-permute-start | bytes 4718600 | tf_op jit(solution)/shard_map/ppermute | solution.py:198
  63.1 7.6 %shard_map.78 = (bf16[2048,256]{1,0:T(8,128)(2,1)S(1)}, bf16[2048,256]{1,0:T(8,128)(2,1)S(1)}) custom-call(s32[2]{0:T(128)S(1)} %get-tuple-element.84.where_ref, f32[1]{0:T(128)} %copy.127.weight_ref, bf16[8192,2048]{1,0:T(8,128)(2,1)} %bitcast.160, bf16[16,4,2048]{2,1,0:T(4,128)(2,1)S(1)} %reshape_reshape.52.mask_ref, ...), custom_call_target="tpu_custom_call" | custom-call | flops 8388608 | bytes 1048576 | tf_op jit(solution)/shard_map/pallas_call | solution.py:171
  72.3 10.3 %shard_map.79 = (bf16[2048,512]{1,0:T(8,128)(2,1)}, f32[512,512]{1,0:T(8,128)S(1)}) custom-call(s32[2]{0:T(128)S(1)} %get-tuple-element.86.where_ref, f32[1]{0:T(128)} %copy.127.weight_ref, bf16[8192,2048]{1,0:T(8,128)(2,1)} %bitcast.161, bf16[16,4,2048]{2,1,0:T(4,128)(2,1)S(1)} %reshape_reshape.52.mask_ref, ...), custom_call_target="tpu_custom_call" | custom-call | flops 8388608 | bytes 1048576 | tf_op jit(solution)/shard_map/pallas_call | solution.py:171
  82.6 1.5 collective-permute-start.12
  84.1 9.1 %shard_map.80 = (f32[2048,512]{1,0:T(8,128)S(1)}, f32[512,512]{1,0:T(8,128)S(1)}) custom-call(s32[2]{0:T(128)S(1)} %pad_add_fusion.1.where_ref, f32[1]{0:T(128)} %copy.127.weight_ref, bf16[8192,2048]{1,0:T(8,128)(2,1)} %bitcast.162, bf16[16,4,2048]{2,1,0:T(4,128)(2,1)S(1)} %reshape_reshape.52.mask_ref, bf16[2048,512]{1,0:T(8,128)(2,1)S(1)} %bitcast_select_fusion.1.f_ref, ...), custom_call_target="tpu_custom_call" | custom-call | flops 8388608 | bytes 1048576 | tf_op jit(solution)/shard_map/pallas_call | solution.py:171
  94.2 2.0 collective-permute-done.7
  96.2 1.5 pad_maximum_fusion.1
  97.7 2.2 bitcast_select_fusion.f_ref
  100.0 7.6 %shard_map.81 = (bf16[2048,256]{1,0:T(8,128)(2,1)S(1)}, bf16[2048,256]{1,0:T(8,128)(2,1)S(1)}) custom-call(s32[2]{0:T(128)S(1)} %pad_add_fusion.3.where_ref, f32[1]{0:T(128)} %copy.127.weight_ref, bf16[8192,2048]{1,0:T(8,128)(2,1)} %bitcast.163, bf16[16,4,2048]{2,1,0:T(4,128)(2,1)S(1)} %reshape_reshape.53.mask_ref, ...), custom_call_target="tpu_custom_call" | custom-call | flops 8388608 | bytes 1048576 | tf_op jit(solution)/shard_map/pallas_call | solution.py:171
  108.2 8.7 %shard_map.82 = (bf16[2048,256]{1,0:T(8,128)(2,1)}, bf16[2048,256]{1,0:T(8,128)(2,1)}) custom-call(s32[2]{0:T(128)S(1)} %get-tuple-element.84.where_ref, f32[1]{0:T(128)} %copy.127.weight_ref, bf16[8192,2048]{1,0:T(8,128)(2,1)} %bitcast.164, bf16[16,4,2048]{2,1,0:T(4,128)(2,1)S(1)} %reshape_reshape.53.mask_ref, bf16[2048,512]{1,0:T(8,128)(2,1)S(1)} %bitcast_select_fusion.f_ref), custom_call_target="tpu_custom_call" | custom-call | flops 8388608 | bytes 1048576 | tf_op jit(solution)/shard_map/pallas_call | solution.py:171
  117.4 9.8 %shard_map.83 = (bf16[2048,256]{1,0:T(8,128)(2,1)}, bf16[2048,256]{1,0:T(8,128)(2,1)S(1)}, f32[512,512]{1,0:T(8,128)S(1)}) custom-call(s32[2]{0:T(128)S(1)} %get-tuple-element.86.where_ref, f32[1]{0:T(128)} %copy.127.weight_ref, bf16[8192,2048]{1,0:T(8,128)(2,1)} %bitcast.165, bf16[16,4,2048]{2,1,0:T(4,128)(2,1)S(1)} %reshape_reshape.53.mask_ref, ...), custom_call_target="tpu_custom_call" | custom-call | flops 8388608 | bytes 1048576 | tf_op jit(solution)/shard_map/pallas_call | solution.py:171
  128.2 1.0 copy-done.12
  129.2 1.5 collective-permute-start.16
  130.7 3.3 %fusion.2 = bf16[2,512,512]{2,1,0:T(8,128)(2,1)} fusion(f32[2,2,512,512]{3,2,1,0:T(8,128)} %bitcast.146, s32[]{:T(128)S(6)} %select_n.289, bf16[2,2,512,512]{3,2,1,0:T(8,128)(2,1)} %bitcast.18), kind=kLoop, calls=%fused_computation.15 | loop fusion | flops 1572864 | bytes 4194308 | tf_op jit(solution)/shard_map/convert_element_type | solution.py:93
  133.9 1.0 copy-done.8
  134.9 1.2 copy-done.9
  136.1 9.5 %shard_map.84 = (f32[2048,256]{1,0:T(8,128)S(1)}, f32[2048,256]{1,0:T(8,128)S(1)}, f32[512,512]{1,0:T(8,128)S(1)}) custom-call(s32[2]{0:T(128)S(1)} %pad_add_fusion.1.where_ref, f32[1]{0:T(128)} %copy.127.weight_ref, bf16[8192,2048]{1,0:T(8,128)(2,1)} %bitcast.166, bf16[16,4,2048]{2,1,0:T(4,128)(2,1)S(1)} %reshape_reshape.53.mask_ref, ...), custom_call_target="tpu_custom_call" | custom-call | flops 8388608 | bytes 1048576 | tf_op jit(solution)/shard_map/pallas_call | solution.py:171
  145.6 1.4 copy-done.6
  148.9 8.3 %collective-permute-start.17 = (bf16[2,512,512]{2,1,0:T(8,128)(2,1)}, bf16[2,512,512]{2,1,0:T(8,128)(2,1)}, u32[]{:S(2)}, u32[]{:S(2)}) collective-permute-start(bf16[2,512,512]{2,1,0:T(8,128)(2,1)} %fusion.2), channel_id=1, source_target_pairs={{0,4},{2,6},{4,0},{6,2},{8,12},{10,14},{12,8},{14,10},{1,5},{3,7},... | collective-permute-start | bytes 3145736 | tf_op jit(solution)/shard_map/ppermute | solution.py:15
  157.9 1.4 fusion.7
  159.3 2.4 fusion.10
  161.7 19.6 %collective-permute-done.17 = bf16[2,512,512]{2,1,0:T(8,128)(2,1)} collective-permute-done((bf16[2,512,512]{2,1,0:T(8,128)(2,1)}, bf16[2,512,512]{2,1,0:T(8,128)(2,1)}, u32[]{:S(2)}, u32[]{:S(2)}) %collective-permute-start.17) | collective-permute-done | bytes 1048608 | tf_op jit(solution)/shard_map/ppermute | solution.py:15
  181.3 2.7 fusion.9
  184.0 2.5 collective-permute-start.18
  186.5 6.3 %collective-permute-done.18 = bf16[2,1,4,2,16,512]{5,4,3,2,0,1:T(8,128)(2,1)S(1)} collective-permute-done((bf16[2,1,4,2,16,512]{5,4,3,2,0,1:T(8,128)(2,1)S(1)}, bf16[2,1,4,2,16,512]{5,4,3,2,0,1:T(8,128)(2,1)S(1)}, u32[]{:S(2)}, u32[]{:S(2)}) %collective-permute-start.18) | collective-permute-done | bytes 262176 | tf_op jit(solution)/shard_map/ppermute | solution.py:15
  192.9 1.1 add_bitcast_fusion.2
  194.0 1.2 fusion.11
  195.2 1.6 collective-permute-start.20
  197.3 2.8 collective-permute-start.23
  200.1 13.5 %collective-permute-done.20 = bf16[2,2,2,16,512]{4,3,2,1,0:T(8,128)(2,1)S(1)} collective-permute-done((bf16[2,2,2,16,512]{4,3,2,1,0:T(8,128)(2,1)S(1)}, bf16[2,2,2,16,512]{4,3,2,1,0:T(8,128)(2,1)S(1)}, u32[]{:S(2)}, u32[]{:S(2)}) %collective-permute-start.20) | collective-permute-done | bytes 131104 | tf_op jit(solution)/shard_map/ppermute | solution.py:15
  215.3 2.7 collective-permute-start.26
  218.0 6.7 %collective-permute-done.21 = bf16[2,1,2,16,512]{4,3,2,1,0:T(8,128)(2,1)S(1)} collective-permute-done((bf16[2,1,2,16,512]{4,3,2,1,0:T(8,128)(2,1)S(1)}, bf16[2,1,2,16,512]{4,3,2,1,0:T(8,128)(2,1)S(1)}, u32[]{:S(2)}, u32[]{:S(2)}) %collective-permute-start.21) | collective-permute-done | bytes 65568 | tf_op jit(solution)/shard_map/ppermute | solution.py:15
  225.6 1.2 fusion.13
  226.8 2.6 collective-permute-start.27
  229.4 1.9 convert_bitcast_fusion
  231.9 4.5 %collective-permute-done.24 = f32[2,2,1,16,512]{4,3,2,1,0:T(8,128)S(1)} collective-permute-done((f32[2,2,1,16,512]{4,3,2,1,0:T(8,128)S(1)}, f32[2,2,1,16,512]{4,3,2,1,0:T(8,128)S(1)}, u32[]{:S(2)}, u32[]{:S(2)}) %collective-permute-start.24) | collective-permute-done | bytes 131104 | tf_op jit(solution)/shard_map/ppermute | solution.py:15
  237.0 3.7 %collective-permute-done.25 = bf16[51,512]{1,0:T(8,128)(2,1)S(1)} collective-permute-done((bf16[51,512]{1,0:T(8,128)(2,1)S(1)}, bf16[51,512]{1,0:T(8,128)(2,1)S(1)}, u32[]{:S(2)}, u32[]{:S(2)}) %collective-permute-start.25) | collective-permute-done | bytes 52256 | tf_op jit(solution)/shard_map/ppermute | solution.py:15
  240.8 1.2 fusion.14
  242.1 1.3 add_bitcast_fusion.1
  244.9 2.0 collective-permute-start.30
  246.9 9.9 %collective-permute-done.28 = bf16[99,512]{1,0:T(8,128)(2,1)} collective-permute-done((bf16[99,512]{1,0:T(8,128)(2,1)}, bf16[99,512]{1,0:T(8,128)(2,1)}, u32[]{:S(2)}, u32[]{:S(2)}) %collective-permute-start.28) | collective-permute-done | bytes 101408 | tf_op jit(solution)/shard_map/ppermute | solution.py:15
  258.7 7.5 %collective-permute-done.29 = bf16[195,512]{1,0:T(8,128)(2,1)S(1)} collective-permute-done((bf16[195,512]{1,0:T(8,128)(2,1)S(1)}, bf16[195,512]{1,0:T(8,128)(2,1)S(1)}, u32[]{:S(2)}, u32[]{:S(2)}) %collective-permute-start.29) | collective-permute-done | bytes 199712 | tf_op jit(solution)/shard_map/ppermute | solution.py:15
  266.3 1.9 add_bitcast_fusion
  268.2 1.0 collective-permute-start.31
  269.2 9.9 %collective-permute-done.31 = bf16[387,512]{1,0:T(8,128)(2,1)S(1)} collective-permute-done((bf16[387,512]{1,0:T(8,128)(2,1)S(1)}, bf16[387,512]{1,0:T(8,128)(2,1)S(1)}, u32[]{:S(2)}, u32[]{:S(2)}) %collective-permute-start.31) | collective-permute-done | bytes 396320 | tf_op jit(solution)/shard_map/ppermute | solution.py:15
  279.6 2.3 collective-permute-done.32
  282.6 1.2 slice.139
  286.2 1.5 pad_maximum_fusion.2
  287.7 1.1 pad_maximum_fusion.3
  (134 shorter events, 19.9 us)
Async XLA Ops:
  0.6 10.0 %copy-start.18 = (s32[2,64,16]{1,2,0:T(8,128)S(1)}, s32[2,64,16]{1,2,0:T(8,128)}, u32[]{:S(2)}) copy-start(s32[2,64,16]{1,2,0:T(8,128)} %param.7) | copy-start | bytes 24580
  3.3 38.8 %collective-permute-start = (bf16[1536,512]{1,0:T(8,128)(2,1)}, bf16[1536,512]{1,0:T(8,128)(2,1)S(1)}, u32[]{:S(2)}, u32[]{:S(2)}) collective-permute-start(bf16[1536,512]{1,0:T(8,128)(2,1)} %dynamic-slice_bitcast_fusion.1), channel_id=1, source_target_pairs={{0,16},{2,18},{4,20},{6,22},{24,8},{26,10},{28,12},{30,14},{1,17},... | collective-permute-start | bytes 4718600 | tf_op jit(solution)/shard_map/ppermute | solution.py:198
  9.4 15.4 %collective-permute-start.1 = (bf16[512,512]{1,0:T(8,128)(2,1)S(1)}, bf16[512,512]{1,0:T(8,128)(2,1)}, u32[]{:S(2)}, u32[]{:S(2)}) collective-permute-start(bf16[512,512]{1,0:T(8,128)(2,1)S(1)} %dynamic-slice_bitcast_fusion.3), channel_id=1, source_target_pairs={{12,28},{14,30},{8,24},{10,26},{20,4},{22,6},{16,0},{18,2},{13,29}... | collective-permute-start | bytes 1572872 | tf_op jit(solution)/shard_map/ppermute | solution.py:198
  24.8 14.7 %collective-permute-start.2 = (bf16[512,512]{1,0:T(8,128)(2,1)}, bf16[512,512]{1,0:T(8,128)(2,1)}, u32[]{:S(2)}, u32[]{:S(2)}) collective-permute-start(bf16[512,512]{1,0:T(8,128)(2,1)} %collective-permute-done.1), channel_id=1, source_target_pairs={{0,12},{2,14},{4,8},{6,10},{8,4},{10,6},{12,0},{14,2},{1,13},{3,15... | collective-permute-start | bytes 1572872 | tf_op jit(solution)/shard_map/ppermute | solution.py:208
  43.3 27.7 %collective-permute-start.8 = (bf16[512,512]{1,0:T(8,128)(2,1)S(1)}, bf16[512,512]{1,0:T(8,128)(2,1)}, u32[]{:S(2)}, u32[]{:S(2)}) collective-permute-start(bf16[512,512]{1,0:T(8,128)(2,1)S(1)} %dynamic-slice_bitcast_fusion.2), channel_id=1, source_target_pairs={{12,28},{14,30},{8,24},{10,26},{20,4},{22,6},{16,0},{18,2},{13,29}... | collective-permute-start | bytes 1572872 | tf_op jit(solution)/shard_map/ppermute | solution.py:198
  55.2 1.0 copy-start.13
  56.2 15.1 %collective-permute-start.3 = (bf16[2048,256]{1,0:T(8,128)(2,1)}, bf16[2048,256]{1,0:T(8,128)(2,1)}, u32[]{:S(2)}, u32[]{:S(2)}) collective-permute-start(bf16[2048,256]{1,0:T(8,128)(2,1)} %get-tuple-element.68), channel_id=1, source_target_pairs={{0,2},{2,0},{4,6},{6,4},{8,10},{10,8},{12,14},{14,12},{1,3},{3,1},... | collective-permute-start | bytes 3145736 | tf_op jit(solution)/shard_map/ppermute | solution.py:15
  56.2 40.0 %collective-permute-start.7 = (bf16[1536,512]{1,0:T(8,128)(2,1)}, bf16[1536,512]{1,0:T(8,128)(2,1)}, u32[]{:S(2)}, u32[]{:S(2)}) collective-permute-start(bf16[1536,512]{1,0:T(8,128)(2,1)} %dynamic-slice_bitcast_fusion), channel_id=1, source_target_pairs={{0,16},{2,18},{4,20},{6,22},{24,8},{26,10},{28,12},{30,14},{1,17},... | collective-permute-start | bytes 4718600 | tf_op jit(solution)/shard_map/ppermute | solution.py:198
  62.8 9.4 %collective-permute-start.4 = (bf16[2048,256]{1,0:T(8,128)(2,1)}, bf16[2048,256]{1,0:T(8,128)(2,1)S(1)}, u32[]{:S(2)}, u32[]{:S(2)}) collective-permute-start(bf16[2048,256]{1,0:T(8,128)(2,1)} %copy-done.13), channel_id=1, source_target_pairs={{0,2},{2,0},{4,6},{6,4},{8,10},{10,8},{12,14},{14,12},{1,3},{3,1},... | collective-permute-start | bytes 3145736 | tf_op jit(solution)/shard_map/ppermute | solution.py:15
  70.7 13.4 %collective-permute-start.5 = (bf16[2048,256]{1,0:T(8,128)(2,1)S(1)}, bf16[2048,256]{1,0:T(8,128)(2,1)S(1)}, u32[]{:S(2)}, u32[]{:S(2)}) collective-permute-start(bf16[2048,256]{1,0:T(8,128)(2,1)S(1)} %get-tuple-element.70), channel_id=1, source_target_pairs={{0,2},{2,0},{4,6},{6,4},{8,10},{10,8},{12,14},{14,12},{1,3},{3,1},... | collective-permute-start | bytes 3145736 | tf_op jit(solution)/shard_map/ppermute | solution.py:15
  71.0 13.1 %collective-permute-start.6 = (bf16[2048,256]{1,0:T(8,128)(2,1)S(1)}, bf16[2048,256]{1,0:T(8,128)(2,1)S(1)}, u32[]{:S(2)}, u32[]{:S(2)}) collective-permute-start(bf16[2048,256]{1,0:T(8,128)(2,1)S(1)} %get-tuple-element.76), channel_id=1, source_target_pairs={{0,2},{2,0},{4,6},{6,4},{8,10},{10,8},{12,14},{14,12},{1,3},{3,1},... | collective-permute-start | bytes 3145736 | tf_op jit(solution)/shard_map/ppermute | solution.py:15
  71.3 23.0 %collective-permute-start.9 = (bf16[512,512]{1,0:T(8,128)(2,1)}, bf16[512,512]{1,0:T(8,128)(2,1)S(1)}, u32[]{:S(2)}, u32[]{:S(2)}) collective-permute-start(bf16[512,512]{1,0:T(8,128)(2,1)} %collective-permute-done.8), channel_id=1, source_target_pairs={{0,12},{2,14},{4,8},{6,10},{8,4},{10,6},{12,0},{14,2},{1,13},{3,15... | collective-permute-start | bytes 1572872 | tf_op jit(solution)/shard_map/ppermute | solution.py:208
  82.6 48.1 %collective-permute-start.12 = (bf16[2048,512]{1,0:T(8,128)(2,1)}, bf16[2048,512]{1,0:T(8,128)(2,1)}, u32[]{:S(2)}, u32[]{:S(2)}) collective-permute-start(bf16[2048,512]{1,0:T(8,128)(2,1)} %get-tuple-element.73), channel_id=1, source_target_pairs={{0,1},{1,0},{2,3},{3,2},{4,5},{5,4},{6,7},{7,6},{8,9},{9,8},{10,11... | collective-permute-start | bytes 6291464 | tf_op jit(solution)/shard_map/ppermute | solution.py:264
  93.2 1.0 copy-start.1
  94.2 3.5 %copy-start = (f32[2048,512]{1,0:T(8,128)}, f32[2048,512]{1,0:T(8,128)S(1)}, u32[]{:S(2)}) copy-start(f32[2048,512]{1,0:T(8,128)S(1)} %get-tuple-element.77) | copy-start | bytes 12582916
  107.6 9.8 %collective-permute-start.10 = (bf16[2048,256]{1,0:T(8,128)(2,1)S(1)}, bf16[2048,256]{1,0:T(8,128)(2,1)S(1)}, u32[]{:S(2)}, u32[]{:S(2)}) collective-permute-start(bf16[2048,256]{1,0:T(8,128)(2,1)S(1)} %get-tuple-element.83), channel_id=1, source_target_pairs={{0,2},{2,0},{4,6},{6,4},{8,10},{10,8},{12,14},{14,12},{1,3},{3,1},... | collective-permute-start | bytes 3145736 | tf_op jit(solution)/shard_map/ppermute | solution.py:15
  107.7 9.7 %collective-permute-start.11 = (bf16[2048,256]{1,0:T(8,128)(2,1)S(1)}, bf16[2048,256]{1,0:T(8,128)(2,1)S(1)}, u32[]{:S(2)}, u32[]{:S(2)}) collective-permute-start(bf16[2048,256]{1,0:T(8,128)(2,1)S(1)} %get-tuple-element.87), channel_id=1, source_target_pairs={{0,2},{2,0},{4,6},{6,4},{8,10},{10,8},{12,14},{14,12},{1,3},{3,1},... | collective-permute-start | bytes 3145736 | tf_op jit(solution)/shard_map/ppermute | solution.py:15
  116.9 17.1 %collective-permute-start.13 = (bf16[2048,256]{1,0:T(8,128)(2,1)}, bf16[2048,256]{1,0:T(8,128)(2,1)S(1)}, u32[]{:S(2)}, u32[]{:S(2)}) collective-permute-start(bf16[2048,256]{1,0:T(8,128)(2,1)} %get-tuple-element.85), channel_id=1, source_target_pairs={{0,2},{2,0},{4,6},{6,4},{8,10},{10,8},{12,14},{14,12},{1,3},{3,1},... | collective-permute-start | bytes 3145736 | tf_op jit(solution)/shard_map/ppermute | solution.py:15
  116.9 18.0 %collective-permute-start.14 = (bf16[2048,256]{1,0:T(8,128)(2,1)}, bf16[2048,256]{1,0:T(8,128)(2,1)}, u32[]{:S(2)}, u32[]{:S(2)}) collective-permute-start(bf16[2048,256]{1,0:T(8,128)(2,1)} %get-tuple-element.91), channel_id=1, source_target_pairs={{0,2},{2,0},{4,6},{6,4},{8,10},{10,8},{12,14},{14,12},{1,3},{3,1},... | collective-permute-start | bytes 3145736 | tf_op jit(solution)/shard_map/ppermute | solution.py:15
  127.2 1.0 copy-start.10
  128.2 1.0 copy-start.12
  129.2 28.0 %collective-permute-start.16 = (bf16[2048,256]{1,0:T(8,128)(2,1)}, bf16[2048,256]{1,0:T(8,128)(2,1)}, u32[]{:S(2)}, u32[]{:S(2)}) collective-permute-start(bf16[2048,256]{1,0:T(8,128)(2,1)} %get-tuple-element.88), channel_id=1, source_target_pairs={{0,1},{1,0},{2,3},{3,2},{4,5},{5,4},{6,7},{7,6},{8,9},{9,8},{10,11... | collective-permute-start | bytes 3145736 | tf_op jit(solution)/shard_map/ppermute | solution.py:264
  130.7 4.2 %copy-start.11 = (f32[512,512]{1,0:T(8,128)S(1)}, f32[512,512]{1,0:T(8,128)}, u32[]{:S(2)}) copy-start(f32[512,512]{1,0:T(8,128)} %copy-done.10) | copy-start | bytes 3145732
  133.9 1.0 copy-start.8
  134.9 1.2 copy-start.9
  136.1 11.8 %copy-start.2 = (f32[512,512]{1,0:T(8,128)S(1)}, f32[512,512]{1,0:T(8,128)}, u32[]{:S(2)}) copy-start(f32[512,512]{1,0:T(8,128)} %copy-done.1) | copy-start | bytes 3145732
  145.6 1.4 copy-start.6
  147.0 1.0 copy-start.3
  147.0 1.8 copy-start.4
  148.9 10.5 %copy-start.7 = (f32[2048,256]{1,0:T(8,128)S(1)}, f32[2048,256]{1,0:T(8,128)}, u32[]{:S(2)}) copy-start(f32[2048,256]{1,0:T(8,128)} %copy-done.6) | copy-start | bytes 6291460
  148.9 9.1 %collective-permute-start.15 = (bf16[2,2,4,1,2,16,512]{6,5,4,2,0,1,3:T(8,128)(2,1)}, bf16[2,2,4,1,2,16,512]{6,5,4,2,0,1,3:T(8,128)(2,1)}, u32[]{:S(2)}, u32[]{:S(2)}) collective-permute-start(bf16[2,2,4,1,2,16,512]{6,5,4,2,0,1,3:T(8,128)(2,1)} %fusion.12), channel_id=1, source_target_pairs={{0,2},{2,0},{4,6},{6,4},{8,10},{10,8},{12,14},{14,12},{1,3},{3,1},... | collective-permute-start | bytes 1572872 | tf_op jit(solution)/shard_map/ppermute | solution.py:15
  148.9 32.4 %collective-permute-start.17 = (bf16[2,512,512]{2,1,0:T(8,128)(2,1)}, bf16[2,512,512]{2,1,0:T(8,128)(2,1)}, u32[]{:S(2)}, u32[]{:S(2)}) collective-permute-start(bf16[2,512,512]{2,1,0:T(8,128)(2,1)} %fusion.2), channel_id=1, source_target_pairs={{0,4},{2,6},{4,0},{6,2},{8,12},{10,14},{12,8},{14,10},{1,5},{3,7},... | collective-permute-start | bytes 3145736 | tf_op jit(solution)/shard_map/ppermute | solution.py:15
  157.2 36.8 %collective-permute-start.19 = (bf16[2048,256]{1,0:T(8,128)(2,1)}, bf16[2048,256]{1,0:T(8,128)(2,1)}, u32[]{:S(2)}, u32[]{:S(2)}) collective-permute-start(bf16[2048,256]{1,0:T(8,128)(2,1)} %copy-done.12), channel_id=1, source_target_pairs={{0,1},{1,0},{2,3},{3,2},{4,5},{5,4},{6,7},{7,6},{8,9},{9,8},{10,11... | collective-permute-start | bytes 3145736 | tf_op jit(solution)/shard_map/ppermute | solution.py:264
  159.3 24.6 %copy-start.14 = (f32[2,2,4,2,16,512]{5,4,3,2,0,1:T(8,128)}, f32[2,2,4,2,16,512]{5,4,3,2,0,1:T(8,128)S(1)}, u32[]{:S(2)}) copy-start(f32[2,2,4,2,16,512]{5,4,3,2,0,1:T(8,128)S(1)} %fusion.7) | copy-start | bytes 3145732
  181.3 12.7 %copy-start.5 = (f32[2048,256]{1,0:T(8,128)S(1)}, f32[2048,256]{1,0:T(8,128)}, u32[]{:S(2)}) copy-start(f32[2048,256]{1,0:T(8,128)} %copy-done.4) | copy-start | bytes 6291460
  184.0 8.9 %collective-permute-start.18 = (bf16[2,1,4,2,16,512]{5,4,3,2,0,1:T(8,128)(2,1)S(1)}, bf16[2,1,4,2,16,512]{5,4,3,2,0,1:T(8,128)(2,1)S(1)}, u32[]{:S(2)}, u32[]{:S(2)}) collective-permute-start(bf16[2,1,4,2,16,512]{5,4,3,2,0,1:T(8,128)(2,1)S(1)} %dynamic-slice_convert_fusion), channel_id=1, source_target_pairs={{0,16},{16,0},{1,17},{17,1},{2,18},{18,2},{3,19},{19,3},{4,20},{20... | collective-permute-start | bytes 786440 | tf_op jit(solution)/shard_map/ppermute | solution.py:15
  195.2 18.4 %collective-permute-start.20 = (bf16[2,2,2,16,512]{4,3,2,1,0:T(8,128)(2,1)S(1)}, bf16[2,2,2,16,512]{4,3,2,1,0:T(8,128)(2,1)S(1)}, u32[]{:S(2)}, u32[]{:S(2)}) collective-permute-start(bf16[2,2,2,16,512]{4,3,2,1,0:T(8,128)(2,1)S(1)} %fusion.15), channel_id=1, source_target_pairs={{0,4},{2,6},{4,0},{6,2},{8,12},{10,14},{12,8},{14,10},{1,5},{3,7},... | collective-permute-start | bytes 393224 | tf_op jit(solution)/shard_map/ppermute | solution.py:15
  196.8 28.8 %collective-permute-start.22 = (bf16[2,512,256]{2,1,0:T(8,128)(2,1)}, bf16[2,512,256]{2,1,0:T(8,128)(2,1)S(1)}, u32[]{:S(2)}, u32[]{:S(2)}) collective-permute-start(bf16[2,512,256]{2,1,0:T(8,128)(2,1)} %fusion.10), channel_id=1, source_target_pairs={{0,4},{2,6},{4,0},{6,2},{8,12},{10,14},{12,8},{14,10},{1,5},{3,7},... | collective-permute-start | bytes 1572872 | tf_op jit(solution)/shard_map/ppermute | solution.py:15
  197.3 32.1 %collective-permute-start.23 = (bf16[1,512,512]{2,1,0:T(8,128)(2,1)}, bf16[1,512,512]{2,1,0:T(8,128)(2,1)S(1)}, u32[]{:S(2)}, u32[]{:S(2)}) collective-permute-start(bf16[1,512,512]{2,1,0:T(8,128)(2,1)} %fusion.9), channel_id=1, source_target_pairs={{0,8},{2,10},{4,12},{6,14},{8,0},{10,2},{12,4},{14,6},{1,9},{3,11}... | collective-permute-start | bytes 1572872 | tf_op jit(solution)/shard_map/ppermute | solution.py:15
  213.7 11.0 %collective-permute-start.21 = (bf16[2,1,2,16,512]{4,3,2,1,0:T(8,128)(2,1)S(1)}, bf16[2,1,2,16,512]{4,3,2,1,0:T(8,128)(2,1)S(1)}, u32[]{:S(2)}, u32[]{:S(2)}) collective-permute-start(bf16[2,1,2,16,512]{4,3,2,1,0:T(8,128)(2,1)S(1)} %dynamic-slice_convert_fusion.2), channel_id=1, source_target_pairs={{0,8},{2,10},{4,12},{6,14},{8,0},{10,2},{12,4},{14,6},{1,9},{3,11}... | collective-permute-start | bytes 196616 | tf_op jit(solution)/shard_map/ppermute | solution.py:15
  215.3 25.5 %collective-permute-start.26 = (bf16[2,512,256]{2,1,0:T(8,128)(2,1)S(1)}, bf16[2,512,256]{2,1,0:T(8,128)(2,1)S(1)}, u32[]{:S(2)}, u32[]{:S(2)}) collective-permute-start(bf16[2,512,256]{2,1,0:T(8,128)(2,1)S(1)} %fusion.11), channel_id=1, source_target_pairs={{0,4},{2,6},{4,0},{6,2},{8,12},{10,14},{12,8},{14,10},{1,5},{3,7},... | collective-permute-start | bytes 1572872 | tf_op jit(solution)/shard_map/ppermute | solution.py:15
  226.8 15.3 %collective-permute-start.27 = (bf16[1,512,256]{2,1,0:T(8,128)(2,1)S(1)}, bf16[1,512,256]{2,1,0:T(8,128)(2,1)S(1)}, u32[]{:S(2)}, u32[]{:S(2)}) collective-permute-start(bf16[1,512,256]{2,1,0:T(8,128)(2,1)S(1)} %fusion.13), channel_id=1, source_target_pairs={{0,8},{2,10},{4,12},{6,14},{8,0},{10,2},{12,4},{14,6},{1,9},{3,11}... | collective-permute-start | bytes 786440 | tf_op jit(solution)/shard_map/ppermute | solution.py:15
  231.3 5.0 %collective-permute-start.24 = (f32[2,2,1,16,512]{4,3,2,1,0:T(8,128)S(1)}, f32[2,2,1,16,512]{4,3,2,1,0:T(8,128)S(1)}, u32[]{:S(2)}, u32[]{:S(2)}) collective-permute-start(f32[2,2,1,16,512]{4,3,2,1,0:T(8,128)S(1)} %fusion.16), channel_id=1, source_target_pairs={{0,1},{1,0},{2,3},{3,2},{4,5},{5,4},{6,7},{7,6},{8,9},{9,8},{10,11... | collective-permute-start | bytes 393224 | tf_op jit(solution)/shard_map/ppermute | solution.py:15
  236.5 4.2 %collective-permute-start.25 = (bf16[51,512]{1,0:T(8,128)(2,1)S(1)}, bf16[51,512]{1,0:T(8,128)(2,1)S(1)}, u32[]{:S(2)}, u32[]{:S(2)}) collective-permute-start(bf16[51,512]{1,0:T(8,128)(2,1)S(1)} %pad_maximum_fusion.8), channel_id=1, source_target_pairs={{0,1},{1,0},{2,3},{3,2},{4,5},{5,4},{6,7},{7,6},{8,9},{9,8},{10,11... | collective-permute-start | bytes 156680 | tf_op jit(solution)/shard_map/ppermute | solution.py:15
  240.8 1.3 copy-start.16
  244.0 12.8 %collective-permute-start.28 = (bf16[99,512]{1,0:T(8,128)(2,1)}, bf16[99,512]{1,0:T(8,128)(2,1)}, u32[]{:S(2)}, u32[]{:S(2)}) collective-permute-start(bf16[99,512]{1,0:T(8,128)(2,1)} %pad_maximum_fusion.7), channel_id=1, source_target_pairs={{0,8},{2,10},{4,12},{6,14},{8,0},{10,2},{12,4},{14,6},{1,9},{3,11}... | collective-permute-start | bytes 304136 | tf_op jit(solution)/shard_map/ppermute | solution.py:15
  244.9 21.3 %copy-start.17 = (bf16[2,512,256]{2,1,0:T(8,128)(2,1)S(1)}, bf16[2,512,256]{2,1,0:T(8,128)(2,1)}, u32[]{:S(2)}) copy-start(bf16[2,512,256]{2,1,0:T(8,128)(2,1)} %copy-done.16) | copy-start | bytes 1572868
  244.9 21.3 %collective-permute-start.30 = (bf16[1,512,256]{2,1,0:T(8,128)(2,1)S(1)}, bf16[1,512,256]{2,1,0:T(8,128)(2,1)S(1)}, u32[]{:S(2)}, u32[]{:S(2)}) collective-permute-start(bf16[1,512,256]{2,1,0:T(8,128)(2,1)S(1)} %fusion.14), channel_id=1, source_target_pairs={{0,8},{2,10},{4,12},{6,14},{8,0},{10,2},{12,4},{14,6},{1,9},{3,11}... | collective-permute-start | bytes 786440 | tf_op jit(solution)/shard_map/ppermute | solution.py:15
  258.5 7.6 %collective-permute-start.29 = (bf16[195,512]{1,0:T(8,128)(2,1)S(1)}, bf16[195,512]{1,0:T(8,128)(2,1)S(1)}, u32[]{:S(2)}, u32[]{:S(2)}) collective-permute-start(bf16[195,512]{1,0:T(8,128)(2,1)S(1)} %pad_maximum_fusion.6), channel_id=1, source_target_pairs={{0,4},{2,6},{4,0},{6,2},{8,12},{10,14},{12,8},{14,10},{1,5},{3,7},... | collective-permute-start | bytes 599048 | tf_op jit(solution)/shard_map/ppermute | solution.py:15
  268.2 10.9 %collective-permute-start.31 = (bf16[387,512]{1,0:T(8,128)(2,1)S(1)}, bf16[387,512]{1,0:T(8,128)(2,1)S(1)}, u32[]{:S(2)}, u32[]{:S(2)}) collective-permute-start(bf16[387,512]{1,0:T(8,128)(2,1)S(1)} %pad_maximum_fusion.5), channel_id=1, source_target_pairs={{0,16},{16,0},{1,17},{17,1},{2,18},{18,2},{3,19},{19,3},{4,20},{20... | collective-permute-start | bytes 1188872 | tf_op jit(solution)/shard_map/ppermute | solution.py:15
  279.3 2.5 collective-permute-start.32
  284.9 1.0 copy-start.15

commit v7 on v6

--- a/solution.py
+++ b/solution.py
@@ -1,3 +1,5 @@
+import functools
+
 import jax
 import jax.numpy as jnp
 from jax import lax
@@ -6,8 +8,8 @@
 from jax.sharding import PartitionSpec as P
 
 CORES = 2
-AWAY = 2
-PIECES = (1, 2)
+SLICES = 4
+PARTS = ((0, 0, 1, 1), (0, 1, 1, 1), (1, 0, 2, 2))
 
 
 def swap(x, axis, mask):
@@ -41,10 +43,12 @@
     return lax.dynamic_index_in_dim(x, index, axis, keepdims=False)
 
 
-def halve(x, axis, index, exchange, kind):
+def halve(x, axis, index, exchange, kind, before_last=None):
     bit = 0
     while x.shape[axis] > 1:
         size = x.shape[axis]
+        if size == 2 and before_last is not None:
+            x = after(x, before_last())
         pairs = x.reshape(x.shape[:axis] + (size // 2, 2) + x.shape[axis + 1:])
         low = (index >> bit) & 1
         send = pick(pairs, 1 - low, axis + 1).astype(kind)
@@ -77,6 +81,7 @@
     def __init__(self, sources, z):
         self.sources, self.z, self.bit = [(x, 0) for x in sources], z, 0
         self.bits = sources[0].shape[0].bit_length() - 1
+        self.total = None
 
     def part(self, flip, *deps):
         total = 0.0
@@ -100,6 +105,8 @@
         return self.bit == self.bits
 
     def result(self, *deps):
+        if self.total is not None:
+            return self.total
         x = self.part(0, *deps)
         return x.reshape(x.shape[1:])
 
@@ -119,8 +126,8 @@
         out_ref[...] = total[:, n * width:(n + 1) * width].astype(out_ref.dtype)
 
 
-def here_kernel(where_ref, weight_ref, a_ref, mask_ref, f_ref, panel_ref, start_ref, *refs):
-    recvs, outs, term_ref = refs[:AWAY], refs[AWAY:-1], refs[-1]
+def here_kernel(slices, where_ref, weight_ref, a_ref, mask_ref, f_ref, panel_ref, start_ref, *refs):
+    recvs, outs, term_ref = refs[:slices], refs[slices:-1], refs[-1]
     total = weighted_product(a_ref, mask_ref, f_ref, weight_ref)
     total = total + jnp.concatenate([r[...].astype(jnp.float32) for r in recvs], axis=1)
     width = total.shape[1] // len(outs)
@@ -140,7 +147,7 @@
 
 
 def product(inverse, mask, factor, place, weight, sizes, merge=None):
-    zs, block, n_pole = sizes
+    zs, block, n_pole, thin = sizes
     cols = inverse.shape[1]
     width = factor.shape[1]
 
@@ -153,14 +160,15 @@
         pl.BlockSpec((1, mask.shape[1], cols), lambda i, w: (block_of(i, w), 0, 0)),
         pl.BlockSpec((cols, width), lambda i, w: (0, 0)),
     ]
-    part = [pl.BlockSpec((block, width // AWAY), lambda i, w: (i, 0))] * AWAY
+    slices = width // thin
+    part = [pl.BlockSpec((block, thin), lambda i, w: (i, 0))] * slices
     if merge is None:
         kernel, extra = away_kernel, ()
-        out_shape = [jax.ShapeDtypeStruct((zs * block, width // AWAY), jnp.bfloat16)] * AWAY
+        out_shape = [jax.ShapeDtypeStruct((zs * block, thin), jnp.bfloat16)] * slices
         out_specs = part
     else:
         recv, panel, start, kind, pieces = merge
-        kernel, extra = here_kernel, (panel, start, *recv)
+        kernel, extra = functools.partial(here_kernel, slices), (panel, start, *recv)
         full = panel.shape[1]
         term = pl.BlockSpec((full, width), lambda i, w: (0, 0))
         in_specs += [pl.BlockSpec((block, full), lambda i, w: (block_of(i, w), 0)), term] + part
@@ -181,9 +189,10 @@
     )(place, weight, inverse, mask, factor, *extra)
 
 
-def fetch_factor(panel, cols, row, col, *deps):
+def fetch_factor(panel, cols, columns, detour, row, col, *deps):
     n_row, n_col = lax.axis_size("row"), lax.axis_size("col")
-    zs, ratio, width = n_col // CORES, n_col // n_row, panel.shape[1]
+    zs, ratio = n_col // CORES, n_col // n_row
+    first, width = columns
 
     def mirror(j):
         return (zs - 1 - j // CORES) * CORES + j % CORES
@@ -199,11 +208,11 @@
             got = arrived if got is None else got + arrived
         return x if got is None else got
 
-    far = cols // 4 if n_row == 2 and zs > 1 else 0
-    own = lax.dynamic_slice(panel, (col % ratio * cols, 0), (cols, width))
+    far = cols // 4 if detour and n_row == 2 and zs > 1 else 0
+    own = lax.dynamic_slice(panel, (col % ratio * cols, first), (cols, width))
     got = [cross(after(own[:cols - far], *deps), lambda j: j)]
     if far > 0:
-        other = lax.dynamic_slice(panel, (mirror(col) % ratio * cols + cols - far, 0), (far, width))
+        other = lax.dynamic_slice(panel, (mirror(col) % ratio * cols + cols - far, first), (far, width))
         crossed = cross(after(other, *deps), mirror)
         got.append(lax.ppermute(crossed, "col", [(j, mirror(j)) for j in range(n_col)]))
     return own, got
@@ -219,16 +228,18 @@
     width = panel_first.shape[2]
     blocks = n_col * n_pole
     block = rows // blocks
-    sizes = (zs, block, n_pole)
+    sizes = (zs, block, n_pole, width // SLICES)
     panels = (panel_first[0], panel_second[0])
     grain = rows // block_masks.shape[1]
     groups = max(1, block // grain)
 
     ratio = n_col // n_row
     mine = row == col // ratio
+    half = width // 2
     own, got = [], []
-    for panel in panels:
-        mine_rows, others = fetch_factor(panel, cols, row, col, *(got[-1] if got else ()))
+    for k, first, size, _ in PARTS:
+        columns = (first * half, size * half)
+        mine_rows, others = fetch_factor(panels[k], cols, columns, k == 0, row, col, *(got[-1] if got else ()))
         own.append(mine_rows)
         got.append(others)
 
@@ -242,20 +253,31 @@
 
     dests = list(range(1, n_pole)) + [0]
     token = tuple(masks)
-    units, terms = [], []
-    for k in range(2):
-        factor = jnp.where(mine, own[k], after(jnp.concatenate(got[k]), *token))
-        received, arrived = {}, [[] for _ in range(PIECES[k])]
+    units, terms = [], [[], []]
+    for part, (k, first, size, pieces) in enumerate(PARTS):
+        wide = size * half
+        factor, start = [], 0
+        for x in got[part]:
+            x = after(x, *token)
+            factor.append(jnp.where(mine, own[part][start:start + x.shape[0]], x))
+            start += x.shape[0]
+        factor = jnp.concatenate(factor)
+        received, arrived = {}, [[] for _ in range(pieces)]
         for d in dests:
+            if d == 0:
+                token += tuple(unit.step() for unit in units[:-1] if not unit.done())
             away = product(inverse, masks[k], factor, place(1 - core, d, *token), weights, sizes)
             token = (away[0],)
             received[d] = [swap_core(x) for x in away]
-        term = jnp.zeros((width, width), jnp.float32)
+        term = jnp.zeros((width, wide), jnp.float32)
         for d in dests:
             if d == 0:
-                token += tuple(unit.step() for unit in units)
+                done = [unit for unit in units if unit.done()]
+                token += tuple(unit.step() for unit in units if not unit.done())
+                for unit in done:
+                    unit.total, *token = lax.optimization_barrier((unit.result(), *token))
             kind = jnp.bfloat16 if d > 0 else jnp.float32
-            merge = (received[d], panels[k], term, kind, PIECES[k])
+            merge = (received[d], panels[k], term, kind, pieces)
             *out, term = product(inverse, masks[k], factor, place(core, d, *token), weights, sizes, merge)
             token = (out[0],)
             if d > 0:
@@ -264,41 +286,43 @@
                     came = lax.ppermute(after(x, *before), "pole", [(i, (i + d) % n_pole) for i in range(n_pole)])
                     before = (came,)
                     arrived[n].append(came)
-        terms.append(term)
+        terms[k].append(term)
         for n, kept in enumerate(out):
             units.append(ZSum([x.reshape(zs, block, x.shape[1]) for x in [kept] + arrived[n]], z))
 
-    zero, early, last = units
+    *zeros, early, last = units
     each = width // (n_row * blocks)
     split = (2, n_row, zs, CORES, n_pole, each, width)
-    term = halve(jnp.stack(terms).reshape(split), 3, core, swap_core, jnp.bfloat16)
+    term = jnp.stack([jnp.concatenate(t, axis=1) for t in terms]).reshape(split)
+    term = halve(term, 3, core, swap_core, jnp.bfloat16)
     term = after(term, early.step(*token))
-    if not zero.done():
-        term = after(term, zero.step())
+    for unit in zeros:
+        while not unit.done():
+            term = after(term, unit.step())
     term = halve(term, 1, row, swap_row, jnp.bfloat16)
-    term = after(term, last.step(term))
-    term = halve(term, 1, z, swap_z, jnp.bfloat16)
-    while not zero.done():
-        term = after(term, zero.step(term))
+    term = halve(term, 1, z, swap_z, jnp.bfloat16, last.step)
     while not early.done():
         term = after(term, early.step(term))
-    first = zero.result(term)
-    squares = jnp.sum(first * first, axis=0)
     base = pick(pick(pick(diag_inverse.reshape(split), core, 3), row, 1), z, 1).astype(jnp.float32) * weight
-    both = halve(jnp.stack([base, after(term, squares)]), 2, pole, swap_pole, jnp.float32)
+    both = halve(jnp.stack([base, term]), 2, pole, swap_pole, jnp.float32)
     base, term = both[0], both[1]
     piece = jnp.stack([base[0] + term[0], base[1], term[1]]).astype(jnp.bfloat16)
     piece = piece[:, None, None, None, None]
+    piece, *firsts = lax.optimization_barrier((piece, *[unit.result() for unit in zeros]))
+    first = jnp.concatenate(firsts, axis=1)
+    squares = jnp.sum(first * first, axis=0)
     for bit in reversed(range(n_pole.bit_length() - 1)):
         piece, squares = double(piece, squares, 4, pole, bit, swap_pole)
+    for bit in reversed(range(zs.bit_length() - 1)):
+        piece, squares = double(piece, squares, 2, z, bit, swap_z)
+        if not last.done():
+            piece = after(piece, last.step(piece))
+    piece, second = lax.optimization_barrier((piece, early.result(piece)))
+    for bit in reversed(range(n_row.bit_length() - 1)):
+        piece, squares = double(piece, squares, 1, row, bit, swap_row)
     while not last.done():
         piece = after(piece, last.step(piece))
-    piece, second = lax.optimization_barrier((piece, early.result(piece)))
-    for bit in reversed(range(zs.bit_length() - 1)):
-        piece, squares = double(piece, squares, 2, z, bit, swap_z)
     piece, *second = lax.optimization_barrier((piece, second, last.result(piece)))
-    for bit in reversed(range(n_row.bit_length() - 1)):
-        piece, squares = double(piece, squares, 1, row, bit, swap_row)
     piece, squares = double(piece, squares, 3, core, 0, swap_core)
     scale = jnp.sqrt(squares / (rows * n_row) + 1e-06)
     piece = piece.reshape(3, width, width).astype(jnp.float32)

time: 290 us -> 290 us (level)
  waiting for transfers between devices: 111 us -> 84.4 us
  Pallas kernels: 71.1 us -> 95.7 us
  other arithmetic: 34.7 us -> 38.9 us
    ppermute x24 -> x34, waiting for transfers between devices: 84.7 us -> 57.3 us  [swap(): return lax.ppermute(x, axis, [(i, i ^ mask) for i in range(size)])]
    pallas_call x8 -> x12, Pallas kernels: 71.1 us -> 95.7 us  [product(): pl.pallas_call(kernel, out_shape=out_shape, grid_spec=pltpu.PrefetchScala...]
    ppermute x24 -> x34, starting transfers between devices: 28.9 us -> 15.9 us  [swap(): return lax.ppermute(x, axis, [(i, i ^ mask) for i in range(size)])]
    ppermute x3 -> x4, waiting for transfers between devices: 0.01 us -> 9.65 us  [body(): lax.ppermute(after(x, *before), 'pole', [(i, (i + d) % n_pole) for i in r...]
    ppermute x4 -> x5, waiting for transfers between devices: 18.7 us -> 12.7 us  [cross(): arrived = lax.ppermute(x, ('row', 'col'), pairs)]
    ppermute x4 -> x5, starting transfers between devices: 14.1 us -> 19.2 us  [cross(): arrived = lax.ppermute(x, ('row', 'col'), pairs)]
    ppermute x2, starting transfers between devices: 2.39 us -> 6.41 us  [fetch_factor(): lax.ppermute(crossed, 'col', [(j, mirror(j)) for j in range(n_col)])]
    slice x2 -> x1, local copies, waits for them, and re-layouts: 5.39 us -> 1.48 us  [body(): factor.append(jnp.where(mine, own[part][start:start + x.shape[0]], x))]
  transfers between devices with their start and end apart: 33 -> 45, of which waited for: 15 -> 19; matrix products, arithmetic and copies ran while one was open for 11% -> 11% of each run, Pallas kernels for 25% -> 33%
where the time goes in v7:
time: 290 us; the launch traced here: 288 us
  Pallas kernels  95.7 us (33%)
  waiting for transfers between devices  84.4 us (29%)
  starting transfers between devices  46.7 us (16%)
  other arithmetic  38.9 us (13%)
  local copies, waits for them, and re-layouts  20.3 us (7%)
    pallas_call x12, Pallas kernels, product(): pl.pallas_call(kernel, out_shape=out_shape, grid_spec=pltpu.PrefetchScala...  95.7 us
    ppermute x34, waiting for transfers between devices, swap(): return lax.ppermute(x, axis, [(i, i ^ mask) for i in range(size)])  57.3 us
    ppermute x5, starting transfers between devices, cross(): arrived = lax.ppermute(x, ('row', 'col'), pairs)  19.2 us
    ppermute x34, starting transfers between devices, swap(): return lax.ppermute(x, axis, [(i, i ^ mask) for i in range(size)])  15.9 us
    convert_element_type x8, other arithmetic, step(): send = self.part(1, *deps).astype(jnp.bfloat16)  15.5 us
    ppermute x5, waiting for transfers between devices, cross(): arrived = lax.ppermute(x, ('row', 'col'), pairs)  12.7 us
    unnamed x66, local copies, waits for them, and re-layouts  11.7 us
    ppermute x4, waiting for transfers between devices, body(): lax.ppermute(after(x, *before), 'pole', [(i, (i + d) % n_pole) for i in r...  9.65 us
  transfers between devices with their start and end apart: 45, of which 19 were waited for; matrix products, arithmetic and copies ran while one was open for 11% of the time, Pallas kernels for 33%

profile of v7, /device:TPU:0, one launch (start us, length us, event | category | flops | bytes accessed | tf_op | source)
XLA Modules:
  0.0 288.3 jit_solution(3033444192938778496)
XLA Ops:
  1.8 1.3 collective-permute-start.1
  3.1 1.5 dynamic-slice_bitcast_fusion.1
  4.6 6.4 %collective-permute-start = (bf16[1536,256]{1,0:T(8,128)(2,1)S(1)}, bf16[1536,256]{1,0:T(8,128)(2,1)}, u32[]{:S(2)}, u32[]{:S(2)}) collective-permute-start(bf16[1536,256]{1,0:T(8,128)(2,1)S(1)} %get-tuple-element.171), channel_id=1, source_target_pairs={{0,16},{2,18},{4,20},{6,22},{24,8},{26,10},{28,12},{30,14},{1,17},... | collective-permute-start | bytes 2359304 | tf_op jit(solution)/shard_map/ppermute | solution.py:207
  11.0 1.4 collective-permute-done.1
  12.4 3.3 %collective-permute-start.2 = (bf16[512,256]{1,0:T(8,128)(2,1)}, bf16[512,256]{1,0:T(8,128)(2,1)S(1)}, u32[]{:S(2)}, u32[]{:S(2)}) collective-permute-start(bf16[512,256]{1,0:T(8,128)(2,1)} %collective-permute-done.1), channel_id=1, source_target_pairs={{0,12},{2,14},{4,8},{6,10},{8,4},{10,6},{12,0},{14,2},{1,13},{3,15... | collective-permute-start | bytes 786440 | tf_op jit(solution)/shard_map/ppermute | solution.py:217
  17.3 4.8 %collective-permute-done.2 = bf16[512,256]{1,0:T(8,128)(2,1)S(1)} collective-permute-done((bf16[512,256]{1,0:T(8,128)(2,1)}, bf16[512,256]{1,0:T(8,128)(2,1)S(1)}, u32[]{:S(2)}, u32[]{:S(2)}) %collective-permute-start.2) | collective-permute-done | bytes 262176 | tf_op jit(solution)/shard_map/ppermute | solution.py:217
  23.1 3.8 %collective-permute-done = bf16[1536,256]{1,0:T(8,128)(2,1)} collective-permute-done((bf16[1536,256]{1,0:T(8,128)(2,1)S(1)}, bf16[1536,256]{1,0:T(8,128)(2,1)}, u32[]{:S(2)}, u32[]{:S(2)}) %collective-permute-start) | collective-permute-done | bytes 786464 | tf_op jit(solution)/shard_map/ppermute | solution.py:207
  26.9 4.5 %collective-permute-start.7 = (bf16[1536,256]{1,0:T(8,128)(2,1)S(1)}, bf16[1536,256]{1,0:T(8,128)(2,1)S(1)}, u32[]{:S(2)}, u32[]{:S(2)}) collective-permute-start(bf16[1536,256]{1,0:T(8,128)(2,1)S(1)} %get-tuple-element.97), channel_id=1, source_target_pairs={{0,16},{2,18},{4,20},{6,22},{24,8},{26,10},{28,12},{30,14},{1,17},... | collective-permute-start | bytes 2359304 | tf_op jit(solution)/shard_map/ppermute | solution.py:207
  31.5 1.3 collective-permute-start.8
  32.9 7.4 %collective-permute-done.8 = bf16[512,256]{1,0:T(8,128)(2,1)S(1)} collective-permute-done((bf16[512,256]{1,0:T(8,128)(2,1)S(1)}, bf16[512,256]{1,0:T(8,128)(2,1)S(1)}, u32[]{:S(2)}, u32[]{:S(2)}) %collective-permute-start.8) | collective-permute-done | bytes 262176 | tf_op jit(solution)/shard_map/ppermute | solution.py:207
  40.3 3.1 %collective-permute-start.9 = (bf16[512,256]{1,0:T(8,128)(2,1)S(1)}, bf16[512,256]{1,0:T(8,128)(2,1)S(1)}, u32[]{:S(2)}, u32[]{:S(2)}) collective-permute-start(bf16[512,256]{1,0:T(8,128)(2,1)S(1)} %collective-permute-done.8), channel_id=1, source_target_pairs={{0,12},{2,14},{4,8},{6,10},{8,4},{10,6},{12,0},{14,2},{1,13},{3,15... | collective-permute-start | bytes 786440 | tf_op jit(solution)/shard_map/ppermute | solution.py:217
  43.4 6.1 %shard_map.77 = (bf16[2048,128]{1,0:T(8,128)(2,1)S(1)}, bf16[2048,128]{1,0:T(8,128)(2,1)S(1)}) custom-call(s32[2]{0:T(128)S(1)} %pad_add_fusion.3.where_ref, f32[1]{0:T(128)} %copy.118.weight_ref, bf16[8192,2048]{1,0:T(8,128)(2,1)} %bitcast.202, bf16[16,4,2048]{2,1,0:T(4,128)(2,1)S(1)} %reshape_reshape.68.mask_ref, bf16[2048,256]{1,0:T(8,128)(2,1)S(1)} %pad_maximum_fusion.1.f_ref), custom_call_target="tpu_custom_call" | custom-call | flops 8388608 | bytes 524288 | tf_op jit(solution)/shard_map/pallas_call | solution.py:179
  50.2 6.8 %shard_map.78 = (bf16[2048,128]{1,0:T(8,128)(2,1)S(1)}, bf16[2048,128]{1,0:T(8,128)(2,1)S(1)}) custom-call(s32[2]{0:T(128)S(1)} %get-tuple-element.116.where_ref, f32[1]{0:T(128)} %copy.118.weight_ref, bf16[8192,2048]{1,0:T(8,128)(2,1)} %bitcast.203, bf16[16,4,2048]{2,1,0:T(4,128)(2,1)S(1)} %reshape_reshape.68.mask_ref, ...), custom_call_target="tpu_custom_call" | custom-call | flops 8388608 | bytes 524288 | tf_op jit(solution)/shard_map/pallas_call | solution.py:179
  57.5 3.1 %dynamic-slice_bitcast_fusion = bf16[2048,512]{1,0:T(8,128)(2,1)} fusion(bf16[1,8192,512]{2,1,0:T(8,128)(2,1)} %param.9, s32[]{:T(128)S(6)} %select_n.320), kind=kLoop, calls=%fused_computation.5 | loop fusion | bytes 4194308 | tf_op jit(solution)/shard_map/dynamic_slice | solution.py:212
  60.6 5.7 %collective-permute-start.15 = (bf16[2048,512]{1,0:T(8,128)(2,1)}, bf16[2048,512]{1,0:T(8,128)(2,1)}, u32[]{:S(2)}, u32[]{:S(2)}) collective-permute-start(bf16[2048,512]{1,0:T(8,128)(2,1)} %dynamic-slice_bitcast_fusion), channel_id=1, source_target_pairs={{0,16},{2,18},{4,20},{6,22},{24,8},{26,10},{28,12},{30,14},{1,17},... | collective-permute-start | bytes 6291464 | tf_op jit(solution)/shard_map/ppermute | solution.py:207
  66.5 8.4 %shard_map.79 = (bf16[2048,256]{1,0:T(8,128)(2,1)}, f32[512,256]{1,0:T(8,128)S(1)}) custom-call(s32[2]{0:T(128)S(1)} %get-tuple-element.118.where_ref, f32[1]{0:T(128)} %copy.118.weight_ref, bf16[8192,2048]{1,0:T(8,128)(2,1)} %bitcast.204, bf16[16,4,2048]{2,1,0:T(4,128)(2,1)S(1)} %reshape_reshape.68.mask_ref, bf16[2048,256]{1,0:T(8,128)(2,1)S(1)} %pad_maximum_fusion.1.f_ref, ...), custom_call_target="tpu_custom_call" | custom-call | flops 8388608 | bytes 524288 | tf_op jit(solution)/shard_map/pallas_call | solution.py:179
  74.9 1.5 collective-permute-start.12
  76.4 7.5 %shard_map.80 = (f32[2048,256]{1,0:T(8,128)S(1)}, f32[512,256]{1,0:T(8,128)S(1)}) custom-call(s32[2]{0:T(128)S(1)} %pad_add_fusion.1.where_ref, f32[1]{0:T(128)} %copy.118.weight_ref, bf16[8192,2048]{1,0:T(8,128)(2,1)} %bitcast.205, bf16[16,4,2048]{2,1,0:T(4,128)(2,1)S(1)} %reshape_reshape.68.mask_ref, bf16[2048,256]{1,0:T(8,128)(2,1)S(1)} %pad_maximum_fusion.1.f_ref, ...), custom_call_target="tpu_custom_call" | custom-call | flops 8388608 | bytes 524288 | tf_op jit(solution)/shard_map/pallas_call | solution.py:179
  85.4 6.8 %shard_map.81 = (bf16[2048,128]{1,0:T(8,128)(2,1)S(1)}, bf16[2048,128]{1,0:T(8,128)(2,1)}) custom-call(s32[2]{0:T(128)S(1)} %pad_add_fusion.3.where_ref, f32[1]{0:T(128)} %copy.118.weight_ref, bf16[8192,2048]{1,0:T(8,128)(2,1)} %bitcast.206, bf16[16,4,2048]{2,1,0:T(4,128)(2,1)S(1)} %reshape_reshape.68.mask_ref, bf16[2048,256]{1,0:T(8,128)(2,1)S(1)} %pad_maximum_fusion.2.f_ref), custom_call_target="tpu_custom_call" | custom-call | flops 8388608 | bytes 524288 | tf_op jit(solution)/shard_map/pallas_call | solution.py:179
  92.7 6.9 %shard_map.82 = (bf16[2048,128]{1,0:T(8,128)(2,1)}, bf16[2048,128]{1,0:T(8,128)(2,1)}) custom-call(s32[2]{0:T(128)S(1)} %get-tuple-element.116.where_ref, f32[1]{0:T(128)} %copy.118.weight_ref, bf16[8192,2048]{1,0:T(8,128)(2,1)} %bitcast.207, bf16[16,4,2048]{2,1,0:T(4,128)(2,1)S(1)} %reshape_reshape.68.mask_ref, bf16[2048,256]{1,0:T(8,128)(2,1)S(1)} %pad_maximum_fusion.2.f_ref), custom_call_target="tpu_custom_call" | custom-call | flops 8388608 | bytes 524288 | tf_op jit(solution)/shard_map/pallas_call | solution.py:179
  100.9 3.4 %copy-done = bf16[1,8192,512]{2,1,0:T(8,128)(2,1)S(1)} copy-done((bf16[1,8192,512]{2,1,0:T(8,128)(2,1)S(1)}, bf16[1,8192,512]{2,1,0:T(8,128)(2,1)}, u32[]{:S(2)}) %copy-start) | copy-done | bytes 8388632
  105.3 8.4 %shard_map.83 = (bf16[2048,256]{1,0:T(8,128)(2,1)}, f32[512,256]{1,0:T(8,128)S(1)}) custom-call(s32[2]{0:T(128)S(1)} %get-tuple-element.118.where_ref, f32[1]{0:T(128)} %copy.118.weight_ref, bf16[8192,2048]{1,0:T(8,128)(2,1)} %bitcast.208, bf16[16,4,2048]{2,1,0:T(4,128)(2,1)S(1)} %reshape_reshape.68.mask_ref, bf16[2048,256]{1,0:T(8,128)(2,1)S(1)} %pad_maximum_fusion.2.f_ref, ...), custom_call_target="tpu_custom_call" | custom-call | flops 8388608 | bytes 524288 | tf_op jit(solution)/shard_map/pallas_call | solution.py:179
  115.5 7.5 %shard_map.84 = (f32[2048,256]{1,0:T(8,128)S(1)}, f32[512,256]{1,0:T(8,128)S(1)}) custom-call(s32[2]{0:T(128)S(1)} %pad_add_fusion.1.where_ref, f32[1]{0:T(128)} %copy.118.weight_ref, bf16[8192,2048]{1,0:T(8,128)(2,1)} %bitcast.209, bf16[16,4,2048]{2,1,0:T(4,128)(2,1)S(1)} %reshape_reshape.68.mask_ref, bf16[2048,256]{1,0:T(8,128)(2,1)S(1)} %pad_maximum_fusion.2.f_ref, ...), custom_call_target="tpu_custom_call" | custom-call | flops 8388608 | bytes 524288 | tf_op jit(solution)/shard_map/pallas_call | solution.py:179
  123.1 3.1 %broadcast_select_fusion.f_ref = bf16[2048,512]{1,0:T(8,128)(2,1)S(1)} fusion(bf16[2048,512]{1,0:T(8,128)(2,1)} %collective-permute-done.15, pred[]{:T(512)S(6)} %eq.39, bf16[1,8192,512]{2,1,0:T(8,128)(2,1)} %param.9, s32[]{:T(128)S(6)} %select_n.320), kind=kLoop, calls=%fused_computation.6 | loop fusion | flops 1048576 | bytes 6291461 | tf_op jit(solution)/shard_map/jit(_where)/select_n | solution.py:262
  126.2 8.8 %shard_map.85 = (bf16[2048,128]{1,0:T(8,128)(2,1)}, bf16[2048,128]{1,0:T(8,128)(2,1)}, bf16[2048,128]{1,0:T(8,128)(2,1)}, bf16[2048,128]{1,0:T(8,128)(2,1)}) custom-call(s32[2]{0:T(128)S(1)} %pad_add_fusion.3.where_ref, f32[1]{0:T(128)} %copy.118.weight_ref, bf16[8192,2048]{1,0:T(8,128)(2,1)} %bitcast.210, ...), custom_call_target="tpu_custom_call" | custom-call | flops 8388608 | bytes 1048576 | tf_op jit(solution)/shard_map/pallas_call | solution.py:179
  136.9 2.0 fusion.21
  138.8 8.7 %shard_map.86 = (bf16[2048,128]{1,0:T(8,128)(2,1)}, bf16[2048,128]{1,0:T(8,128)(2,1)}, bf16[2048,128]{1,0:T(8,128)(2,1)}, bf16[2048,128]{1,0:T(8,128)(2,1)}) custom-call(s32[2]{0:T(128)S(1)} %get-tuple-element.116.where_ref, f32[1]{0:T(128)} %copy.118.weight_ref, bf16[8192,2048]{1,0:T(8,128)(2,1)} %bitcast.211, ...), custom_call_target="tpu_custom_call" | custom-call | flops 8388608 | bytes 1048576 | tf_op jit(solution)/shard_map/pallas_call | solution.py:179
  148.7 10.3 %shard_map.87 = (bf16[2048,256]{1,0:T(8,128)(2,1)}, bf16[2048,256]{1,0:T(8,128)(2,1)}, f32[512,512]{1,0:T(8,128)S(1)}) custom-call(s32[2]{0:T(128)S(1)} %get-tuple-element.118.where_ref, f32[1]{0:T(128)} %copy.118.weight_ref, bf16[8192,2048]{1,0:T(8,128)(2,1)} %bitcast.212, bf16[16,4,2048]{2,1,0:T(4,128)(2,1)S(1)} %reshape_reshape.69.mask_ref, ...), custom_call_target="tpu_custom_call" | custom-call | flops 8388608 | bytes 1048576 | tf_op jit(solution)/shard_map/pallas_call | solution.py:179
  159.1 1.6 collective-permute-start.26
  160.8 2.3 fusion.14
  163.1 2.0 collective-permute-start.28
  165.1 9.6 %shard_map.88 = (f32[2048,256]{1,0:T(8,128)S(1)}, f32[2048,256]{1,0:T(8,128)S(1)}, f32[512,512]{1,0:T(8,128)S(1)}) custom-call(s32[2]{0:T(128)S(1)} %pad_add_fusion.1.where_ref, f32[1]{0:T(128)} %copy.118.weight_ref, bf16[8192,2048]{1,0:T(8,128)(2,1)} %bitcast.213, bf16[16,4,2048]{2,1,0:T(4,128)(2,1)S(1)} %reshape_reshape.69.mask_ref, ...), custom_call_target="tpu_custom_call" | custom-call | flops 8388608 | bytes 1048576 | tf_op jit(solution)/shard_map/pallas_call | solution.py:179
  174.8 1.3 copy-done.3
  176.1 1.4 copy-done.7
  177.7 2.0 fusion.20
  179.6 1.4 fusion.9
  181.0 3.6 %collective-permute-done.26 = bf16[2048,256]{1,0:T(8,128)(2,1)} collective-permute-done((bf16[2048,256]{1,0:T(8,128)(2,1)}, bf16[2048,256]{1,0:T(8,128)(2,1)}, u32[]{:S(2)}, u32[]{:S(2)}) %collective-permute-start.26) | collective-permute-done | bytes 1048608 | tf_op jit(solution)/shard_map/ppermute | solution.py:286
  184.6 1.5 collective-permute-start.31
  186.1 2.1 fusion.11
  188.4 7.2 %collective-permute-done.29 = bf16[2,1,4,2,16,512]{5,4,3,2,0,1:T(8,128)(2,1)S(1)} collective-permute-done((bf16[2,1,4,2,16,512]{5,4,3,2,0,1:T(8,128)(2,1)S(1)}, bf16[2,1,4,2,16,512]{5,4,3,2,0,1:T(8,128)(2,1)S(1)}, u32[]{:S(2)}, u32[]{:S(2)}) %collective-permute-start.29) | collective-permute-done | bytes 262176 | tf_op jit(solution)/shard_map/ppermute | solution.py:17
  196.7 2.1 collective-permute-start.30
  199.8 3.3 %collective-permute-done.30 = bf16[2,2,2,16,512]{4,3,2,0,1:T(8,128)(2,1)S(1)} collective-permute-done((bf16[2,2,2,16,512]{4,3,2,0,1:T(8,128)(2,1)S(1)}, bf16[2,2,2,16,512]{4,3,2,0,1:T(8,128)(2,1)S(1)}, u32[]{:S(2)}, u32[]{:S(2)}) %collective-permute-start.30) | collective-permute-done | bytes 131104 | tf_op jit(solution)/shard_map/ppermute | solution.py:17
  203.2 6.1 %collective-permute-done.31 = bf16[2048,256]{1,0:T(8,128)(2,1)} collective-permute-done((bf16[2048,256]{1,0:T(8,128)(2,1)}, bf16[2048,256]{1,0:T(8,128)(2,1)}, u32[]{:S(2)}, u32[]{:S(2)}) %collective-permute-start.31) | collective-permute-done | bytes 1048608 | tf_op jit(solution)/shard_map/ppermute | solution.py:286
  209.2 2.0 fusion.15
  212.2 1.3 fusion.19
  213.5 2.1 collective-permute-start.36
  215.6 5.4 %collective-permute-done.32 = bf16[2,1,2,16,512]{4,3,2,0,1:T(8,128)(2,1)S(1)} collective-permute-done((bf16[2,1,2,16,512]{4,3,2,0,1:T(8,128)(2,1)S(1)}, bf16[2,1,2,16,512]{4,3,2,0,1:T(8,128)(2,1)S(1)}, u32[]{:S(2)}, u32[]{:S(2)}) %collective-permute-start.32) | collective-permute-done | bytes 65568 | tf_op jit(solution)/shard_map/ppermute | solution.py:17
  221.8 2.1 fusion.22
  224.0 4.7 %collective-permute-done.36 = bf16[1,512,256]{2,1,0:T(8,128)(2,1)S(1)} collective-permute-done((bf16[1,512,256]{2,1,0:T(8,128)(2,1)S(1)}, bf16[1,512,256]{2,1,0:T(8,128)(2,1)S(1)}, u32[]{:S(2)}, u32[]{:S(2)}) %collective-permute-start.36) | collective-permute-done | bytes 262176 | tf_op jit(solution)/shard_map/ppermute | solution.py:17
  228.7 1.3 fusion.17
  230.2 1.4 collective-permute-start.37
  231.6 2.8 collective-permute-done.37
  234.6 1.7 collective-permute-start.38
  236.3 8.6 %collective-permute-done.38 = bf16[99,512]{1,0:T(8,128)(2,1)S(1)} collective-permute-done((bf16[99,512]{1,0:T(8,128)(2,1)S(1)}, bf16[99,512]{1,0:T(8,128)(2,1)S(1)}, u32[]{:S(2)}, u32[]{:S(2)}) %collective-permute-start.38) | collective-permute-done | bytes 101408 | tf_op jit(solution)/shard_map/ppermute | solution.py:17
  245.0 2.1 collective-permute-done.39
  247.1 1.9 fusion.23
  249.3 1.6 collective-permute-start.41
  250.9 7.4 %collective-permute-done.40 = bf16[195,512]{1,0:T(8,128)(2,1)S(1)} collective-permute-done((bf16[195,512]{1,0:T(8,128)(2,1)S(1)}, bf16[195,512]{1,0:T(8,128)(2,1)S(1)}, u32[]{:S(2)}, u32[]{:S(2)}) %collective-permute-start.40) | collective-permute-done | bytes 199712 | tf_op jit(solution)/shard_map/ppermute | solution.py:17
  259.1 3.5 %collective-permute-done.41 = bf16[1,512,256]{2,1,0:T(8,128)(2,1)} collective-permute-done((bf16[1,512,256]{2,1,0:T(8,128)(2,1)}, bf16[1,512,256]{2,1,0:T(8,128)(2,1)}, u32[]{:S(2)}, u32[]{:S(2)}) %collective-permute-start.41) | collective-permute-done | bytes 262176 | tf_op jit(solution)/shard_map/ppermute | solution.py:17
  262.6 2.2 add_bitcast_fusion.1
  266.3 8.2 %collective-permute-done.42 = bf16[387,512]{1,0:T(8,128)(2,1)} collective-permute-done((bf16[387,512]{1,0:T(8,128)(2,1)}, bf16[387,512]{1,0:T(8,128)(2,1)}, u32[]{:S(2)}, u32[]{:S(2)}) %collective-permute-start.42) | collective-permute-done | bytes 396320 | tf_op jit(solution)/shard_map/ppermute | solution.py:17
  276.7 2.0 add_bitcast_fusion
  280.6 2.4 collective-permute-done.44
  285.7 1.5 pad_maximum_fusion
  (199 shorter events, 28.7 us)
Async XLA Ops:
  0.7 10.3 %copy-start.30 = (s32[2,64,16]{1,2,0:T(8,128)S(1)}, s32[2,64,16]{1,2,0:T(8,128)}, u32[]{:S(2)}) copy-start(s32[2,64,16]{1,2,0:T(8,128)} %param.7) | copy-start | bytes 24580
  1.8 10.7 %collective-permute-start.1 = (bf16[512,256]{1,0:T(8,128)(2,1)S(1)}, bf16[512,256]{1,0:T(8,128)(2,1)}, u32[]{:S(2)}, u32[]{:S(2)}) collective-permute-start(bf16[512,256]{1,0:T(8,128)(2,1)S(1)} %get-tuple-element.173), channel_id=1, source_target_pairs={{12,28},{14,30},{8,24},{10,26},{20,4},{22,6},{16,0},{18,2},{13,29}... | collective-permute-start | bytes 786440 | tf_op jit(solution)/shard_map/ppermute | solution.py:207
  4.6 28.3 %copy-start.20 = (bf16[1536,256]{1,0:T(8,128)(2,1)}, bf16[1536,256]{1,0:T(8,128)(2,1)S(1)}, u32[]{:S(2)}) copy-start(bf16[1536,256]{1,0:T(8,128)(2,1)S(1)} %get-tuple-element.97) | copy-start | bytes 2359300
  4.6 22.3 %collective-permute-start = (bf16[1536,256]{1,0:T(8,128)(2,1)S(1)}, bf16[1536,256]{1,0:T(8,128)(2,1)}, u32[]{:S(2)}, u32[]{:S(2)}) collective-permute-start(bf16[1536,256]{1,0:T(8,128)(2,1)S(1)} %get-tuple-element.171), channel_id=1, source_target_pairs={{0,16},{2,18},{4,20},{6,22},{24,8},{26,10},{28,12},{30,14},{1,17},... | collective-permute-start | bytes 2359304 | tf_op jit(solution)/shard_map/ppermute | solution.py:207
  12.4 9.6 %collective-permute-start.2 = (bf16[512,256]{1,0:T(8,128)(2,1)}, bf16[512,256]{1,0:T(8,128)(2,1)S(1)}, u32[]{:S(2)}, u32[]{:S(2)}) collective-permute-start(bf16[512,256]{1,0:T(8,128)(2,1)} %collective-permute-done.1), channel_id=1, source_target_pairs={{0,12},{2,14},{4,8},{6,10},{8,4},{10,6},{12,0},{14,2},{1,13},{3,15... | collective-permute-start | bytes 786440 | tf_op jit(solution)/shard_map/ppermute | solution.py:217
  26.9 33.7 %collective-permute-start.7 = (bf16[1536,256]{1,0:T(8,128)(2,1)S(1)}, bf16[1536,256]{1,0:T(8,128)(2,1)S(1)}, u32[]{:S(2)}, u32[]{:S(2)}) collective-permute-start(bf16[1536,256]{1,0:T(8,128)(2,1)S(1)} %get-tuple-element.97), channel_id=1, source_target_pairs={{0,16},{2,18},{4,20},{6,22},{24,8},{26,10},{28,12},{30,14},{1,17},... | collective-permute-start | bytes 2359304 | tf_op jit(solution)/shard_map/ppermute | solution.py:207
  31.5 8.8 %collective-permute-start.8 = (bf16[512,256]{1,0:T(8,128)(2,1)S(1)}, bf16[512,256]{1,0:T(8,128)(2,1)S(1)}, u32[]{:S(2)}, u32[]{:S(2)}) collective-permute-start(bf16[512,256]{1,0:T(8,128)(2,1)S(1)} %get-tuple-element.99), channel_id=1, source_target_pairs={{12,28},{14,30},{8,24},{10,26},{20,4},{22,6},{16,0},{18,2},{13,29}... | collective-permute-start | bytes 786440 | tf_op jit(solution)/shard_map/ppermute | solution.py:207
  40.3 16.8 %collective-permute-start.9 = (bf16[512,256]{1,0:T(8,128)(2,1)S(1)}, bf16[512,256]{1,0:T(8,128)(2,1)S(1)}, u32[]{:S(2)}, u32[]{:S(2)}) collective-permute-start(bf16[512,256]{1,0:T(8,128)(2,1)S(1)} %collective-permute-done.8), channel_id=1, source_target_pairs={{0,12},{2,14},{4,8},{6,10},{8,4},{10,6},{12,0},{14,2},{1,13},{3,15... | collective-permute-start | bytes 786440 | tf_op jit(solution)/shard_map/ppermute | solution.py:217
  49.5 16.9 %collective-permute-start.3 = (bf16[2048,128]{1,0:T(8,128)(2,1)S(1)}, bf16[2048,128]{1,0:T(8,128)(2,1)S(1)}, u32[]{:S(2)}, u32[]{:S(2)}) collective-permute-start(bf16[2048,128]{1,0:T(8,128)(2,1)S(1)} %get-tuple-element.85), channel_id=1, source_target_pairs={{0,2},{2,0},{4,6},{6,4},{8,10},{10,8},{12,14},{14,12},{1,3},{3,1},... | collective-permute-start | bytes 1572872 | tf_op jit(solution)/shard_map/ppermute | solution.py:17
  49.6 16.8 %collective-permute-start.4 = (bf16[2048,128]{1,0:T(8,128)(2,1)S(1)}, bf16[2048,128]{1,0:T(8,128)(2,1)S(1)}, u32[]{:S(2)}, u32[]{:S(2)}) collective-permute-start(bf16[2048,128]{1,0:T(8,128)(2,1)S(1)} %get-tuple-element.89), channel_id=1, source_target_pairs={{0,2},{2,0},{4,6},{6,4},{8,10},{10,8},{12,14},{14,12},{1,3},{3,1},... | collective-permute-start | bytes 1572872 | tf_op jit(solution)/shard_map/ppermute | solution.py:17
  50.2 16.3 %slice-start = ((s8[8388608]{0:T(1024)(128)(4,1)}), s8[4194304]{0:T(1024)(128)(4,1)S(1)}, s32[]{:S(2)}) async-start(s8[8388608]{0:T(1024)(128)(4,1)} %bitcast.182), calls=%async_computation | async-start | bytes 8388608
  50.2 16.3 %slice-start.1 = ((s8[8388608]{0:T(1024)(128)(4,1)}), s8[4194304]{0:T(1024)(128)(4,1)S(1)}, s32[]{:S(2)}) async-start(s8[8388608]{0:T(1024)(128)(4,1)} %bitcast.182), calls=%async_computation.1 | async-start | bytes 8388608
  56.9 19.4 %collective-permute-start.5 = (bf16[2048,128]{1,0:T(8,128)(2,1)S(1)}, bf16[2048,128]{1,0:T(8,128)(2,1)S(1)}, u32[]{:S(2)}, u32[]{:S(2)}) collective-permute-start(bf16[2048,128]{1,0:T(8,128)(2,1)S(1)} %get-tuple-element.87), channel_id=1, source_target_pairs={{0,2},{2,0},{4,6},{6,4},{8,10},{10,8},{12,14},{14,12},{1,3},{3,1},... | collective-permute-start | bytes 1572872 | tf_op jit(solution)/shard_map/ppermute | solution.py:17
  57.1 19.3 %collective-permute-start.6 = (bf16[2048,128]{1,0:T(8,128)(2,1)S(1)}, bf16[2048,128]{1,0:T(8,128)(2,1)S(1)}, u32[]{:S(2)}, u32[]{:S(2)}) collective-permute-start(bf16[2048,128]{1,0:T(8,128)(2,1)S(1)} %get-tuple-element.93), channel_id=1, source_target_pairs={{0,2},{2,0},{4,6},{6,4},{8,10},{10,8},{12,14},{14,12},{1,3},{3,1},... | collective-permute-start | bytes 1572872 | tf_op jit(solution)/shard_map/ppermute | solution.py:17
  60.6 62.5 %collective-permute-start.15 = (bf16[2048,512]{1,0:T(8,128)(2,1)}, bf16[2048,512]{1,0:T(8,128)(2,1)}, u32[]{:S(2)}, u32[]{:S(2)}) collective-permute-start(bf16[2048,512]{1,0:T(8,128)(2,1)} %dynamic-slice_bitcast_fusion), channel_id=1, source_target_pairs={{0,16},{2,18},{4,20},{6,22},{24,8},{26,10},{28,12},{30,14},{1,17},... | collective-permute-start | bytes 6291464 | tf_op jit(solution)/shard_map/ppermute | solution.py:207
  74.9 39.4 %collective-permute-start.12 = (bf16[2048,256]{1,0:T(8,128)(2,1)}, bf16[2048,256]{1,0:T(8,128)(2,1)}, u32[]{:S(2)}, u32[]{:S(2)}) collective-permute-start(bf16[2048,256]{1,0:T(8,128)(2,1)} %get-tuple-element.90), channel_id=1, source_target_pairs={{0,1},{1,0},{2,3},{3,2},{4,5},{5,4},{6,7},{7,6},{8,9},{9,8},{10,11... | collective-permute-start | bytes 3145736 | tf_op jit(solution)/shard_map/ppermute | solution.py:286
  76.4 7.7 %copy-start.21 = (bf16[1536,256]{1,0:T(8,128)(2,1)S(1)}, bf16[1536,256]{1,0:T(8,128)(2,1)}, u32[]{:S(2)}) copy-start(bf16[1536,256]{1,0:T(8,128)(2,1)} %copy-done.20) | copy-start | bytes 2359300
  92.2 7.4 %collective-permute-start.10 = (bf16[2048,128]{1,0:T(8,128)(2,1)S(1)}, bf16[2048,128]{1,0:T(8,128)(2,1)S(1)}, u32[]{:S(2)}, u32[]{:S(2)}) collective-permute-start(bf16[2048,128]{1,0:T(8,128)(2,1)S(1)} %get-tuple-element.101), channel_id=1, source_target_pairs={{0,2},{2,0},{4,6},{6,4},{8,10},{10,8},{12,14},{14,12},{1,3},{3,1},... | collective-permute-start | bytes 1572872 | tf_op jit(solution)/shard_map/ppermute | solution.py:17
  92.2 8.7 %collective-permute-start.11 = (bf16[2048,128]{1,0:T(8,128)(2,1)}, bf16[2048,128]{1,0:T(8,128)(2,1)}, u32[]{:S(2)}, u32[]{:S(2)}) collective-permute-start(bf16[2048,128]{1,0:T(8,128)(2,1)} %get-tuple-element.105), channel_id=1, source_target_pairs={{0,2},{2,0},{4,6},{6,4},{8,10},{10,8},{12,14},{14,12},{1,3},{3,1},... | collective-permute-start | bytes 1572872 | tf_op jit(solution)/shard_map/ppermute | solution.py:17
  99.6 15.9 %collective-permute-start.13 = (bf16[2048,128]{1,0:T(8,128)(2,1)}, bf16[2048,128]{1,0:T(8,128)(2,1)S(1)}, u32[]{:S(2)}, u32[]{:S(2)}) collective-permute-start(bf16[2048,128]{1,0:T(8,128)(2,1)} %get-tuple-element.103), channel_id=1, source_target_pairs={{0,2},{2,0},{4,6},{6,4},{8,10},{10,8},{12,14},{14,12},{1,3},{3,1},... | collective-permute-start | bytes 1572872 | tf_op jit(solution)/shard_map/ppermute | solution.py:17
  100.4 15.1 %collective-permute-start.14 = (bf16[2048,128]{1,0:T(8,128)(2,1)}, bf16[2048,128]{1,0:T(8,128)(2,1)S(1)}, u32[]{:S(2)}, u32[]{:S(2)}) collective-permute-start(bf16[2048,128]{1,0:T(8,128)(2,1)} %get-tuple-element.109), channel_id=1, source_target_pairs={{0,2},{2,0},{4,6},{6,4},{8,10},{10,8},{12,14},{14,12},{1,3},{3,1},... | collective-permute-start | bytes 1572872 | tf_op jit(solution)/shard_map/ppermute | solution.py:17
  100.9 3.4 %copy-start = (bf16[1,8192,512]{2,1,0:T(8,128)(2,1)S(1)}, bf16[1,8192,512]{2,1,0:T(8,128)(2,1)}, u32[]{:S(2)}) copy-start(bf16[1,8192,512]{2,1,0:T(8,128)(2,1)} %param.8) | copy-start | bytes 25165828
  105.3 8.9 %copy-start.2 = (f32[2048,256]{1,0:T(8,128)S(1)}, f32[2048,256]{1,0:T(8,128)}, u32[]{:S(2)}) copy-start(f32[2048,256]{1,0:T(8,128)} %copy-done.1) | copy-start | bytes 6291460
  113.8 45.3 %collective-permute-start.27 = (bf16[2048,256]{1,0:T(8,128)(2,1)}, bf16[2048,256]{1,0:T(8,128)(2,1)}, u32[]{:S(2)}, u32[]{:S(2)}) collective-permute-start(bf16[2048,256]{1,0:T(8,128)(2,1)} %get-tuple-element.106), channel_id=1, source_target_pairs={{0,1},{1,0},{2,3},{3,2},{4,5},{5,4},{6,7},{7,6},{8,9},{9,8},{10,11... | collective-permute-start | bytes 3145736 | tf_op jit(solution)/shard_map/ppermute | solution.py:286
  115.4 20.1 %collective-permute-start.16 = (bf16[2,512,256]{2,1,0:T(8,128)(2,1)S(1)}, bf16[2,512,256]{2,1,0:T(8,128)(2,1)S(1)}, u32[]{:S(2)}, u32[]{:S(2)}) collective-permute-start(bf16[2,512,256]{2,1,0:T(8,128)(2,1)S(1)} %fusion.13), channel_id=1, source_target_pairs={{0,4},{2,6},{4,0},{6,2},{8,12},{10,14},{12,8},{14,10},{1,5},{3,7},... | collective-permute-start | bytes 1572872 | tf_op jit(solution)/shard_map/ppermute | solution.py:17
  123.1 3.2 %copy-start.5 = (f32[2048,256]{1,0:T(8,128)}, f32[2048,256]{1,0:T(8,128)S(1)}, u32[]{:S(2)}) copy-start(f32[2048,256]{1,0:T(8,128)S(1)} %get-tuple-element.112) | copy-start | bytes 6291460
  135.0 12.5 %collective-permute-start.17 = (bf16[2048,128]{1,0:T(8,128)(2,1)}, bf16[2048,128]{1,0:T(8,128)(2,1)S(1)}, u32[]{:S(2)}, u32[]{:S(2)}) collective-permute-start(bf16[2048,128]{1,0:T(8,128)(2,1)} %get-tuple-element.115), channel_id=1, source_target_pairs={{0,2},{2,0},{4,6},{6,4},{8,10},{10,8},{12,14},{14,12},{1,3},{3,1},... | collective-permute-start | bytes 1572872 | tf_op jit(solution)/shard_map/ppermute | solution.py:17
  135.0 12.6 %collective-permute-start.18 = (bf16[2048,128]{1,0:T(8,128)(2,1)}, bf16[2048,128]{1,0:T(8,128)(2,1)S(1)}, u32[]{:S(2)}, u32[]{:S(2)}) collective-permute-start(bf16[2048,128]{1,0:T(8,128)(2,1)} %get-tuple-element.119), channel_id=1, source_target_pairs={{0,2},{2,0},{4,6},{6,4},{8,10},{10,8},{12,14},{14,12},{1,3},{3,1},... | collective-permute-start | bytes 1572872 | tf_op jit(solution)/shard_map/ppermute | solution.py:17
  135.5 12.6 %collective-permute-start.19 = (bf16[2048,128]{1,0:T(8,128)(2,1)}, bf16[2048,128]{1,0:T(8,128)(2,1)}, u32[]{:S(2)}, u32[]{:S(2)}) collective-permute-start(bf16[2048,128]{1,0:T(8,128)(2,1)} %get-tuple-element.120), channel_id=1, source_target_pairs={{0,2},{2,0},{4,6},{6,4},{8,10},{10,8},{12,14},{14,12},{1,3},{3,1},... | collective-permute-start | bytes 1572872 | tf_op jit(solution)/shard_map/ppermute | solution.py:17
  136.4 11.8 %collective-permute-start.20 = (bf16[2048,128]{1,0:T(8,128)(2,1)}, bf16[2048,128]{1,0:T(8,128)(2,1)}, u32[]{:S(2)}, u32[]{:S(2)}) collective-permute-start(bf16[2048,128]{1,0:T(8,128)(2,1)} %get-tuple-element.121), channel_id=1, source_target_pairs={{0,2},{2,0},{4,6},{6,4},{8,10},{10,8},{12,14},{14,12},{1,3},{3,1},... | collective-permute-start | bytes 1572872 | tf_op jit(solution)/shard_map/ppermute | solution.py:17
  147.5 15.6 %collective-permute-start.21 = (bf16[2048,128]{1,0:T(8,128)(2,1)}, bf16[2048,128]{1,0:T(8,128)(2,1)}, u32[]{:S(2)}, u32[]{:S(2)}) collective-permute-start(bf16[2048,128]{1,0:T(8,128)(2,1)} %get-tuple-element.117), channel_id=1, source_target_pairs={{0,2},{2,0},{4,6},{6,4},{8,10},{10,8},{12,14},{14,12},{1,3},{3,1},... | collective-permute-start | bytes 1572872 | tf_op jit(solution)/shard_map/ppermute | solution.py:17
  147.6 17.5 %collective-permute-start.22 = (bf16[2048,128]{1,0:T(8,128)(2,1)}, bf16[2048,128]{1,0:T(8,128)(2,1)}, u32[]{:S(2)}, u32[]{:S(2)}) collective-permute-start(bf16[2048,128]{1,0:T(8,128)(2,1)} %get-tuple-element.123), channel_id=1, source_target_pairs={{0,2},{2,0},{4,6},{6,4},{8,10},{10,8},{12,14},{14,12},{1,3},{3,1},... | collective-permute-start | bytes 1572872 | tf_op jit(solution)/shard_map/ppermute | solution.py:17
  148.1 17.1 %collective-permute-start.23 = (bf16[2048,128]{1,0:T(8,128)(2,1)}, bf16[2048,128]{1,0:T(8,128)(2,1)}, u32[]{:S(2)}, u32[]{:S(2)}) collective-permute-start(bf16[2048,128]{1,0:T(8,128)(2,1)} %get-tuple-element.124), channel_id=1, source_target_pairs={{0,2},{2,0},{4,6},{6,4},{8,10},{10,8},{12,14},{14,12},{1,3},{3,1},... | collective-permute-start | bytes 1572872 | tf_op jit(solution)/shard_map/ppermute | solution.py:17
  148.2 17.0 %collective-permute-start.24 = (bf16[2048,128]{1,0:T(8,128)(2,1)}, bf16[2048,128]{1,0:T(8,128)(2,1)}, u32[]{:S(2)}, u32[]{:S(2)}) collective-permute-start(bf16[2048,128]{1,0:T(8,128)(2,1)} %get-tuple-element.125), channel_id=1, source_target_pairs={{0,2},{2,0},{4,6},{6,4},{8,10},{10,8},{12,14},{14,12},{1,3},{3,1},... | collective-permute-start | bytes 1572872 | tf_op jit(solution)/shard_map/ppermute | solution.py:17
  148.7 11.9 %copy-start.12 = (f32[512,256]{1,0:T(8,128)S(1)}, f32[512,256]{1,0:T(8,128)}, u32[]{:S(2)}) copy-start(f32[512,256]{1,0:T(8,128)} %copy-done.11) | copy-start | bytes 1572868
  148.7 11.9 %copy-start.14 = (f32[512,256]{1,0:T(8,128)S(1)}, f32[512,256]{1,0:T(8,128)}, u32[]{:S(2)}) copy-start(f32[512,256]{1,0:T(8,128)} %copy-done.13) | copy-start | bytes 1572868
  159.1 25.5 %collective-permute-start.26 = (bf16[2048,256]{1,0:T(8,128)(2,1)}, bf16[2048,256]{1,0:T(8,128)(2,1)}, u32[]{:S(2)}, u32[]{:S(2)}) collective-permute-start(bf16[2048,256]{1,0:T(8,128)(2,1)} %get-tuple-element.129), channel_id=1, source_target_pairs={{0,1},{1,0},{2,3},{3,2},{4,5},{5,4},{6,7},{7,6},{8,9},{9,8},{10,11... | collective-permute-start | bytes 3145736 | tf_op jit(solution)/shard_map/ppermute | solution.py:286
  160.8 16.7 %copy-start.15 = (f32[512,512]{1,0:T(8,128)}, f32[512,512]{1,0:T(8,128)S(1)}, u32[]{:S(2)}) copy-start(f32[512,512]{1,0:T(8,128)S(1)} %pad_maximum_fusion.3) | copy-start | bytes 3145732
  163.1 14.5 %collective-permute-start.28 = (bf16[2,512,256]{2,1,0:T(8,128)(2,1)}, bf16[2,512,256]{2,1,0:T(8,128)(2,1)}, u32[]{:S(2)}, u32[]{:S(2)}) collective-permute-start(bf16[2,512,256]{2,1,0:T(8,128)(2,1)} %fusion.14), channel_id=1, source_target_pairs={{0,4},{2,6},{4,0},{6,2},{8,12},{10,14},{12,8},{14,10},{1,5},{3,7},... | collective-permute-start | bytes 1572872 | tf_op jit(solution)/shard_map/ppermute | solution.py:17
  177.6 2.1 collective-permute-start.25
  179.6 6.5 %copy-start.8 = (f32[2048,256]{1,0:T(8,128)S(1)}, f32[2048,256]{1,0:T(8,128)}, u32[]{:S(2)}) copy-start(f32[2048,256]{1,0:T(8,128)} %copy-done.7) | copy-start | bytes 6291460
  181.0 7.2 %copy-start.19 = (f32[2,2,4,2,16,512]{5,4,3,2,0,1:T(8,128)}, f32[2,2,4,2,16,512]{5,4,3,2,0,1:T(8,128)S(1)}, u32[]{:S(2)}) copy-start(f32[2,2,4,2,16,512]{5,4,3,2,0,1:T(8,128)S(1)} %fusion.9) | copy-start | bytes 3145732
  184.6 24.6 %collective-permute-start.31 = (bf16[2048,256]{1,0:T(8,128)(2,1)}, bf16[2048,256]{1,0:T(8,128)(2,1)}, u32[]{:S(2)}, u32[]{:S(2)}) collective-permute-start(bf16[2048,256]{1,0:T(8,128)(2,1)} %get-tuple-element.135), channel_id=1, source_target_pairs={{0,1},{1,0},{2,3},{3,2},{4,5},{5,4},{6,7},{7,6},{8,9},{9,8},{10,11... | collective-permute-start | bytes 3145736 | tf_op jit(solution)/shard_map/ppermute | solution.py:286
  186.1 13.5 %copy-start.27 = (bf16[1,512,256]{2,1,0:T(8,128)(2,1)S(1)}, bf16[1,512,256]{2,1,0:T(8,128)(2,1)}, u32[]{:S(2)}) copy-start(bf16[1,512,256]{2,1,0:T(8,128)(2,1)} %fusion.21) | copy-start | bytes 786436
  186.1 23.1 %copy-start.4 = (f32[2048,256]{1,0:T(8,128)S(1)}, f32[2048,256]{1,0:T(8,128)}, u32[]{:S(2)}) copy-start(f32[2048,256]{1,0:T(8,128)} %copy-done.3) | copy-start | bytes 6291460
  188.3 7.2 %collective-permute-start.29 = (bf16[2,1,4,2,16,512]{5,4,3,2,0,1:T(8,128)(2,1)S(1)}, bf16[2,1,4,2,16,512]{5,4,3,2,0,1:T(8,128)(2,1)S(1)}, u32[]{:S(2)}, u32[]{:S(2)}) collective-permute-start(bf16[2,1,4,2,16,512]{5,4,3,2,0,1:T(8,128)(2,1)S(1)} %dynamic-slice_convert_fusion), channel_id=1, source_target_pairs={{0,16},{16,0},{1,17},{17,1},{2,18},{18,2},{3,19},{19,3},{4,20},{20... | collective-permute-start | bytes 786440 | tf_op jit(solution)/shard_map/ppermute | solution.py:17
  196.7 6.4 %collective-permute-start.30 = (bf16[2,2,2,16,512]{4,3,2,0,1:T(8,128)(2,1)S(1)}, bf16[2,2,2,16,512]{4,3,2,0,1:T(8,128)(2,1)S(1)}, u32[]{:S(2)}, u32[]{:S(2)}) collective-permute-start(bf16[2,2,2,16,512]{4,3,2,0,1:T(8,128)(2,1)S(1)} %fusion.26), channel_id=1, source_target_pairs={{0,4},{2,6},{4,0},{6,2},{8,12},{10,14},{12,8},{14,10},{1,5},{3,7},... | collective-permute-start | bytes 393224 | tf_op jit(solution)/shard_map/ppermute | solution.py:17
  199.6 12.5 %collective-permute-start.35 = (bf16[1,512,256]{2,1,0:T(8,128)(2,1)S(1)}, bf16[1,512,256]{2,1,0:T(8,128)(2,1)S(1)}, u32[]{:S(2)}, u32[]{:S(2)}) collective-permute-start(bf16[1,512,256]{2,1,0:T(8,128)(2,1)S(1)} %copy-done.27), channel_id=1, source_target_pairs={{0,8},{2,10},{4,12},{6,14},{8,0},{10,2},{12,4},{14,6},{1,9},{3,11}... | collective-permute-start | bytes 786440 | tf_op jit(solution)/shard_map/ppermute | solution.py:17
  199.7 22.1 %collective-permute-start.33 = (bf16[2,512,256]{2,1,0:T(8,128)(2,1)}, bf16[2,512,256]{2,1,0:T(8,128)(2,1)S(1)}, u32[]{:S(2)}, u32[]{:S(2)}) collective-permute-start(bf16[2,512,256]{2,1,0:T(8,128)(2,1)} %fusion.11), channel_id=1, source_target_pairs={{0,4},{2,6},{4,0},{6,2},{8,12},{10,14},{12,8},{14,10},{1,5},{3,7},... | collective-permute-start | bytes 1572872 | tf_op jit(solution)/shard_map/ppermute | solution.py:17
  203.1 10.3 %copy-start.28 = (bf16[1,512,256]{2,1,0:T(8,128)(2,1)S(1)}, bf16[1,512,256]{2,1,0:T(8,128)(2,1)}, u32[]{:S(2)}) copy-start(bf16[1,512,256]{2,1,0:T(8,128)(2,1)} %fusion.20) | copy-start | bytes 786436
  211.2 9.8 %collective-permute-start.32 = (bf16[2,1,2,16,512]{4,3,2,0,1:T(8,128)(2,1)S(1)}, bf16[2,1,2,16,512]{4,3,2,0,1:T(8,128)(2,1)S(1)}, u32[]{:S(2)}, u32[]{:S(2)}) collective-permute-start(bf16[2,1,2,16,512]{4,3,2,0,1:T(8,128)(2,1)S(1)} %dynamic-slice_convert_fusion.1), channel_id=1, source_target_pairs={{0,8},{2,10},{4,12},{6,14},{8,0},{10,2},{12,4},{14,6},{1,9},{3,11}... | collective-permute-start | bytes 196616 | tf_op jit(solution)/shard_map/ppermute | solution.py:17
  213.5 15.2 %collective-permute-start.36 = (bf16[1,512,256]{2,1,0:T(8,128)(2,1)S(1)}, bf16[1,512,256]{2,1,0:T(8,128)(2,1)S(1)}, u32[]{:S(2)}, u32[]{:S(2)}) collective-permute-start(bf16[1,512,256]{2,1,0:T(8,128)(2,1)S(1)} %copy-done.28), channel_id=1, source_target_pairs={{0,8},{2,10},{4,12},{6,14},{8,0},{10,2},{12,4},{14,6},{1,9},{3,11}... | collective-permute-start | bytes 786440 | tf_op jit(solution)/shard_map/ppermute | solution.py:17
  221.8 8.2 %copy-start.25 = (bf16[2,512,256]{2,1,0:T(8,128)(2,1)}, bf16[2,512,256]{2,1,0:T(8,128)(2,1)S(1)}, u32[]{:S(2)}) copy-start(bf16[2,512,256]{2,1,0:T(8,128)(2,1)S(1)} %collective-permute-done.33) | copy-start | bytes 1572868
  223.9 6.1 %collective-permute-start.34 = (f32[2,2,1,16,512]{4,3,2,1,0:T(8,128)S(1)}, f32[2,2,1,16,512]{4,3,2,1,0:T(8,128)S(1)}, u32[]{:S(2)}, u32[]{:S(2)}) collective-permute-start(f32[2,2,1,16,512]{4,3,2,1,0:T(8,128)S(1)} %fusion.27), channel_id=1, source_target_pairs={{0,1},{1,0},{2,3},{3,2},{4,5},{5,4},{6,7},{7,6},{8,9},{9,8},{10,11... | collective-permute-start | bytes 393224 | tf_op jit(solution)/shard_map/ppermute | solution.py:17
  229.9 19.1 %copy-start.16 = (f32[512,256]{1,0:T(8,128)}, f32[512,256]{1,0:T(8,128)S(1)}, u32[]{:S(2)}) copy-start(f32[512,256]{1,0:T(8,128)S(1)} %fusion.17) | copy-start | bytes 1572868
  230.2 4.2 %collective-permute-start.37 = (bf16[51,512]{1,0:T(8,128)(2,1)S(1)}, bf16[51,512]{1,0:T(8,128)(2,1)S(1)}, u32[]{:S(2)}, u32[]{:S(2)}) collective-permute-start(bf16[51,512]{1,0:T(8,128)(2,1)S(1)} %pad_maximum_fusion.9), channel_id=1, source_target_pairs={{0,1},{1,0},{2,3},{3,2},{4,5},{5,4},{6,7},{7,6},{8,9},{9,8},{10,11... | collective-permute-start | bytes 156680 | tf_op jit(solution)/shard_map/ppermute | solution.py:17
  231.6 15.5 %collective-permute-start.39 = (bf16[2,512,256]{2,1,0:T(8,128)(2,1)}, bf16[2,512,256]{2,1,0:T(8,128)(2,1)S(1)}, u32[]{:S(2)}, u32[]{:S(2)}) collective-permute-start(bf16[2,512,256]{2,1,0:T(8,128)(2,1)} %fusion.15), channel_id=1, source_target_pairs={{0,4},{2,6},{4,0},{6,2},{8,12},{10,14},{12,8},{14,10},{1,5},{3,7},... | collective-permute-start | bytes 1572872 | tf_op jit(solution)/shard_map/ppermute | solution.py:17
  234.6 10.4 %collective-permute-start.38 = (bf16[99,512]{1,0:T(8,128)(2,1)S(1)}, bf16[99,512]{1,0:T(8,128)(2,1)S(1)}, u32[]{:S(2)}, u32[]{:S(2)}) collective-permute-start(bf16[99,512]{1,0:T(8,128)(2,1)S(1)} %pad_maximum_fusion.8), channel_id=1, source_target_pairs={{0,8},{2,10},{4,12},{6,14},{8,0},{10,2},{12,4},{14,6},{1,9},{3,11}... | collective-permute-start | bytes 304136 | tf_op jit(solution)/shard_map/ppermute | solution.py:17
  249.1 9.2 %collective-permute-start.40 = (bf16[195,512]{1,0:T(8,128)(2,1)S(1)}, bf16[195,512]{1,0:T(8,128)(2,1)S(1)}, u32[]{:S(2)}, u32[]{:S(2)}) collective-permute-start(bf16[195,512]{1,0:T(8,128)(2,1)S(1)} %pad_maximum_fusion.7), channel_id=1, source_target_pairs={{0,4},{2,6},{4,0},{6,2},{8,12},{10,14},{12,8},{14,10},{1,5},{3,7},... | collective-permute-start | bytes 599048 | tf_op jit(solution)/shard_map/ppermute | solution.py:17
  249.3 13.3 %collective-permute-start.41 = (bf16[1,512,256]{2,1,0:T(8,128)(2,1)}, bf16[1,512,256]{2,1,0:T(8,128)(2,1)}, u32[]{:S(2)}, u32[]{:S(2)}) collective-permute-start(bf16[1,512,256]{2,1,0:T(8,128)(2,1)} %fusion.22), channel_id=1, source_target_pairs={{0,8},{2,10},{4,12},{6,14},{8,0},{10,2},{12,4},{14,6},{1,9},{3,11}... | collective-permute-start | bytes 786440 | tf_op jit(solution)/shard_map/ppermute | solution.py:17
  259.1 16.4 %copy-start.18 = (bf16[3,1,2,2,1,2,16,512]{7,6,5,3,2,0,4,1:T(8,128)(2,1)}, bf16[3,1,2,2,1,2,16,512]{7,6,5,3,2,0,4,1:T(8,128)(2,1)S(1)}, u32[]{:S(2)}) copy-start(bf16[3,1,2,2,1,2,16,512]{7,6,5,3,2,0,4,1:T(8,128)(2,1)S(1)} %copy.79) | copy-start | bytes 1179652
  266.3 8.2 %collective-permute-start.42 = (bf16[387,512]{1,0:T(8,128)(2,1)}, bf16[387,512]{1,0:T(8,128)(2,1)}, u32[]{:S(2)}, u32[]{:S(2)}) collective-permute-start(bf16[387,512]{1,0:T(8,128)(2,1)} %pad_maximum_fusion.6), channel_id=1, source_target_pairs={{0,16},{16,0},{1,17},{17,1},{2,18},{18,2},{3,19},{19,3},{4,20},{20... | collective-permute-start | bytes 1188872 | tf_op jit(solution)/shard_map/ppermute | solution.py:17
  266.3 10.5 %collective-permute-start.43 = (bf16[1,512,256]{2,1,0:T(8,128)(2,1)}, bf16[1,512,256]{2,1,0:T(8,128)(2,1)}, u32[]{:S(2)}, u32[]{:S(2)}) collective-permute-start(bf16[1,512,256]{2,1,0:T(8,128)(2,1)} %fusion.23), channel_id=1, source_target_pairs={{0,8},{2,10},{4,12},{6,14},{8,0},{10,2},{12,4},{14,6},{1,9},{3,11}... | collective-permute-start | bytes 786440 | tf_op jit(solution)/shard_map/ppermute | solution.py:17
  280.5 2.5 collective-permute-start.44
  (14 other events, 19.7 us)

commit v8 on v7

--- a/solution.py
+++ b/solution.py
@@ -43,12 +43,10 @@
     return lax.dynamic_index_in_dim(x, index, axis, keepdims=False)
 
 
-def halve(x, axis, index, exchange, kind, before_last=None):
+def halve(x, axis, index, exchange, kind):
     bit = 0
     while x.shape[axis] > 1:
         size = x.shape[axis]
-        if size == 2 and before_last is not None:
-            x = after(x, before_last())
         pairs = x.reshape(x.shape[:axis] + (size // 2, 2) + x.shape[axis + 1:])
         low = (index >> bit) & 1
         send = pick(pairs, 1 - low, axis + 1).astype(kind)
@@ -66,12 +64,26 @@
     return jnp.stack(terms)
 
 
-def double(x, squares, axis, index, bit, exchange):
+def with_squares(x, squares, exchange, mask):
     count = x.size // x.shape[-1]
     message = jnp.concatenate([x.reshape(count, x.shape[-1]), split_three(squares)])
-    other = exchange(message, 1 << bit)
-    squares = squares + jnp.sum(other[count:].astype(jnp.float32), axis=0)
-    other = other[:count].reshape(x.shape)
+    other = exchange(message, mask)
+    return other[:count].reshape(x.shape), squares + jnp.sum(other[count:].astype(jnp.float32), axis=0)
+
+
+def add_both(x, squares, exchange, mask, exact=False):
+    if exact:
+        count = x.size // x.shape[-1]
+        message = jnp.concatenate([x.reshape(count, x.shape[-1]), squares[None]])
+        message = message + exchange(message, mask)
+        return message[:count].reshape(x.shape), message[count]
+    x = lax.reduce_precision(x, 8, 7)
+    other, squares = with_squares(x.astype(jnp.bfloat16), squares, exchange, mask)
+    return x + other.astype(jnp.float32), squares
+
+
+def double(x, squares, axis, index, bit, exchange):
+    other, squares = with_squares(x, squares, exchange, 1 << bit)
     low = (index >> bit) & 1
     both = jnp.where(low == 0, jnp.stack([x, other], axis + 1), jnp.stack([other, x], axis + 1))
     return both.reshape(x.shape[:axis] + (2 * x.shape[axis],) + x.shape[axis + 1:]), squares
@@ -274,11 +286,13 @@
             if d == 0:
                 done = [unit for unit in units if unit.done()]
                 token += tuple(unit.step() for unit in units if not unit.done())
-                for unit in done:
-                    unit.total, *token = lax.optimization_barrier((unit.result(), *token))
             kind = jnp.bfloat16 if d > 0 else jnp.float32
             merge = (received[d], panels[k], term, kind, pieces)
-            *out, term = product(inverse, masks[k], factor, place(core, d, *token), weights, sizes, merge)
+            spot = place(core, d, *token)
+            if d == 0:
+                for unit in done:
+                    spot, unit.total = lax.optimization_barrier((spot, unit.result()))
+            *out, term = product(inverse, masks[k], factor, spot, weights, sizes, merge)
             token = (out[0],)
             if d > 0:
                 before = ()
@@ -291,39 +305,36 @@
             units.append(ZSum([x.reshape(zs, block, x.shape[1]) for x in [kept] + arrived[n]], z))
 
     *zeros, early, last = units
-    each = width // (n_row * blocks)
-    split = (2, n_row, zs, CORES, n_pole, each, width)
+    split = (2, n_row, CORES, width // (n_row * CORES), width)
     term = jnp.stack([jnp.concatenate(t, axis=1) for t in terms]).reshape(split)
-    term = halve(term, 3, core, swap_core, jnp.bfloat16)
+    term = halve(term, 2, core, swap_core, jnp.float32)
     term = after(term, early.step(*token))
     for unit in zeros:
         while not unit.done():
             term = after(term, unit.step())
     term = halve(term, 1, row, swap_row, jnp.bfloat16)
-    term = halve(term, 1, z, swap_z, jnp.bfloat16, last.step)
+    term, *firsts = lax.optimization_barrier((term, *[unit.result() for unit in zeros]))
+    first = jnp.concatenate(firsts, axis=1)
+    squares = jnp.sum(first * first, axis=0)
+    bits = zs.bit_length() - 1
+    for bit in range(bits):
+        if bit == 0:
+            term = after(term, last.step(term))
+        term, squares = add_both(term, squares, swap_z, 1 << bit)
     while not early.done():
         term = after(term, early.step(term))
-    base = pick(pick(pick(diag_inverse.reshape(split), core, 3), row, 1), z, 1).astype(jnp.float32) * weight
-    both = halve(jnp.stack([base, term]), 2, pole, swap_pole, jnp.float32)
-    base, term = both[0], both[1]
-    piece = jnp.stack([base[0] + term[0], base[1], term[1]]).astype(jnp.bfloat16)
-    piece = piece[:, None, None, None, None]
-    piece, *firsts = lax.optimization_barrier((piece, *[unit.result() for unit in zeros]))
-    first = jnp.concatenate(firsts, axis=1)
-    squares = jnp.sum(first * first, axis=0)
-    for bit in reversed(range(n_pole.bit_length() - 1)):
-        piece, squares = double(piece, squares, 4, pole, bit, swap_pole)
-    for bit in reversed(range(zs.bit_length() - 1)):
-        piece, squares = double(piece, squares, 2, z, bit, swap_z)
-        if not last.done():
-            piece = after(piece, last.step(piece))
-    piece, second = lax.optimization_barrier((piece, early.result(piece)))
+    base = pick(pick(diag_inverse.reshape(split), core, 2), row, 1).astype(jnp.float32) * weight
+    term = jnp.stack([base[0] + term[0], base[1], term[1]])
+    for bit in range(n_pole.bit_length() - 1):
+        term, squares = add_both(term, squares, swap_pole, 1 << bit, exact=True)
+    while not last.done():
+        term = after(term, last.step(term))
+    piece = term.astype(jnp.bfloat16)[:, None, None]
     for bit in reversed(range(n_row.bit_length() - 1)):
         piece, squares = double(piece, squares, 1, row, bit, swap_row)
-    while not last.done():
-        piece = after(piece, last.step(piece))
-    piece, *second = lax.optimization_barrier((piece, second, last.result(piece)))
-    piece, squares = double(piece, squares, 3, core, 0, swap_core)
+    piece, second = lax.optimization_barrier((piece, early.result(piece)))
+    piece, squares = double(piece, squares, 2, core, 0, swap_core)
+    second = [second, last.result()]
     scale = jnp.sqrt(squares / (rows * n_row) + 1e-06)
     piece = piece.reshape(3, width, width).astype(jnp.float32)
     scaled = piece[1] + piece[2] / (scale[:, None] * scale)

time: 290 us -> 319 us (1.10)
  waiting for transfers between devices: 84.4 us -> 103 us
  other arithmetic: 38.9 us -> 45.4 us
  local copies, waits for them, and re-layouts: 20.3 us -> 24.9 us
    ppermute x34 -> x31, waiting for transfers between devices: 57.3 us -> 75.2 us  [swap(): return lax.ppermute(x, axis, [(i, i ^ mask) for i in range(size)])]
    unnamed x66 -> x60, local copies, waits for them, and re-layouts: 11.7 us -> 13.9 us
    ppermute x34 -> x31, starting transfers between devices: 15.9 us -> 16.4 us  [swap(): return lax.ppermute(x, axis, [(i, i ^ mask) for i in range(size)])]
  transfers between devices with their start and end apart: 45 -> 42, of which waited for: 19 -> 13; matrix products, arithmetic and copies ran while one was open for 11% -> 12% of each run, Pallas kernels for 33% -> 30%
where the time goes in v8:
time: 319 us; the launch traced here: 317 us
  waiting for transfers between devices  103 us (32%)
  Pallas kernels  95.8 us (30%)
  other arithmetic  45.4 us (14%)
  starting transfers between devices  45.3 us (14%)
  local copies, waits for them, and re-layouts  24.9 us (8%)
    pallas_call x12, Pallas kernels, product(): pl.pallas_call(kernel, out_shape=out_shape, grid_spec=pltpu.PrefetchScala...  95.8 us
    ppermute x31, waiting for transfers between devices, swap(): return lax.ppermute(x, axis, [(i, i ^ mask) for i in range(size)])  75.2 us
    ppermute x5, starting transfers between devices, cross(): arrived = lax.ppermute(x, ('row', 'col'), pairs)  18.3 us
    ppermute x31, starting transfers between devices, swap(): return lax.ppermute(x, axis, [(i, i ^ mask) for i in range(size)])  16.4 us
    convert_element_type x8, other arithmetic, step(): send = self.part(1, *deps).astype(jnp.bfloat16)  14.8 us
    unnamed x60, local copies, waits for them, and re-layouts  13.9 us
    ppermute x5, waiting for transfers between devices, cross(): arrived = lax.ppermute(x, ('row', 'col'), pairs)  13.5 us
    ppermute x4, waiting for transfers between devices, body(): lax.ppermute(after(x, *before), 'pole', [(i, (i + d) % n_pole) for i in r...  10 us
  transfers between devices with their start and end apart: 42, of which 13 were waited for; matrix products, arithmetic and copies ran while one was open for 12% of the time, Pallas kernels for 30%

profile of v8, /device:TPU:0, one launch (start us, length us, event | category | flops | bytes accessed | tf_op | source)
XLA Modules:
  0.0 317.0 jit_solution(13417163053564231537)
XLA Ops:
  1.8 1.3 collective-permute-start.1
  3.1 2.4 dynamic-slice_bitcast_fusion.1
  5.4 5.6 %collective-permute-start = (bf16[1536,256]{1,0:T(8,128)(2,1)S(1)}, bf16[1536,256]{1,0:T(8,128)(2,1)S(1)}, u32[]{:S(2)}, u32[]{:S(2)}) collective-permute-start(bf16[1536,256]{1,0:T(8,128)(2,1)S(1)} %get-tuple-element.161), channel_id=1, source_target_pairs={{0,16},{2,18},{4,20},{6,22},{24,8},{26,10},{28,12},{30,14},{1,17},... | collective-permute-start | bytes 2359304 | tf_op jit(solution)/shard_map/ppermute | solution.py:219
  11.0 1.4 collective-permute-done.1
  12.4 3.3 %collective-permute-start.2 = (bf16[512,256]{1,0:T(8,128)(2,1)}, bf16[512,256]{1,0:T(8,128)(2,1)S(1)}, u32[]{:S(2)}, u32[]{:S(2)}) collective-permute-start(bf16[512,256]{1,0:T(8,128)(2,1)} %collective-permute-done.1), channel_id=1, source_target_pairs={{0,12},{2,14},{4,8},{6,10},{8,4},{10,6},{12,0},{14,2},{1,13},{3,15... | collective-permute-start | bytes 786440 | tf_op jit(solution)/shard_map/ppermute | solution.py:229
  17.3 4.8 %collective-permute-done.2 = bf16[512,256]{1,0:T(8,128)(2,1)S(1)} collective-permute-done((bf16[512,256]{1,0:T(8,128)(2,1)}, bf16[512,256]{1,0:T(8,128)(2,1)S(1)}, u32[]{:S(2)}, u32[]{:S(2)}) %collective-permute-start.2) | collective-permute-done | bytes 262176 | tf_op jit(solution)/shard_map/ppermute | solution.py:229
  23.1 4.7 %collective-permute-done = bf16[1536,256]{1,0:T(8,128)(2,1)S(1)} collective-permute-done((bf16[1536,256]{1,0:T(8,128)(2,1)S(1)}, bf16[1536,256]{1,0:T(8,128)(2,1)S(1)}, u32[]{:S(2)}, u32[]{:S(2)}) %collective-permute-start) | collective-permute-done | bytes 786464 | tf_op jit(solution)/shard_map/ppermute | solution.py:219
  27.8 4.4 %collective-permute-start.7 = (bf16[1536,256]{1,0:T(8,128)(2,1)}, bf16[1536,256]{1,0:T(8,128)(2,1)S(1)}, u32[]{:S(2)}, u32[]{:S(2)}) collective-permute-start(bf16[1536,256]{1,0:T(8,128)(2,1)} %get-tuple-element.94), channel_id=1, source_target_pairs={{0,16},{2,18},{4,20},{6,22},{24,8},{26,10},{28,12},{30,14},{1,17},... | collective-permute-start | bytes 2359304 | tf_op jit(solution)/shard_map/ppermute | solution.py:219
  32.2 1.3 collective-permute-start.8
  33.6 7.4 %collective-permute-done.8 = bf16[512,256]{1,0:T(8,128)(2,1)S(1)} collective-permute-done((bf16[512,256]{1,0:T(8,128)(2,1)S(1)}, bf16[512,256]{1,0:T(8,128)(2,1)S(1)}, u32[]{:S(2)}, u32[]{:S(2)}) %collective-permute-start.8) | collective-permute-done | bytes 262176 | tf_op jit(solution)/shard_map/ppermute | solution.py:219
  41.0 3.1 collective-permute-start.9
  44.2 6.1 %shard_map.77 = (bf16[2048,128]{1,0:T(8,128)(2,1)S(1)}, bf16[2048,128]{1,0:T(8,128)(2,1)S(1)}) custom-call(s32[2]{0:T(128)S(1)} %pad_add_fusion.3.where_ref, f32[1]{0:T(128)} %copy.45.weight_ref, bf16[8192,2048]{1,0:T(8,128)(2,1)} %bitcast.188, bf16[16,4,2048]{2,1,0:T(4,128)(2,1)S(1)} %reshape_reshape.64.mask_ref, bf16[2048,256]{1,0:T(8,128)(2,1)S(1)} %pad_maximum_fusion.1.f_ref), custom_call_target="tpu_custom_call" | custom-call | flops 8388608 | bytes 524288 | tf_op jit(solution)/shard_map/pallas_call | solution.py:191
  50.9 6.8 %shard_map.78 = (bf16[2048,128]{1,0:T(8,128)(2,1)S(1)}, bf16[2048,128]{1,0:T(8,128)(2,1)S(1)}) custom-call(s32[2]{0:T(128)S(1)} %get-tuple-element.113.where_ref, f32[1]{0:T(128)} %copy.45.weight_ref, bf16[8192,2048]{1,0:T(8,128)(2,1)} %bitcast.189, bf16[16,4,2048]{2,1,0:T(4,128)(2,1)S(1)} %reshape_reshape.64.mask_ref, ...), custom_call_target="tpu_custom_call" | custom-call | flops 8388608 | bytes 524288 | tf_op jit(solution)/shard_map/pallas_call | solution.py:191
  58.3 3.1 dynamic-slice_bitcast_fusion
  61.4 5.8 %collective-permute-start.15 = (bf16[2048,512]{1,0:T(8,128)(2,1)}, bf16[2048,512]{1,0:T(8,128)(2,1)}, u32[]{:S(2)}, u32[]{:S(2)}) collective-permute-start(bf16[2048,512]{1,0:T(8,128)(2,1)} %dynamic-slice_bitcast_fusion), channel_id=1, source_target_pairs={{0,16},{2,18},{4,20},{6,22},{24,8},{26,10},{28,12},{30,14},{1,17},... | collective-permute-start | bytes 6291464 | tf_op jit(solution)/shard_map/ppermute | solution.py:219
  67.3 8.3 %shard_map.79 = (bf16[2048,256]{1,0:T(8,128)(2,1)}, f32[512,256]{1,0:T(8,128)S(1)}) custom-call(s32[2]{0:T(128)S(1)} %get-tuple-element.115.where_ref, f32[1]{0:T(128)} %copy.45.weight_ref, bf16[8192,2048]{1,0:T(8,128)(2,1)} %bitcast.190, bf16[16,4,2048]{2,1,0:T(4,128)(2,1)S(1)} %reshape_reshape.64.mask_ref, bf16[2048,256]{1,0:T(8,128)(2,1)S(1)} %pad_maximum_fusion.1.f_ref, ...), custom_call_target="tpu_custom_call" | custom-call | flops 8388608 | bytes 524288 | tf_op jit(solution)/shard_map/pallas_call | solution.py:191
  75.6 1.5 collective-permute-start.12
  77.2 7.5 %shard_map.80 = (f32[2048,256]{1,0:T(8,128)S(1)}, f32[512,256]{1,0:T(8,128)S(1)}) custom-call(s32[2]{0:T(128)S(1)} %pad_add_fusion.1.where_ref, f32[1]{0:T(128)} %copy.45.weight_ref, bf16[8192,2048]{1,0:T(8,128)(2,1)} %bitcast.191, bf16[16,4,2048]{2,1,0:T(4,128)(2,1)S(1)} %reshape_reshape.64.mask_ref, bf16[2048,256]{1,0:T(8,128)(2,1)S(1)} %pad_maximum_fusion.1.f_ref, ...), custom_call_target="tpu_custom_call" | custom-call | flops 8388608 | bytes 524288 | tf_op jit(solution)/shard_map/pallas_call | solution.py:191
  85.5 1.8 broadcast_select_fusion.1
  87.4 6.8 %shard_map.81 = (bf16[2048,128]{1,0:T(8,128)(2,1)S(1)}, bf16[2048,128]{1,0:T(8,128)(2,1)}) custom-call(s32[2]{0:T(128)S(1)} %pad_add_fusion.3.where_ref, f32[1]{0:T(128)} %copy.45.weight_ref, bf16[8192,2048]{1,0:T(8,128)(2,1)} %bitcast.192, bf16[16,4,2048]{2,1,0:T(4,128)(2,1)S(1)} %reshape_reshape.64.mask_ref, bf16[2048,256]{1,0:T(8,128)(2,1)S(1)} %pad_maximum_fusion.2.f_ref), custom_call_target="tpu_custom_call" | custom-call | flops 8388608 | bytes 524288 | tf_op jit(solution)/shard_map/pallas_call | solution.py:191
  94.7 6.9 %shard_map.82 = (bf16[2048,128]{1,0:T(8,128)(2,1)}, bf16[2048,128]{1,0:T(8,128)(2,1)}) custom-call(s32[2]{0:T(128)S(1)} %get-tuple-element.113.where_ref, f32[1]{0:T(128)} %copy.45.weight_ref, bf16[8192,2048]{1,0:T(8,128)(2,1)} %bitcast.193, bf16[16,4,2048]{2,1,0:T(4,128)(2,1)S(1)} %reshape_reshape.64.mask_ref, bf16[2048,256]{1,0:T(8,128)(2,1)S(1)} %pad_maximum_fusion.2.f_ref), custom_call_target="tpu_custom_call" | custom-call | flops 8388608 | bytes 524288 | tf_op jit(solution)/shard_map/pallas_call | solution.py:191
  102.9 3.4 %copy-done = bf16[1,8192,512]{2,1,0:T(8,128)(2,1)S(1)} copy-done((bf16[1,8192,512]{2,1,0:T(8,128)(2,1)S(1)}, bf16[1,8192,512]{2,1,0:T(8,128)(2,1)}, u32[]{:S(2)}) %copy-start) | copy-done | bytes 8388632
  107.4 8.4 %shard_map.83 = (bf16[2048,256]{1,0:T(8,128)(2,1)}, f32[512,256]{1,0:T(8,128)S(1)}) custom-call(s32[2]{0:T(128)S(1)} %get-tuple-element.115.where_ref, f32[1]{0:T(128)} %copy.45.weight_ref, bf16[8192,2048]{1,0:T(8,128)(2,1)} %bitcast.194, bf16[16,4,2048]{2,1,0:T(4,128)(2,1)S(1)} %reshape_reshape.64.mask_ref, bf16[2048,256]{1,0:T(8,128)(2,1)S(1)} %pad_maximum_fusion.2.f_ref, ...), custom_call_target="tpu_custom_call" | custom-call | flops 8388608 | bytes 524288 | tf_op jit(solution)/shard_map/pallas_call | solution.py:191
  116.3 1.2 fusion.14
  117.5 7.5 %shard_map.84 = (f32[2048,256]{1,0:T(8,128)S(1)}, f32[512,256]{1,0:T(8,128)S(1)}) custom-call(s32[2]{0:T(128)S(1)} %pad_add_fusion.1.where_ref, f32[1]{0:T(128)} %copy.45.weight_ref, bf16[8192,2048]{1,0:T(8,128)(2,1)} %bitcast.195, bf16[16,4,2048]{2,1,0:T(4,128)(2,1)S(1)} %reshape_reshape.64.mask_ref, bf16[2048,256]{1,0:T(8,128)(2,1)S(1)} %pad_maximum_fusion.2.f_ref, ...), custom_call_target="tpu_custom_call" | custom-call | flops 8388608 | bytes 524288 | tf_op jit(solution)/shard_map/pallas_call | solution.py:191
  125.9 2.9 broadcast_select_fusion.f_ref
  128.8 8.7 %shard_map.85 = (bf16[2048,128]{1,0:T(8,128)(2,1)}, bf16[2048,128]{1,0:T(8,128)(2,1)}, bf16[2048,128]{1,0:T(8,128)(2,1)}, bf16[2048,128]{1,0:T(8,128)(2,1)}) custom-call(s32[2]{0:T(128)S(1)} %pad_add_fusion.3.where_ref, f32[1]{0:T(128)} %copy.45.weight_ref, bf16[8192,2048]{1,0:T(8,128)(2,1)} %bitcast.196, bf16[16,4,2048]{2,1,0:T(4,128)(2,1)S(1)} %reshape_reshape.65.mask_ref, ...), custom_call_target="tpu_custom_call" | custom-call | flops 8388608 | bytes 1048576 | tf_op jit(solution)/shard_map/pallas_call | solution.py:191
  139.4 2.0 fusion.23
  141.4 8.7 %shard_map.86 = (bf16[2048,128]{1,0:T(8,128)(2,1)}, bf16[2048,128]{1,0:T(8,128)(2,1)}, bf16[2048,128]{1,0:T(8,128)(2,1)}, bf16[2048,128]{1,0:T(8,128)(2,1)}) custom-call(s32[2]{0:T(128)S(1)} %get-tuple-element.113.where_ref, f32[1]{0:T(128)} %copy.45.weight_ref, bf16[8192,2048]{1,0:T(8,128)(2,1)} %bitcast.197, ...), custom_call_target="tpu_custom_call" | custom-call | flops 8388608 | bytes 1048576 | tf_op jit(solution)/shard_map/pallas_call | solution.py:191
  151.1 1.3 pad_maximum_fusion.3
  152.6 10.5 %shard_map.87 = (bf16[2048,256]{1,0:T(8,128)(2,1)}, bf16[2048,256]{1,0:T(8,128)(2,1)S(1)}, f32[512,512]{1,0:T(8,128)S(1)}) custom-call(s32[2]{0:T(128)S(1)} %get-tuple-element.115.where_ref, f32[1]{0:T(128)} %copy.45.weight_ref, bf16[8192,2048]{1,0:T(8,128)(2,1)} %bitcast.198, bf16[16,4,2048]{2,1,0:T(4,128)(2,1)S(1)} %reshape_reshape.65.mask_ref, ...), custom_call_target="tpu_custom_call" | custom-call | flops 8388608 | bytes 1048576 | tf_op jit(solution)/shard_map/pallas_call | solution.py:191
  163.1 1.6 collective-permute-start.28
  164.7 2.1 fusion.22
  166.9 2.0 fusion.15
  168.9 9.6 %shard_map.88 = (f32[2048,256]{1,0:T(8,128)S(1)}, f32[2048,256]{1,0:T(8,128)S(1)}, f32[512,512]{1,0:T(8,128)S(1)}) custom-call(s32[2]{0:T(128)S(1)} %pad_add_fusion.1.where_ref, f32[1]{0:T(128)} %copy.45.weight_ref, bf16[8192,2048]{1,0:T(8,128)(2,1)} %bitcast.199, bf16[16,4,2048]{2,1,0:T(4,128)(2,1)S(1)} %reshape_reshape.65.mask_ref, ...), custom_call_target="tpu_custom_call" | custom-call | flops 8388608 | bytes 1048576 | tf_op jit(solution)/shard_map/pallas_call | solution.py:191
  178.5 1.3 copy-done.1
  179.8 1.3 copy-done.5
  182.2 2.0 collective-permute-start.29
  184.2 12.9 %collective-permute-done.29 = bf16[2,512,256]{2,1,0:T(8,128)(2,1)} collective-permute-done((bf16[2,512,256]{2,1,0:T(8,128)(2,1)}, bf16[2,512,256]{2,1,0:T(8,128)(2,1)}, u32[]{:S(2)}, u32[]{:S(2)}) %collective-permute-start.29) | collective-permute-done | bytes 524320 | tf_op jit(solution)/shard_map/ppermute | solution.py:17
  197.2 1.9 fusion.20
  199.1 2.9 collective-permute-start.31
  202.5 2.0 fusion.12
  204.5 1.4 fusion.6
  207.0 7.2 %collective-permute-done.31 = bf16[1,512,256]{2,1,0:T(8,128)(2,1)S(1)} collective-permute-done((bf16[1,512,256]{2,1,0:T(8,128)(2,1)}, bf16[1,512,256]{2,1,0:T(8,128)(2,1)S(1)}, u32[]{:S(2)}, u32[]{:S(2)}) %collective-permute-start.31) | collective-permute-done | bytes 262176 | tf_op jit(solution)/shard_map/ppermute | solution.py:17
  214.2 1.3 fusion.19
  215.5 1.3 add_bitcast_fusion.1
  217.0 10.0 %collective-permute-done.32 = bf16[2048,256]{1,0:T(8,128)(2,1)} collective-permute-done((bf16[2048,256]{1,0:T(8,128)(2,1)}, bf16[2048,256]{1,0:T(8,128)(2,1)}, u32[]{:S(2)}, u32[]{:S(2)}) %collective-permute-start.32) | collective-permute-done | bytes 1048608 | tf_op jit(solution)/shard_map/ppermute | solution.py:300
  227.0 2.0 fusion.13
  229.8 1.6 collective-permute-start.33
  231.8 7.7 %collective-permute-done.33 = bf16[259,512]{1,0:T(8,128)(2,1)} collective-permute-done((bf16[259,512]{1,0:T(8,128)(2,1)}, bf16[259,512]{1,0:T(8,128)(2,1)}, u32[]{:S(2)}, u32[]{:S(2)}) %collective-permute-start.33) | collective-permute-done | bytes 265248 | tf_op jit(solution)/shard_map/ppermute | solution.py:17
  242.7 11.8 %collective-permute-done.34 = bf16[259,512]{1,0:T(8,128)(2,1)S(1)} collective-permute-done((bf16[259,512]{1,0:T(8,128)(2,1)S(1)}, bf16[259,512]{1,0:T(8,128)(2,1)S(1)}, u32[]{:S(2)}, u32[]{:S(2)}) %collective-permute-start.34) | collective-permute-done | bytes 265248 | tf_op jit(solution)/shard_map/ppermute | solution.py:17
  254.7 2.1 fusion.25
  258.1 15.7 %collective-permute-done.36 = f32[385,512]{1,0:T(8,128)S(1)} collective-permute-done((f32[385,512]{1,0:T(8,128)S(1)}, f32[385,512]{1,0:T(8,128)S(1)}, u32[]{:S(2)}, u32[]{:S(2)}) %collective-permute-start.36) | collective-permute-done | bytes 788512 | tf_op jit(solution)/shard_map/ppermute | solution.py:17
  275.7 1.7 fusion.26
  278.2 2.5 collective-permute-start.39
  280.7 5.6 %collective-permute-done.38 = bf16[387,512]{1,0:T(8,128)(2,1)} collective-permute-done((bf16[387,512]{1,0:T(8,128)(2,1)}, bf16[387,512]{1,0:T(8,128)(2,1)}, u32[]{:S(2)}, u32[]{:S(2)}) %collective-permute-start.38) | collective-permute-done | bytes 396320 | tf_op jit(solution)/shard_map/ppermute | solution.py:17
  287.4 1.2 maximum_select_fusion.1
  288.7 1.2 collective-permute-done.39
  289.8 2.2 add_bitcast_fusion
  294.4 1.4 collective-permute-start.40
  296.9 13.0 %collective-permute-done.40 = bf16[1,512,256]{2,1,0:T(8,128)(2,1)S(1)} collective-permute-done((bf16[1,512,256]{2,1,0:T(8,128)(2,1)}, bf16[1,512,256]{2,1,0:T(8,128)(2,1)S(1)}, u32[]{:S(2)}, u32[]{:S(2)}) %collective-permute-start.40) | collective-permute-done | bytes 262176 | tf_op jit(solution)/shard_map/ppermute | solution.py:17
  309.8 1.1 fusion.17
  311.7 1.2 slice.145
  314.5 1.5 pad_maximum_fusion
  (173 shorter events, 31.8 us)
Async XLA Ops:
  0.7 10.3 %copy-start.27 = (s32[2,64,16]{1,2,0:T(8,128)S(1)}, s32[2,64,16]{1,2,0:T(8,128)}, u32[]{:S(2)}) copy-start(s32[2,64,16]{1,2,0:T(8,128)} %param.7) | copy-start | bytes 24580
  1.8 10.7 %collective-permute-start.1 = (bf16[512,256]{1,0:T(8,128)(2,1)S(1)}, bf16[512,256]{1,0:T(8,128)(2,1)}, u32[]{:S(2)}, u32[]{:S(2)}) collective-permute-start(bf16[512,256]{1,0:T(8,128)(2,1)S(1)} %get-tuple-element.163), channel_id=1, source_target_pairs={{12,28},{14,30},{8,24},{10,26},{20,4},{22,6},{16,0},{18,2},{13,29}... | collective-permute-start | bytes 786440 | tf_op jit(solution)/shard_map/ppermute | solution.py:219
  5.4 22.3 %collective-permute-start = (bf16[1536,256]{1,0:T(8,128)(2,1)S(1)}, bf16[1536,256]{1,0:T(8,128)(2,1)S(1)}, u32[]{:S(2)}, u32[]{:S(2)}) collective-permute-start(bf16[1536,256]{1,0:T(8,128)(2,1)S(1)} %get-tuple-element.161), channel_id=1, source_target_pairs={{0,16},{2,18},{4,20},{6,22},{24,8},{26,10},{28,12},{30,14},{1,17},... | collective-permute-start | bytes 2359304 | tf_op jit(solution)/shard_map/ppermute | solution.py:219
  12.4 9.6 %collective-permute-start.2 = (bf16[512,256]{1,0:T(8,128)(2,1)}, bf16[512,256]{1,0:T(8,128)(2,1)S(1)}, u32[]{:S(2)}, u32[]{:S(2)}) collective-permute-start(bf16[512,256]{1,0:T(8,128)(2,1)} %collective-permute-done.1), channel_id=1, source_target_pairs={{0,12},{2,14},{4,8},{6,10},{8,4},{10,6},{12,0},{14,2},{1,13},{3,15... | collective-permute-start | bytes 786440 | tf_op jit(solution)/shard_map/ppermute | solution.py:229
  27.8 33.6 %collective-permute-start.7 = (bf16[1536,256]{1,0:T(8,128)(2,1)}, bf16[1536,256]{1,0:T(8,128)(2,1)S(1)}, u32[]{:S(2)}, u32[]{:S(2)}) collective-permute-start(bf16[1536,256]{1,0:T(8,128)(2,1)} %get-tuple-element.94), channel_id=1, source_target_pairs={{0,16},{2,18},{4,20},{6,22},{24,8},{26,10},{28,12},{30,14},{1,17},... | collective-permute-start | bytes 2359304 | tf_op jit(solution)/shard_map/ppermute | solution.py:219
  32.2 8.8 %collective-permute-start.8 = (bf16[512,256]{1,0:T(8,128)(2,1)S(1)}, bf16[512,256]{1,0:T(8,128)(2,1)S(1)}, u32[]{:S(2)}, u32[]{:S(2)}) collective-permute-start(bf16[512,256]{1,0:T(8,128)(2,1)S(1)} %get-tuple-element.96), channel_id=1, source_target_pairs={{12,28},{14,30},{8,24},{10,26},{20,4},{22,6},{16,0},{18,2},{13,29}... | collective-permute-start | bytes 786440 | tf_op jit(solution)/shard_map/ppermute | solution.py:219
  41.0 16.8 %collective-permute-start.9 = (bf16[512,256]{1,0:T(8,128)(2,1)S(1)}, bf16[512,256]{1,0:T(8,128)(2,1)S(1)}, u32[]{:S(2)}, u32[]{:S(2)}) collective-permute-start(bf16[512,256]{1,0:T(8,128)(2,1)S(1)} %collective-permute-done.8), channel_id=1, source_target_pairs={{0,12},{2,14},{4,8},{6,10},{8,4},{10,6},{12,0},{14,2},{1,13},{3,15... | collective-permute-start | bytes 786440 | tf_op jit(solution)/shard_map/ppermute | solution.py:229
  50.3 17.0 %collective-permute-start.3 = (bf16[2048,128]{1,0:T(8,128)(2,1)S(1)}, bf16[2048,128]{1,0:T(8,128)(2,1)S(1)}, u32[]{:S(2)}, u32[]{:S(2)}) collective-permute-start(bf16[2048,128]{1,0:T(8,128)(2,1)S(1)} %get-tuple-element.82), channel_id=1, source_target_pairs={{0,2},{2,0},{4,6},{6,4},{8,10},{10,8},{12,14},{14,12},{1,3},{3,1},... | collective-permute-start | bytes 1572872 | tf_op jit(solution)/shard_map/ppermute | solution.py:17
  50.3 16.9 %collective-permute-start.4 = (bf16[2048,128]{1,0:T(8,128)(2,1)S(1)}, bf16[2048,128]{1,0:T(8,128)(2,1)S(1)}, u32[]{:S(2)}, u32[]{:S(2)}) collective-permute-start(bf16[2048,128]{1,0:T(8,128)(2,1)S(1)} %get-tuple-element.86), channel_id=1, source_target_pairs={{0,2},{2,0},{4,6},{6,4},{8,10},{10,8},{12,14},{14,12},{1,3},{3,1},... | collective-permute-start | bytes 1572872 | tf_op jit(solution)/shard_map/ppermute | solution.py:17
  50.9 16.3 %slice-start = ((s8[8388608]{0:T(1024)(128)(4,1)}), s8[4194304]{0:T(1024)(128)(4,1)S(1)}, s32[]{:S(2)}) async-start(s8[8388608]{0:T(1024)(128)(4,1)} %bitcast.168), calls=%async_computation | async-start | bytes 8388608
  50.9 16.4 %slice-start.1 = ((s8[8388608]{0:T(1024)(128)(4,1)}), s8[4194304]{0:T(1024)(128)(4,1)S(1)}, s32[]{:S(2)}) async-start(s8[8388608]{0:T(1024)(128)(4,1)} %bitcast.168), calls=%async_computation.1 | async-start | bytes 8388608
  57.7 19.5 %collective-permute-start.5 = (bf16[2048,128]{1,0:T(8,128)(2,1)S(1)}, bf16[2048,128]{1,0:T(8,128)(2,1)S(1)}, u32[]{:S(2)}, u32[]{:S(2)}) collective-permute-start(bf16[2048,128]{1,0:T(8,128)(2,1)S(1)} %get-tuple-element.84), channel_id=1, source_target_pairs={{0,2},{2,0},{4,6},{6,4},{8,10},{10,8},{12,14},{14,12},{1,3},{3,1},... | collective-permute-start | bytes 1572872 | tf_op jit(solution)/shard_map/ppermute | solution.py:17
  57.8 19.3 %collective-permute-start.6 = (bf16[2048,128]{1,0:T(8,128)(2,1)S(1)}, bf16[2048,128]{1,0:T(8,128)(2,1)S(1)}, u32[]{:S(2)}, u32[]{:S(2)}) collective-permute-start(bf16[2048,128]{1,0:T(8,128)(2,1)S(1)} %get-tuple-element.90), channel_id=1, source_target_pairs={{0,2},{2,0},{4,6},{6,4},{8,10},{10,8},{12,14},{14,12},{1,3},{3,1},... | collective-permute-start | bytes 1572872 | tf_op jit(solution)/shard_map/ppermute | solution.py:17
  61.4 64.5 %collective-permute-start.15 = (bf16[2048,512]{1,0:T(8,128)(2,1)}, bf16[2048,512]{1,0:T(8,128)(2,1)}, u32[]{:S(2)}, u32[]{:S(2)}) collective-permute-start(bf16[2048,512]{1,0:T(8,128)(2,1)} %dynamic-slice_bitcast_fusion), channel_id=1, source_target_pairs={{0,16},{2,18},{4,20},{6,22},{24,8},{26,10},{28,12},{30,14},{1,17},... | collective-permute-start | bytes 6291464 | tf_op jit(solution)/shard_map/ppermute | solution.py:219
  75.6 40.6 %collective-permute-start.12 = (bf16[2048,256]{1,0:T(8,128)(2,1)}, bf16[2048,256]{1,0:T(8,128)(2,1)}, u32[]{:S(2)}, u32[]{:S(2)}) collective-permute-start(bf16[2048,256]{1,0:T(8,128)(2,1)} %get-tuple-element.87), channel_id=1, source_target_pairs={{0,1},{1,0},{2,3},{3,2},{4,5},{5,4},{6,7},{7,6},{8,9},{9,8},{10,11... | collective-permute-start | bytes 3145736 | tf_op jit(solution)/shard_map/ppermute | solution.py:300
  85.5 2.0 copy-start.7
  94.2 7.4 %collective-permute-start.10 = (bf16[2048,128]{1,0:T(8,128)(2,1)S(1)}, bf16[2048,128]{1,0:T(8,128)(2,1)S(1)}, u32[]{:S(2)}, u32[]{:S(2)}) collective-permute-start(bf16[2048,128]{1,0:T(8,128)(2,1)S(1)} %get-tuple-element.98), channel_id=1, source_target_pairs={{0,2},{2,0},{4,6},{6,4},{8,10},{10,8},{12,14},{14,12},{1,3},{3,1},... | collective-permute-start | bytes 1572872 | tf_op jit(solution)/shard_map/ppermute | solution.py:17
  94.2 8.7 %collective-permute-start.11 = (bf16[2048,128]{1,0:T(8,128)(2,1)}, bf16[2048,128]{1,0:T(8,128)(2,1)}, u32[]{:S(2)}, u32[]{:S(2)}) collective-permute-start(bf16[2048,128]{1,0:T(8,128)(2,1)} %get-tuple-element.102), channel_id=1, source_target_pairs={{0,2},{2,0},{4,6},{6,4},{8,10},{10,8},{12,14},{14,12},{1,3},{3,1},... | collective-permute-start | bytes 1572872 | tf_op jit(solution)/shard_map/ppermute | solution.py:17
  101.6 15.9 %collective-permute-start.13 = (bf16[2048,128]{1,0:T(8,128)(2,1)}, bf16[2048,128]{1,0:T(8,128)(2,1)S(1)}, u32[]{:S(2)}, u32[]{:S(2)}) collective-permute-start(bf16[2048,128]{1,0:T(8,128)(2,1)} %get-tuple-element.100), channel_id=1, source_target_pairs={{0,2},{2,0},{4,6},{6,4},{8,10},{10,8},{12,14},{14,12},{1,3},{3,1},... | collective-permute-start | bytes 1572872 | tf_op jit(solution)/shard_map/ppermute | solution.py:17
  102.4 15.1 %collective-permute-start.14 = (bf16[2048,128]{1,0:T(8,128)(2,1)}, bf16[2048,128]{1,0:T(8,128)(2,1)S(1)}, u32[]{:S(2)}, u32[]{:S(2)}) collective-permute-start(bf16[2048,128]{1,0:T(8,128)(2,1)} %get-tuple-element.106), channel_id=1, source_target_pairs={{0,2},{2,0},{4,6},{6,4},{8,10},{10,8},{12,14},{14,12},{1,3},{3,1},... | collective-permute-start | bytes 1572872 | tf_op jit(solution)/shard_map/ppermute | solution.py:17
  102.9 3.4 %copy-start = (bf16[1,8192,512]{2,1,0:T(8,128)(2,1)S(1)}, bf16[1,8192,512]{2,1,0:T(8,128)(2,1)}, u32[]{:S(2)}) copy-start(bf16[1,8192,512]{2,1,0:T(8,128)(2,1)} %param.8) | copy-start | bytes 25165828
  106.3 1.0 copy-start.10
  107.4 8.9 %copy-start.8 = (f32[2048,256]{1,0:T(8,128)S(1)}, f32[2048,256]{1,0:T(8,128)}, u32[]{:S(2)}) copy-start(f32[2048,256]{1,0:T(8,128)} %copy-done.7) | copy-start | bytes 6291460
  115.8 25.6 %collective-permute-start.21 = (bf16[2048,256]{1,0:T(8,128)(2,1)}, bf16[2048,256]{1,0:T(8,128)(2,1)}, u32[]{:S(2)}, u32[]{:S(2)}) collective-permute-start(bf16[2048,256]{1,0:T(8,128)(2,1)} %get-tuple-element.103), channel_id=1, source_target_pairs={{0,1},{1,0},{2,3},{3,2},{4,5},{5,4},{6,7},{7,6},{8,9},{9,8},{10,11... | collective-permute-start | bytes 3145736 | tf_op jit(solution)/shard_map/ppermute | solution.py:300
  117.4 20.6 %collective-permute-start.16 = (bf16[2,512,256]{2,1,0:T(8,128)(2,1)S(1)}, bf16[2,512,256]{2,1,0:T(8,128)(2,1)S(1)}, u32[]{:S(2)}, u32[]{:S(2)}) collective-permute-start(bf16[2,512,256]{2,1,0:T(8,128)(2,1)S(1)} %fusion.14), channel_id=1, source_target_pairs={{0,4},{2,6},{4,0},{6,2},{8,12},{10,14},{12,8},{14,10},{1,5},{3,7},... | collective-permute-start | bytes 1572872 | tf_op jit(solution)/shard_map/ppermute | solution.py:17
  125.9 2.9 copy-start.3
  137.5 12.6 %collective-permute-start.17 = (bf16[2048,128]{1,0:T(8,128)(2,1)}, bf16[2048,128]{1,0:T(8,128)(2,1)S(1)}, u32[]{:S(2)}, u32[]{:S(2)}) collective-permute-start(bf16[2048,128]{1,0:T(8,128)(2,1)} %get-tuple-element.112), channel_id=1, source_target_pairs={{0,2},{2,0},{4,6},{6,4},{8,10},{10,8},{12,14},{14,12},{1,3},{3,1},... | collective-permute-start | bytes 1572872 | tf_op jit(solution)/shard_map/ppermute | solution.py:17
  137.5 12.6 %collective-permute-start.18 = (bf16[2048,128]{1,0:T(8,128)(2,1)}, bf16[2048,128]{1,0:T(8,128)(2,1)S(1)}, u32[]{:S(2)}, u32[]{:S(2)}) collective-permute-start(bf16[2048,128]{1,0:T(8,128)(2,1)} %get-tuple-element.116), channel_id=1, source_target_pairs={{0,2},{2,0},{4,6},{6,4},{8,10},{10,8},{12,14},{14,12},{1,3},{3,1},... | collective-permute-start | bytes 1572872 | tf_op jit(solution)/shard_map/ppermute | solution.py:17
  138.0 12.6 %collective-permute-start.19 = (bf16[2048,128]{1,0:T(8,128)(2,1)}, bf16[2048,128]{1,0:T(8,128)(2,1)}, u32[]{:S(2)}, u32[]{:S(2)}) collective-permute-start(bf16[2048,128]{1,0:T(8,128)(2,1)} %get-tuple-element.117), channel_id=1, source_target_pairs={{0,2},{2,0},{4,6},{6,4},{8,10},{10,8},{12,14},{14,12},{1,3},{3,1},... | collective-permute-start | bytes 1572872 | tf_op jit(solution)/shard_map/ppermute | solution.py:17
  138.9 11.8 %collective-permute-start.20 = (bf16[2048,128]{1,0:T(8,128)(2,1)}, bf16[2048,128]{1,0:T(8,128)(2,1)}, u32[]{:S(2)}, u32[]{:S(2)}) collective-permute-start(bf16[2048,128]{1,0:T(8,128)(2,1)} %get-tuple-element.118), channel_id=1, source_target_pairs={{0,2},{2,0},{4,6},{6,4},{8,10},{10,8},{12,14},{14,12},{1,3},{3,1},... | collective-permute-start | bytes 1572872 | tf_op jit(solution)/shard_map/ppermute | solution.py:17
  141.4 21.8 %collective-permute-start.22 = (bf16[1,512,256]{2,1,0:T(8,128)(2,1)}, bf16[1,512,256]{2,1,0:T(8,128)(2,1)}, u32[]{:S(2)}, u32[]{:S(2)}) collective-permute-start(bf16[1,512,256]{2,1,0:T(8,128)(2,1)} %fusion.23), channel_id=1, source_target_pairs={{0,8},{2,10},{4,12},{6,14},{8,0},{10,2},{12,4},{14,6},{1,9},{3,11}... | collective-permute-start | bytes 786440 | tf_op jit(solution)/shard_map/ppermute | solution.py:17
  150.1 18.8 %collective-permute-start.23 = (bf16[2048,128]{1,0:T(8,128)(2,1)}, bf16[2048,128]{1,0:T(8,128)(2,1)}, u32[]{:S(2)}, u32[]{:S(2)}) collective-permute-start(bf16[2048,128]{1,0:T(8,128)(2,1)} %get-tuple-element.114), channel_id=1, source_target_pairs={{0,2},{2,0},{4,6},{6,4},{8,10},{10,8},{12,14},{14,12},{1,3},{3,1},... | collective-permute-start | bytes 1572872 | tf_op jit(solution)/shard_map/ppermute | solution.py:17
  150.2 18.7 %collective-permute-start.24 = (bf16[2048,128]{1,0:T(8,128)(2,1)}, bf16[2048,128]{1,0:T(8,128)(2,1)}, u32[]{:S(2)}, u32[]{:S(2)}) collective-permute-start(bf16[2048,128]{1,0:T(8,128)(2,1)} %get-tuple-element.123), channel_id=1, source_target_pairs={{0,2},{2,0},{4,6},{6,4},{8,10},{10,8},{12,14},{14,12},{1,3},{3,1},... | collective-permute-start | bytes 1572872 | tf_op jit(solution)/shard_map/ppermute | solution.py:17
  150.6 18.2 %collective-permute-start.25 = (bf16[2048,128]{1,0:T(8,128)(2,1)}, bf16[2048,128]{1,0:T(8,128)(2,1)}, u32[]{:S(2)}, u32[]{:S(2)}) collective-permute-start(bf16[2048,128]{1,0:T(8,128)(2,1)} %get-tuple-element.124), channel_id=1, source_target_pairs={{0,2},{2,0},{4,6},{6,4},{8,10},{10,8},{12,14},{14,12},{1,3},{3,1},... | collective-permute-start | bytes 1572872 | tf_op jit(solution)/shard_map/ppermute | solution.py:17
  150.7 18.1 %collective-permute-start.26 = (bf16[2048,128]{1,0:T(8,128)(2,1)}, bf16[2048,128]{1,0:T(8,128)(2,1)}, u32[]{:S(2)}, u32[]{:S(2)}) collective-permute-start(bf16[2048,128]{1,0:T(8,128)(2,1)} %get-tuple-element.125), channel_id=1, source_target_pairs={{0,2},{2,0},{4,6},{6,4},{8,10},{10,8},{12,14},{14,12},{1,3},{3,1},... | collective-permute-start | bytes 1572872 | tf_op jit(solution)/shard_map/ppermute | solution.py:17
  152.5 28.7 %copy-start.14 = (f32[512,512]{1,0:T(8,128)}, f32[512,512]{1,0:T(8,128)S(1)}, u32[]{:S(2)}) copy-start(f32[512,512]{1,0:T(8,128)S(1)} %pad_maximum_fusion.3) | copy-start | bytes 3145732
  152.6 12.2 %copy-start.24 = (bf16[2,512,256]{2,1,0:T(8,128)(2,1)S(1)}, bf16[2,512,256]{2,1,0:T(8,128)(2,1)}, u32[]{:S(2)}) copy-start(bf16[2,512,256]{2,1,0:T(8,128)(2,1)} %copy-done.23) | copy-start | bytes 1572868
  152.6 14.3 %copy-start.4 = (f32[2048,256]{1,0:T(8,128)S(1)}, f32[2048,256]{1,0:T(8,128)}, u32[]{:S(2)}) copy-start(f32[2048,256]{1,0:T(8,128)} %copy-done.3) | copy-start | bytes 6291460
  163.1 5.7 %copy-start.13 = (bf16[2048,256]{1,0:T(8,128)(2,1)}, bf16[2048,256]{1,0:T(8,128)(2,1)S(1)}, u32[]{:S(2)}) copy-start(bf16[2048,256]{1,0:T(8,128)(2,1)S(1)} %get-tuple-element.139) | copy-start | bytes 3145732
  163.1 38.9 %collective-permute-start.28 = (bf16[2048,256]{1,0:T(8,128)(2,1)}, bf16[2048,256]{1,0:T(8,128)(2,1)}, u32[]{:S(2)}, u32[]{:S(2)}) collective-permute-start(bf16[2048,256]{1,0:T(8,128)(2,1)} %get-tuple-element.119), channel_id=1, source_target_pairs={{0,1},{1,0},{2,3},{3,2},{4,5},{5,4},{6,7},{7,6},{8,9},{9,8},{10,11... | collective-permute-start | bytes 3145736 | tf_op jit(solution)/shard_map/ppermute | solution.py:300
  178.5 1.3 copy-start.1
  179.8 1.3 copy-start.5
  181.2 21.4 %copy-start.6 = (f32[2048,256]{1,0:T(8,128)S(1)}, f32[2048,256]{1,0:T(8,128)}, u32[]{:S(2)}) copy-start(f32[2048,256]{1,0:T(8,128)} %copy-done.5) | copy-start | bytes 6291460
  182.2 22.3 %collective-permute-start.27 = (f32[2,2,1,128,512]{4,3,1,0,2:T(8,128)}, f32[2,2,1,128,512]{4,3,1,0,2:T(8,128)}, u32[]{:S(2)}, u32[]{:S(2)}) collective-permute-start(f32[2,2,1,128,512]{4,3,1,0,2:T(8,128)} %fusion.2), channel_id=1, source_target_pairs={{0,2},{2,0},{4,6},{6,4},{8,10},{10,8},{12,14},{14,12},{1,3},{3,1},... | collective-permute-start | bytes 3145736 | tf_op jit(solution)/shard_map/ppermute | solution.py:17
  182.2 14.9 %collective-permute-start.29 = (bf16[2,512,256]{2,1,0:T(8,128)(2,1)}, bf16[2,512,256]{2,1,0:T(8,128)(2,1)}, u32[]{:S(2)}, u32[]{:S(2)}) collective-permute-start(bf16[2,512,256]{2,1,0:T(8,128)(2,1)} %fusion.15), channel_id=1, source_target_pairs={{0,4},{2,6},{4,0},{6,2},{8,12},{10,14},{12,8},{14,10},{1,5},{3,7},... | collective-permute-start | bytes 1572872 | tf_op jit(solution)/shard_map/ppermute | solution.py:17
  184.2 20.3 %copy-start.15 = (f32[512,512]{1,0:T(8,128)S(1)}, f32[512,512]{1,0:T(8,128)}, u32[]{:S(2)}) copy-start(f32[512,512]{1,0:T(8,128)} %copy-done.14) | copy-start | bytes 3145732
  199.1 15.1 %collective-permute-start.31 = (bf16[1,512,256]{2,1,0:T(8,128)(2,1)}, bf16[1,512,256]{2,1,0:T(8,128)(2,1)S(1)}, u32[]{:S(2)}, u32[]{:S(2)}) collective-permute-start(bf16[1,512,256]{2,1,0:T(8,128)(2,1)} %fusion.20), channel_id=1, source_target_pairs={{0,8},{2,10},{4,12},{6,14},{8,0},{10,2},{12,4},{14,6},{1,9},{3,11}... | collective-permute-start | bytes 786440 | tf_op jit(solution)/shard_map/ppermute | solution.py:17
  202.0 25.0 %collective-permute-start.32 = (bf16[2048,256]{1,0:T(8,128)(2,1)}, bf16[2048,256]{1,0:T(8,128)(2,1)}, u32[]{:S(2)}, u32[]{:S(2)}) collective-permute-start(bf16[2048,256]{1,0:T(8,128)(2,1)} %copy-done.13), channel_id=1, source_target_pairs={{0,1},{1,0},{2,3},{3,2},{4,5},{5,4},{6,7},{7,6},{8,9},{9,8},{10,11... | collective-permute-start | bytes 3145736 | tf_op jit(solution)/shard_map/ppermute | solution.py:300
  206.9 10.0 %copy-start.16 = (f32[512,256]{1,0:T(8,128)S(1)}, f32[512,256]{1,0:T(8,128)}, u32[]{:S(2)}) copy-start(f32[512,256]{1,0:T(8,128)} %fusion.22) | copy-start | bytes 1572868
  206.9 8.6 %collective-permute-start.30 = (bf16[2,1,128,512]{3,2,1,0:T(8,128)(2,1)S(1)}, bf16[2,1,128,512]{3,2,1,0:T(8,128)(2,1)S(1)}, u32[]{:S(2)}, u32[]{:S(2)}) collective-permute-start(bf16[2,1,128,512]{3,2,1,0:T(8,128)(2,1)S(1)} %dynamic-slice_convert_fusion), channel_id=1, source_target_pairs={{0,16},{16,0},{1,17},{17,1},{2,18},{18,2},{3,19},{19,3},{4,20},{20... | collective-permute-start | bytes 786440 | tf_op jit(solution)/shard_map/ppermute | solution.py:17
  207.0 20.0 %copy-start.2 = (f32[2048,256]{1,0:T(8,128)S(1)}, f32[2048,256]{1,0:T(8,128)}, u32[]{:S(2)}) copy-start(f32[2048,256]{1,0:T(8,128)} %copy-done.1) | copy-start | bytes 6291460
  215.5 1.3 copy-start.17
  229.8 9.7 %collective-permute-start.33 = (bf16[259,512]{1,0:T(8,128)(2,1)}, bf16[259,512]{1,0:T(8,128)(2,1)}, u32[]{:S(2)}, u32[]{:S(2)}) collective-permute-start(bf16[259,512]{1,0:T(8,128)(2,1)} %pad_maximum_fusion.9), channel_id=1, source_target_pairs={{0,4},{2,6},{4,0},{6,2},{8,12},{10,14},{12,8},{14,10},{1,5},{3,7},... | collective-permute-start | bytes 795656 | tf_op jit(solution)/shard_map/ppermute | solution.py:17
  231.3 23.4 %collective-permute-start.35 = (bf16[2,512,256]{2,1,0:T(8,128)(2,1)}, bf16[2,512,256]{2,1,0:T(8,128)(2,1)S(1)}, u32[]{:S(2)}, u32[]{:S(2)}) collective-permute-start(bf16[2,512,256]{2,1,0:T(8,128)(2,1)} %fusion.12), channel_id=1, source_target_pairs={{0,4},{2,6},{4,0},{6,2},{8,12},{10,14},{12,8},{14,10},{1,5},{3,7},... | collective-permute-start | bytes 1572872 | tf_op jit(solution)/shard_map/ppermute | solution.py:17
  241.3 13.2 %collective-permute-start.34 = (bf16[259,512]{1,0:T(8,128)(2,1)S(1)}, bf16[259,512]{1,0:T(8,128)(2,1)S(1)}, u32[]{:S(2)}, u32[]{:S(2)}) collective-permute-start(bf16[259,512]{1,0:T(8,128)(2,1)S(1)} %pad_maximum_fusion.10), channel_id=1, source_target_pairs={{0,8},{2,10},{4,12},{6,14},{8,0},{10,2},{12,4},{14,6},{1,9},{3,11}... | collective-permute-start | bytes 795656 | tf_op jit(solution)/shard_map/ppermute | solution.py:17
  254.7 2.3 copy-start.25
  257.0 16.8 %collective-permute-start.36 = (f32[385,512]{1,0:T(8,128)S(1)}, f32[385,512]{1,0:T(8,128)S(1)}, u32[]{:S(2)}, u32[]{:S(2)}) collective-permute-start(f32[385,512]{1,0:T(8,128)S(1)} %pad_maximum_fusion.5), channel_id=1, source_target_pairs={{0,1},{1,0},{2,3},{3,2},{4,5},{5,4},{6,7},{7,6},{8,9},{9,8},{10,11... | collective-permute-start | bytes 2365448 | tf_op jit(solution)/shard_map/ppermute | solution.py:17
  257.9 17.0 %collective-permute-start.37 = (bf16[2,512,256]{2,1,0:T(8,128)(2,1)S(1)}, bf16[2,512,256]{2,1,0:T(8,128)(2,1)S(1)}, u32[]{:S(2)}, u32[]{:S(2)}) collective-permute-start(bf16[2,512,256]{2,1,0:T(8,128)(2,1)S(1)} %copy-done.22), channel_id=1, source_target_pairs={{0,4},{2,6},{4,0},{6,2},{8,12},{10,14},{12,8},{14,10},{1,5},{3,7},... | collective-permute-start | bytes 1572872 | tf_op jit(solution)/shard_map/ppermute | solution.py:17
  274.0 13.4 %copy-start.18 = (bf16[384,512]{1,0:T(8,128)(2,1)}, bf16[384,512]{1,0:T(8,128)(2,1)S(1)}, u32[]{:S(2)}) copy-start(bf16[384,512]{1,0:T(8,128)(2,1)S(1)} %slice.140) | copy-start | bytes 1179652
  278.2 8.2 %collective-permute-start.38 = (bf16[387,512]{1,0:T(8,128)(2,1)}, bf16[387,512]{1,0:T(8,128)(2,1)}, u32[]{:S(2)}, u32[]{:S(2)}) collective-permute-start(bf16[387,512]{1,0:T(8,128)(2,1)} %pad_maximum_fusion.8), channel_id=1, source_target_pairs={{0,16},{16,0},{1,17},{17,1},{2,18},{18,2},{3,19},{19,3},{4,20},{20... | collective-permute-start | bytes 1188872 | tf_op jit(solution)/shard_map/ppermute | solution.py:17
  278.2 11.6 %collective-permute-start.39 = (bf16[1,512,256]{2,1,0:T(8,128)(2,1)}, bf16[1,512,256]{2,1,0:T(8,128)(2,1)}, u32[]{:S(2)}, u32[]{:S(2)}) collective-permute-start(bf16[1,512,256]{2,1,0:T(8,128)(2,1)} %fusion.25), channel_id=1, source_target_pairs={{0,8},{2,10},{4,12},{6,14},{8,0},{10,2},{12,4},{14,6},{1,9},{3,11}... | collective-permute-start | bytes 786440 | tf_op jit(solution)/shard_map/ppermute | solution.py:17
  294.4 16.6 %collective-permute-start.41 = (bf16[771,512]{1,0:T(8,128)(2,1)}, bf16[771,512]{1,0:T(8,128)(2,1)}, u32[]{:S(2)}, u32[]{:S(2)}) collective-permute-start(bf16[771,512]{1,0:T(8,128)(2,1)} %pad_maximum_fusion.6), channel_id=1, source_target_pairs={{0,2},{2,0},{4,6},{6,4},{8,10},{10,8},{12,14},{14,12},{1,3},{3,1},... | collective-permute-start | bytes 2368520 | tf_op jit(solution)/shard_map/ppermute | solution.py:17
  294.4 15.4 %collective-permute-start.40 = (bf16[1,512,256]{2,1,0:T(8,128)(2,1)}, bf16[1,512,256]{2,1,0:T(8,128)(2,1)S(1)}, u32[]{:S(2)}, u32[]{:S(2)}) collective-permute-start(bf16[1,512,256]{2,1,0:T(8,128)(2,1)} %fusion.26), channel_id=1, source_target_pairs={{0,8},{2,10},{4,12},{6,14},{8,0},{10,2},{12,4},{14,6},{1,9},{3,11}... | collective-permute-start | bytes 786440 | tf_op jit(solution)/shard_map/ppermute | solution.py:17
  313.1 1.0 copy-start.20
  (8 other events, 7.0 us)

commit v9 on v7

--- a/solution.py
+++ b/solution.py
@@ -9,7 +9,7 @@
 
 CORES = 2
 SLICES = 4
-PARTS = ((0, 0, 1, 1), (0, 1, 1, 1), (1, 0, 2, 2))
+PARTS = ((0, 0, 2, 1), (1, 0, 2, 2))
 
 
 def swap(x, axis, mask):
@@ -48,7 +48,7 @@
     while x.shape[axis] > 1:
         size = x.shape[axis]
         if size == 2 and before_last is not None:
-            x = after(x, before_last())
+            x = before_last(x)
         pairs = x.reshape(x.shape[:axis] + (size // 2, 2) + x.shape[axis + 1:])
         low = (index >> bit) & 1
         send = pick(pairs, 1 - low, axis + 1).astype(kind)
@@ -262,22 +262,16 @@
             factor.append(jnp.where(mine, own[part][start:start + x.shape[0]], x))
             start += x.shape[0]
         factor = jnp.concatenate(factor)
-        received, arrived = {}, [[] for _ in range(pieces)]
-        for d in dests:
-            if d == 0:
-                token += tuple(unit.step() for unit in units[:-1] if not unit.done())
-            away = product(inverse, masks[k], factor, place(1 - core, d, *token), weights, sizes)
-            token = (away[0],)
-            received[d] = [swap_core(x) for x in away]
+        arrived = [[] for _ in range(pieces)]
         term = jnp.zeros((width, wide), jnp.float32)
         for d in dests:
             if d == 0:
-                done = [unit for unit in units if unit.done()]
                 token += tuple(unit.step() for unit in units if not unit.done())
-                for unit in done:
-                    unit.total, *token = lax.optimization_barrier((unit.result(), *token))
+            away = product(inverse, masks[k], factor, place(1 - core, d, *token), weights, sizes)
+            token = (away[0],)
+            received = [swap_core(x) for x in away]
             kind = jnp.bfloat16 if d > 0 else jnp.float32
-            merge = (received[d], panels[k], term, kind, pieces)
+            merge = (received, panels[k], term, kind, pieces)
             *out, term = product(inverse, masks[k], factor, place(core, d, *token), weights, sizes, merge)
             token = (out[0],)
             if d > 0:
@@ -291,18 +285,25 @@
             units.append(ZSum([x.reshape(zs, block, x.shape[1]) for x in [kept] + arrived[n]], z))
 
     *zeros, early, last = units
+
+    def arrivals(x):
+        x = after(x, last.step())
+        while not early.done():
+            x = after(x, early.step())
+        for unit in zeros:
+            x, unit.total = lax.optimization_barrier((x, unit.result()))
+        return x
+
     each = width // (n_row * blocks)
     split = (2, n_row, zs, CORES, n_pole, each, width)
     term = jnp.stack([jnp.concatenate(t, axis=1) for t in terms]).reshape(split)
-    term = halve(term, 3, core, swap_core, jnp.bfloat16)
     term = after(term, early.step(*token))
     for unit in zeros:
         while not unit.done():
             term = after(term, unit.step())
+    term = halve(term, 3, core, swap_core, jnp.bfloat16)
     term = halve(term, 1, row, swap_row, jnp.bfloat16)
-    term = halve(term, 1, z, swap_z, jnp.bfloat16, last.step)
-    while not early.done():
-        term = after(term, early.step(term))
+    term = halve(term, 1, z, swap_z, jnp.bfloat16, arrivals)
     base = pick(pick(pick(diag_inverse.reshape(split), core, 3), row, 1), z, 1).astype(jnp.float32) * weight
     both = halve(jnp.stack([base, term]), 2, pole, swap_pole, jnp.float32)
     base, term = both[0], both[1]
@@ -313,11 +314,11 @@
     squares = jnp.sum(first * first, axis=0)
     for bit in reversed(range(n_pole.bit_length() - 1)):
         piece, squares = double(piece, squares, 4, pole, bit, swap_pole)
+    piece, second = lax.optimization_barrier((piece, early.result(piece)))
     for bit in reversed(range(zs.bit_length() - 1)):
-        piece, squares = double(piece, squares, 2, z, bit, swap_z)
         if not last.done():
             piece = after(piece, last.step(piece))
-    piece, second = lax.optimization_barrier((piece, early.result(piece)))
+        piece, squares = double(piece, squares, 2, z, bit, swap_z)
     for bit in reversed(range(n_row.bit_length() - 1)):
         piece, squares = double(piece, squares, 1, row, bit, swap_row)
     while not last.done():

time: 290 us -> 297 us (1.024)
  waiting for transfers between devices: 84.4 us -> 119 us
  Pallas kernels: 95.7 us -> 72.7 us
  starting transfers between devices: 46.7 us -> 40.6 us
  local copies, waits for them, and re-layouts: 20.3 us -> 25.3 us
  other arithmetic: 38.9 us -> 35.8 us
    ppermute x34 -> x32, waiting for transfers between devices: 57.3 us -> 83 us  [swap(): return lax.ppermute(x, axis, [(i, i ^ mask) for i in range(size)])]
    pallas_call x12 -> x8, Pallas kernels: 95.7 us -> 72.7 us  [product(): pl.pallas_call(kernel, out_shape=out_shape, grid_spec=pltpu.PrefetchScala...]
    ppermute x5 -> x3, starting transfers between devices: 19.2 us -> 11.8 us  [cross(): arrived = lax.ppermute(x, ('row', 'col'), pairs)]
    ppermute x34 -> x32, starting transfers between devices: 15.9 us -> 22.7 us  [swap(): return lax.ppermute(x, axis, [(i, i ^ mask) for i in range(size)])]
    ppermute x2 -> x1, starting transfers between devices: 6.41 us -> 1.55 us  [fetch_factor(): lax.ppermute(crossed, 'col', [(j, mirror(j)) for j in range(n_col)])]
    ppermute x2 -> x1, waiting for transfers between devices: 4.79 us -> 8.38 us  [fetch_factor(): lax.ppermute(crossed, 'col', [(j, mirror(j)) for j in range(n_col)])]
    ppermute x5 -> x3, waiting for transfers between devices: 12.7 us -> 15.6 us  [cross(): arrived = lax.ppermute(x, ('row', 'col'), pairs)]
    unnamed x66 -> x58, local copies, waits for them, and re-layouts: 11.7 us -> 14.4 us
  transfers between devices with their start and end apart: 45 -> 39, of which waited for: 19 -> 29; matrix products, arithmetic and copies ran while one was open for 11% -> 10% of each run, Pallas kernels for 33% -> 18%
where the time goes in v9:
time: 297 us; the launch traced here: 296 us
  waiting for transfers between devices  119 us (40%)
  Pallas kernels  72.7 us (24%)
  starting transfers between devices  40.6 us (14%)
  other arithmetic  35.8 us (12%)
  local copies, waits for them, and re-layouts  25.3 us (9%)
    ppermute x32, waiting for transfers between devices, swap(): return lax.ppermute(x, axis, [(i, i ^ mask) for i in range(size)])  83 us
    pallas_call x8, Pallas kernels, product(): pl.pallas_call(kernel, out_shape=out_shape, grid_spec=pltpu.PrefetchScala...  72.7 us
    ppermute x32, starting transfers between devices, swap(): return lax.ppermute(x, axis, [(i, i ^ mask) for i in range(size)])  22.7 us
    ppermute x3, waiting for transfers between devices, cross(): arrived = lax.ppermute(x, ('row', 'col'), pairs)  15.6 us
    unnamed x58, local copies, waits for them, and re-layouts  14.4 us
    convert_element_type x6, other arithmetic, step(): send = self.part(1, *deps).astype(jnp.bfloat16)  13.5 us
    ppermute x3, waiting for transfers between devices, body(): lax.ppermute(after(x, *before), 'pole', [(i, (i + d) % n_pole) for i in r...  12.3 us
    ppermute x3, starting transfers between devices, cross(): arrived = lax.ppermute(x, ('row', 'col'), pairs)  11.8 us
  transfers between devices with their start and end apart: 39, of which 29 were waited for; matrix products, arithmetic and copies ran while one was open for 10% of the time, Pallas kernels for 18%

profile of v9, /device:TPU:0, one launch (start us, length us, event | category | flops | bytes accessed | tf_op | source)
XLA Modules:
  0.0 295.7 jit_solution(5379888702996237092)
XLA Ops:
  0.7 2.7 dynamic-slice_bitcast_fusion.1
  3.3 4.9 %collective-permute-start = (bf16[1536,512]{1,0:T(8,128)(2,1)}, bf16[1536,512]{1,0:T(8,128)(2,1)S(1)}, u32[]{:S(2)}, u32[]{:S(2)}) collective-permute-start(bf16[1536,512]{1,0:T(8,128)(2,1)} %dynamic-slice_bitcast_fusion.1), channel_id=1, source_target_pairs={{0,16},{2,18},{4,20},{6,22},{24,8},{26,10},{28,12},{30,14},{1,17},... | collective-permute-start | bytes 4718600 | tf_op jit(solution)/shard_map/ppermute | solution.py:207
  8.3 1.1 dynamic-slice_bitcast_fusion.3
  9.4 1.3 collective-permute-start.1
  10.7 14.0 %collective-permute-done.1 = bf16[512,512]{1,0:T(8,128)(2,1)} collective-permute-done((bf16[512,512]{1,0:T(8,128)(2,1)S(1)}, bf16[512,512]{1,0:T(8,128)(2,1)}, u32[]{:S(2)}, u32[]{:S(2)}) %collective-permute-start.1) | collective-permute-done | bytes 524320 | tf_op jit(solution)/shard_map/ppermute | solution.py:207
  24.8 1.6 collective-permute-start.2
  27.9 3.1 %dynamic-slice_bitcast_fusion = bf16[2048,512]{1,0:T(8,128)(2,1)} fusion(bf16[1,8192,512]{2,1,0:T(8,128)(2,1)} %param.9, s32[]{:T(128)S(6)} %select_n.298), kind=kLoop, calls=%fused_computation.5 | loop fusion | bytes 4194308 | tf_op jit(solution)/shard_map/dynamic_slice | solution.py:212
  31.0 8.4 %collective-permute-done.2 = bf16[512,512]{1,0:T(8,128)(2,1)S(1)} collective-permute-done((bf16[512,512]{1,0:T(8,128)(2,1)}, bf16[512,512]{1,0:T(8,128)(2,1)S(1)}, u32[]{:S(2)}, u32[]{:S(2)}) %collective-permute-start.2) | collective-permute-done | bytes 524320 | tf_op jit(solution)/shard_map/ppermute | solution.py:217
  39.4 1.2 fusion.11
  40.5 1.6 collective-permute-done
  42.1 5.6 %collective-permute-start.11 = (bf16[2048,512]{1,0:T(8,128)(2,1)}, bf16[2048,512]{1,0:T(8,128)(2,1)}, u32[]{:S(2)}, u32[]{:S(2)}) collective-permute-start(bf16[2048,512]{1,0:T(8,128)(2,1)} %dynamic-slice_bitcast_fusion), channel_id=1, source_target_pairs={{0,16},{2,18},{4,20},{6,22},{24,8},{26,10},{28,12},{30,14},{1,17},... | collective-permute-start | bytes 6291464 | tf_op jit(solution)/shard_map/ppermute | solution.py:207
  47.7 1.8 broadcast_select_fusion.1
  49.7 8.7 %shard_map.77 = (bf16[2048,128]{1,0:T(8,128)(2,1)}, bf16[2048,128]{1,0:T(8,128)(2,1)}, bf16[2048,128]{1,0:T(8,128)(2,1)}, bf16[2048,128]{1,0:T(8,128)(2,1)}) custom-call(s32[2]{0:T(128)S(1)} %pad_add_fusion.3.where_ref, f32[1]{0:T(128)} %copy.96.weight_ref, bf16[8192,2048]{1,0:T(8,128)(2,1)} %bitcast.149, bf16[16,4,2048]{2,1,0:T(4,128)(2,1)S(1)} %reshape_reshape.55.mask_ref, ...), custom_call_target="tpu_custom_call" | custom-call | flops 8388608 | bytes 1048576 | tf_op jit(solution)/shard_map/pallas_call | solution.py:179
  63.9 1.0 copy-done.14
  65.0 1.0 copy-done.16
  66.0 10.3 %shard_map.78 = (bf16[2048,512]{1,0:T(8,128)(2,1)}, f32[512,512]{1,0:T(8,128)S(1)}) custom-call(s32[2]{0:T(128)S(1)} %get-tuple-element.90.where_ref, f32[1]{0:T(128)} %copy.96.weight_ref, bf16[8192,2048]{1,0:T(8,128)(2,1)} %bitcast.150, bf16[16,4,2048]{2,1,0:T(4,128)(2,1)S(1)} %copy-done.1, bf16[2048,512]{1,0:T(8,128)(2,1)S(1)} %pad_maximum_fusion.f_ref, ...), custom_call_target="tpu_custom_call" | custom-call | flops 8388608 | bytes 1048576 | tf_op jit(solution)/shard_map/pallas_call | solution.py:179
  76.3 1.5 collective-permute-start.16
  77.9 7.6 %shard_map.79 = (bf16[2048,128]{1,0:T(8,128)(2,1)S(1)}, bf16[2048,128]{1,0:T(8,128)(2,1)S(1)}, bf16[2048,128]{1,0:T(8,128)(2,1)S(1)}, bf16[2048,128]{1,0:T(8,128)(2,1)S(1)}) custom-call(s32[2]{0:T(128)S(1)} %pad_add_fusion.where_ref, f32[1]{0:T(128)} %copy.96.weight_ref, bf16[8192,2048]{1,0:T(8,128)(2,1)} %bitcast.151, bf16[16,4,2048]{2,1,0:T(4,128)(2,1)S(1)} %copy-done.2, ...), custom_call_target="tpu_custom_call" | custom-call | flops 8388608 | bytes 1048576 | tf_op jit(solution)/shard_map/pallas_call | solution.py:179
  86.2 1.3 collective-permute-done.10.refs_3_
  89.8 9.1 %shard_map.80 = (f32[2048,512]{1,0:T(8,128)S(1)}, f32[512,512]{1,0:T(8,128)S(1)}) custom-call(s32[2]{0:T(128)S(1)} %get-tuple-element.97.where_ref, f32[1]{0:T(128)} %copy.96.weight_ref, bf16[8192,2048]{1,0:T(8,128)(2,1)} %bitcast.152, bf16[16,4,2048]{2,1,0:T(4,128)(2,1)S(1)} %copy-done.2, bf16[2048,512]{1,0:T(8,128)(2,1)S(1)} %pad_maximum_fusion.f_ref, ...), custom_call_target="tpu_custom_call" | custom-call | flops 8388608 | bytes 1048576 | tf_op jit(solution)/shard_map/pallas_call | solution.py:179
  98.9 2.0 copy-done.3
  100.9 2.6 broadcast_select_fusion.f_ref
  103.4 8.7 %shard_map.81 = (bf16[2048,128]{1,0:T(8,128)(2,1)}, bf16[2048,128]{1,0:T(8,128)(2,1)}, bf16[2048,128]{1,0:T(8,128)(2,1)}, bf16[2048,128]{1,0:T(8,128)(2,1)}) custom-call(s32[2]{0:T(128)S(1)} %pad_add_fusion.3.where_ref, f32[1]{0:T(128)} %copy.96.weight_ref, bf16[8192,2048]{1,0:T(8,128)(2,1)} %bitcast.153, bf16[16,4,2048]{2,1,0:T(4,128)(2,1)S(1)} %reshape_reshape.56.mask_ref, ...), custom_call_target="tpu_custom_call" | custom-call | flops 8388608 | bytes 1048576 | tf_op jit(solution)/shard_map/pallas_call | solution.py:179
  113.2 11.2 %collective-permute-done.16 = bf16[2048,512]{1,0:T(8,128)(2,1)} collective-permute-done((bf16[2048,512]{1,0:T(8,128)(2,1)}, bf16[2048,512]{1,0:T(8,128)(2,1)}, u32[]{:S(2)}, u32[]{:S(2)}) %collective-permute-start.16) | collective-permute-done | bytes 2097184 | tf_op jit(solution)/shard_map/ppermute | solution.py:280
  124.3 3.2 %fusion.2 = bf16[2,512,512]{2,1,0:T(8,128)(2,1)} fusion(f32[2,2,512,512]{3,2,1,0:T(8,128)} %bitcast.138, s32[]{:T(128)S(6)} %select_n.306, bf16[2,2,512,512]{3,2,1,0:T(8,128)(2,1)} %bitcast.18), kind=kLoop, calls=%fused_computation.11 | loop fusion | flops 1572864 | bytes 4194308 | tf_op jit(solution)/shard_map/convert_element_type | solution.py:98
  127.5 10.2 %shard_map.82 = (bf16[2048,256]{1,0:T(8,128)(2,1)}, bf16[2048,256]{1,0:T(8,128)(2,1)S(1)}, f32[512,512]{1,0:T(8,128)S(1)}) custom-call(s32[2]{0:T(128)S(1)} %get-tuple-element.90.where_ref, f32[1]{0:T(128)} %copy.96.weight_ref, bf16[8192,2048]{1,0:T(8,128)(2,1)} %bitcast.154, bf16[16,4,2048]{2,1,0:T(4,128)(2,1)S(1)} %reshape_reshape.56.mask_ref, ...), custom_call_target="tpu_custom_call" | custom-call | flops 8388608 | bytes 1048576 | tf_op jit(solution)/shard_map/pallas_call | solution.py:179
  138.7 1.0 copy-done.17
  139.7 8.5 %shard_map.83 = (bf16[2048,128]{1,0:T(8,128)(2,1)S(1)}, bf16[2048,128]{1,0:T(8,128)(2,1)}, bf16[2048,128]{1,0:T(8,128)(2,1)}, bf16[2048,128]{1,0:T(8,128)(2,1)}) custom-call(s32[2]{0:T(128)S(1)} %pad_add_fusion.where_ref, f32[1]{0:T(128)} %copy.96.weight_ref, bf16[8192,2048]{1,0:T(8,128)(2,1)} %bitcast.155, ...), custom_call_target="tpu_custom_call" | custom-call | flops 8388608 | bytes 1048576 | tf_op jit(solution)/shard_map/pallas_call | solution.py:179
  148.3 1.5 collective-permute-start.21
  149.8 7.3 %collective-permute-start.22 = (bf16[2,512,512]{2,1,0:T(8,128)(2,1)}, bf16[2,512,512]{2,1,0:T(8,128)(2,1)}, u32[]{:S(2)}, u32[]{:S(2)}) collective-permute-start(bf16[2,512,512]{2,1,0:T(8,128)(2,1)} %fusion.2), channel_id=1, source_target_pairs={{0,4},{2,6},{4,0},{6,2},{8,12},{10,14},{12,8},{14,10},{1,5},{3,7},... | collective-permute-start | bytes 3145736 | tf_op jit(solution)/shard_map/ppermute | solution.py:17
  160.9 1.0 copy-done.12
  162.0 9.6 %shard_map.84 = (f32[2048,256]{1,0:T(8,128)S(1)}, f32[2048,256]{1,0:T(8,128)S(1)}, f32[512,512]{1,0:T(8,128)S(1)}) custom-call(s32[2]{0:T(128)S(1)} %get-tuple-element.97.where_ref, f32[1]{0:T(128)} %copy.96.weight_ref, bf16[8192,2048]{1,0:T(8,128)(2,1)} %bitcast.156, bf16[16,4,2048]{2,1,0:T(4,128)(2,1)S(1)} %reshape_reshape.56.mask_ref, ...), custom_call_target="tpu_custom_call" | custom-call | flops 8388608 | bytes 1048576 | tf_op jit(solution)/shard_map/pallas_call | solution.py:179
  173.1 1.1 collective-permute-done.21
  174.2 2.0 fusion.9
  176.1 4.9 %collective-permute-done.22 = bf16[2,512,512]{2,1,0:T(8,128)(2,1)} collective-permute-done((bf16[2,512,512]{2,1,0:T(8,128)(2,1)}, bf16[2,512,512]{2,1,0:T(8,128)(2,1)}, u32[]{:S(2)}, u32[]{:S(2)}) %collective-permute-start.22) | collective-permute-done | bytes 1048608 | tf_op jit(solution)/shard_map/ppermute | solution.py:17
  181.0 2.5 fusion.8
  184.4 2.2 collective-permute-done.23
  186.7 1.3 convert_add_fusion
  188.1 3.8 %collective-permute-start.28 = (bf16[1,512,512]{2,1,0:T(8,128)(2,1)}, bf16[1,512,512]{2,1,0:T(8,128)(2,1)}, u32[]{:S(2)}, u32[]{:S(2)}) collective-permute-start(bf16[1,512,512]{2,1,0:T(8,128)(2,1)} %fusion.8), channel_id=1, source_target_pairs={{0,8},{2,10},{4,12},{6,14},{8,0},{10,2},{12,4},{14,6},{1,9},{3,11}... | collective-permute-start | bytes 1572872 | tf_op jit(solution)/shard_map/ppermute | solution.py:17
  191.9 1.5 collective-permute-start.26
  193.5 3.0 %collective-permute-done.24 = bf16[2,1,4,2,16,512]{5,4,3,2,0,1:T(8,128)(2,1)S(1)} collective-permute-done((bf16[2,1,4,2,16,512]{5,4,3,2,0,1:T(8,128)(2,1)S(1)}, bf16[2,1,4,2,16,512]{5,4,3,2,0,1:T(8,128)(2,1)S(1)}, u32[]{:S(2)}, u32[]{:S(2)}) %collective-permute-start.24) | collective-permute-done | bytes 262176 | tf_op jit(solution)/shard_map/ppermute | solution.py:17
  196.4 1.1 bitcast_add_fusion.5
  197.6 2.5 collective-permute-start.25
  200.1 15.4 %collective-permute-done.28 = bf16[1,512,512]{2,1,0:T(8,128)(2,1)} collective-permute-done((bf16[1,512,512]{2,1,0:T(8,128)(2,1)}, bf16[1,512,512]{2,1,0:T(8,128)(2,1)}, u32[]{:S(2)}, u32[]{:S(2)}) %collective-permute-start.28) | collective-permute-done | bytes 524320 | tf_op jit(solution)/shard_map/ppermute | solution.py:17
  215.5 2.9 fusion.7
  218.4 2.1 fusion.12
  220.6 2.0 fusion.10
  223.6 4.3 %collective-permute-done.29 = bf16[2,1,2,16,512]{4,3,2,0,1:T(8,128)(2,1)S(1)} collective-permute-done((bf16[2,1,2,16,512]{4,3,2,0,1:T(8,128)(2,1)S(1)}, bf16[2,1,2,16,512]{4,3,2,0,1:T(8,128)(2,1)S(1)}, u32[]{:S(2)}, u32[]{:S(2)}) %collective-permute-start.29) | collective-permute-done | bytes 65568 | tf_op jit(solution)/shard_map/ppermute | solution.py:17
  228.0 1.6 collective-permute-start.30
  229.6 3.5 %collective-permute-done.30 = f32[2,2,1,16,512]{4,3,2,1,0:T(8,128)} collective-permute-done((f32[2,2,1,16,512]{4,3,2,1,0:T(8,128)S(1)}, f32[2,2,1,16,512]{4,3,2,1,0:T(8,128)}, u32[]{:S(2)}, u32[]{:S(2)}) %collective-permute-start.30) | collective-permute-done | bytes 131104 | tf_op jit(solution)/shard_map/ppermute | solution.py:17
  235.0 1.6 collective-permute-start.31
  236.6 2.7 collective-permute-done.31
  239.3 2.5 collective-permute-done.32
  241.8 2.2 add_bitcast_fusion.1
  244.0 8.6 %collective-permute-done.33 = bf16[2,512,256]{2,1,0:T(8,128)(2,1)S(1)} collective-permute-done((bf16[2,512,256]{2,1,0:T(8,128)(2,1)}, bf16[2,512,256]{2,1,0:T(8,128)(2,1)S(1)}, u32[]{:S(2)}, u32[]{:S(2)}) %collective-permute-start.33) | collective-permute-done | bytes 524320 | tf_op jit(solution)/shard_map/ppermute | solution.py:17
  253.4 1.7 fusion.14
  255.5 7.2 %collective-permute-done.34 = bf16[99,512]{1,0:T(8,128)(2,1)S(1)} collective-permute-done((bf16[99,512]{1,0:T(8,128)(2,1)S(1)}, bf16[99,512]{1,0:T(8,128)(2,1)S(1)}, u32[]{:S(2)}, u32[]{:S(2)}) %collective-permute-start.34) | collective-permute-done | bytes 101408 | tf_op jit(solution)/shard_map/ppermute | solution.py:17
  263.0 7.0 %collective-permute-done.35 = bf16[195,512]{1,0:T(8,128)(2,1)S(1)} collective-permute-done((bf16[195,512]{1,0:T(8,128)(2,1)S(1)}, bf16[195,512]{1,0:T(8,128)(2,1)S(1)}, u32[]{:S(2)}, u32[]{:S(2)}) %collective-permute-start.35) | collective-permute-done | bytes 199712 | tf_op jit(solution)/shard_map/ppermute | solution.py:17
  272.5 8.7 %collective-permute-done.36 = bf16[387,512]{1,0:T(8,128)(2,1)} collective-permute-done((bf16[387,512]{1,0:T(8,128)(2,1)S(1)}, bf16[387,512]{1,0:T(8,128)(2,1)}, u32[]{:S(2)}, u32[]{:S(2)}) %collective-permute-start.36) | collective-permute-done | bytes 396320 | tf_op jit(solution)/shard_map/ppermute | solution.py:17
  282.3 3.1 %collective-permute-done.37 = bf16[1,512,256]{2,1,0:T(8,128)(2,1)S(1)} collective-permute-done((bf16[1,512,256]{2,1,0:T(8,128)(2,1)}, bf16[1,512,256]{2,1,0:T(8,128)(2,1)S(1)}, u32[]{:S(2)}, u32[]{:S(2)}) %collective-permute-start.37) | collective-permute-done | bytes 262176 | tf_op jit(solution)/shard_map/ppermute | solution.py:17
  286.1 1.2 add_bitcast_fusion
  288.3 2.3 collective-permute-done.38
  293.1 1.5 pad_maximum_fusion.2
  294.6 1.1 pad_maximum_fusion.3
  (165 shorter events, 29.9 us)
Async XLA Ops:
  0.6 10.0 %copy-start.28 = (s32[2,64,16]{1,2,0:T(8,128)S(1)}, s32[2,64,16]{1,2,0:T(8,128)}, u32[]{:S(2)}) copy-start(s32[2,64,16]{1,2,0:T(8,128)} %param.7) | copy-start | bytes 24580
  3.3 38.8 %collective-permute-start = (bf16[1536,512]{1,0:T(8,128)(2,1)}, bf16[1536,512]{1,0:T(8,128)(2,1)S(1)}, u32[]{:S(2)}, u32[]{:S(2)}) collective-permute-start(bf16[1536,512]{1,0:T(8,128)(2,1)} %dynamic-slice_bitcast_fusion.1), channel_id=1, source_target_pairs={{0,16},{2,18},{4,20},{6,22},{24,8},{26,10},{28,12},{30,14},{1,17},... | collective-permute-start | bytes 4718600 | tf_op jit(solution)/shard_map/ppermute | solution.py:207
  9.4 15.4 %collective-permute-start.1 = (bf16[512,512]{1,0:T(8,128)(2,1)S(1)}, bf16[512,512]{1,0:T(8,128)(2,1)}, u32[]{:S(2)}, u32[]{:S(2)}) collective-permute-start(bf16[512,512]{1,0:T(8,128)(2,1)S(1)} %dynamic-slice_bitcast_fusion.3), channel_id=1, source_target_pairs={{12,28},{14,30},{8,24},{10,26},{20,4},{22,6},{16,0},{18,2},{13,29}... | collective-permute-start | bytes 1572872 | tf_op jit(solution)/shard_map/ppermute | solution.py:207
  24.8 14.6 %collective-permute-start.2 = (bf16[512,512]{1,0:T(8,128)(2,1)}, bf16[512,512]{1,0:T(8,128)(2,1)S(1)}, u32[]{:S(2)}, u32[]{:S(2)}) collective-permute-start(bf16[512,512]{1,0:T(8,128)(2,1)} %collective-permute-done.1), channel_id=1, source_target_pairs={{0,12},{2,14},{4,8},{6,10},{8,4},{10,6},{12,0},{14,2},{1,13},{3,15... | collective-permute-start | bytes 1572872 | tf_op jit(solution)/shard_map/ppermute | solution.py:217
  26.7 23.0 %copy-start = (bf16[16,4,2048]{2,1,0:T(4,128)(2,1)}, bf16[16,4,2048]{2,1,0:T(4,128)(2,1)S(1)}, u32[]{:S(2)}) copy-start(bf16[16,4,2048]{2,1,0:T(4,128)(2,1)S(1)} %reshape_reshape.55.mask_ref) | copy-start | bytes 786436
  42.1 58.8 %collective-permute-start.11 = (bf16[2048,512]{1,0:T(8,128)(2,1)}, bf16[2048,512]{1,0:T(8,128)(2,1)}, u32[]{:S(2)}, u32[]{:S(2)}) collective-permute-start(bf16[2048,512]{1,0:T(8,128)(2,1)} %dynamic-slice_bitcast_fusion), channel_id=1, source_target_pairs={{0,16},{2,18},{4,20},{6,22},{24,8},{26,10},{28,12},{30,14},{1,17},... | collective-permute-start | bytes 6291464 | tf_op jit(solution)/shard_map/ppermute | solution.py:207
  58.4 2.1 collective-permute-start.3
  58.4 3.6 %collective-permute-start.4 = (bf16[2048,128]{1,0:T(8,128)(2,1)}, bf16[2048,128]{1,0:T(8,128)(2,1)S(1)}, u32[]{:S(2)}, u32[]{:S(2)}) collective-permute-start(bf16[2048,128]{1,0:T(8,128)(2,1)} %get-tuple-element.73), channel_id=1, source_target_pairs={{0,2},{2,0},{4,6},{6,4},{8,10},{10,8},{12,14},{14,12},{1,3},{3,1},... | collective-permute-start | bytes 1572872 | tf_op jit(solution)/shard_map/ppermute | solution.py:17
  58.9 3.9 %collective-permute-start.5 = (bf16[2048,128]{1,0:T(8,128)(2,1)}, bf16[2048,128]{1,0:T(8,128)(2,1)}, u32[]{:S(2)}, u32[]{:S(2)}) collective-permute-start(bf16[2048,128]{1,0:T(8,128)(2,1)} %get-tuple-element.74), channel_id=1, source_target_pairs={{0,2},{2,0},{4,6},{6,4},{8,10},{10,8},{12,14},{14,12},{1,3},{3,1},... | collective-permute-start | bytes 1572872 | tf_op jit(solution)/shard_map/ppermute | solution.py:17
  58.9 4.0 %collective-permute-start.6 = (bf16[2048,128]{1,0:T(8,128)(2,1)}, bf16[2048,128]{1,0:T(8,128)(2,1)}, u32[]{:S(2)}, u32[]{:S(2)}) collective-permute-start(bf16[2048,128]{1,0:T(8,128)(2,1)} %get-tuple-element.75), channel_id=1, source_target_pairs={{0,2},{2,0},{4,6},{6,4},{8,10},{10,8},{12,14},{14,12},{1,3},{3,1},... | collective-permute-start | bytes 1572872 | tf_op jit(solution)/shard_map/ppermute | solution.py:17
  60.5 0.8 copy-start.13
  63.0 1.0 copy-start.1
  63.9 1.0 copy-start.14
  65.0 1.0 copy-start.16
  66.0 11.9 %copy-start.2 = (bf16[16,4,2048]{2,1,0:T(4,128)(2,1)S(1)}, bf16[16,4,2048]{2,1,0:T(4,128)(2,1)}, u32[]{:S(2)}) copy-start(bf16[16,4,2048]{2,1,0:T(4,128)(2,1)} %copy-done) | copy-start | bytes 786436
  76.3 48.0 %collective-permute-start.16 = (bf16[2048,512]{1,0:T(8,128)(2,1)}, bf16[2048,512]{1,0:T(8,128)(2,1)}, u32[]{:S(2)}, u32[]{:S(2)}) collective-permute-start(bf16[2048,512]{1,0:T(8,128)(2,1)} %get-tuple-element.76), channel_id=1, source_target_pairs={{0,1},{1,0},{2,3},{3,2},{4,5},{5,4},{6,7},{7,6},{8,9},{9,8},{10,11... | collective-permute-start | bytes 6291464 | tf_op jit(solution)/shard_map/ppermute | solution.py:280
  85.6 2.0 collective-permute-start.10
  85.6 2.6 collective-permute-start.7
  86.1 2.9 collective-permute-start.8
  87.5 2.2 collective-permute-start.9
  98.9 2.0 copy-start.3
  100.9 2.6 copy-start.9
  112.1 15.4 %collective-permute-start.12 = (bf16[2048,128]{1,0:T(8,128)(2,1)}, bf16[2048,128]{1,0:T(8,128)(2,1)}, u32[]{:S(2)}, u32[]{:S(2)}) collective-permute-start(bf16[2048,128]{1,0:T(8,128)(2,1)} %get-tuple-element.89), channel_id=1, source_target_pairs={{0,2},{2,0},{4,6},{6,4},{8,10},{10,8},{12,14},{14,12},{1,3},{3,1},... | collective-permute-start | bytes 1572872 | tf_op jit(solution)/shard_map/ppermute | solution.py:17
  112.3 15.2 %collective-permute-start.13 = (bf16[2048,128]{1,0:T(8,128)(2,1)}, bf16[2048,128]{1,0:T(8,128)(2,1)}, u32[]{:S(2)}, u32[]{:S(2)}) collective-permute-start(bf16[2048,128]{1,0:T(8,128)(2,1)} %get-tuple-element.91), channel_id=1, source_target_pairs={{0,2},{2,0},{4,6},{6,4},{8,10},{10,8},{12,14},{14,12},{1,3},{3,1},... | collective-permute-start | bytes 1572872 | tf_op jit(solution)/shard_map/ppermute | solution.py:17
  112.7 14.9 %collective-permute-start.14 = (bf16[2048,128]{1,0:T(8,128)(2,1)}, bf16[2048,128]{1,0:T(8,128)(2,1)}, u32[]{:S(2)}, u32[]{:S(2)}) collective-permute-start(bf16[2048,128]{1,0:T(8,128)(2,1)} %get-tuple-element.92), channel_id=1, source_target_pairs={{0,2},{2,0},{4,6},{6,4},{8,10},{10,8},{12,14},{14,12},{1,3},{3,1},... | collective-permute-start | bytes 1572872 | tf_op jit(solution)/shard_map/ppermute | solution.py:17
  112.8 14.7 %collective-permute-start.15 = (bf16[2048,128]{1,0:T(8,128)(2,1)}, bf16[2048,128]{1,0:T(8,128)(2,1)}, u32[]{:S(2)}, u32[]{:S(2)}) collective-permute-start(bf16[2048,128]{1,0:T(8,128)(2,1)} %get-tuple-element.93), channel_id=1, source_target_pairs={{0,2},{2,0},{4,6},{6,4},{8,10},{10,8},{12,14},{14,12},{1,3},{3,1},... | collective-permute-start | bytes 1572872 | tf_op jit(solution)/shard_map/ppermute | solution.py:17
  137.7 1.0 copy-start.7
  138.7 1.0 copy-start.17
  139.7 21.2 %copy-start.8 = (f32[512,512]{1,0:T(8,128)S(1)}, f32[512,512]{1,0:T(8,128)}, u32[]{:S(2)}) copy-start(f32[512,512]{1,0:T(8,128)} %copy-done.7) | copy-start | bytes 3145732
  148.3 9.4 %collective-permute-start.17 = (bf16[2048,128]{1,0:T(8,128)(2,1)S(1)}, bf16[2048,128]{1,0:T(8,128)(2,1)S(1)}, u32[]{:S(2)}, u32[]{:S(2)}) collective-permute-start(bf16[2048,128]{1,0:T(8,128)(2,1)S(1)} %get-tuple-element.96), channel_id=1, source_target_pairs={{0,2},{2,0},{4,6},{6,4},{8,10},{10,8},{12,14},{14,12},{1,3},{3,1},... | collective-permute-start | bytes 1572872 | tf_op jit(solution)/shard_map/ppermute | solution.py:17
  148.3 25.9 %collective-permute-start.21 = (bf16[2048,256]{1,0:T(8,128)(2,1)}, bf16[2048,256]{1,0:T(8,128)(2,1)}, u32[]{:S(2)}, u32[]{:S(2)}) collective-permute-start(bf16[2048,256]{1,0:T(8,128)(2,1)} %get-tuple-element.94), channel_id=1, source_target_pairs={{0,1},{1,0},{2,3},{3,2},{4,5},{5,4},{6,7},{7,6},{8,9},{9,8},{10,11... | collective-permute-start | bytes 3145736 | tf_op jit(solution)/shard_map/ppermute | solution.py:280
  149.8 31.2 %collective-permute-start.22 = (bf16[2,512,512]{2,1,0:T(8,128)(2,1)}, bf16[2,512,512]{2,1,0:T(8,128)(2,1)}, u32[]{:S(2)}, u32[]{:S(2)}) collective-permute-start(bf16[2,512,512]{2,1,0:T(8,128)(2,1)} %fusion.2), channel_id=1, source_target_pairs={{0,4},{2,6},{4,0},{6,2},{8,12},{10,14},{12,8},{14,10},{1,5},{3,7},... | collective-permute-start | bytes 3145736 | tf_op jit(solution)/shard_map/ppermute | solution.py:17
  157.2 2.3 collective-permute-start.18
  157.2 3.0 %collective-permute-start.19 = (bf16[2048,128]{1,0:T(8,128)(2,1)}, bf16[2048,128]{1,0:T(8,128)(2,1)}, u32[]{:S(2)}, u32[]{:S(2)}) collective-permute-start(bf16[2048,128]{1,0:T(8,128)(2,1)} %get-tuple-element.100), channel_id=1, source_target_pairs={{0,2},{2,0},{4,6},{6,4},{8,10},{10,8},{12,14},{14,12},{1,3},{3,1},... | collective-permute-start | bytes 1572872 | tf_op jit(solution)/shard_map/ppermute | solution.py:17
  157.7 0.8 copy-start.11
  158.5 2.4 collective-permute-start.20
  160.9 1.0 copy-start.12
  162.0 9.6 %copy-start.10 = (f32[512,512]{1,0:T(8,128)S(1)}, f32[512,512]{1,0:T(8,128)}, u32[]{:S(2)}) copy-start(f32[512,512]{1,0:T(8,128)} %copy-done.9) | copy-start | bytes 3145732
  171.6 1.3 copy-start.4
  171.6 2.6 copy-start.6
  183.6 8.4 %copy-start.18 = (bf16[2048,256]{1,0:T(8,128)(2,1)S(1)}, bf16[2048,256]{1,0:T(8,128)(2,1)}, u32[]{:S(2)}) copy-start(bf16[2048,256]{1,0:T(8,128)(2,1)} %copy-done.17) | copy-start | bytes 3145732
  184.4 2.3 collective-permute-start.23
  188.0 4.0 %copy-start.20 = (f32[2,2,4,1,2,16,512]{6,5,4,2,0,3,1:T(8,128)}, f32[2,2,4,1,2,16,512]{6,5,4,2,0,3,1:T(8,128)S(1)}, u32[]{:S(2)}) copy-start(f32[2,2,4,1,2,16,512]{6,5,4,2,0,3,1:T(8,128)S(1)} %convert_add_fusion) | copy-start | bytes 3145732
  188.0 8.4 %collective-permute-start.24 = (bf16[2,1,4,2,16,512]{5,4,3,2,0,1:T(8,128)(2,1)S(1)}, bf16[2,1,4,2,16,512]{5,4,3,2,0,1:T(8,128)(2,1)S(1)}, u32[]{:S(2)}, u32[]{:S(2)}) collective-permute-start(bf16[2,1,4,2,16,512]{5,4,3,2,0,1:T(8,128)(2,1)S(1)} %fusion.13), channel_id=1, source_target_pairs={{0,16},{16,0},{1,17},{17,1},{2,18},{18,2},{3,19},{19,3},{4,20},{20... | collective-permute-start | bytes 786440 | tf_op jit(solution)/shard_map/ppermute | solution.py:17
  188.1 27.4 %collective-permute-start.28 = (bf16[1,512,512]{2,1,0:T(8,128)(2,1)}, bf16[1,512,512]{2,1,0:T(8,128)(2,1)}, u32[]{:S(2)}, u32[]{:S(2)}) collective-permute-start(bf16[1,512,512]{2,1,0:T(8,128)(2,1)} %fusion.8), channel_id=1, source_target_pairs={{0,8},{2,10},{4,12},{6,14},{8,0},{10,2},{12,4},{14,6},{1,9},{3,11}... | collective-permute-start | bytes 1572872 | tf_op jit(solution)/shard_map/ppermute | solution.py:17
  191.9 28.6 %collective-permute-start.26 = (bf16[2048,256]{1,0:T(8,128)(2,1)S(1)}, bf16[2048,256]{1,0:T(8,128)(2,1)}, u32[]{:S(2)}, u32[]{:S(2)}) collective-permute-start(bf16[2048,256]{1,0:T(8,128)(2,1)S(1)} %copy-done.18), channel_id=1, source_target_pairs={{0,1},{1,0},{2,3},{3,2},{4,5},{5,4},{6,7},{7,6},{8,9},{9,8},{10,11... | collective-permute-start | bytes 3145736 | tf_op jit(solution)/shard_map/ppermute | solution.py:280
  193.5 25.0 %collective-permute-start.27 = (bf16[2,512,256]{2,1,0:T(8,128)(2,1)}, bf16[2,512,256]{2,1,0:T(8,128)(2,1)S(1)}, u32[]{:S(2)}, u32[]{:S(2)}) collective-permute-start(bf16[2,512,256]{2,1,0:T(8,128)(2,1)} %fusion.9), channel_id=1, source_target_pairs={{0,4},{2,6},{4,0},{6,2},{8,12},{10,14},{12,8},{14,10},{1,5},{3,7},... | collective-permute-start | bytes 1572872 | tf_op jit(solution)/shard_map/ppermute | solution.py:17
  197.6 23.0 %copy-start.5 = (f32[2048,256]{1,0:T(8,128)S(1)}, f32[2048,256]{1,0:T(8,128)}, u32[]{:S(2)}) copy-start(f32[2048,256]{1,0:T(8,128)} %copy-done.4) | copy-start | bytes 6291460
  197.6 23.0 %collective-permute-start.25 = (bf16[2,2,2,16,512]{4,3,2,0,1:T(8,128)(2,1)S(1)}, bf16[2,2,2,16,512]{4,3,2,0,1:T(8,128)(2,1)S(1)}, u32[]{:S(2)}, u32[]{:S(2)}) collective-permute-start(bf16[2,2,2,16,512]{4,3,2,0,1:T(8,128)(2,1)S(1)} %fusion.15), channel_id=1, source_target_pairs={{0,4},{2,6},{4,0},{6,2},{8,12},{10,14},{12,8},{14,10},{1,5},{3,7},... | collective-permute-start | bytes 393224 | tf_op jit(solution)/shard_map/ppermute | solution.py:17
  218.4 4.2 %copy-start.23 = (bf16[2,512,256]{2,1,0:T(8,128)(2,1)}, bf16[2,512,256]{2,1,0:T(8,128)(2,1)S(1)}, u32[]{:S(2)}) copy-start(bf16[2,512,256]{2,1,0:T(8,128)(2,1)S(1)} %collective-permute-done.27) | copy-start | bytes 1572868
  220.6 13.5 %copy-start.19 = (f32[512,512]{1,0:T(8,128)S(1)}, f32[512,512]{1,0:T(8,128)}, u32[]{:S(2)}) copy-start(f32[512,512]{1,0:T(8,128)} %fusion.7) | copy-start | bytes 3145732
  222.7 5.2 %collective-permute-start.29 = (bf16[2,1,2,16,512]{4,3,2,0,1:T(8,128)(2,1)S(1)}, bf16[2,1,2,16,512]{4,3,2,0,1:T(8,128)(2,1)S(1)}, u32[]{:S(2)}, u32[]{:S(2)}) collective-permute-start(bf16[2,1,2,16,512]{4,3,2,0,1:T(8,128)(2,1)S(1)} %dynamic-slice_convert_fusion.2), channel_id=1, source_target_pairs={{0,8},{2,10},{4,12},{6,14},{8,0},{10,2},{12,4},{14,6},{1,9},{3,11}... | collective-permute-start | bytes 196616 | tf_op jit(solution)/shard_map/ppermute | solution.py:17
  228.0 5.1 %collective-permute-start.30 = (f32[2,2,1,16,512]{4,3,2,1,0:T(8,128)S(1)}, f32[2,2,1,16,512]{4,3,2,1,0:T(8,128)}, u32[]{:S(2)}, u32[]{:S(2)}) collective-permute-start(f32[2,2,1,16,512]{4,3,2,1,0:T(8,128)S(1)} %fusion.16), channel_id=1, source_target_pairs={{0,1},{1,0},{2,3},{3,2},{4,5},{5,4},{6,7},{7,6},{8,9},{9,8},{10,11... | collective-permute-start | bytes 393224 | tf_op jit(solution)/shard_map/ppermute | solution.py:17
  229.5 12.2 %collective-permute-start.32 = (bf16[1,512,256]{2,1,0:T(8,128)(2,1)}, bf16[1,512,256]{2,1,0:T(8,128)(2,1)}, u32[]{:S(2)}, u32[]{:S(2)}) collective-permute-start(bf16[1,512,256]{2,1,0:T(8,128)(2,1)} %fusion.12), channel_id=1, source_target_pairs={{0,8},{2,10},{4,12},{6,14},{8,0},{10,2},{12,4},{14,6},{1,9},{3,11}... | collective-permute-start | bytes 786440 | tf_op jit(solution)/shard_map/ppermute | solution.py:17
  235.0 4.2 %collective-permute-start.31 = (bf16[51,512]{1,0:T(8,128)(2,1)S(1)}, bf16[51,512]{1,0:T(8,128)(2,1)S(1)}, u32[]{:S(2)}, u32[]{:S(2)}) collective-permute-start(bf16[51,512]{1,0:T(8,128)(2,1)S(1)} %pad_maximum_fusion.8), channel_id=1, source_target_pairs={{0,1},{1,0},{2,3},{3,2},{4,5},{5,4},{6,7},{7,6},{8,9},{9,8},{10,11... | collective-permute-start | bytes 156680 | tf_op jit(solution)/shard_map/ppermute | solution.py:17
  236.6 16.0 %collective-permute-start.33 = (bf16[2,512,256]{2,1,0:T(8,128)(2,1)}, bf16[2,512,256]{2,1,0:T(8,128)(2,1)S(1)}, u32[]{:S(2)}, u32[]{:S(2)}) collective-permute-start(bf16[2,512,256]{2,1,0:T(8,128)(2,1)} %fusion.10), channel_id=1, source_target_pairs={{0,4},{2,6},{4,0},{6,2},{8,12},{10,14},{12,8},{14,10},{1,5},{3,7},... | collective-permute-start | bytes 1572872 | tf_op jit(solution)/shard_map/ppermute | solution.py:17
  255.2 7.5 %collective-permute-start.34 = (bf16[99,512]{1,0:T(8,128)(2,1)S(1)}, bf16[99,512]{1,0:T(8,128)(2,1)S(1)}, u32[]{:S(2)}, u32[]{:S(2)}) collective-permute-start(bf16[99,512]{1,0:T(8,128)(2,1)S(1)} %pad_maximum_fusion.7), channel_id=1, source_target_pairs={{0,8},{2,10},{4,12},{6,14},{8,0},{10,2},{12,4},{14,6},{1,9},{3,11}... | collective-permute-start | bytes 304136 | tf_op jit(solution)/shard_map/ppermute | solution.py:17
  262.8 7.1 %collective-permute-start.35 = (bf16[195,512]{1,0:T(8,128)(2,1)S(1)}, bf16[195,512]{1,0:T(8,128)(2,1)S(1)}, u32[]{:S(2)}, u32[]{:S(2)}) collective-permute-start(bf16[195,512]{1,0:T(8,128)(2,1)S(1)} %pad_maximum_fusion.6), channel_id=1, source_target_pairs={{0,4},{2,6},{4,0},{6,2},{8,12},{10,14},{12,8},{14,10},{1,5},{3,7},... | collective-permute-start | bytes 599048 | tf_op jit(solution)/shard_map/ppermute | solution.py:17
  270.7 10.5 %collective-permute-start.36 = (bf16[387,512]{1,0:T(8,128)(2,1)S(1)}, bf16[387,512]{1,0:T(8,128)(2,1)}, u32[]{:S(2)}, u32[]{:S(2)}) collective-permute-start(bf16[387,512]{1,0:T(8,128)(2,1)S(1)} %pad_maximum_fusion.5), channel_id=1, source_target_pairs={{0,16},{16,0},{1,17},{17,1},{2,18},{18,2},{3,19},{19,3},{4,20},{20... | collective-permute-start | bytes 1188872 | tf_op jit(solution)/shard_map/ppermute | solution.py:17
  271.6 13.8 %collective-permute-start.37 = (bf16[1,512,256]{2,1,0:T(8,128)(2,1)}, bf16[1,512,256]{2,1,0:T(8,128)(2,1)S(1)}, u32[]{:S(2)}, u32[]{:S(2)}) collective-permute-start(bf16[1,512,256]{2,1,0:T(8,128)(2,1)} %fusion.14), channel_id=1, source_target_pairs={{0,8},{2,10},{4,12},{6,14},{8,0},{10,2},{12,4},{14,6},{1,9},{3,11}... | collective-permute-start | bytes 786440 | tf_op jit(solution)/shard_map/ppermute | solution.py:17
  282.3 5.8 %copy-start.27 = (f32[1,512]{1,0:T(1,128)S(1)}, f32[1,512]{1,0:T(1,128)}, u32[]{:S(2)}) copy-start(f32[1,512]{1,0:T(1,128)} %copy-done.26) | copy-start | bytes 6148
  288.2 2.4 collective-permute-start.38
  291.8 1.0 copy-start.22
  293.1 1.5 copy-start.21
  (4 other events, 2.9 us)

commit v10 on v5

--- a/solution.py
+++ b/solution.py
@@ -276,17 +276,17 @@
         piece, squares = double(piece, squares, 4, pole, bit, swap_pole)
     while not last.done():
         piece = after(piece, last.step(piece))
+    piece, second = lax.optimization_barrier((piece, early.result(piece)))
     for bit in reversed(range(zs.bit_length() - 1)):
         piece, squares = double(piece, squares, 2, z, bit, swap_z)
+    piece, *second = lax.optimization_barrier((piece, second, last.result(piece)))
     for bit in reversed(range(n_row.bit_length() - 1)):
         piece, squares = double(piece, squares, 1, row, bit, swap_row)
-    second = jnp.concatenate([early.result(), last.result()], axis=1)
-    piece = after(piece, second)
     piece, squares = double(piece, squares, 3, core, 0, swap_core)
     scale = jnp.sqrt(squares / (rows * n_row) + 1e-06)
     piece = piece.reshape(3, width, width).astype(jnp.float32)
     scaled = piece[1] + piece[2] / (scale[:, None] * scale)
-    second = second / scale
+    second = jnp.concatenate(second, axis=1) / scale
     return jnp.stack([first.astype(jnp.bfloat16), second.astype(jnp.bfloat16)]), jnp.stack([piece[0], scaled])
 
 

time: 289 us -> 280 us (0.969)
  other arithmetic: 30.4 us -> 26.4 us
    unnamed x50 -> x46, local copies, waits for them, and re-layouts: 7.95 us -> 7.25 us
  transfers between devices with their start and end apart: 29 -> 29, of which waited for: 16 -> 15; matrix products, arithmetic and copies ran while one was open for 9% -> 9% of each run, Pallas kernels for 26% -> 26%
where the time goes in v10:
time: 280 us; the launch traced here: 279 us
  waiting for transfers between devices  131 us (47%)
  Pallas kernels  73.6 us (26%)
  starting transfers between devices  30.1 us (11%)
  other arithmetic  26.4 us (9%)
  local copies, waits for them, and re-layouts  16.4 us (6%)
    ppermute x26, waiting for transfers between devices, swap(): return lax.ppermute(x, axis, [(i, i ^ mask) for i in range(size)])  127 us
    pallas_call x8, Pallas kernels, product(): pl.pallas_call(kernel, out_shape=out_shape, grid_spec=pltpu.PrefetchScala...  73.6 us
    ppermute x26, starting transfers between devices, swap(): return lax.ppermute(x, axis, [(i, i ^ mask) for i in range(size)])  25.7 us
    convert_element_type x6, other arithmetic, step(): send = self.part(1, *deps).astype(jnp.bfloat16)  8.72 us
    unnamed x46, local copies, waits for them, and re-layouts  7.25 us
    dynamic_slice x2, local copies, waits for them, and re-layouts, body(): piece = lax.dynamic_slice(panel, (col % ratio * cols, 0), (cols, width))  6.16 us
  transfers between devices with their start and end apart: 29, of which 15 were waited for; matrix products, arithmetic and copies ran while one was open for 9% of the time, Pallas kernels for 26%

profile of v10, /device:TPU:0, one launch (start us, length us, event | category | flops | bytes accessed | tf_op | source)
XLA Modules:
  0.0 279.5 jit_solution(16139137060611931517)
XLA Ops:
  0.7 3.0 %dynamic-slice_bitcast_fusion.1 = bf16[2048,512]{1,0:T(8,128)(2,1)} fusion(bf16[1,8192,512]{2,1,0:T(8,128)(2,1)} %param.8, s32[]{:T(128)S(6)} %select_n.267), kind=kLoop, calls=%fused_computation.8 | loop fusion | bytes 4194308 | tf_op jit(solution)/shard_map/dynamic_slice | solution.py:216
  3.7 2.9 %collective-permute-start = (bf16[2048,512]{1,0:T(8,128)(2,1)}, bf16[2048,512]{1,0:T(8,128)(2,1)S(1)}, u32[]{:S(2)}, u32[]{:S(2)}) collective-permute-start(bf16[2048,512]{1,0:T(8,128)(2,1)} %dynamic-slice_bitcast_fusion.1), channel_id=1, source_target_pairs={{0,16},{16,0},{1,17},{17,1},{2,18},{18,2},{3,19},{19,3},{4,20},{20... | collective-permute-start | bytes 6291464 | tf_op jit(solution)/shard_map/ppermute | solution.py:15
  8.2 3.1 %dynamic-slice_bitcast_fusion = bf16[2048,512]{1,0:T(8,128)(2,1)} fusion(bf16[1,8192,512]{2,1,0:T(8,128)(2,1)} %param.9, s32[]{:T(128)S(6)} %select_n.267), kind=kLoop, calls=%fused_computation.7 | loop fusion | bytes 4194308 | tf_op jit(solution)/shard_map/dynamic_slice | solution.py:216
  11.3 41.2 %collective-permute-done = bf16[2048,512]{1,0:T(8,128)(2,1)S(1)} collective-permute-done((bf16[2048,512]{1,0:T(8,128)(2,1)}, bf16[2048,512]{1,0:T(8,128)(2,1)S(1)}, u32[]{:S(2)}, u32[]{:S(2)}) %collective-permute-start) | collective-permute-done | bytes 2097184 | tf_op jit(solution)/shard_map/ppermute | solution.py:15
  52.5 1.3 copy-done.17
  53.8 1.7 collective-permute-start.5
  55.5 2.2 broadcast_select_fusion.1.f_ref
  57.7 8.7 %shard_map.77 = (bf16[2048,256]{1,0:T(8,128)(2,1)}, bf16[2048,256]{1,0:T(8,128)(2,1)}) custom-call(s32[2]{0:T(128)S(1)} %pad_add_fusion.3.where_ref, f32[1]{0:T(128)} %copy.127.weight_ref, bf16[8192,2048]{1,0:T(8,128)(2,1)} %bitcast.155, bf16[16,4,2048]{2,1,0:T(4,128)(2,1)S(1)} %reshape_reshape.52.mask_ref, bf16[2048,512]{1,0:T(8,128)(2,1)S(1)} %broadcast_select_fusion.1.f_ref), custom_call_target="tpu_custom_call" | custom-call | flops 8388608 | bytes 1048576 | tf_op jit(solution)/shard_map/pallas_call | solution.py:171
  66.4 0.5 collective-permute-start.2
  67.0 7.7 %shard_map.78 = (bf16[2048,256]{1,0:T(8,128)(2,1)S(1)}, bf16[2048,256]{1,0:T(8,128)(2,1)S(1)}) custom-call(s32[2]{0:T(128)S(1)} %get-tuple-element.81.where_ref, f32[1]{0:T(128)} %copy.127.weight_ref, bf16[8192,2048]{1,0:T(8,128)(2,1)} %bitcast.156, bf16[16,4,2048]{2,1,0:T(4,128)(2,1)S(1)} %reshape_reshape.52.mask_ref, ...), custom_call_target="tpu_custom_call" | custom-call | flops 8388608 | bytes 1048576 | tf_op jit(solution)/shard_map/pallas_call | solution.py:171
  75.4 0.9 copy-done.1
  76.3 10.5 %shard_map.79 = (bf16[2048,512]{1,0:T(8,128)(2,1)}, f32[512,512]{1,0:T(8,128)S(1)}) custom-call(s32[2]{0:T(128)S(1)} %get-tuple-element.83.where_ref, f32[1]{0:T(128)} %copy.127.weight_ref, bf16[8192,2048]{1,0:T(8,128)(2,1)} %bitcast.157, bf16[16,4,2048]{2,1,0:T(4,128)(2,1)S(1)} %copy-done.1, bf16[2048,512]{1,0:T(8,128)(2,1)S(1)} %broadcast_select_fusion.1.f_ref, ...), custom_call_target="tpu_custom_call" | custom-call | flops 8388608 | bytes 1048576 | tf_op jit(solution)/shard_map/pallas_call | solution.py:171
  86.8 1.5 collective-permute-start.8
  88.4 9.2 %shard_map.80 = (f32[2048,512]{1,0:T(8,128)S(1)}, f32[512,512]{1,0:T(8,128)S(1)}) custom-call(s32[2]{0:T(128)S(1)} %pad_add_fusion.1.where_ref, f32[1]{0:T(128)} %copy.127.weight_ref, bf16[8192,2048]{1,0:T(8,128)(2,1)} %bitcast.158, bf16[16,4,2048]{2,1,0:T(4,128)(2,1)S(1)} %copy-done.2, bf16[2048,512]{1,0:T(8,128)(2,1)S(1)} %broadcast_select_fusion.1.f_ref, ...), custom_call_target="tpu_custom_call" | custom-call | flops 8388608 | bytes 1048576 | tf_op jit(solution)/shard_map/pallas_call | solution.py:171
  97.6 2.0 copy-done.3
  99.6 1.3 collective-permute-done.5
  100.9 2.2 broadcast_select_fusion.f_ref
  103.1 8.7 %shard_map.81 = (bf16[2048,256]{1,0:T(8,128)(2,1)}, bf16[2048,256]{1,0:T(8,128)(2,1)}) custom-call(s32[2]{0:T(128)S(1)} %pad_add_fusion.3.where_ref, f32[1]{0:T(128)} %copy.127.weight_ref, bf16[8192,2048]{1,0:T(8,128)(2,1)} %bitcast.159, bf16[16,4,2048]{2,1,0:T(4,128)(2,1)S(1)} %reshape_reshape.53.mask_ref, bf16[2048,512]{1,0:T(8,128)(2,1)S(1)} %broadcast_select_fusion.f_ref), custom_call_target="tpu_custom_call" | custom-call | flops 8388608 | bytes 1048576 | tf_op jit(solution)/shard_map/pallas_call | solution.py:171
  111.8 0.5 collective-permute-start.7
  112.3 8.7 %shard_map.82 = (bf16[2048,256]{1,0:T(8,128)(2,1)}, bf16[2048,256]{1,0:T(8,128)(2,1)}) custom-call(s32[2]{0:T(128)S(1)} %get-tuple-element.81.where_ref, f32[1]{0:T(128)} %copy.127.weight_ref, bf16[8192,2048]{1,0:T(8,128)(2,1)} %bitcast.160, bf16[16,4,2048]{2,1,0:T(4,128)(2,1)S(1)} %reshape_reshape.53.mask_ref, bf16[2048,512]{1,0:T(8,128)(2,1)S(1)} %broadcast_select_fusion.f_ref), custom_call_target="tpu_custom_call" | custom-call | flops 8388608 | bytes 1048576 | tf_op jit(solution)/shard_map/pallas_call | solution.py:171
  121.1 0.5 collective-permute-start.9
  121.6 10.5 %shard_map.83 = (bf16[2048,256]{1,0:T(8,128)(2,1)}, bf16[2048,256]{1,0:T(8,128)(2,1)S(1)}, f32[512,512]{1,0:T(8,128)S(1)}) custom-call(s32[2]{0:T(128)S(1)} %get-tuple-element.83.where_ref, f32[1]{0:T(128)} %copy.127.weight_ref, bf16[8192,2048]{1,0:T(8,128)(2,1)} %bitcast.161, bf16[16,4,2048]{2,1,0:T(4,128)(2,1)S(1)} %reshape_reshape.53.mask_ref, ...), custom_call_target="tpu_custom_call" | custom-call | flops 8388608 | bytes 1048576 | tf_op jit(solution)/shard_map/pallas_call | solution.py:171
  132.1 1.5 collective-permute-start.12
  133.6 1.1 collective-permute-done.8
  134.7 2.5 fusion.2
  137.3 9.6 %shard_map.84 = (f32[2048,256]{1,0:T(8,128)S(1)}, f32[2048,256]{1,0:T(8,128)S(1)}, f32[512,512]{1,0:T(8,128)S(1)}) custom-call(s32[2]{0:T(128)S(1)} %pad_add_fusion.1.where_ref, f32[1]{0:T(128)} %copy.127.weight_ref, bf16[8192,2048]{1,0:T(8,128)(2,1)} %bitcast.162, bf16[16,4,2048]{2,1,0:T(4,128)(2,1)S(1)} %reshape_reshape.53.mask_ref, ...), custom_call_target="tpu_custom_call" | custom-call | flops 8388608 | bytes 1048576 | tf_op jit(solution)/shard_map/pallas_call | solution.py:171
  146.9 1.3 copy-done.9
  148.2 1.4 copy-done.11
  149.6 0.9 fusion.12
  150.7 1.6 collective-permute-start.14
  152.3 0.7 collective-permute-done.11
  153.0 1.4 fusion.7
  154.4 3.1 %collective-permute-done.12 = bf16[2048,256]{1,0:T(8,128)(2,1)} collective-permute-done((bf16[2048,256]{1,0:T(8,128)(2,1)}, bf16[2048,256]{1,0:T(8,128)(2,1)}, u32[]{:S(2)}, u32[]{:S(2)}) %collective-permute-start.12) | collective-permute-done | bytes 1048608 | tf_op jit(solution)/shard_map/ppermute | solution.py:249
  157.5 2.0 fusion.10
  159.5 2.1 collective-permute-start.13
  161.7 15.0 %collective-permute-done.14 = bf16[2,512,512]{2,1,0:T(8,128)(2,1)} collective-permute-done((bf16[2,512,512]{2,1,0:T(8,128)(2,1)}, bf16[2,512,512]{2,1,0:T(8,128)(2,1)}, u32[]{:S(2)}, u32[]{:S(2)}) %collective-permute-start.14) | collective-permute-done | bytes 1048608 | tf_op jit(solution)/shard_map/ppermute | solution.py:15
  176.6 2.6 fusion.9
  179.4 1.7 collective-permute-start.15
  181.5 3.2 %collective-permute-start.18 = (bf16[1,512,512]{2,1,0:T(8,128)(2,1)}, bf16[1,512,512]{2,1,0:T(8,128)(2,1)S(1)}, u32[]{:S(2)}, u32[]{:S(2)}) collective-permute-start(bf16[1,512,512]{2,1,0:T(8,128)(2,1)} %fusion.9), channel_id=1, source_target_pairs={{0,8},{2,10},{4,12},{6,14},{8,0},{10,2},{12,4},{14,6},{1,9},{3,11}... | collective-permute-start | bytes 1572872 | tf_op jit(solution)/shard_map/ppermute | solution.py:15
  184.7 1.5 collective-permute-start.19
  186.2 11.6 %collective-permute-done.15 = bf16[2,2,2,16,512]{4,3,2,1,0:T(8,128)(2,1)S(1)} collective-permute-done((bf16[2,2,2,16,512]{4,3,2,1,0:T(8,128)(2,1)S(1)}, bf16[2,2,2,16,512]{4,3,2,1,0:T(8,128)(2,1)S(1)}, u32[]{:S(2)}, u32[]{:S(2)}) %collective-permute-start.15) | collective-permute-done | bytes 131104 | tf_op jit(solution)/shard_map/ppermute | solution.py:15
  197.8 0.7 collective-permute-start.16
  198.5 0.9 multiply_bitcast_fusion
  199.4 12.4 %collective-permute-done.16 = bf16[2,1,2,16,512]{4,3,2,1,0:T(8,128)(2,1)S(1)} collective-permute-done((bf16[2,1,2,16,512]{4,3,2,1,0:T(8,128)(2,1)S(1)}, bf16[2,1,2,16,512]{4,3,2,1,0:T(8,128)(2,1)S(1)}, u32[]{:S(2)}, u32[]{:S(2)}) %collective-permute-start.16) | collective-permute-done | bytes 65568 | tf_op jit(solution)/shard_map/ppermute | solution.py:15
  211.8 1.4 fusion.13
  213.3 2.7 convert_bitcast_fusion
  216.2 1.6 collective-permute-start.20
  217.8 2.7 collective-permute-start.22
  220.5 1.1 collective-permute-done.20
  221.7 1.6 collective-permute-start.21
  223.3 2.6 collective-permute-done.21
  226.1 7.0 %collective-permute-done.22 = bf16[2,512,256]{2,1,0:T(8,128)(2,1)S(1)} collective-permute-done((bf16[2,512,256]{2,1,0:T(8,128)(2,1)S(1)}, bf16[2,512,256]{2,1,0:T(8,128)(2,1)S(1)}, u32[]{:S(2)}, u32[]{:S(2)}) %collective-permute-start.22) | collective-permute-done | bytes 524320 | tf_op jit(solution)/shard_map/ppermute | solution.py:15
  233.1 1.3 add_bitcast_fusion.1
  234.5 2.8 collective-permute-start.24
  237.5 11.1 %collective-permute-done.24 = bf16[99,512]{1,0:T(8,128)(2,1)S(1)} collective-permute-done((bf16[99,512]{1,0:T(8,128)(2,1)S(1)}, bf16[99,512]{1,0:T(8,128)(2,1)S(1)}, u32[]{:S(2)}, u32[]{:S(2)}) %collective-permute-start.24) | collective-permute-done | bytes 101408 | tf_op jit(solution)/shard_map/ppermute | solution.py:15
  248.9 9.2 %collective-permute-done.25 = bf16[195,512]{1,0:T(8,128)(2,1)S(1)} collective-permute-done((bf16[195,512]{1,0:T(8,128)(2,1)S(1)}, bf16[195,512]{1,0:T(8,128)(2,1)S(1)}, u32[]{:S(2)}, u32[]{:S(2)}) %collective-permute-start.25) | collective-permute-done | bytes 199712 | tf_op jit(solution)/shard_map/ppermute | solution.py:15
  258.2 1.1 add_bitcast_fusion
  259.5 11.2 %collective-permute-done.27 = bf16[387,512]{1,0:T(8,128)(2,1)S(1)} collective-permute-done((bf16[387,512]{1,0:T(8,128)(2,1)S(1)}, bf16[387,512]{1,0:T(8,128)(2,1)S(1)}, u32[]{:S(2)}, u32[]{:S(2)}) %collective-permute-start.27) | collective-permute-done | bytes 396320 | tf_op jit(solution)/shard_map/ppermute | solution.py:15
  271.1 2.3 collective-permute-done.28
  273.4 0.7 convert_reduce_fusion
  274.1 1.2 slice.123
  275.8 0.6 fusion.34
  276.9 1.5 pad_maximum_fusion
  278.4 1.1 pad_maximum_fusion.1
  (130 shorter events, 5.3 us)
Async XLA Ops:
  0.6 6.0 %copy-start.22 = (s32[2,64,16]{1,2,0:T(8,128)S(1)}, s32[2,64,16]{1,2,0:T(8,128)}, u32[]{:S(2)}) copy-start(s32[2,64,16]{1,2,0:T(8,128)} %param.7) | copy-start | bytes 24580
  3.7 48.8 %collective-permute-start = (bf16[2048,512]{1,0:T(8,128)(2,1)}, bf16[2048,512]{1,0:T(8,128)(2,1)S(1)}, u32[]{:S(2)}, u32[]{:S(2)}) collective-permute-start(bf16[2048,512]{1,0:T(8,128)(2,1)} %dynamic-slice_bitcast_fusion.1), channel_id=1, source_target_pairs={{0,16},{16,0},{1,17},{17,1},{2,18},{18,2},{3,19},{19,3},{4,20},{20... | collective-permute-start | bytes 6291464 | tf_op jit(solution)/shard_map/ppermute | solution.py:15
  7.0 60.0 %copy-start = (bf16[16,4,2048]{2,1,0:T(4,128)(2,1)}, bf16[16,4,2048]{2,1,0:T(4,128)(2,1)S(1)}, u32[]{:S(2)}) copy-start(bf16[16,4,2048]{2,1,0:T(4,128)(2,1)S(1)} %reshape_reshape.52.mask_ref) | copy-start | bytes 786436
  52.5 1.3 copy-start.17
  53.8 47.1 %collective-permute-start.5 = (bf16[2048,512]{1,0:T(8,128)(2,1)}, bf16[2048,512]{1,0:T(8,128)(2,1)}, u32[]{:S(2)}, u32[]{:S(2)}) collective-permute-start(bf16[2048,512]{1,0:T(8,128)(2,1)} %dynamic-slice_bitcast_fusion), channel_id=1, source_target_pairs={{0,16},{16,0},{1,17},{17,1},{2,18},{18,2},{3,19},{19,3},{4,20},{20... | collective-permute-start | bytes 6291464 | tf_op jit(solution)/shard_map/ppermute | solution.py:15
  66.4 8.8 %collective-permute-start.1 = (bf16[2048,256]{1,0:T(8,128)(2,1)}, bf16[2048,256]{1,0:T(8,128)(2,1)}, u32[]{:S(2)}, u32[]{:S(2)}) collective-permute-start(bf16[2048,256]{1,0:T(8,128)(2,1)} %get-tuple-element.66), channel_id=1, source_target_pairs={{0,2},{2,0},{4,6},{6,4},{8,10},{10,8},{12,14},{14,12},{1,3},{3,1},... | collective-permute-start | bytes 3145736 | tf_op jit(solution)/shard_map/ppermute | solution.py:15
  66.4 8.8 %collective-permute-start.2 = (bf16[2048,256]{1,0:T(8,128)(2,1)}, bf16[2048,256]{1,0:T(8,128)(2,1)}, u32[]{:S(2)}, u32[]{:S(2)}) collective-permute-start(bf16[2048,256]{1,0:T(8,128)(2,1)} %get-tuple-element.70), channel_id=1, source_target_pairs={{0,2},{2,0},{4,6},{6,4},{8,10},{10,8},{12,14},{14,12},{1,3},{3,1},... | collective-permute-start | bytes 3145736 | tf_op jit(solution)/shard_map/ppermute | solution.py:15
  74.7 13.7 %collective-permute-start.3 = (bf16[2048,256]{1,0:T(8,128)(2,1)S(1)}, bf16[2048,256]{1,0:T(8,128)(2,1)S(1)}, u32[]{:S(2)}, u32[]{:S(2)}) collective-permute-start(bf16[2048,256]{1,0:T(8,128)(2,1)S(1)} %get-tuple-element.68), channel_id=1, source_target_pairs={{0,2},{2,0},{4,6},{6,4},{8,10},{10,8},{12,14},{14,12},{1,3},{3,1},... | collective-permute-start | bytes 3145736 | tf_op jit(solution)/shard_map/ppermute | solution.py:15
  74.8 13.7 %collective-permute-start.4 = (bf16[2048,256]{1,0:T(8,128)(2,1)S(1)}, bf16[2048,256]{1,0:T(8,128)(2,1)S(1)}, u32[]{:S(2)}, u32[]{:S(2)}) collective-permute-start(bf16[2048,256]{1,0:T(8,128)(2,1)S(1)} %get-tuple-element.74), channel_id=1, source_target_pairs={{0,2},{2,0},{4,6},{6,4},{8,10},{10,8},{12,14},{14,12},{1,3},{3,1},... | collective-permute-start | bytes 3145736 | tf_op jit(solution)/shard_map/ppermute | solution.py:15
  75.4 1.0 copy-start.1
  76.3 12.1 %copy-start.2 = (bf16[16,4,2048]{2,1,0:T(4,128)(2,1)S(1)}, bf16[16,4,2048]{2,1,0:T(4,128)(2,1)}, u32[]{:S(2)}) copy-start(bf16[16,4,2048]{2,1,0:T(4,128)(2,1)} %copy-done) | copy-start | bytes 786436
  86.8 47.9 %collective-permute-start.8 = (bf16[2048,512]{1,0:T(8,128)(2,1)}, bf16[2048,512]{1,0:T(8,128)(2,1)}, u32[]{:S(2)}, u32[]{:S(2)}) collective-permute-start(bf16[2048,512]{1,0:T(8,128)(2,1)} %get-tuple-element.71), channel_id=1, source_target_pairs={{0,1},{1,0},{2,3},{3,2},{4,5},{5,4},{6,7},{7,6},{8,9},{9,8},{10,11... | collective-permute-start | bytes 6291464 | tf_op jit(solution)/shard_map/ppermute | solution.py:249
  97.6 2.0 copy-start.3
  99.6 3.5 %copy-start.5 = (f32[512,512]{1,0:T(8,128)}, f32[512,512]{1,0:T(8,128)S(1)}, u32[]{:S(2)}) copy-start(f32[512,512]{1,0:T(8,128)S(1)} %get-tuple-element.76) | copy-start | bytes 3145732
  111.8 9.8 %collective-permute-start.6 = (bf16[2048,256]{1,0:T(8,128)(2,1)}, bf16[2048,256]{1,0:T(8,128)(2,1)}, u32[]{:S(2)}, u32[]{:S(2)}) collective-permute-start(bf16[2048,256]{1,0:T(8,128)(2,1)} %get-tuple-element.80), channel_id=1, source_target_pairs={{0,2},{2,0},{4,6},{6,4},{8,10},{10,8},{12,14},{14,12},{1,3},{3,1},... | collective-permute-start | bytes 3145736 | tf_op jit(solution)/shard_map/ppermute | solution.py:15
  111.8 9.8 %collective-permute-start.7 = (bf16[2048,256]{1,0:T(8,128)(2,1)}, bf16[2048,256]{1,0:T(8,128)(2,1)}, u32[]{:S(2)}, u32[]{:S(2)}) collective-permute-start(bf16[2048,256]{1,0:T(8,128)(2,1)} %get-tuple-element.84), channel_id=1, source_target_pairs={{0,2},{2,0},{4,6},{6,4},{8,10},{10,8},{12,14},{14,12},{1,3},{3,1},... | collective-permute-start | bytes 3145736 | tf_op jit(solution)/shard_map/ppermute | solution.py:15
  121.1 16.2 %collective-permute-start.10 = (bf16[2048,256]{1,0:T(8,128)(2,1)}, bf16[2048,256]{1,0:T(8,128)(2,1)}, u32[]{:S(2)}, u32[]{:S(2)}) collective-permute-start(bf16[2048,256]{1,0:T(8,128)(2,1)} %get-tuple-element.88), channel_id=1, source_target_pairs={{0,2},{2,0},{4,6},{6,4},{8,10},{10,8},{12,14},{14,12},{1,3},{3,1},... | collective-permute-start | bytes 3145736 | tf_op jit(solution)/shard_map/ppermute | solution.py:15
  121.1 16.2 %collective-permute-start.9 = (bf16[2048,256]{1,0:T(8,128)(2,1)}, bf16[2048,256]{1,0:T(8,128)(2,1)}, u32[]{:S(2)}, u32[]{:S(2)}) collective-permute-start(bf16[2048,256]{1,0:T(8,128)(2,1)} %get-tuple-element.82), channel_id=1, source_target_pairs={{0,2},{2,0},{4,6},{6,4},{8,10},{10,8},{12,14},{14,12},{1,3},{3,1},... | collective-permute-start | bytes 3145736 | tf_op jit(solution)/shard_map/ppermute | solution.py:15
  121.6 13.1 %copy-start.4 = (f32[2048,512]{1,0:T(8,128)S(1)}, f32[2048,512]{1,0:T(8,128)}, u32[]{:S(2)}) copy-start(f32[2048,512]{1,0:T(8,128)} %copy-done.3) | copy-start | bytes 12582916
  132.1 5.1 %copy-start.13 = (bf16[2048,256]{1,0:T(8,128)(2,1)}, bf16[2048,256]{1,0:T(8,128)(2,1)S(1)}, u32[]{:S(2)}) copy-start(bf16[2048,256]{1,0:T(8,128)(2,1)S(1)} %get-tuple-element.106) | copy-start | bytes 3145732
  132.1 25.4 %collective-permute-start.12 = (bf16[2048,256]{1,0:T(8,128)(2,1)}, bf16[2048,256]{1,0:T(8,128)(2,1)}, u32[]{:S(2)}, u32[]{:S(2)}) collective-permute-start(bf16[2048,256]{1,0:T(8,128)(2,1)} %get-tuple-element.85), channel_id=1, source_target_pairs={{0,1},{1,0},{2,3},{3,2},{4,5},{5,4},{6,7},{7,6},{8,9},{9,8},{10,11... | collective-permute-start | bytes 3145736 | tf_op jit(solution)/shard_map/ppermute | solution.py:249
  137.3 12.3 %copy-start.6 = (f32[512,512]{1,0:T(8,128)S(1)}, f32[512,512]{1,0:T(8,128)}, u32[]{:S(2)}) copy-start(f32[512,512]{1,0:T(8,128)} %copy-done.5) | copy-start | bytes 3145732
  146.9 1.3 copy-start.9
  148.2 1.4 copy-start.11
  149.6 1.1 copy-start.8
  149.6 3.4 %copy-start.7 = (f32[512,512]{1,0:T(8,128)S(1)}, f32[512,512]{1,0:T(8,128)}, u32[]{:S(2)}) copy-start(f32[512,512]{1,0:T(8,128)} %copy-done.5) | copy-start | bytes 3145732
  150.7 6.8 %copy-start.12 = (f32[2048,256]{1,0:T(8,128)S(1)}, f32[2048,256]{1,0:T(8,128)}, u32[]{:S(2)}) copy-start(f32[2048,256]{1,0:T(8,128)} %copy-done.11) | copy-start | bytes 6291460
  150.7 2.3 collective-permute-start.11
  150.7 25.9 %collective-permute-start.14 = (bf16[2,512,512]{2,1,0:T(8,128)(2,1)}, bf16[2,512,512]{2,1,0:T(8,128)(2,1)}, u32[]{:S(2)}, u32[]{:S(2)}) collective-permute-start(bf16[2,512,512]{2,1,0:T(8,128)(2,1)} %fusion.2), channel_id=1, source_target_pairs={{0,4},{2,6},{4,0},{6,2},{8,12},{10,14},{12,8},{14,10},{1,5},{3,7},... | collective-permute-start | bytes 3145736 | tf_op jit(solution)/shard_map/ppermute | solution.py:15
  154.4 5.1 %copy-start.15 = (f32[2,2,4,2,16,512]{5,4,3,2,0,1:T(8,128)}, f32[2,2,4,2,16,512]{5,4,3,2,0,1:T(8,128)S(1)}, u32[]{:S(2)}) copy-start(f32[2,2,4,2,16,512]{5,4,3,2,0,1:T(8,128)S(1)} %fusion.7) | copy-start | bytes 3145732
  159.5 19.7 %copy-start.16 = (f32[2,2,4,2,16,512]{5,4,3,2,0,1:T(8,128)S(1)}, f32[2,2,4,2,16,512]{5,4,3,2,0,1:T(8,128)}, u32[]{:S(2)}) copy-start(f32[2,2,4,2,16,512]{5,4,3,2,0,1:T(8,128)} %copy-done.15) | copy-start | bytes 3145732
  159.5 19.7 %collective-permute-start.13 = (bf16[2,1,4,2,16,512]{5,4,3,2,0,1:T(8,128)(2,1)S(1)}, bf16[2,1,4,2,16,512]{5,4,3,2,0,1:T(8,128)(2,1)S(1)}, u32[]{:S(2)}, u32[]{:S(2)}) collective-permute-start(bf16[2,1,4,2,16,512]{5,4,3,2,0,1:T(8,128)(2,1)S(1)} %dynamic-slice_convert_fusion), channel_id=1, source_target_pairs={{0,16},{16,0},{1,17},{17,1},{2,18},{18,2},{3,19},{19,3},{4,20},{20... | collective-permute-start | bytes 786440 | tf_op jit(solution)/shard_map/ppermute | solution.py:15
  176.6 8.1 %copy-start.14 = (bf16[2048,256]{1,0:T(8,128)(2,1)S(1)}, bf16[2048,256]{1,0:T(8,128)(2,1)}, u32[]{:S(2)}) copy-start(bf16[2048,256]{1,0:T(8,128)(2,1)} %copy-done.13) | copy-start | bytes 3145732
  179.4 18.4 %collective-permute-start.15 = (bf16[2,2,2,16,512]{4,3,2,1,0:T(8,128)(2,1)S(1)}, bf16[2,2,2,16,512]{4,3,2,1,0:T(8,128)(2,1)S(1)}, u32[]{:S(2)}, u32[]{:S(2)}) collective-permute-start(bf16[2,2,2,16,512]{4,3,2,1,0:T(8,128)(2,1)S(1)} %fusion.15), channel_id=1, source_target_pairs={{0,4},{2,6},{4,0},{6,2},{8,12},{10,14},{12,8},{14,10},{1,5},{3,7},... | collective-permute-start | bytes 393224 | tf_op jit(solution)/shard_map/ppermute | solution.py:15
  181.0 30.8 %collective-permute-start.17 = (bf16[2,512,256]{2,1,0:T(8,128)(2,1)}, bf16[2,512,256]{2,1,0:T(8,128)(2,1)S(1)}, u32[]{:S(2)}, u32[]{:S(2)}) collective-permute-start(bf16[2,512,256]{2,1,0:T(8,128)(2,1)} %fusion.10), channel_id=1, source_target_pairs={{0,4},{2,6},{4,0},{6,2},{8,12},{10,14},{12,8},{14,10},{1,5},{3,7},... | collective-permute-start | bytes 1572872 | tf_op jit(solution)/shard_map/ppermute | solution.py:15
  181.5 31.8 %collective-permute-start.18 = (bf16[1,512,512]{2,1,0:T(8,128)(2,1)}, bf16[1,512,512]{2,1,0:T(8,128)(2,1)S(1)}, u32[]{:S(2)}, u32[]{:S(2)}) collective-permute-start(bf16[1,512,512]{2,1,0:T(8,128)(2,1)} %fusion.9), channel_id=1, source_target_pairs={{0,8},{2,10},{4,12},{6,14},{8,0},{10,2},{12,4},{14,6},{1,9},{3,11}... | collective-permute-start | bytes 1572872 | tf_op jit(solution)/shard_map/ppermute | solution.py:15
  184.7 31.3 %collective-permute-start.19 = (bf16[2048,256]{1,0:T(8,128)(2,1)S(1)}, bf16[2048,256]{1,0:T(8,128)(2,1)S(1)}, u32[]{:S(2)}, u32[]{:S(2)}) collective-permute-start(bf16[2048,256]{1,0:T(8,128)(2,1)S(1)} %copy-done.14), channel_id=1, source_target_pairs={{0,1},{1,0},{2,3},{3,2},{4,5},{5,4},{6,7},{7,6},{8,9},{9,8},{10,11... | collective-permute-start | bytes 3145736 | tf_op jit(solution)/shard_map/ppermute | solution.py:249
  197.8 14.0 %collective-permute-start.16 = (bf16[2,1,2,16,512]{4,3,2,1,0:T(8,128)(2,1)S(1)}, bf16[2,1,2,16,512]{4,3,2,1,0:T(8,128)(2,1)S(1)}, u32[]{:S(2)}, u32[]{:S(2)}) collective-permute-start(bf16[2,1,2,16,512]{4,3,2,1,0:T(8,128)(2,1)S(1)} %dynamic-slice_convert_fusion.2), channel_id=1, source_target_pairs={{0,8},{2,10},{4,12},{6,14},{8,0},{10,2},{12,4},{14,6},{1,9},{3,11}... | collective-permute-start | bytes 196616 | tf_op jit(solution)/shard_map/ppermute | solution.py:15
  211.8 4.2 %copy-start.10 = (f32[2048,256]{1,0:T(8,128)S(1)}, f32[2048,256]{1,0:T(8,128)}, u32[]{:S(2)}) copy-start(f32[2048,256]{1,0:T(8,128)} %copy-done.9) | copy-start | bytes 6291460
  213.2 19.9 %collective-permute-start.23 = (bf16[1,512,256]{2,1,0:T(8,128)(2,1)S(1)}, bf16[1,512,256]{2,1,0:T(8,128)(2,1)S(1)}, u32[]{:S(2)}, u32[]{:S(2)}) collective-permute-start(bf16[1,512,256]{2,1,0:T(8,128)(2,1)S(1)} %fusion.13), channel_id=1, source_target_pairs={{0,8},{2,10},{4,12},{6,14},{8,0},{10,2},{12,4},{14,6},{1,9},{3,11}... | collective-permute-start | bytes 786440 | tf_op jit(solution)/shard_map/ppermute | solution.py:15
  216.0 17.1 %copy-start.19 = (bf16[2048,256]{1,0:T(8,128)(2,1)}, bf16[2048,256]{1,0:T(8,128)(2,1)S(1)}, u32[]{:S(2)}) copy-start(bf16[2048,256]{1,0:T(8,128)(2,1)S(1)} %collective-permute-done.19) | copy-start | bytes 3145732
  216.2 5.4 %collective-permute-start.20 = (f32[2,2,1,16,512]{4,3,2,1,0:T(8,128)S(1)}, f32[2,2,1,16,512]{4,3,2,1,0:T(8,128)S(1)}, u32[]{:S(2)}, u32[]{:S(2)}) collective-permute-start(f32[2,2,1,16,512]{4,3,2,1,0:T(8,128)S(1)} %fusion.16), channel_id=1, source_target_pairs={{0,1},{1,0},{2,3},{3,2},{4,5},{5,4},{6,7},{7,6},{8,9},{9,8},{10,11... | collective-permute-start | bytes 393224 | tf_op jit(solution)/shard_map/ppermute | solution.py:15
  217.8 15.2 %collective-permute-start.22 = (bf16[2,512,256]{2,1,0:T(8,128)(2,1)S(1)}, bf16[2,512,256]{2,1,0:T(8,128)(2,1)S(1)}, u32[]{:S(2)}, u32[]{:S(2)}) collective-permute-start(bf16[2,512,256]{2,1,0:T(8,128)(2,1)S(1)} %fusion.11), channel_id=1, source_target_pairs={{0,4},{2,6},{4,0},{6,2},{8,12},{10,14},{12,8},{14,10},{1,5},{3,7},... | collective-permute-start | bytes 1572872 | tf_op jit(solution)/shard_map/ppermute | solution.py:15
  221.7 4.2 %collective-permute-start.21 = (bf16[51,512]{1,0:T(8,128)(2,1)S(1)}, bf16[51,512]{1,0:T(8,128)(2,1)S(1)}, u32[]{:S(2)}, u32[]{:S(2)}) collective-permute-start(bf16[51,512]{1,0:T(8,128)(2,1)S(1)} %pad_maximum_fusion.6), channel_id=1, source_target_pairs={{0,1},{1,0},{2,3},{3,2},{4,5},{5,4},{6,7},{7,6},{8,9},{9,8},{10,11... | collective-permute-start | bytes 156680 | tf_op jit(solution)/shard_map/ppermute | solution.py:15
  233.0 1.4 copy-start.20
  234.5 14.1 %collective-permute-start.24 = (bf16[99,512]{1,0:T(8,128)(2,1)S(1)}, bf16[99,512]{1,0:T(8,128)(2,1)S(1)}, u32[]{:S(2)}, u32[]{:S(2)}) collective-permute-start(bf16[99,512]{1,0:T(8,128)(2,1)S(1)} %pad_maximum_fusion.5), channel_id=1, source_target_pairs={{0,8},{2,10},{4,12},{6,14},{8,0},{10,2},{12,4},{14,6},{1,9},{3,11}... | collective-permute-start | bytes 304136 | tf_op jit(solution)/shard_map/ppermute | solution.py:15
  237.3 20.9 %copy-start.21 = (bf16[2,512,256]{2,1,0:T(8,128)(2,1)S(1)}, bf16[2,512,256]{2,1,0:T(8,128)(2,1)}, u32[]{:S(2)}) copy-start(bf16[2,512,256]{2,1,0:T(8,128)(2,1)} %copy-done.20) | copy-start | bytes 1572868
  237.3 20.9 %collective-permute-start.26 = (bf16[1,512,256]{2,1,0:T(8,128)(2,1)S(1)}, bf16[1,512,256]{2,1,0:T(8,128)(2,1)S(1)}, u32[]{:S(2)}, u32[]{:S(2)}) collective-permute-start(bf16[1,512,256]{2,1,0:T(8,128)(2,1)S(1)} %fusion.14), channel_id=1, source_target_pairs={{0,8},{2,10},{4,12},{6,14},{8,0},{10,2},{12,4},{14,6},{1,9},{3,11}... | collective-permute-start | bytes 786440 | tf_op jit(solution)/shard_map/ppermute | solution.py:15
  248.8 9.3 %collective-permute-start.25 = (bf16[195,512]{1,0:T(8,128)(2,1)S(1)}, bf16[195,512]{1,0:T(8,128)(2,1)S(1)}, u32[]{:S(2)}, u32[]{:S(2)}) collective-permute-start(bf16[195,512]{1,0:T(8,128)(2,1)S(1)} %pad_maximum_fusion.4), channel_id=1, source_target_pairs={{0,4},{2,6},{4,0},{6,2},{8,12},{10,14},{12,8},{14,10},{1,5},{3,7},... | collective-permute-start | bytes 599048 | tf_op jit(solution)/shard_map/ppermute | solution.py:15
  259.4 11.3 %collective-permute-start.27 = (bf16[387,512]{1,0:T(8,128)(2,1)S(1)}, bf16[387,512]{1,0:T(8,128)(2,1)S(1)}, u32[]{:S(2)}, u32[]{:S(2)}) collective-permute-start(bf16[387,512]{1,0:T(8,128)(2,1)S(1)} %pad_maximum_fusion.3), channel_id=1, source_target_pairs={{0,16},{16,0},{1,17},{17,1},{2,18},{18,2},{3,19},{19,3},{4,20},{20... | collective-permute-start | bytes 1188872 | tf_op jit(solution)/shard_map/ppermute | solution.py:15
  270.9 2.5 collective-permute-start.28
  276.9 1.5 copy-start.18
